TPU v7x, 32 devices: a whole 2x2x4 slice. The times are simulated.
32 devices in a mesh: expert: 8 (over y, x, core), hidden: 4 (over z).
Axes of the slice: x: 2, y: 2, z: 4, core: 2. Of those that a mesh axis runs over, the one named last changes fastest.
Arguments:
- tokens: bfloat16 [2, 32, 512, 768], P(None, ('expert', 'hidden')), may hold values from -6 to 6
- cotangent: bfloat16 [2, 32, 512, 768], P(None, ('expert', 'hidden')), may hold values from -6 to 6
- lengths: int32 [2, 32], P(None, ('expert', 'hidden')), may hold values from 256 to 512
- routes: int32 [2, 32, 512, 1], P(None, ('expert', 'hidden')), may hold values from 0 to 63
- gain_attn: float32 [768], replicated, may hold values from 0.1 to 1.9
- w_query: bfloat16 [768, 768], replicated, may hold values from -0.21875 to 0.21875
- w_key: bfloat16 [768, 768], replicated, may hold values from -0.21875 to 0.21875
- w_value: bfloat16 [768, 768], replicated, may hold values from -0.21875 to 0.21875
- w_output: bfloat16 [768, 768], replicated, may hold values from -1.75 to 1.75
- bucket_head_bias: float32 [32, 12], replicated, may hold values from -4 to 4
- gain_ffn: float32 [768], replicated, may hold values from 0.1 to 1.9
- w_router: bfloat16 [768, 64], replicated, may hold values from -0.107910156 to 0.107910156
- w_inner: bfloat16 [64, 768, 3072], P('expert', None, 'hidden'), may hold values from -0.21875 to 0.21875
- w_outer: bfloat16 [64, 3072, 768], P('expert', 'hidden'), may hold values from -10.375 to 10.375
Outputs:
- layer_out: bfloat16 [2, 32, 512, 768], P(None, ('expert', 'hidden'))
- tokens_grad: bfloat16 [2, 32, 512, 768], P(None, ('expert', 'hidden'))
- gain_attn_grad: float32 [768], replicated
- query_grad: float32 [768, 768], replicated
- key_grad: float32 [768, 768], replicated
- value_grad: float32 [768, 768], replicated
- output_grad: float32 [768, 768], replicated
- bias_grad: float32 [32, 12], replicated
- gain_ffn_grad: float32 [768], replicated
- router_grad: float32 [768, 64], replicated
- inner_grad: float32 [64, 768, 3072], P('expert', None, 'hidden')
- outer_grad: float32 [64, 3072, 768], P('expert', 'hidden')
All inputs are finite; a program needn't handle non-finite values.
Results may differ from a plain program's by a relative error of at most 0.018.
Values may be sent and summed in bfloat16 or wider, within the bound.
No kernel may reach another device: no remote copies, remote signals or barrier semaphores. Data moves between devices by JAX's collectives and lax.ppermute only.
A program may use at most 320 MiB of HBM per device.

v0:
```python
import jax
import jax.numpy as jnp
import numpy as np
from jax import lax
from jax.sharding import PartitionSpec as P

HEADS = 12
HEAD_DIM = 64
BUCKETS = 32
MAXDIST = 128


epsilon = 1e-06
negative = -1e30


def bucket_table(length):
    offsets = np.arange(length)[None, :] - np.arange(length)[:, None]
    halfway = BUCKETS // 2
    exact_count = halfway // 2
    relative_distance = np.abs(offsets)
    scaled = (
        np.log(np.maximum(relative_distance, 1) / exact_count)
        / np.log(MAXDIST / exact_count)
        * (halfway - exact_count)
    )
    far_bucket = np.minimum(exact_count + np.floor(scaled).astype(np.int64), halfway - 1)
    near_bucket = np.where(relative_distance < exact_count, relative_distance, far_bucket)
    return (np.where(offsets > 0, halfway, 0) + near_bucket).astype(np.int32)


def rms_norm(values, gain_vector):
    return (
        values
        * lax.rsqrt(jnp.mean(values * values, axis=-1, keepdims=True) + epsilon)
        * gain_vector
    )


def block_scores(queries, key_heads, position_bias_heads, true_mask, first_row, block_rows):
    query_heads = queries.reshape(block_rows, HEADS, HEAD_DIM)
    bias_block = lax.dynamic_slice_in_dim(position_bias_heads, first_row, block_rows, 1)
    scores = jnp.einsum(
        "qhc,khc->hqk", query_heads, key_heads, preferred_element_type=jnp.float32
    ) * HEAD_DIM ** (-0.5)
    scores = jnp.where(true_mask[None, None, :], scores + bias_block, negative)
    return (query_heads, scores)


def attention_forward(queries, key_rows, value_rows, position_bias_heads, true_mask):
    length = queries.shape[0]
    block_rows = min(length, 512)
    key_heads = key_rows.reshape(length, HEADS, HEAD_DIM)
    value_heads = value_rows.reshape(length, HEADS, HEAD_DIM)

    def one_block(first_row):
        query_heads, scores = block_scores(
            queries, key_heads, position_bias_heads, true_mask, first_row, block_rows
        )
        highest = jnp.max(scores, axis=-1, keepdims=True)
        log_total = highest + jnp.log(jnp.sum(jnp.exp(scores - highest), axis=-1, keepdims=True))
        weight_tensors = jnp.exp(scores - log_total).astype(jnp.bfloat16)
        mixed = jnp.einsum(
            "hqk,khc->qhc", weight_tensors, value_heads, preferred_element_type=jnp.float32
        )
        return (mixed.reshape(block_rows, HEADS * HEAD_DIM).astype(jnp.bfloat16), log_total)

    block_starts = jnp.arange(length // block_rows, dtype=jnp.int32) * block_rows
    mixed, log_totals = lax.map(one_block, block_starts)
    return (mixed.reshape(length, HEADS * HEAD_DIM), log_totals)


def attention_backward(
    queries,
    key_rows,
    value_rows,
    position_bias_heads,
    true_mask,
    log_totals,
    mixed_grad,
    expert_selector,
):
    length = queries.shape[0]
    model_width = HEADS * HEAD_DIM
    block_rows = min(length, 512)
    key_heads = key_rows.reshape(length, HEADS, HEAD_DIM)
    value_heads = value_rows.reshape(length, HEADS, HEAD_DIM)
    score_scale = HEAD_DIM ** (-0.5)

    def one_back(carry, packed):
        key_total, value_total, bias_total = carry
        first_row, log_total = packed
        query_heads, scores = block_scores(
            queries, key_heads, position_bias_heads, true_mask, first_row, block_rows
        )
        grad_heads = mixed_grad.reshape(block_rows, HEADS, HEAD_DIM)
        selector_block = lax.dynamic_slice_in_dim(expert_selector, first_row, block_rows, 1)
        attn_probs = jnp.exp(scores - log_total)
        prob_grad = jnp.einsum(
            "qhc,khc->hqk", grad_heads, value_heads, preferred_element_type=jnp.float32
        )
        inner_sum = jnp.sum(attn_probs * prob_grad, axis=-1, keepdims=True)
        score_grad = (attn_probs * (prob_grad - inner_sum)).astype(jnp.bfloat16)
        query_part = (
            jnp.einsum("hqk,khc->qhc", score_grad, key_heads, preferred_element_type=jnp.float32)
            * score_scale
        )
        key_part = (
            jnp.einsum("hqk,qhc->khc", score_grad, query_heads, preferred_element_type=jnp.float32)
            * score_scale
        )
        value_part = jnp.einsum(
            "hqk,qhc->khc",
            attn_probs.astype(jnp.bfloat16),
            grad_heads,
            preferred_element_type=jnp.float32,
        )
        bias_part = jnp.einsum(
            "eoi,poi->pe",
            score_grad.astype(jnp.float32),
            selector_block,
            precision=lax.Precision.HIGHEST,
        )
        carry = (
            key_total + key_part.reshape(length, model_width),
            value_total + value_part.reshape(length, model_width),
            bias_total + bias_part,
        )
        return (carry, query_part.reshape(block_rows, model_width))

    block_starts = jnp.arange(length // block_rows, dtype=jnp.int32) * block_rows
    initial = (
        jnp.zeros((length, model_width), jnp.float32),
        jnp.zeros((length, model_width), jnp.float32),
        jnp.zeros((BUCKETS, HEADS), jnp.float32),
    )
    carry, query_parts = lax.scan(one_back, initial, (block_starts, log_totals))
    return (query_parts.reshape(length, model_width), carry[0], carry[1], carry[2])


def expert_forward(gathered, w_inner):
    pre_act = jnp.einsum("secd,edf->secf", gathered, w_inner, preferred_element_type=jnp.float32)
    return (pre_act, jax.nn.gelu(pre_act).astype(jnp.bfloat16))


def expert_backward(gathered, grad_gathered, pre_act, activation, w_outer):
    outer_part = jnp.einsum(
        "secf,secd->efd", activation, grad_gathered, preferred_element_type=jnp.float32
    )
    act_grad = jnp.einsum(
        "secd,efd->secf", grad_gathered, w_outer, preferred_element_type=jnp.float32
    )
    pre_grad = jax.vjp(jax.nn.gelu, pre_act)[1](act_grad)[0].astype(jnp.bfloat16)
    inner_part = jnp.einsum(
        "secd,secf->edf", gathered, pre_grad, preferred_element_type=jnp.float32
    )
    return (outer_part, inner_part, pre_grad)


def shards(
    tokens,
    cotangent,
    lengths,
    routes,
    gain_attn,
    w_query,
    w_key,
    w_value,
    w_output,
    bucket_head_bias,
    gain_ffn,
    w_router,
    w_inner,
    w_outer,
):
    batches = tokens.shape[0]
    length = tokens.shape[2]
    model_width = tokens.shape[3]
    experts = w_router.shape[1]
    local_experts = w_inner.shape[0]
    expert_count = lax.axis_size("expert")
    capacity = (5 * length + 4 * experts - 1) // (4 * experts)
    slot_count = experts * capacity
    slot_shape = (expert_count, local_experts, capacity, model_width)
    bucket_ids = jnp.asarray(bucket_table(length))
    expert_selector = (
        bucket_ids[None, :, :] == jnp.arange(BUCKETS, dtype=jnp.int32)[:, None, None]
    ).astype(jnp.float32)
    position_bias_heads = jnp.einsum(
        "jua,jy->yua", expert_selector, bucket_head_bias, precision=lax.Precision.HIGHEST
    )
    positions = jnp.arange(length, dtype=jnp.int32)
    lower_ones = (positions[:, None] > positions[None, :]).astype(jnp.bfloat16)
    slot_ids = jnp.arange(slot_count, dtype=jnp.int32)
    expert_ids = jnp.arange(experts, dtype=jnp.int32)
    shared = (
        jnp.zeros_like(gain_attn),
        jnp.zeros(w_query.shape, jnp.float32),
        jnp.zeros(w_key.shape, jnp.float32),
        jnp.zeros(w_value.shape, jnp.float32),
        jnp.zeros(w_output.shape, jnp.float32),
        jnp.zeros_like(bucket_head_bias),
        jnp.zeros_like(gain_ffn),
        jnp.zeros(w_router.shape, jnp.float32),
    )
    inner_total = jnp.zeros(w_inner.shape, jnp.float32)
    outer_total = jnp.zeros(w_outer.shape, jnp.float32)
    layer_rows = []
    token_grads = []
    for batch_index in range(batches):
        hidden_in = tokens[batch_index, 0].astype(jnp.float32)
        upstream = cotangent[batch_index, 0].astype(jnp.float32)
        true_mask = positions < lengths[batch_index, 0]
        token_route = routes[batch_index, 0, :, 0]
        normed_attn, norm_attn_back = jax.vjp(rms_norm, hidden_in, gain_attn)
        normed_low = normed_attn.astype(jnp.bfloat16)
        queries = jnp.dot(normed_low, w_query, preferred_element_type=jnp.float32).astype(
            jnp.bfloat16
        )
        key_rows = jnp.dot(normed_low, w_key, preferred_element_type=jnp.float32).astype(
            jnp.bfloat16
        )
        value_rows = jnp.dot(normed_low, w_value, preferred_element_type=jnp.float32).astype(
            jnp.bfloat16
        )
        mixed, log_totals = attention_forward(
            queries, key_rows, value_rows, position_bias_heads, true_mask
        )
        residual = hidden_in + jnp.dot(mixed, w_output, preferred_element_type=jnp.float32)
        normed_ffn, norm_ffn_back = jax.vjp(rms_norm, residual, gain_ffn)
        routed = normed_ffn.astype(jnp.bfloat16)
        router_logits = jnp.dot(routed, w_router, preferred_element_type=jnp.float32)
        router_probs = jax.nn.softmax(router_logits, axis=-1)
        chosen = token_route[:, None] == expert_ids[None, :]
        chosen_float = chosen.astype(jnp.float32)
        gate_prob = jnp.sum(router_probs * chosen_float, axis=-1)
        counted = (chosen & true_mask[:, None]).astype(jnp.bfloat16)
        earlier_counts = jnp.dot(lower_ones, counted, preferred_element_type=jnp.float32)
        queue_rank = jnp.sum(earlier_counts * chosen_float, axis=-1).astype(jnp.int32)
        kept_mask = true_mask & (queue_rank < capacity)
        slot_index = token_route * capacity + queue_rank
        dispatch = ((slot_ids[:, None] == slot_index[None, :]) & kept_mask[None, :]).astype(
            jnp.bfloat16
        )
        slot_input = (
            jnp.dot(dispatch, routed, preferred_element_type=jnp.float32)
            .astype(jnp.bfloat16)
            .reshape(slot_shape)
        )
        arrived = lax.all_to_all(slot_input, "expert", split_axis=0, concat_axis=0, tiled=True)
        gathered = lax.all_gather(arrived, "hidden", axis=0, tiled=True)
        pre_act, activation = expert_forward(gathered, w_inner)
        summed = lax.psum_scatter(
            jnp.einsum(
                "secf,efd->secd", activation, w_outer, preferred_element_type=jnp.float32
            ).astype(jnp.bfloat16),
            "hidden",
            scatter_dimension=0,
            tiled=True,
        )
        slot_output = lax.all_to_all(summed, "expert", split_axis=0, concat_axis=0, tiled=True)
        returned = jnp.einsum(
            "sl,sd->ld",
            dispatch,
            slot_output.reshape(slot_count, model_width),
            preferred_element_type=jnp.float32,
        )
        layer_rows.append(
            jnp.where(true_mask[:, None], residual + gate_prob[:, None] * returned, 0.0).astype(
                jnp.bfloat16
            )
        )
        out_grad = jnp.where(true_mask[:, None], upstream, 0.0)
        gate_grad = jnp.sum(out_grad * returned, axis=-1)
        slot_grad = jnp.dot(
            dispatch,
            (gate_prob[:, None] * out_grad).astype(jnp.bfloat16),
            preferred_element_type=jnp.float32,
        )
        slot_grad = slot_grad.astype(jnp.bfloat16).reshape(slot_shape)
        grad_arrived = lax.all_to_all(slot_grad, "expert", split_axis=0, concat_axis=0, tiled=True)
        grad_gathered = lax.all_gather(grad_arrived, "hidden", axis=0, tiled=True)
        outer_part, inner_part, pre_grad = expert_backward(
            gathered, grad_gathered, pre_act, activation, w_outer
        )
        input_sum = lax.psum_scatter(
            jnp.einsum(
                "secf,edf->secd", pre_grad, w_inner, preferred_element_type=jnp.float32
            ).astype(jnp.bfloat16),
            "hidden",
            scatter_dimension=0,
            tiled=True,
        )
        input_slots = lax.all_to_all(input_sum, "expert", split_axis=0, concat_axis=0, tiled=True)
        outer_total = outer_total + outer_part
        inner_total = inner_total + inner_part
        prob_grad = chosen_float * gate_grad[:, None]
        logit_grad = router_probs * (
            prob_grad - jnp.sum(router_probs * prob_grad, axis=-1, keepdims=True)
        )
        logit_grad = logit_grad.astype(jnp.bfloat16)
        router_part = jnp.einsum(
            "ld,le->de", routed, logit_grad, preferred_element_type=jnp.float32
        )
        routed_grad = jnp.einsum(
            "le,de->ld", logit_grad, w_router, preferred_element_type=jnp.float32
        )
        routed_grad = routed_grad + jnp.einsum(
            "sl,sd->ld",
            dispatch,
            input_slots.reshape(slot_count, model_width),
            preferred_element_type=jnp.float32,
        )
        residual_part, gain_ffn_part = norm_ffn_back(routed_grad)
        residual_grad = out_grad + residual_part
        attended_low = residual_grad.astype(jnp.bfloat16)
        output_part = jnp.einsum(
            "ld,le->de", mixed, attended_low, preferred_element_type=jnp.float32
        )
        mixed_grad = jnp.einsum(
            "le,de->ld", attended_low, w_output, preferred_element_type=jnp.float32
        ).astype(jnp.bfloat16)
        query_back, key_back, value_back, bias_part = attention_backward(
            queries,
            key_rows,
            value_rows,
            position_bias_heads,
            true_mask,
            log_totals,
            mixed_grad,
            expert_selector,
        )
        query_low = query_back.astype(jnp.bfloat16)
        key_reduced_precision = key_back.astype(jnp.bfloat16)
        value_low = value_back.astype(jnp.bfloat16)
        query_part = jnp.einsum(
            "ld,le->de", normed_low, query_low, preferred_element_type=jnp.float32
        )
        key_part = jnp.einsum(
            "ld,le->de", normed_low, key_reduced_precision, preferred_element_type=jnp.float32
        )
        value_part = jnp.einsum(
            "ld,le->de", normed_low, value_low, preferred_element_type=jnp.float32
        )
        normed_grad = (
            jnp.einsum("le,de->ld", query_low, w_query, preferred_element_type=jnp.float32)
            + jnp.einsum(
                "le,de->ld", key_reduced_precision, w_key, preferred_element_type=jnp.float32
            )
            + jnp.einsum("le,de->ld", value_low, w_value, preferred_element_type=jnp.float32)
        )
        input_part, gain_attn_part = norm_attn_back(normed_grad)
        token_grads.append((residual_grad + input_part).astype(jnp.bfloat16))
        grad_terms = (
            gain_attn_part,
            query_part,
            key_part,
            value_part,
            output_part,
            bias_part,
            gain_ffn_part,
            router_part,
        )
        grad_terms = lax.psum(
            (
                grad_terms[0],
                grad_terms[1],
                grad_terms[2],
                grad_terms[3],
                grad_terms[4],
                grad_terms[5],
                grad_terms[6],
                grad_terms[7],
            ),
            ("expert", "hidden"),
        )
        shared = jax.tree.map(jnp.add, shared, grad_terms)
    layer_out = jnp.stack(layer_rows)[:, None]
    tokens_grad = jnp.stack(token_grads)[:, None]
    return (
        layer_out,
        tokens_grad,
        shared[0],
        shared[1],
        shared[2],
        shared[3],
        shared[4],
        shared[5],
        shared[6],
        shared[7],
        inner_total,
        outer_total,
    )


def solution(mesh):
    placed = (
        P(None, ("expert", "hidden"), None, None),
        P(None, ("expert", "hidden"), None, None),
        P(None, ("expert", "hidden")),
        P(None, ("expert", "hidden"), None, None),
        P(),
        P(),
        P(),
        P(),
        P(),
        P(),
        P(),
        P(),
        P("expert", None, "hidden"),
        P("expert", "hidden", None),
    )
    return jax.shard_map(
        shards,
        mesh=mesh,
        in_specs=placed,
        out_specs=(
            P(None, ("expert", "hidden"), None, None),
            P(None, ("expert", "hidden"), None, None),
            P(),
            P(),
            P(),
            P(),
            P(),
            P(),
            P(),
            P(),
            P("expert", None, "hidden"),
            P("expert", "hidden", None),
        ),
        check_vma=False,
    )
```

profile of v0, /device:TPU:0, one launch (start us, length us, event | category | flops | bytes accessed | tf_op | source)
XLA Modules:
  0.0 1118.1 jit_solution(4235515031773506541)
XLA Ops:
  28.8 15.2 %fusion.2 = f32[512,512,12]{0,2,1:T(8,128)} fusion(s32[512,512]{0,1:T(8,128)} %constant.128.clone, f32[32,12]{0,1:T(8,128)} %param.24), kind=kOutput, calls=%fused_computation.3 | convolution fusion | flops 1216348160 | bytes 13633024 | tf_op jit(solution)/shard_map/jua,jy->yua/dot_general | solution.py:189
  44.0 15.8 %fusion.240 = (f32[12,512]{1,0:T(8,128)S(1)}, f32[12,512,512]{1,2,0:T(8,128)S(1)}) fusion(f32[512,512,12]{0,2,1:T(8,128)} %fusion.2, bf16[512,12,64]{0,2,1:T(8,128)(2,1)S(1)} %bitcast.380, bf16[512,12,64]{0,2,1:T(8,128)(2,1)S(1)} %bitcast.368, pred[512]{0:T(512)(128)(4,1)S(1)} %iota_compare_fusion.18), kind=kOutput, calls=%fused_computation.283 | convolution fusion | flops 415229952 | bytes 26763776 | tf_op jit(solution)/shard_map/while/body/eval_jaxpr/qhc,khc->hqk/dot_general | solution.py:43
  73.9 16.4 %fusion.241 = (f32[12,512]{1,0:T(8,128)S(1)}, f32[12,512,512]{1,2,0:T(8,128)S(1)}) fusion(f32[512,512,12]{0,2,1:T(8,128)} %fusion.2, bf16[512,12,64]{0,2,1:T(8,128)(2,1)} %bitcast.382, bf16[512,12,64]{0,2,1:T(8,128)(2,1)S(1)} %bitcast.370, pred[512]{0:T(512)(128)(4,1)} %copy-done.115), kind=kOutput, calls=%fused_computation.284 | convolution fusion | flops 415229952 | bytes 26763776 | tf_op jit(solution)/shard_map/while/body/eval_jaxpr/qhc,khc->hqk/dot_general | solution.py:43
  104.1 19.8 %all_to_all.40 = bf16[8,8,10,768]{3,1,2,0:T(8,128)(2,1)S(1)} all-to-all(bf16[8,8,10,768]{3,1,2,0:T(8,128)(2,1)S(1)} %copy.135), channel_id=1, replica_groups=mesh['expert'=8,'hidden'=4] {'expert'}, dimensions={0} | all-to-all | bytes 1966080 | tf_op jit(solution)/shard_map/all_to_all | solution.py:250
  130.9 17.1 %all_to_all.41 = bf16[8,8,10,768]{3,1,2,0:T(8,128)(2,1)S(1)} all-to-all(bf16[8,8,10,768]{3,1,2,0:T(8,128)(2,1)S(1)} %copy.127), channel_id=1, replica_groups=mesh['expert'=8,'hidden'=4] {'expert'}, dimensions={0} | all-to-all | bytes 1966080 | tf_op jit(solution)/shard_map/all_to_all | solution.py:250
  149.3 51.8 %all-gather.7.cloned.1.call-done = bf16[32,8,10,768]{3,0,2,1:T(8,128)(2,1)} async-done(((bf16[8,8,10,768]{3,0,2,1:T(8,128)(2,1)}), bf16[32,8,10,768]{3,0,2,1:T(8,128)(2,1)}) %all-gather.7.cloned.1.call-update) | async-done | bytes 3932176 | tf_op jit(solution)/shard_map/all_gather | solution.py:251
  201.1 8.1 fusion.22
  209.2 12.0 %convert_bitcast_fusion.2 = bf16[32,8,10,768]{3,0,2,1:T(8,128)(2,1)} fusion(bf16[8,768,768]{2,1,0:T(8,128)(2,1)} %param.28, f32[8,32,10,768]{3,1,2,0:T(8,128)S(1)} %fusion.22), kind=kOutput, calls=%fused_computation.75 | convolution fusion | flops 3039559680 | bytes 21233664 | tf_op jit(solution)/shard_map/secf,efd->secd/dot_general | solution.py:254
  221.2 7.3 copy.178
  228.5 6.4 reshape.406
  235.0 43.3 %all-gather.5.cloned.1.call-done = bf16[32,8,10,768]{3,0,2,1:T(8,128)(2,1)} async-done(((bf16[8,8,10,768]{3,0,2,1:T(8,128)(2,1)}), bf16[32,8,10,768]{3,0,2,1:T(8,128)(2,1)}) %all-gather.5.cloned.1.call-update) | async-done | bytes 3932176 | tf_op jit(solution)/shard_map/all_gather | solution.py:251
  278.3 8.1 fusion.24
  286.4 12.0 %convert_bitcast_fusion.3 = bf16[32,8,10,768]{3,0,2,1:T(8,128)(2,1)} fusion(bf16[8,768,768]{2,1,0:T(8,128)(2,1)} %param.28, f32[8,32,10,768]{3,1,2,0:T(8,128)S(1)} %fusion.24), kind=kOutput, calls=%fused_computation.76 | convolution fusion | flops 3039559680 | bytes 21233664 | tf_op jit(solution)/shard_map/secf,efd->secd/dot_general | solution.py:254
  298.4 7.4 copy.176
  305.8 6.4 reshape.404
  312.2 40.2 %reduce-scatter.15.cloned.1.call-done = bf16[8,61440]{1,0:T(8,128)(2,1)} async-done(((bf16[32,61440]{1,0:T(8,128)(2,1)}), bf16[8,61440]{1,0:T(8,128)(2,1)}) %reduce-scatter.15.cloned.1.call-update) | async-done | bytes 983056
  358.6 69.1 %reduce-scatter.13.cloned.1.call-done = bf16[8,61440]{1,0:T(8,128)(2,1)} async-done(((bf16[32,61440]{1,0:T(8,128)(2,1)}), bf16[8,61440]{1,0:T(8,128)(2,1)}) %reduce-scatter.13.cloned.1.call-update) | async-done | bytes 983056
  441.4 7.7 all-to-all-done.1
  451.7 5.1 fusion.104
  462.4 17.2 %all_to_all.42 = bf16[8,8,10,768]{3,1,2,0:T(8,128)(2,1)S(1)} all-to-all(bf16[8,8,10,768]{3,1,2,0:T(8,128)(2,1)S(1)} %copy.147), channel_id=1, replica_groups=mesh['expert'=8,'hidden'=4] {'expert'}, dimensions={0} | all-to-all | bytes 1966080 | tf_op jit(solution)/shard_map/all_to_all | solution.py:281
  489.1 17.1 %all_to_all.43 = bf16[8,8,10,768]{3,1,2,0:T(8,128)(2,1)S(1)} all-to-all(bf16[8,8,10,768]{3,1,2,0:T(8,128)(2,1)S(1)} %copy.139), channel_id=1, replica_groups=mesh['expert'=8,'hidden'=4] {'expert'}, dimensions={0} | all-to-all | bytes 1966080 | tf_op jit(solution)/shard_map/all_to_all | solution.py:281
  507.5 48.5 %all-gather.11.cloned.1.call-done = bf16[32,8,10,768]{3,0,2,1:T(8,128)(2,1)} async-done(((bf16[8,8,10,768]{3,0,2,1:T(8,128)(2,1)}), bf16[32,8,10,768]{3,0,2,1:T(8,128)(2,1)}) %all-gather.11.cloned.1.call-update) | async-done | bytes 3932176 | tf_op jit(solution)/shard_map/all_gather | solution.py:282
  556.0 12.6 %fusion.41 = bf16[32,8,10,768]{3,0,2,1:T(8,128)(2,1)} fusion(f32[8,32,10,768]{3,1,2,0:T(8,128)} %copy-done.21, bf16[32,8,10,768]{3,0,2,1:T(8,128)(2,1)} %all-gather.11.cloned.1.call-done, bf16[8,768,768]{2,1,0:T(8,128)(2,1)} %param.28), kind=kOutput, calls=%fused_computation.58 | convolution fusion | flops 3059220480 | bytes 25165824 | tf_op jit(solution)/shard_map/secd,efd->secf/dot_general | solution.py:150
  568.6 8.2 convert_bitcast_fusion
  576.8 5.2 copy.182
  582.0 6.4 reshape.410
  592.7 40.3 %all-gather.9.cloned.1.call-done = bf16[32,8,10,768]{3,0,2,1:T(8,128)(2,1)} async-done(((bf16[8,8,10,768]{3,0,2,1:T(8,128)(2,1)}), bf16[32,8,10,768]{3,0,2,1:T(8,128)(2,1)}) %all-gather.9.cloned.1.call-update) | async-done | bytes 3932176 | tf_op jit(solution)/shard_map/all_gather | solution.py:282
  633.1 12.8 %fusion.34 = bf16[32,8,10,768]{3,0,2,1:T(8,128)(2,1)} fusion(f32[8,32,10,768]{3,1,2,0:T(8,128)} %copy-done.22, bf16[32,8,10,768]{3,0,2,1:T(8,128)(2,1)} %all-gather.9.cloned.1.call-done, bf16[8,768,768]{2,1,0:T(8,128)(2,1)} %param.28), kind=kOutput, calls=%fused_computation.51 | convolution fusion | flops 3059220480 | bytes 25165824 | tf_op jit(solution)/shard_map/secd,efd->secf/dot_general | solution.py:150
  645.9 8.2 convert_bitcast_fusion.1
  654.1 5.2 copy.180
  659.3 6.4 reshape.408
  665.7 12.5 %fusion.248 = f32[8,768,768,1]{2,1,3,0:T(8,128)} fusion(bf16[32,8,10,768]{3,0,2,1:T(8,128)(2,1)} %all-gather.5.cloned.1.call-done, bf16[32,8,10,768]{3,0,2,1:T(8,128)(2,1)} %fusion.34), kind=kOutput, calls=%fused_computation.291 | convolution fusion | flops 3019898880 | bytes 26738688 | tf_op jit(solution)/shard_map/secd,secf->edf/dot_general | solution.py:154
  678.2 14.5 %fusion.233 = f32[8,768,768,1]{2,1,3,0:T(8,128)} fusion(bf16[32,8,10,768]{3,0,2,1:T(8,128)(2,1)S(1)} %copy-done.131, f32[8,32,10,768]{3,1,2,0:T(8,128)} %copy-done.22), kind=kOutput, calls=%fused_computation.280 | convolution fusion | flops 3037593600 | bytes 30670848 | tf_op jit(solution)/shard_map/secf,secd->efd/dot_general | solution.py:147
  692.7 13.9 %reduce-scatter.19.cloned.1.call-done = bf16[8,61440]{1,0:T(8,128)(2,1)} async-done(((bf16[32,61440]{1,0:T(8,128)(2,1)}), bf16[8,61440]{1,0:T(8,128)(2,1)}) %reduce-scatter.19.cloned.1.call-update) | async-done | bytes 983056
  709.1 4.2 all-to-all-start.7
  713.3 17.2 %bitcast_add_fusion = f32[8,768,768]{2,1,0:T(8,128)} fusion(f32[8,768,768,1]{2,1,3,0:T(8,128)} %fusion.233, bf16[32,8,10,768]{3,0,2,1:T(8,128)(2,1)} %all-gather.11.cloned.1.call-done, f32[8,32,10,768]{3,1,2,0:T(8,128)} %copy-done.21), kind=kOutput, calls=%fused_computation.4 | convolution fusion | flops 3042312192 | bytes 49545216 | tf_op jit(solution)/shard_map/secf,secd->efd/dot_general | solution.py:147
  730.5 51.5 %reduce-scatter.17.cloned.1.call-done = bf16[8,61440]{1,0:T(8,128)(2,1)} async-done(((bf16[32,61440]{1,0:T(8,128)(2,1)}), bf16[8,61440]{1,0:T(8,128)(2,1)}) %reduce-scatter.17.cloned.1.call-update) | async-done | bytes 983056
  784.5 4.2 all-to-all-start.5
  788.8 15.5 %bitcast_add_fusion.1 = f32[8,768,768]{2,1,0:T(8,128)} fusion(f32[8,768,768,1]{2,1,3,0:T(8,128)} %fusion.248, bf16[32,8,10,768]{3,0,2,1:T(8,128)(2,1)} %all-gather.7.cloned.1.call-done, bf16[32,8,10,768]{3,0,2,1:T(8,128)(2,1)} %fusion.41), kind=kOutput, calls=%fused_computation.5 | convolution fusion | flops 3024617472 | bytes 45613056 | tf_op jit(solution)/shard_map/secd,secf->edf/dot_general | solution.py:154
  828.8 10.7 multiply_reduce_fusion
  841.6 7.1 multiply_convert_fusion
  859.7 7.7 fusion.109
  867.4 9.0 multiply_reduce_fusion.1
  876.4 7.1 multiply_convert_fusion.1
  916.0 7.9 fusion.132
  923.9 8.8 fusion.138
  932.7 42.4 %all-reduce = (f32[768]{0:T(1024)}, f32[32,12]{0,1:T(8,128)}, f32[768]{0:T(1024)}) all-reduce(f32[768]{0:T(1024)} %add.272, f32[32,12]{0,1:T(8,128)} %fusion.138, f32[768]{0:T(1024)} %add.278), channel_id=1, replica_groups=mesh['expert'=8,'hidden'=4] {'expert','hidden'}, use_global_device_ids=true, to_apply=%region_31.32 | all-reduce | flops 1920 | bytes 15360 | tf_op jit(solution)/shard_map/psum | solution.py:364
  981.9 118.7 %all-reduce.4.cloned.1.call-done = (f32[768,768]{1,0:T(8,128)}, f32[768,768]{1,0:T(8,128)}, f32[768,768]{1,0:T(8,128)}, f32[768,768]{1,0:T(8,128)}, f32[768,64]{0,1:T(8,128)}) async-done(((f32[768,768]{1,0:T(8,128)}, f32[768,768]{1,0:T(8,128)}, f32[768,768]{1,0:T(8,128)}, f32[768,768]{1,0:T(8,128)}, f32[768,64]{0,1:T(8,128)}), (f32[768,768]{1,0:T(8,128)}, f32[768,768]{1,0:T(8,128)}, f32[768,768]{1,0:T(8,128)}, ...) | async-done | bytes 9633808 | tf_op jit(solution)/shard_map/psum | solution.py:364
  (441 shorter events, 192.0 us)
Async XLA Ops:
  7.2 193.9 %all-gather.7.cloned.1.call-start = ((), (), s32[]{:S(2)}) async-start(), calls=%async_computation.13 | async-start | bytes 4915200 | tf_op jit(solution)/shard_map/all_gather | solution.py:251
  9.2 7.4 copy-start.77
  21.2 104.9 %copy-start.85 = (s32[1,1,512,1]{2,3,1,0:T(1,128)}, s32[1,1,512,1]{2,3,1,0:T(1,128)S(1)}, u32[]{:S(2)}) copy-start(s32[1,1,512,1]{2,3,1,0:T(1,128)S(1)} %get-tuple-element.220) | copy-start | bytes 6148
  22.0 435.4 %copy-start.102 = (s32[512]{0:T(512)}, s32[512]{0:T(512)S(1)}, u32[]{:S(2)}) copy-start(s32[512]{0:T(512)S(1)} %convert_add_fusion) | copy-start | bytes 6148
  28.1 15.9 %copy-start.17 = (bf16[512,768]{0,1:T(8,128)(2,1)}, bf16[512,768]{0,1:T(8,128)(2,1)S(1)}, u32[]{:S(2)}) copy-start(bf16[512,768]{0,1:T(8,128)(2,1)S(1)} %copy.123) | copy-start | bytes 2359300
  28.8 15.2 %copy-start.118 = (pred[512]{0:T(512)(128)(4,1)}, pred[512]{0:T(512)(128)(4,1)S(1)}, u32[]{:S(2)}) copy-start(pred[512]{0:T(512)(128)(4,1)S(1)} %iota_compare_fusion.18) | copy-start | bytes 1540
  28.8 15.2 %copy-start.28 = (bf16[512,768]{0,1:T(8,128)(2,1)S(1)}, bf16[512,768]{0,1:T(8,128)(2,1)}, u32[]{:S(2)}) copy-start(bf16[512,768]{0,1:T(8,128)(2,1)} %copy.122) | copy-start | bytes 2359300
  68.9 29.1 %copy-start.81 = (f32[512]{0:T(512)}, f32[512]{0:T(512)S(1)}, u32[]{:S(2)}) copy-start(f32[512]{0:T(512)S(1)} %fusion.202) | copy-start | bytes 6148
  73.9 16.5 %copy-start.19 = (bf16[512,768]{0,1:T(8,128)(2,1)}, bf16[512,768]{0,1:T(8,128)(2,1)S(1)}, u32[]{:S(2)}) copy-start(bf16[512,768]{0,1:T(8,128)(2,1)S(1)} %copy.133) | copy-start | bytes 2359300
  104.1 21.1 %copy-start.119 = (pred[512]{0:T(512)(128)(4,1)S(1)}, pred[512]{0:T(512)(128)(4,1)}, u32[]{:S(2)}) copy-start(pred[512]{0:T(512)(128)(4,1)} %copy-done.118) | copy-start | bytes 1540
  104.1 22.7 %copy-start.45 = (bf16[512,768]{1,0:T(8,128)(2,1)S(1)}, bf16[512,768]{1,0:T(8,128)(2,1)}, u32[]{:S(2)}) copy-start(bf16[512,768]{1,0:T(8,128)(2,1)} %get-tuple-element.222) | copy-start | bytes 2359300
  125.2 153.2 %all-gather.5.cloned.1.call-start = ((), (), s32[]{:S(2)}) async-start(), calls=%async_computation.12 | async-start | bytes 4915200 | tf_op jit(solution)/shard_map/all_gather | solution.py:251
  149.2 203.2 %reduce-scatter.15.cloned.1.call-start = ((), (), s32[]{:S(2)}) async-start(), calls=%async_computation.17 | async-start | bytes 4915200
  209.2 12.0 %copy-start.21 = (f32[8,32,10,768]{3,1,2,0:T(8,128)}, f32[8,32,10,768]{3,1,2,0:T(8,128)S(1)}, u32[]{:S(2)}) copy-start(f32[8,32,10,768]{3,1,2,0:T(8,128)S(1)} %fusion.22) | copy-start | bytes 23592964
  234.9 192.8 %reduce-scatter.13.cloned.1.call-start = ((), (), s32[]{:S(2)}) async-start(), calls=%async_computation.16 | async-start | bytes 4915200
  286.4 12.0 %copy-start.22 = (f32[8,32,10,768]{3,1,2,0:T(8,128)}, f32[8,32,10,768]{3,1,2,0:T(8,128)S(1)}, u32[]{:S(2)}) copy-start(f32[8,32,10,768]{3,1,2,0:T(8,128)S(1)} %fusion.24) | copy-start | bytes 23592964
  354.9 75.2 %all-to-all-start.3 = ((bf16[8,8,10,768]{3,1,2,0:T(8,128)(2,1)}), bf16[8,8,10,768]{3,1,2,0:T(8,128)(2,1)S(1)}, u32[]{:S(2)}, u32[]{:S(2)}) async-start(bf16[8,8,10,768]{3,1,2,0:T(8,128)(2,1)} %copy.137), calls=%async_computation.3 | async-start | bytes 1966080 | tf_op jit(solution)/shard_map/all_to_all | solution.py:261
  358.5 75.9 %copy-start.63 = (bf16[768,64]{0,1:T(8,128)(2,1)S(1)}, bf16[768,64]{0,1:T(8,128)(2,1)}, u32[]{:S(2)}) copy-start(bf16[768,64]{0,1:T(8,128)(2,1)} %param.26) | copy-start | bytes 294916
  430.1 19.0 %all-to-all-start.1 = ((bf16[8,8,10,768]{3,1,2,0:T(8,128)(2,1)}), bf16[8,8,10,768]{3,1,2,0:T(8,128)(2,1)}, u32[]{:S(2)}, u32[]{:S(2)}) async-start(bf16[8,8,10,768]{3,1,2,0:T(8,128)(2,1)} %copy.129), calls=%async_computation.1 | async-start | bytes 1966080 | tf_op jit(solution)/shard_map/all_to_all | solution.py:261
  434.4 121.7 %all-gather.11.cloned.1.call-start = ((), (), s32[]{:S(2)}) async-start(), calls=%async_computation.15 | async-start | bytes 4915200 | tf_op jit(solution)/shard_map/all_gather | solution.py:282
  462.4 19.0 %copy-start.46 = (bf16[512,768]{1,0:T(8,128)(2,1)S(1)}, bf16[512,768]{1,0:T(8,128)(2,1)}, u32[]{:S(2)}) copy-start(bf16[512,768]{1,0:T(8,128)(2,1)} %get-tuple-element.222) | copy-start | bytes 2359300
  462.4 19.0 %copy-start.64 = (bf16[768,64]{0,1:T(8,128)(2,1)S(1)}, bf16[768,64]{0,1:T(8,128)(2,1)}, u32[]{:S(2)}) copy-start(bf16[768,64]{0,1:T(8,128)(2,1)} %param.26) | copy-start | bytes 294916
  480.9 152.2 %all-gather.9.cloned.1.call-start = ((), (), s32[]{:S(2)}) async-start(), calls=%async_computation.14 | async-start | bytes 4915200 | tf_op jit(solution)/shard_map/all_gather | solution.py:282
  507.5 199.2 %reduce-scatter.19.cloned.1.call-start = ((), (), s32[]{:S(2)}) async-start(), calls=%async_computation.19 | async-start | bytes 4915200
  588.5 193.5 %reduce-scatter.17.cloned.1.call-start = ((), (), s32[]{:S(2)}) async-start(), calls=%async_computation.18 | async-start | bytes 4915200
  665.7 12.5 %copy-start.131 = (bf16[32,8,10,768]{3,0,2,1:T(8,128)(2,1)S(1)}, bf16[32,8,10,768]{3,0,2,1:T(8,128)(2,1)}, u32[]{:S(2)}) copy-start(bf16[32,8,10,768]{3,0,2,1:T(8,128)(2,1)} %all-gather.9.cloned.1.call-done) | copy-start | bytes 11796484
  709.1 75.4 %all-to-all-start.7 = ((bf16[8,8,10,768]{3,1,2,0:T(8,128)(2,1)}), bf16[8,8,10,768]{3,1,2,0:T(8,128)(2,1)}, u32[]{:S(2)}, u32[]{:S(2)}) async-start(bf16[8,8,10,768]{3,1,2,0:T(8,128)(2,1)} %copy.149), calls=%async_computation.7 | async-start | bytes 1966080 | tf_op jit(solution)/shard_map/all_to_all | solution.py:294
  784.5 25.5 %all-to-all-start.5 = ((bf16[8,8,10,768]{3,1,2,0:T(8,128)(2,1)}), bf16[8,8,10,768]{3,1,2,0:T(8,128)(2,1)}, u32[]{:S(2)}, u32[]{:S(2)}) async-start(bf16[8,8,10,768]{3,1,2,0:T(8,128)(2,1)} %copy.141), calls=%async_computation.5 | async-start | bytes 1966080 | tf_op jit(solution)/shard_map/all_to_all | solution.py:294
  788.7 311.9 %all-reduce.4.cloned.1.call-start = ((), (), s32[]{:S(2)}) async-start(), calls=%async_computation.20 | async-start | bytes 19267584 | tf_op jit(solution)/shard_map/psum | solution.py:364
  806.9 11.6 %copy-start.80 = (f32[768]{0:T(1024)S(1)}, f32[768]{0:T(1024)}, u32[]{:S(2)}) copy-start(f32[768]{0:T(1024)} %param.25) | copy-start | bytes 9220
  806.9 11.6 %copy-start.84 = (f32[512]{0:T(512)S(1)}, f32[512]{0:T(512)}, u32[]{:S(2)}) copy-start(f32[512]{0:T(512)} %copy-done.83) | copy-start | bytes 6148
  806.9 11.6 %copy-start.106 = (s32[512]{0:T(512)S(1)}, s32[512]{0:T(512)}, u32[]{:S(2)}) copy-start(s32[512]{0:T(512)} %copy-done.104) | copy-start | bytes 6148
  823.6 33.0 %copy-start.14 = (f32[512,768]{1,0:T(8,128)}, f32[512,768]{1,0:T(8,128)S(1)}, u32[]{:S(2)}) copy-start(f32[512,768]{1,0:T(8,128)S(1)} %get-tuple-element.214) | copy-start | bytes 4718596
  828.7 10.8 slice-start.3
  828.8 11.4 %slice-start.4 = ((s8[12582912]{0:T(1024)(128)(4,1)}), s8[4194304]{0:T(1024)(128)(4,1)S(1)}, s32[]{:S(2)}) async-start(s8[12582912]{0:T(1024)(128)(4,1)} %bitcast.362), calls=%async_computation.25 | async-start | bytes 8388608
  828.8 12.9 %slice-start.5 = ((s8[12582912]{0:T(1024)(128)(4,1)}), s8[4194304]{0:T(1024)(128)(4,1)S(1)}, s32[]{:S(2)}) async-start(s8[12582912]{0:T(1024)(128)(4,1)} %bitcast.362), calls=%async_computation.26 | async-start | bytes 8388608
  828.8 12.8 %copy-start.70 = (f32[12,512]{1,0:T(8,128)S(1)}, f32[12,512]{1,0:T(8,128)}, u32[]{:S(2)}) copy-start(f32[12,512]{1,0:T(8,128)} %copy-done.69) | copy-start | bytes 73732
  859.7 7.7 copy-start.24
  859.7 7.7 copy-start.68
  859.7 16.7 %slice-start = ((s8[12582912]{0:T(1024)(128)(4,1)}), s8[4194304]{0:T(1024)(128)(4,1)S(1)}, s32[]{:S(2)}) async-start(s8[12582912]{0:T(1024)(128)(4,1)} %bitcast.360), calls=%async_computation.21 | async-start | bytes 8388608
  859.7 16.7 %slice-start.1 = ((s8[12582912]{0:T(1024)(128)(4,1)}), s8[4194304]{0:T(1024)(128)(4,1)S(1)}, s32[]{:S(2)}) async-start(s8[12582912]{0:T(1024)(128)(4,1)} %bitcast.360), calls=%async_computation.22 | async-start | bytes 8388608
  867.4 9.0 slice-start.2
  876.4 7.1 copy-start.18
  908.0 7.9 slice-start.8
  911.6 12.3 %slice-start.6 = ((s8[6291456]{0:T(1024)(128)(4,1)}), s8[4194304]{0:T(1024)(128)(4,1)S(1)}, s32[]{:S(2)}) async-start(s8[6291456]{0:T(1024)(128)(4,1)} %bitcast.364), calls=%async_computation.27 | async-start | bytes 8388608
  916.0 7.9 slice-start.7
  923.9 51.3 %copy-start.40 = (bf16[1,512,768]{2,1,0:T(8,128)(2,1)S(1)}, bf16[1,512,768]{2,1,0:T(8,128)(2,1)}, u32[]{:S(2)}) copy-start(bf16[1,512,768]{2,1,0:T(8,128)(2,1)} %get-tuple-element.216) | copy-start | bytes 2359300
  932.7 45.0 %copy-start.89 = (f32[512]{0:T(512)S(1)}, f32[512]{0:T(512)}, u32[]{:S(2)}) copy-start(f32[512]{0:T(512)} %copy-done.88) | copy-start | bytes 6148
  (115 other events, 303.1 us)
Sparse Core Ops, SparseCore 0:
  125.3 75.8 all-gather.6
  203.3 75.0 all-gather.4
  281.2 71.2 reduce-scatter.14
  354.6 73.0 reduce-scatter.12
  481.0 74.9 all-gather.10
  558.0 74.9 all-gather.8
  635.4 71.2 reduce-scatter.18
  709.0 73.0 reduce-scatter.16
  903.0 197.5 all-reduce.3
where the time goes:
time: 1120 us
  waiting for transfers between devices  485 us (43%)
  matrix products  313 us (28%)
  local copies, waits for them, and re-layouts  137 us (12%)
  blocking collectives  114 us (10%)
  other arithmetic  36.1 us (3%)
  starting transfers between devices  17.1 us (2%)
  between operations  15.9 us (1%)
    unnamed x13, waiting for transfers between devices  175 us
    psum x1, waiting for transfers between devices, shards(): lax.psum((grad_terms[0], grad_terms[1], grad_terms[2], grad_terms[3], gra...  119 us
    all_gather x2, waiting for transfers between devices, shards(): gathered = lax.all_gather(arrived, 'hidden', axis=0, tiled=True)  95.2 us
    all_gather x2, waiting for transfers between devices, shards(): grad_gathered = lax.all_gather(grad_arrived, 'hidden', axis=0, tiled=True)  88.9 us
    unnamed x313, local copies, waits for them, and re-layouts  81.9 us
    psum x1, blocking collectives, shards(): lax.psum((grad_terms[0], grad_terms[1], grad_terms[2], grad_terms[3], gra...  42.4 us
    all_to_all x2, blocking collectives, shards(): lax.all_to_all(slot_input, 'expert', split_axis=0, concat_axis=0, tiled=T...  36.9 us
    all_to_all x2, blocking collectives, shards(): lax.all_to_all(slot_grad, 'expert', split_axis=0, concat_axis=0, tiled=True)  34.3 us
  transfers between devices with their start and end apart: 13, of which 10 were waited for; matrix products, arithmetic and copies ran while one was open for 24% of the time, Pallas kernels for 0%

commit v1 on v0

v1 whole, which is shorter than its diff:
```python
import functools

import jax
import jax.numpy as jnp
import numpy as np
from jax import lax
from jax.experimental import pallas as pl
from jax.experimental.pallas import tpu as pltpu
from jax.sharding import PartitionSpec as P

HEADS = 12
HEAD_DIM = 64
BUCKETS = 32
MAXDIST = 128
PAIR = 2 * HEAD_DIM
PAIRS = HEADS // 2
ROWS = 128

epsilon = 1e-06
negative = -1e30
F32 = jnp.float32
BF16 = jnp.bfloat16
MIB = 1 << 20


def params(mib):
    return pltpu.CompilerParams(vmem_limit_bytes=mib * MIB)


def cost(flops, moved, special=0):
    return pl.CostEstimate(flops=int(flops), bytes_accessed=int(moved), transcendentals=int(special))


def offset_bucket(offsets):
    halfway = BUCKETS // 2
    exact_count = halfway // 2
    relative_distance = np.abs(offsets)
    scaled = (
        np.log(np.maximum(relative_distance, 1) / exact_count)
        / np.log(MAXDIST / exact_count)
        * (halfway - exact_count)
    )
    far_bucket = np.minimum(exact_count + np.floor(scaled).astype(np.int64), halfway - 1)
    near_bucket = np.where(relative_distance < exact_count, relative_distance, far_bucket)
    return (np.where(offsets > 0, halfway, 0) + near_bucket).astype(np.int32)


def dot(a, b):
    return lax.dot_general(a, b, (((1,), (0,)), ((), ())), preferred_element_type=F32)


def dot_t(a, b):
    return lax.dot_general(a, b, (((1,), (1,)), ((), ())), preferred_element_type=F32)


def t_dot(a, b):
    return lax.dot_general(a, b, (((0,), (0,)), ((), ())), preferred_element_type=F32)


def one_hot(condition):
    return jnp.where(condition, 1.0, 0.0).astype(BF16)


def iota(shape, axis):
    return lax.broadcasted_iota(jnp.int32, shape, axis)


def prep_kernel(experts, capacity, len_ref, row_ref, col_ref, cot_ref, srow_ref, scol_ref, slots_ref):
    length = row_ref.shape[-1]
    count = len_ref[pl.program_id(0)]
    row = row_ref[0]
    col = col_ref[0]
    valid_row = iota((1, length), 1) < count
    valid_col = iota((length, 1), 0) < count
    chosen_row = iota((experts, length), 0) == row
    chosen_col = iota((length, experts), 1) == col
    before = one_hot(iota((length, length), 0) < iota((length, length), 1))
    after = one_hot(iota((length, length), 1) < iota((length, length), 0))
    earlier_row = dot(one_hot(chosen_row & valid_row), before)
    rank_row = jnp.sum(jnp.where(chosen_row, earlier_row, 0.0), axis=0, keepdims=True).astype(jnp.int32)
    earlier_col = dot(after, one_hot(chosen_col & valid_col))
    rank_col = jnp.sum(jnp.where(chosen_col, earlier_col, 0.0), axis=1, keepdims=True).astype(jnp.int32)
    slot_row = jnp.where(valid_row & (rank_row < capacity), row * capacity + rank_row, -1)
    srow_ref[0] = slot_row
    scol_ref[0] = jnp.where(valid_col & (rank_col < capacity), col * capacity + rank_col, -1)
    dispatch = one_hot(iota((experts * capacity, length), 0) == slot_row)
    slots_ref[0] = dot(dispatch, cot_ref[0]).astype(BF16)


def prep(lengths, routes, cotangent, experts, capacity):
    batches, length, width = cotangent.shape
    slots = experts * capacity
    block = lambda *shape: pl.BlockSpec((1,) + shape, lambda b: (b, 0, 0))
    return pl.pallas_call(
        functools.partial(prep_kernel, experts, capacity),
        grid=(batches,),
        in_specs=[
            pl.BlockSpec(memory_space=pltpu.SMEM),
            block(1, length),
            block(length, 1),
            block(length, width),
        ],
        out_specs=[block(1, length), block(length, 1), block(slots, width)],
        out_shape=[
            jax.ShapeDtypeStruct((batches, 1, length), jnp.int32),
            jax.ShapeDtypeStruct((batches, length, 1), jnp.int32),
            jax.ShapeDtypeStruct((batches, slots, width), BF16),
        ],
        compiler_params=params(32),
        cost_estimate=cost(2 * batches * slots * length * width, 4 * batches * slots * width),
    )(lengths, routes.reshape(batches, 1, length), routes.reshape(batches, length, 1), cotangent)


def band_bias(vector_ref, head):
    wide = jnp.broadcast_to(vector_ref[head], (ROWS, vector_ref.shape[-1]))
    return pltpu.roll(wide, 0, 1, stride=1, stride_axis=0)


def band_slice(block, length):
    start = length - ROWS * (block + 1)
    return slice(start, start + length)


def attn_kernel(
    capacity,
    len_ref,
    tok_ref,
    gain_ref,
    wq_ref,
    wk_ref,
    wv_ref,
    wo_ref,
    vec_ref,
    gffn_ref,
    wr_ref,
    srow_ref,
    rcol_ref,
    qkv_ref,
    mixed_ref,
    lse_ref,
    res_ref,
    probs_ref,
    gate_ref,
    slots_ref,
    band_ref,
):
    length, width = tok_ref.shape
    count = len_ref[0]
    tokens = tok_ref[...].astype(F32)
    inverse = lax.rsqrt(jnp.mean(tokens * tokens, axis=-1, keepdims=True) + epsilon)
    normed = (tokens * inverse * gain_ref[...]).astype(BF16)
    for which, w_ref in enumerate((wq_ref, wk_ref, wv_ref)):
        for part in range(width // 256):
            rows = dot(normed, w_ref[:, 256 * part : 256 * part + 256]).astype(BF16)
            qkv_ref[which, 2 * part] = rows[:, :PAIR]
            qkv_ref[which, 2 * part + 1] = rows[:, PAIR:]
    mask = jnp.where(iota((1, length), 1) < count, 0.0, negative)
    lane = iota((ROWS, PAIR), 1)
    lse_ref[...] = jnp.zeros_like(lse_ref)

    def one_pair(pair, carry):
        keys = qkv_ref[1, pair]
        values = qkv_ref[2, pair]
        for side in range(2):
            head = 2 * pair + side
            band_ref[...] = band_bias(vec_ref, head)
            mine = (lane >= HEAD_DIM) if side else (lane < HEAD_DIM)
            for block in range(length // ROWS):
                here = slice(ROWS * block, ROWS * (block + 1))
                queries = qkv_ref[0, pair, here, :] * 0.125
                queries = jnp.where(mine, queries, jnp.zeros_like(queries))
                scores = dot_t(queries, keys) + band_ref[:, band_slice(block, length)] + mask
                highest = jnp.max(scores, axis=-1, keepdims=True)
                powers = jnp.exp(scores - highest)
                total = jnp.sum(powers, axis=-1, keepdims=True)
                mixed = (dot(powers.astype(BF16), values) / total).astype(BF16)
                column = iota((ROWS, lse_ref.shape[1]), 1)
                lse_ref[here, :] = jnp.where(column == head, highest + jnp.log(total), lse_ref[here, :])
                if side:
                    mixed = jnp.where(mine, mixed, mixed_ref[pair, here, :])
                mixed_ref[pair, here, :] = mixed
        return carry

    lax.fori_loop(0, PAIRS, one_pair, 0)
    mixed_all = jnp.concatenate([mixed_ref[p] for p in range(PAIRS)], axis=1)
    residual = tokens + dot(mixed_all, wo_ref[...])
    res_ref[...] = residual
    inverse = lax.rsqrt(jnp.mean(residual * residual, axis=-1, keepdims=True) + epsilon)
    routed = (residual * inverse * gffn_ref[...]).astype(BF16)
    logits = dot(routed, wr_ref[...])
    powers = jnp.exp(logits - jnp.max(logits, axis=-1, keepdims=True))
    probs = powers / jnp.sum(powers, axis=-1, keepdims=True)
    probs_ref[...] = probs
    gate = jnp.sum(jnp.where(iota(probs.shape, 1) == rcol_ref[...], probs, 0.0), axis=-1, keepdims=True)
    first = gate.astype(BF16).astype(F32)
    second = (gate - first).astype(BF16).astype(F32)
    third = gate - first - second
    column = iota((length, PAIR), 1)
    pieces = jnp.where(column == 0, first, jnp.where(column == 1, second, jnp.where(column == 2, third, 0.0)))
    dispatch = one_hot(iota((slots_ref.shape[0], length), 0) == srow_ref[...])
    gate_ref[...] = jnp.sum(dot(dispatch, pieces.astype(BF16)), axis=-1, keepdims=True)
    slots_ref[...] = dot(dispatch, routed).astype(BF16)


def attention_forward(count, tokens, gain, wq, wk, wv, wo, vector, gain_ffn, w_router, srow, rcol, capacity):
    length, width = tokens.shape
    experts = w_router.shape[1]
    slots = experts * capacity
    vmem = pl.BlockSpec(memory_space=pltpu.VMEM)
    return pl.pallas_call(
        functools.partial(attn_kernel, capacity),
        in_specs=[pl.BlockSpec(memory_space=pltpu.SMEM)] + [vmem] * 11,
        out_specs=[vmem] * 7,
        out_shape=[
            jax.ShapeDtypeStruct((3, PAIRS, length, PAIR), BF16),
            jax.ShapeDtypeStruct((PAIRS, length, PAIR), BF16),
            jax.ShapeDtypeStruct((length, 128), F32),
            jax.ShapeDtypeStruct((length, width), F32),
            jax.ShapeDtypeStruct((length, experts), F32),
            jax.ShapeDtypeStruct((slots, 1), F32),
            jax.ShapeDtypeStruct((slots, width), BF16),
        ],
        scratch_shapes=[pltpu.VMEM((ROWS, vector.shape[-1]), F32)],
        compiler_params=params(48),
        cost_estimate=cost(14e9, 14e6, HEADS * length * length),
    )(count, tokens, gain, wq, wk, wv, wo, vector, gain_ffn, w_router, srow, rcol)


GELU_SCALE = 0.7978845608028654
GELU_CUBIC = 0.044715


def expert_kernel(x_ref, c_ref, wi_ref, wo_ref, out_ref, in_ref, act_ref, pre_ref):
    planes, _, rows, width = x_ref.shape
    inputs = x_ref[...].reshape(planes * rows, width)
    grads = c_ref[...].reshape(planes * rows, width)
    pre = dot(inputs, wi_ref[0])
    square = pre * pre
    curve = jnp.tanh(GELU_SCALE * pre * (1.0 + GELU_CUBIC * square))
    half = 0.5 * (1.0 + curve)
    act = (pre * half).astype(BF16)
    slope = half + 0.5 * pre * (1.0 - curve * curve) * (GELU_SCALE * (1.0 + 3.0 * GELU_CUBIC * square))
    act_ref[0] = act
    out_ref[...] = dot(act, wo_ref[0]).astype(BF16).reshape(planes, 1, rows, width)
    pre_grad = (slope * dot_t(grads, wo_ref[0])).astype(BF16)
    pre_ref[0] = pre_grad
    in_ref[...] = dot_t(pre_grad, wi_ref[0]).astype(BF16).reshape(planes, 1, rows, width)


def experts_both(x, c, w_inner, w_outer):
    planes, local, rows, width = x.shape
    hidden = w_inner.shape[2]
    slab = pl.BlockSpec((planes, 1, rows, width), lambda e: (0, e, 0, 0))
    weight = lambda a, b: pl.BlockSpec((1, a, b), lambda e: (e, 0, 0))
    total = planes * rows
    return pl.pallas_call(
        expert_kernel,
        grid=(local,),
        in_specs=[slab, slab, weight(width, hidden), weight(hidden, width)],
        out_specs=[slab, slab, weight(total, hidden), weight(total, hidden)],
        out_shape=[
            jax.ShapeDtypeStruct(x.shape, BF16),
            jax.ShapeDtypeStruct(x.shape, BF16),
            jax.ShapeDtypeStruct((local, total, hidden), BF16),
            jax.ShapeDtypeStruct((local, total, hidden), BF16),
        ],
        compiler_params=params(40),
        cost_estimate=cost(
            8 * local * total * width * hidden, 4 * local * hidden * width + 12 * local * total * width, local * total * hidden
        ),
    )(x, c, w_inner, w_outer)


def expert_grad_kernel(batches, *refs):
    xs, cs, acts, pres = (refs[k * batches : (k + 1) * batches] for k in range(4))
    gate_ref, outer_ref, inner_ref = refs[4 * batches :]
    rows = acts[0].shape[1]
    width = xs[0].shape[-1]
    outer = inner = None
    for b in range(batches):
        gate = gate_ref[0, b * rows : (b + 1) * rows, :]
        grads = (cs[b][...].reshape(rows, width).astype(F32) * gate).astype(BF16)
        pre_grad = (pres[b][0].astype(F32) * gate).astype(BF16)
        outer_part = t_dot(acts[b][0], grads)
        inner_part = t_dot(xs[b][...].reshape(rows, width), pre_grad)
        outer = outer_part if outer is None else outer + outer_part
        inner = inner_part if inner is None else inner + inner_part
    outer_ref[0] = outer
    inner_ref[0] = inner


def expert_grads(xs, cs, acts, pres, gates):
    batches = len(xs)
    planes, local, rows, width = xs[0].shape
    hidden = acts[0].shape[2]
    slab = pl.BlockSpec((planes, 1, rows, width), lambda e: (0, e, 0, 0))
    mat = lambda a, b: pl.BlockSpec((1, a, b), lambda e: (e, 0, 0))
    total = planes * rows
    return pl.pallas_call(
        functools.partial(expert_grad_kernel, batches),
        grid=(local,),
        in_specs=[slab] * (2 * batches) + [mat(total, hidden)] * (2 * batches) + [mat(batches * total, 1)],
        out_specs=[mat(hidden, width), mat(width, hidden)],
        out_shape=[
            jax.ShapeDtypeStruct((local, hidden, width), F32),
            jax.ShapeDtypeStruct((local, width, hidden), F32),
        ],
        compiler_params=params(48),
        cost_estimate=cost(
            4 * batches * local * total * width * hidden, 8 * local * hidden * width + 8 * batches * local * total * width
        ),
    )(*xs, *cs, *acts, *pres, gates)


def combine_kernel(
    len_ref,
    out_ref,
    in_ref,
    scol_ref,
    rcol_ref,
    res_ref,
    probs_ref,
    cot_ref,
    gffn_ref,
    wr_ref,
    wo_ref,
    mixed_ref,
    layer_ref,
    resgrad_ref,
    mgrad_ref,
    ograd_ref,
    rgrad_ref,
    ggrad_ref,
):
    length, width = cot_ref.shape
    slots = out_ref.shape[0]
    valid = iota((length, 1), 0) < len_ref[0]
    collect = one_hot(iota((length, slots), 1) == scol_ref[...])
    returned = dot(collect, out_ref[...])
    residual = res_ref[...]
    probs = probs_ref[...]
    chosen = iota(probs.shape, 1) == rcol_ref[...]
    gate = jnp.sum(jnp.where(chosen, probs, 0.0), axis=-1, keepdims=True)
    layer_ref[...] = jnp.where(valid, residual + gate * returned, 0.0).astype(BF16)
    out_grad = jnp.where(valid, cot_ref[...].astype(F32), 0.0)
    gate_grad = jnp.sum(out_grad * returned, axis=-1, keepdims=True)
    prob_grad = jnp.where(chosen, gate_grad, 0.0)
    logit_grad = (probs * (prob_grad - jnp.sum(probs * prob_grad, axis=-1, keepdims=True))).astype(BF16)
    inverse = lax.rsqrt(jnp.mean(residual * residual, axis=-1, keepdims=True) + epsilon)
    gain = gffn_ref[...]
    scaled = residual * inverse
    routed = (scaled * gain).astype(BF16)
    rgrad_ref[...] = t_dot(logit_grad, routed)
    routed_grad = dot_t(logit_grad, wr_ref[...]) + gate * dot(collect, in_ref[...])
    ggrad_ref[...] = jnp.sum(routed_grad * scaled, axis=0, keepdims=True)
    upstream = routed_grad * gain
    middle = jnp.mean(upstream * scaled, axis=-1, keepdims=True)
    residual_grad = out_grad + inverse * (upstream - scaled * middle)
    resgrad_ref[...] = residual_grad
    attended = residual_grad.astype(BF16)
    mixed_all = jnp.concatenate([mixed_ref[p] for p in range(PAIRS)], axis=1)
    ograd_ref[...] = t_dot(mixed_all, attended)
    mixed_grad = dot_t(attended, wo_ref[...]).astype(BF16)
    for pair in range(PAIRS):
        mgrad_ref[pair] = mixed_grad[:, pair * PAIR : (pair + 1) * PAIR]


def combine(count, outs, ins, scol, rcol, residual, probs, cot, gain_ffn, w_router, w_output, mixed):
    length, width = cot.shape
    experts = w_router.shape[1]
    vmem = pl.BlockSpec(memory_space=pltpu.VMEM)
    return pl.pallas_call(
        combine_kernel,
        in_specs=[pl.BlockSpec(memory_space=pltpu.SMEM)] + [vmem] * 11,
        out_specs=[vmem] * 6,
        out_shape=[
            jax.ShapeDtypeStruct((length, width), BF16),
            jax.ShapeDtypeStruct((length, width), F32),
            jax.ShapeDtypeStruct((PAIRS, length, PAIR), BF16),
            jax.ShapeDtypeStruct((width, width), F32),
            jax.ShapeDtypeStruct((experts, width), F32),
            jax.ShapeDtypeStruct((1, width), F32),
        ],
        compiler_params=params(48),
        cost_estimate=cost(8e9, 12e6),
    )(count, outs, ins, scol, rcol, residual, probs, cot, gain_ffn, w_router, w_output, mixed)


def attn_back_kernel(
    len_ref,
    qkv_ref,
    lse_ref,
    vec_ref,
    mgrad_ref,
    tok_ref,
    gain_ref,
    wq_ref,
    wk_ref,
    wv_ref,
    resgrad_ref,
    wgrad_ref,
    diag_ref,
    tgrad_ref,
    ggrad_ref,
    band_ref,
    probs_ref,
    sgrad_ref,
    spread_ref,
    low_ref,
    kt_ref,
    vt_ref,
):
    length, width = tok_ref.shape
    mask = jnp.where(iota((1, length), 1) < len_ref[0], 0.0, negative)
    lane = iota((ROWS, PAIR), 1)

    def one_pair(pair, carry):
        keys = qkv_ref[1, pair]
        values = qkv_ref[2, pair]
        queries_t = qkv_ref[0, pair].T
        grads_t = mgrad_ref[pair].T
        for side in range(2):
            head = 2 * pair + side
            band_ref[...] = band_bias(vec_ref, head)
            spread_ref[...] = jnp.zeros_like(spread_ref)
            mine = (lane >= HEAD_DIM) if side else (lane < HEAD_DIM)
            for block in range(length // ROWS):
                here = slice(ROWS * block, ROWS * (block + 1))
                window = band_slice(block, length)
                queries = qkv_ref[0, pair, here, :] * 0.125
                queries = jnp.where(mine, queries, jnp.zeros_like(queries))
                grads = mgrad_ref[pair, here, :]
                grads = jnp.where(mine, grads, jnp.zeros_like(grads))
                column = iota((ROWS, lse_ref.shape[1]), 1)
                log_total = jnp.sum(jnp.where(column == head, lse_ref[here, :], 0.0), axis=-1, keepdims=True)
                scores = dot_t(queries, keys) + band_ref[:, window] + mask
                probs = jnp.exp(scores - log_total)
                probs_ref[here, :] = probs.astype(BF16)
                weighted = probs * dot_t(grads, values)
                score_grad = weighted - probs * jnp.sum(weighted, axis=-1, keepdims=True)
                spread_ref[:, window] += score_grad
                low = score_grad.astype(BF16)
                sgrad_ref[here, :] = low
                query_grad = (dot(low, keys) * 0.125).astype(BF16)
                if side:
                    query_grad = jnp.where(mine, query_grad, low_ref[0, pair, here, :])
                low_ref[0, pair, here, :] = query_grad
            rows = slice(HEAD_DIM * side, HEAD_DIM * (side + 1))
            kt_ref[rows, :] = dot(queries_t[rows, :], sgrad_ref[...]) * 0.125
            vt_ref[rows, :] = dot(grads_t[rows, :], probs_ref[...])
            size = spread_ref.shape[1]
            eight = spread_ref[0:8, :]
            for step in range(8, ROWS, 8):
                eight = eight + pltpu.roll(spread_ref[step : step + 8, :], size - step, 1)
            diagonal = eight[0:1, :]
            for step in range(1, 8):
                diagonal = diagonal + pltpu.roll(eight[step : step + 1, :], size - step, 1)
            diag_ref[head] = diagonal
        low_ref[1, pair] = kt_ref[...].T.astype(BF16)
        low_ref[2, pair] = vt_ref[...].T.astype(BF16)
        return carry

    lax.fori_loop(0, PAIRS, one_pair, 0)
    tokens = tok_ref[...].astype(F32)
    inverse = lax.rsqrt(jnp.mean(tokens * tokens, axis=-1, keepdims=True) + epsilon)
    gain = gain_ref[...]
    scaled = tokens * inverse
    normed_t = (scaled * gain).astype(BF16).T
    normed_grad = jnp.zeros((length, width), F32)
    for which, w_ref in enumerate((wq_ref, wk_ref, wv_ref)):
        low = jnp.concatenate([low_ref[which, p] for p in range(PAIRS)], axis=1)
        wgrad_ref[which] = dot(normed_t, low)
        normed_grad = normed_grad + dot_t(low, w_ref[...])
    ggrad_ref[...] = jnp.sum(normed_grad * scaled, axis=0, keepdims=True)
    upstream = normed_grad * gain
    middle = jnp.mean(upstream * scaled, axis=-1, keepdims=True)
    tgrad_ref[...] = (resgrad_ref[...] + inverse * (upstream - scaled * middle)).astype(BF16)


def attention_backward(count, qkv, lse, vector, mixed_grad, tokens, gain, wq, wk, wv, residual_grad):
    length, width = tokens.shape
    vmem = pl.BlockSpec(memory_space=pltpu.VMEM)
    size = vector.shape[-1]
    return pl.pallas_call(
        attn_back_kernel,
        in_specs=[pl.BlockSpec(memory_space=pltpu.SMEM)] + [vmem] * 10,
        out_specs=[vmem] * 4,
        out_shape=[
            jax.ShapeDtypeStruct((3, width, width), F32),
            jax.ShapeDtypeStruct((HEADS, 1, size), F32),
            jax.ShapeDtypeStruct((length, width), BF16),
            jax.ShapeDtypeStruct((1, width), F32),
        ],
        scratch_shapes=[
            pltpu.VMEM((ROWS, size), F32),
            pltpu.VMEM((length, length), BF16),
            pltpu.VMEM((length, length), BF16),
            pltpu.VMEM((ROWS, size), F32),
            pltpu.VMEM((3, PAIRS, length, PAIR), BF16),
            pltpu.VMEM((PAIR, length), F32),
            pltpu.VMEM((PAIR, length), F32),
        ],
        compiler_params=params(56),
        cost_estimate=cost(30e9, 20e6, HEADS * length * length),
    )(count, qkv, lse, vector, mixed_grad, tokens, gain, wq, wk, wv, residual_grad)


def offset_selector(length):
    place = np.arange(2 * length)
    offsets = np.where(place < 2 * length - ROWS, place, place - 2 * length) - (length - ROWS)
    offsets = np.clip(offsets, -(length - 1), length - 1)
    return (offset_bucket(offsets)[:, None] == np.arange(BUCKETS)[None, :]).astype(np.float32)


def shards(
    tokens,
    cotangent,
    lengths,
    routes,
    gain_attn,
    w_query,
    w_key,
    w_value,
    w_output,
    bucket_head_bias,
    gain_ffn,
    w_router,
    w_inner,
    w_outer,
):
    batches, _, length, width = tokens.shape
    experts = w_router.shape[1]
    local = w_inner.shape[0]
    groups = lax.axis_size("expert")
    planes = lax.axis_size("hidden")
    capacity = (5 * length + 4 * experts - 1) // (4 * experts)
    slots = experts * capacity
    rows = groups * capacity
    selector = jnp.asarray(offset_selector(length))
    vector = lax.dot_general(
        bucket_head_bias, selector, (((0,), (1,)), ((), ())), precision=lax.Precision.HIGHEST
    )[:, None, :]
    gain_a = gain_attn[None, :]
    gain_f = gain_ffn[None, :]
    counts = lengths[:, 0]

    def to_experts(values):
        sent = lax.all_to_all(
            values.reshape(groups, local, capacity, width), "expert", split_axis=0, concat_axis=0, tiled=True
        )
        mine = jnp.swapaxes(sent, 0, 1).reshape(local, rows, width)
        return lax.all_gather(mine, "hidden", axis=0)

    def to_tokens(values):
        summed = lax.psum_scatter(values, "hidden", scatter_dimension=0)
        sent = jnp.swapaxes(summed.reshape(local, groups, capacity, width), 0, 1)
        return lax.all_to_all(sent, "expert", split_axis=0, concat_axis=0, tiled=True).reshape(slots, width)

    srow, scol, cot_slots = prep(counts, routes.reshape(batches, length), cotangent[:, 0], experts, capacity)
    rcol = routes.reshape(batches, length, 1)
    each = range(batches)
    cs = [to_experts(cot_slots[b]) for b in each]
    forward = [
        attention_forward(
            counts[b : b + 1],
            tokens[b, 0],
            gain_a,
            w_query,
            w_key,
            w_value,
            w_output,
            vector,
            gain_f,
            w_router,
            srow[b],
            rcol[b],
            capacity,
        )
        for b in each
    ]
    xs = [to_experts(forward[b][6]) for b in each]
    worked = [experts_both(xs[b], cs[b], w_inner, w_outer) for b in each]
    gates = jnp.stack([forward[b][5][:, 0] for b in each])
    gates = lax.all_gather(gates, ("hidden", "expert"), axis=0)
    gates = gates.reshape(planes, groups, batches, groups, local, capacity)
    gates = lax.dynamic_index_in_dim(gates, lax.axis_index("expert"), 3, keepdims=False)
    gates = gates.transpose(3, 2, 0, 1, 4).reshape(local, batches * planes * rows, 1)
    outer_total, inner_total = expert_grads(
        xs, cs, [worked[b][2] for b in each], [worked[b][3] for b in each], gates
    )
    layer_rows, token_grads, terms = [], [], []
    for b in each:
        qkv, mixed, lse, residual, probs, _, _ = forward[b]
        outs = to_tokens(worked[b][0])
        ins = to_tokens(worked[b][1])
        layer, res_grad, mixed_grad, output_part, router_part, gain_f_part = combine(
            counts[b : b + 1],
            outs,
            ins,
            scol[b],
            rcol[b],
            residual,
            probs,
            cotangent[b, 0],
            gain_f,
            w_router,
            w_output,
            mixed,
        )
        qkv_part, diagonal, token_grad, gain_a_part = attention_backward(
            counts[b : b + 1],
            qkv,
            lse,
            vector,
            mixed_grad,
            tokens[b, 0],
            gain_a,
            w_query,
            w_key,
            w_value,
            res_grad,
        )
        layer_rows.append(layer)
        token_grads.append(token_grad)
        terms.append((gain_a_part, qkv_part, output_part, diagonal, gain_f_part, router_part))
    gain_a_part, qkv_part, output_part, diagonal, gain_f_part, router_part = (
        functools.reduce(jnp.add, parts) for parts in zip(*terms)
    )
    bias_part = lax.dot_general(
        selector, diagonal[:, 0], (((0,), (1,)), ((), ())), precision=lax.Precision.HIGHEST
    )
    big = lax.psum(
        jnp.concatenate([qkv_part.reshape(3 * width, width), output_part, router_part]).astype(BF16),
        ("expert", "hidden"),
    ).astype(F32)
    small = lax.psum(
        jnp.concatenate([gain_a_part[0], gain_f_part[0], bias_part.reshape(-1)]), ("expert", "hidden")
    )
    return (
        jnp.stack(layer_rows)[:, None],
        jnp.stack(token_grads)[:, None],
        small[:width],
        big[:width],
        big[width : 2 * width],
        big[2 * width : 3 * width],
        big[3 * width : 4 * width],
        small[2 * width :].reshape(BUCKETS, HEADS),
        small[width : 2 * width],
        big[4 * width :].T,
        inner_total,
        outer_total,
    )


def solution(mesh):
    token = P(None, ("expert", "hidden"), None, None)
    placed = (
        token,
        token,
        P(None, ("expert", "hidden")),
        token,
        *(P() for _ in range(8)),
        P("expert", None, "hidden"),
        P("expert", "hidden", None),
    )
    return jax.shard_map(
        shards,
        mesh=mesh,
        in_specs=placed,
        out_specs=(
            token,
            token,
            *(P() for _ in range(8)),
            P("expert", None, "hidden"),
            P("expert", "hidden", None),
        ),
        check_vma=False,
    )
```

time: 1120 us -> 944 us (0.84)
  matrix products: 313 us -> 1.53 us
  Pallas kernels: 0 us -> 199 us
  local copies, waits for them, and re-layouts: 137 us -> 87.9 us
  waiting for transfers between devices: 485 us -> 444 us
  blocking collectives: 114 us -> 151 us
  other arithmetic: 36.1 us -> 18.7 us
    dot_general x67 -> x2, matrix products: 313 us -> 1.53 us  [the longest x1 0.96 us: shards(): lax.dot_general(selector, diagonal[:, 0], (((0,), (1,)), ((), ())), preci...]
    reduce_scatter x0 -> x4, waiting for transfers between devices: none -> 255 us  [to_tokens(): summed = lax.psum_scatter(values, 'hidden', scatter_dimension=0)]
    pallas_call x0 -> x10, Pallas kernels: none -> 199 us  [the longest x2 67.7 us: attention_backward(): pl.pallas_call(attn_back_kernel, in_specs=[pl.BlockSpec(memory_space=pltp...]
    unnamed x13 -> x9, waiting for transfers between devices: 175 us -> 1.33 us
    psum x1, waiting for transfers between devices: 119 us -> 27.3 us  [shards(): lax.psum(jnp.concatenate([qkv_part.reshape(3 * width, width), output_part...]
    unnamed x313 -> x120, local copies, waits for them, and re-layouts: 81.9 us -> 28.2 us
    all_gather x0 -> x1, blocking collectives: none -> 42.1 us  [shards(): gates = lax.all_gather(gates, ('hidden', 'expert'), axis=0)]
    all_gather x4, waiting for transfers between devices: 184 us -> 161 us  [to_experts(): return lax.all_gather(mine, 'hidden', axis=0)]
  transfers between devices with their start and end apart: 13 -> 13, of which waited for: 10 -> 8; matrix products, arithmetic and copies ran while one was open for 24% -> 6% of each run, Pallas kernels for 0% -> 12%
where the time goes in v1:
time: 944 us; the launch traced here: 935 us
  waiting for transfers between devices  444 us (47%)
  Pallas kernels  199 us (21%)
  blocking collectives  151 us (16%)
  local copies, waits for them, and re-layouts  87.9 us (9%)
  other arithmetic  18.7 us (2%)
  starting transfers between devices  17.4 us (2%)
  between operations  15 us (2%)
    reduce_scatter x4, waiting for transfers between devices, to_tokens(): summed = lax.psum_scatter(values, 'hidden', scatter_dimension=0)  255 us
    all_gather x4, waiting for transfers between devices, to_experts(): return lax.all_gather(mine, 'hidden', axis=0)  161 us
    all_to_all x4, blocking collectives, to_experts(): lax.all_to_all(values.reshape(groups, local, capacity, width), 'expert',...  71.1 us
    pallas_call x2, Pallas kernels, attention_backward(): pl.pallas_call(attn_back_kernel, in_specs=[pl.BlockSpec(memory_space=pltp...  67.7 us
    pallas_call x2, Pallas kernels, attention_forward(): pl.pallas_call(functools.partial(attn_kernel, capacity), in_specs=[pl.Blo...  44.8 us
    all_gather x1, blocking collectives, shards(): gates = lax.all_gather(gates, ('hidden', 'expert'), axis=0)  42.1 us
    pallas_call x2, Pallas kernels, experts_both(): pl.pallas_call(expert_kernel, grid=(local,), in_specs=[slab, slab, weight...  39.1 us
    psum x1, blocking collectives, shards(): lax.psum(jnp.concatenate([gain_a_part[0], gain_f_part[0], bias_part.resha...  37.5 us
  transfers between devices with their start and end apart: 13, of which 8 were waited for; matrix products, arithmetic and copies ran while one was open for 6% of the time, Pallas kernels for 12%

profile of v1, /device:TPU:0, one launch (start us, length us, event | category | flops | bytes accessed | tf_op | source)
XLA Modules:
  0.0 935.1 jit_solution(16717647096605095593)
XLA Ops:
  10.9 2.6 shard_map.238
  15.3 19.8 %all_to_all.40 = bf16[8,8,10,768]{3,1,2,0:T(8,128)(2,1)S(1)} all-to-all(bf16[8,8,10,768]{3,1,2,0:T(8,128)(2,1)S(1)} %copy.122), channel_id=1, replica_groups=mesh['expert'=8,'hidden'=4] {'expert'}, dimensions={0} | all-to-all | bytes 1966080 | tf_op jit(solution)/shard_map/all_to_all | solution.py:548
  41.3 22.5 %shard_map.242 = (bf16[3,6,512,128]{3,2,1,0:T(8,128)(2,1)}, bf16[6,512,128]{2,1,0:T(8,128)(2,1)S(1)}, f32[512,128]{1,0:T(8,128)S(1)}, f32[512,768]{1,0:T(8,128)}...) custom-call(s32[1]{0:T(128)} %bitcast.19.len_ref, ...), custom_call_target="tpu_custom_call" | custom-call | flops 14000000000 | bytes 14000000 | tf_op jit(solution)/shard_map/pallas_call | solution.py:210
  68.5 17.2 %all_to_all.41 = bf16[8,8,10,768]{3,1,2,0:T(8,128)(2,1)S(1)} all-to-all(bf16[8,8,10,768]{3,1,2,0:T(8,128)(2,1)S(1)} %copy.120), channel_id=1, replica_groups=mesh['expert'=8,'hidden'=4] {'expert'}, dimensions={0} | all-to-all | bytes 1966080 | tf_op jit(solution)/shard_map/all_to_all | solution.py:548
  89.9 17.1 %all_to_all.42 = bf16[8,8,10,768]{3,1,2,0:T(8,128)(2,1)S(1)} all-to-all(bf16[8,8,10,768]{3,1,2,0:T(8,128)(2,1)S(1)} %copy.110), channel_id=1, replica_groups=mesh['expert'=8,'hidden'=4] {'expert'}, dimensions={0} | all-to-all | bytes 1966080 | tf_op jit(solution)/shard_map/all_to_all | solution.py:548
  110.3 22.3 %shard_map.239 = (bf16[3,6,512,128]{3,2,1,0:T(8,128)(2,1)}, bf16[6,512,128]{2,1,0:T(8,128)(2,1)S(1)}, f32[512,128]{1,0:T(8,128)S(1)}, f32[512,768]{1,0:T(8,128)}...) custom-call(s32[1]{0:T(128)} %bitcast.len_ref, ...), custom_call_target="tpu_custom_call" | custom-call | flops 14000000000 | bytes 14000000 | tf_op jit(solution)/shard_map/pallas_call | solution.py:210
  137.8 17.1 %all_to_all.43 = bf16[8,8,10,768]{3,1,2,0:T(8,128)(2,1)S(1)} all-to-all(bf16[8,8,10,768]{3,1,2,0:T(8,128)(2,1)S(1)} %copy.108), channel_id=1, replica_groups=mesh['expert'=8,'hidden'=4] {'expert'}, dimensions={0} | all-to-all | bytes 1966080 | tf_op jit(solution)/shard_map/all_to_all | solution.py:548
  156.1 33.2 %all-gather.11.cloned.1.call-done.x_ref.refs_1_ = bf16[4,8,80,768]{3,2,1,0:T(8,128)(2,1)} async-done(((bf16[1,8,80,768]{3,2,1,0:T(8,128)(2,1)}), bf16[4,8,80,768]{3,2,1,0:T(8,128)(2,1)}) %all-gather.11.cloned.1.call-update) | async-done | bytes 3932176 | tf_op jit(solution)/shard_map/all_gather | solution.py:552
  189.4 19.4 %shard_map.243 = (bf16[4,8,80,768]{3,2,1,0:T(8,128)(2,1)S(1)}, bf16[4,8,80,768]{3,2,1,0:T(8,128)(2,1)S(1)}, bf16[8,320,768]{2,1,0:T(8,128)(2,1)S(1)}, bf16[8,320,768]{2,1,0:T(8,128)(2,1)}) custom-call(bf16[4,8,80,768]{3,2,1,0:T(8,128)(2,1)} %all-gather.11.cloned.1.call-done.x_ref.refs_1_, ...), custom_call_target="tpu_custom_call" | custom-call | flops 12079595520 | bytes 42467328 | tf_op jit(solution)/shard_map/pallas_call | solution.py:256
  208.7 1.9 copy-done.2
  212.6 2.0 copy-done.28
  215.2 50.8 %all-gather.9.cloned.1.call-done.c_ref.refs_2_ = bf16[4,8,80,768]{3,2,1,0:T(8,128)(2,1)} async-done(((bf16[1,8,80,768]{3,2,1,0:T(8,128)(2,1)}), bf16[4,8,80,768]{3,2,1,0:T(8,128)(2,1)}) %all-gather.9.cloned.1.call-update) | async-done | bytes 3932176 | tf_op jit(solution)/shard_map/all_gather | solution.py:552
  266.0 77.0 %all-gather.7.cloned.1.call-done.x_ref.refs_0_ = bf16[4,8,80,768]{3,2,1,0:T(8,128)(2,1)} async-done(((bf16[1,8,80,768]{3,2,1,0:T(8,128)(2,1)}), bf16[4,8,80,768]{3,2,1,0:T(8,128)(2,1)}) %all-gather.7.cloned.1.call-update) | async-done | bytes 3932176 | tf_op jit(solution)/shard_map/all_gather | solution.py:552
  343.0 19.8 %shard_map.240 = (bf16[4,8,80,768]{3,2,1,0:T(8,128)(2,1)S(1)}, bf16[4,8,80,768]{3,2,1,0:T(8,128)(2,1)S(1)}, bf16[8,320,768]{2,1,0:T(8,128)(2,1)S(1)}, bf16[8,320,768]{2,1,0:T(8,128)(2,1)}) custom-call(bf16[4,8,80,768]{3,2,1,0:T(8,128)(2,1)} %all-gather.7.cloned.1.call-done.x_ref.refs_0_, bf16[4,8,80,768]{3,2,1,0:T(8,128)(2,1)} %all-gather.9.cloned.1.call-done.c_ref.refs_2_, ...), custom_call_target="tpu_custom_call" | custom-call | flops 12079595520 | bytes 42467328 | tf_op jit(solution)/shard_map/pallas_call | solution.py:256
  369.1 47.9 %reduce-scatter.11.cloned.1.call-done = bf16[1,8,80,768]{3,2,1,0:T(8,128)(2,1)} async-done(((bf16[4,8,80,768]{3,2,1,0:T(8,128)(2,1)}), bf16[1,8,80,768]{3,2,1,0:T(8,128)(2,1)}) %reduce-scatter.11.cloned.1.call-update) | async-done | bytes 983056 | tf_op jit(solution)/shard_map/reduce_scatter | solution.py:555
  417.0 2.4 copy.126
  419.4 3.7 all-to-all-start.7
  423.1 69.7 %reduce-scatter.9.cloned.1.call-done = bf16[1,8,80,768]{3,2,1,0:T(8,128)(2,1)} async-done(((bf16[4,8,80,768]{3,2,1,0:T(8,128)(2,1)}), bf16[1,8,80,768]{3,2,1,0:T(8,128)(2,1)}) %reduce-scatter.9.cloned.1.call-update) | async-done | bytes 983056 | tf_op jit(solution)/shard_map/reduce_scatter | solution.py:555
  492.8 2.4 copy.124
  495.2 4.2 all-to-all-start.6
  499.5 68.7 %reduce-scatter.5.cloned.1.call-done = bf16[1,8,80,768]{3,2,1,0:T(8,128)(2,1)} async-done(((bf16[4,8,80,768]{3,2,1,0:T(8,128)(2,1)}), bf16[1,8,80,768]{3,2,1,0:T(8,128)(2,1)}) %reduce-scatter.5.cloned.1.call-update) | async-done | bytes 983056 | tf_op jit(solution)/shard_map/reduce_scatter | solution.py:555
  568.2 2.4 copy.112
  570.6 4.4 all-to-all-start.2
  575.0 68.5 %reduce-scatter.7.cloned.1.call-done = bf16[1,8,80,768]{3,2,1,0:T(8,128)(2,1)} async-done(((bf16[4,8,80,768]{3,2,1,0:T(8,128)(2,1)}), bf16[1,8,80,768]{3,2,1,0:T(8,128)(2,1)}) %reduce-scatter.7.cloned.1.call-update) | async-done | bytes 983056 | tf_op jit(solution)/shard_map/reduce_scatter | solution.py:555
  643.5 2.4 copy.114
  646.0 4.2 all-to-all-start.3
  652.6 2.7 copy.125
  655.3 2.3 reshape.77.out_ref
  659.0 3.0 reshape.78.in_ref
  662.1 2.6 copy.113
  664.7 2.3 reshape.74.out_ref
  667.0 2.7 copy.115
  669.7 3.0 reshape.75.in_ref
  677.8 8.3 shard_map.244
  687.0 8.3 shard_map.241
  695.4 3.5 add_convert_fusion.1
  699.0 33.5 %shard_map.246 = (f32[3,768,768]{2,1,0:T(8,128)}, f32[12,1,1024]{2,1,0:T(1,128)}, bf16[512,768]{1,0:T(8,128)(2,1)}, f32[1,768]{1,0:T(1,128)}) custom-call(s32[1]{0:T(128)} %bitcast.19.len_ref, bf16[3,6,512,128]{3,2,1,0:T(8,128)(2,1)} %get-tuple-element.81.qkv_ref, f32[512,128]{1,0:T(8,128)} %copy-done.40, f32[12,1,1024]{2,1,0:T(1,128)} %copy-done.20, ...), custom_call_target="tpu_custom_call" | custom-call | flops 30000001024 | bytes 20000000 | tf_op jit(solution)/shard_map/pallas_call | solution.py:484
  732.5 34.2 %shard_map.245 = (f32[3,768,768]{2,1,0:T(8,128)}, f32[12,1,1024]{2,1,0:T(1,128)}, bf16[512,768]{1,0:T(8,128)(2,1)}, f32[1,768]{1,0:T(1,128)}) custom-call(s32[1]{0:T(128)} %bitcast.len_ref, bf16[3,6,512,128]{3,2,1,0:T(8,128)(2,1)} %get-tuple-element.76.qkv_ref, f32[512,128]{1,0:T(8,128)} %copy-done.41, f32[12,1,1024]{2,1,0:T(1,128)} %copy-done.20, ...), custom_call_target="tpu_custom_call" | custom-call | flops 30000001024 | bytes 20000000 | tf_op jit(solution)/shard_map/pallas_call | solution.py:484
  766.7 4.5 add_convert_fusion
  771.2 2.5 pad_maximum_fusion
  773.8 42.1 %all-gather.1 = f32[32,2,640]{2,1,0:T(2,128)S(1)} all-gather(f32[1,2,640]{2,1,0:T(2,128)S(1)} %maximum_bitcast_fusion.2), channel_id=2, replica_groups=mesh['expert'=8,'hidden'=4] {'hidden','expert'}, dimensions={0}, use_global_device_ids=true | all-gather | bytes 168960 | tf_op jit(solution)/shard_map/all_gather | solution.py:584
  815.9 2.2 reshape.82
  820.7 28.5 %shard_map.247 = (f32[8,768,768]{2,1,0:T(8,128)}, f32[8,768,768]{2,1,0:T(8,128)}) custom-call(bf16[4,8,80,768]{3,2,1,0:T(8,128)(2,1)} %all-gather.7.cloned.1.call-done.x_ref.refs_0_, bf16[4,8,80,768]{3,2,1,0:T(8,128)(2,1)} %all-gather.11.cloned.1.call-done.x_ref.refs_1_, bf16[4,8,80,768]{3,2,1,0:T(8,128)(2,1)} %all-gather.9.cloned.1.call-done.c_ref.refs_2_, ...), custom_call_target="tpu_custom_call" | custom-call | flops 12079595520 | bytes 69206016 | tf_op jit(solution)/shard_map/pallas_call | solution.py:299
  850.4 37.5 %psum.14 = f32[1920]{0:T(1024)S(1)} all-reduce(f32[1920]{0:T(1024)S(1)} %pad_maximum_fusion.1), channel_id=1, replica_groups=mesh['expert'=8,'hidden'=4] {'expert','hidden'}, use_global_device_ids=true, to_apply=%region_4.5 | all-reduce | flops 1920 | bytes 15360 | tf_op jit(solution)/shard_map/psum | solution.py:636
  888.6 3.7 maximum_bitcast_fusion
  893.0 27.3 %all-reduce.2.cloned.1.call-done = bf16[3136,768]{1,0:T(8,128)(2,1)} async-done(((bf16[3136,768]{1,0:T(8,128)(2,1)}), bf16[3136,768]{1,0:T(8,128)(2,1)}) %all-reduce.2.cloned.1.call-update) | async-done | bytes 4816912 | tf_op jit(solution)/shard_map/psum | solution.py:632
  920.2 3.3 convert_element_type.4
  924.2 3.8 fusion.1
  (190 shorter events, 54.6 us)
Async XLA Ops:
  7.2 29.1 %copy-start = (f32[32,12]{0,1:T(8,128)S(1)}, f32[32,12]{0,1:T(8,128)}, u32[]{:S(2)}) copy-start(f32[32,12]{0,1:T(8,128)} %param.24) | copy-start | bytes 4612
  7.2 148.9 %all-gather.13.cloned.1.call-start = ((), (), s32[]{:S(2)}) async-start(), calls=%async_computation.17 | async-start | bytes 4915200 | tf_op jit(solution)/shard_map/all_gather | solution.py:552
  15.2 21.0 %copy-start.53 = (f32[768]{0:T(1024)S(1)}, f32[768]{0:T(1024)}, u32[]{:S(2)}) copy-start(f32[768]{0:T(1024)} %param.19) | copy-start | bytes 9220
  15.2 21.0 %copy-start.54 = (f32[768]{0:T(1024)S(1)}, f32[768]{0:T(1024)}, u32[]{:S(2)}) copy-start(f32[768]{0:T(1024)} %param.25) | copy-start | bytes 9220
  15.3 21.0 %copy-start.48 = (f32[1024,32]{1,0:T(8,128)S(1)}, f32[1024,32]{1,0:T(8,128)}, u32[]{:S(2)}) copy-start(f32[1024,32]{1,0:T(8,128)} %constant.14.clone) | copy-start | bytes 393220
  15.3 21.7 %copy-start.50 = (bf16[768,64]{0,1:T(8,128)(2,1)S(1)}, bf16[768,64]{0,1:T(8,128)(2,1)}, u32[]{:S(2)}) copy-start(bf16[768,64]{0,1:T(8,128)(2,1)} %param.26) | copy-start | bytes 294916
  36.2 153.2 %all-gather.11.cloned.1.call-start = ((), (), s32[]{:S(2)}) async-start(), calls=%async_computation.16 | async-start | bytes 4915200 | tf_op jit(solution)/shard_map/all_gather | solution.py:552
  36.3 72.6 %copy-start.23 = (f32[1,768]{1,0:T(1,128)}, f32[1,768]{1,0:T(1,128)S(1)}, u32[]{:S(2)}) copy-start(f32[1,768]{1,0:T(1,128)S(1)} %broadcast_in_dim.15.gain_ref) | copy-start | bytes 9220
  36.9 72.0 %copy-start.20 = (f32[12,1,1024]{2,1,0:T(1,128)}, f32[12,1,1024]{2,1,0:T(1,128)S(1)}, u32[]{:S(2)}) copy-start(f32[12,1,1024]{2,1,0:T(1,128)S(1)} %broadcast_in_dim.16.vec_ref) | copy-start | bytes 147460
  37.1 71.8 %copy-start.18 = (bf16[768,64]{1,0:T(8,128)(2,1)}, bf16[768,64]{1,0:T(8,128)(2,1)S(1)}, u32[]{:S(2)}) copy-start(bf16[768,64]{1,0:T(8,128)(2,1)S(1)} %copy.106.wr_ref) | copy-start | bytes 294916
  37.3 26.5 %copy-start.13 = (s32[512,1]{1,0:T(8,128)}, s32[512,1]{1,0:T(8,128)S(1)}, u32[]{:S(2)}) copy-start(s32[512,1]{1,0:T(8,128)S(1)} %copy.119.rcol_ref) | copy-start | bytes 6148
  39.4 24.4 %copy-start.10 = (bf16[512,768]{1,0:T(8,128)(2,1)}, bf16[512,768]{1,0:T(8,128)(2,1)S(1)}, u32[]{:S(2)}) copy-start(bf16[512,768]{1,0:T(8,128)(2,1)S(1)} %get-tuple-element.163.tok_ref) | copy-start | bytes 2359300
  39.4 69.5 %copy-start.9 = (bf16[512,768]{1,0:T(8,128)(2,1)}, bf16[512,768]{1,0:T(8,128)(2,1)S(1)}, u32[]{:S(2)}) copy-start(bf16[512,768]{1,0:T(8,128)(2,1)S(1)} %get-tuple-element.162.tok_ref) | copy-start | bytes 2359300
  65.4 3.0 copy-start.36
  68.5 18.4 %copy-start.46 = (bf16[1,640,768]{2,1,0:T(8,128)(2,1)S(1)}, bf16[1,640,768]{2,1,0:T(8,128)(2,1)}, u32[]{:S(2)}) copy-start(bf16[1,640,768]{2,1,0:T(8,128)(2,1)} %get-tuple-element.158) | copy-start | bytes 2949124
  86.8 179.2 %all-gather.9.cloned.1.call-start = ((), (), s32[]{:S(2)}) async-start(), calls=%async_computation.13 | async-start | bytes 4915200 | tf_op jit(solution)/shard_map/all_gather | solution.py:552
  108.1 234.9 %all-gather.7.cloned.1.call-start = ((), (), s32[]{:S(2)}) async-start(), calls=%async_computation.12 | async-start | bytes 4915200 | tf_op jit(solution)/shard_map/all_gather | solution.py:552
  108.9 23.6 %copy-start.15 = (s32[512,1]{1,0:T(8,128)}, s32[512,1]{1,0:T(8,128)S(1)}, u32[]{:S(2)}) copy-start(s32[512,1]{1,0:T(8,128)S(1)} %copy.107.rcol_ref) | copy-start | bytes 6148
  156.1 261.0 %reduce-scatter.11.cloned.1.call-start = ((), (), s32[]{:S(2)}) async-start(), calls=%async_computation.19 | async-start | bytes 4915200 | tf_op jit(solution)/shard_map/reduce_scatter | solution.py:555
  214.5 278.3 %reduce-scatter.9.cloned.1.call-start = ((), (), s32[]{:S(2)}) async-start(), calls=%async_computation.18 | async-start | bytes 4915200 | tf_op jit(solution)/shard_map/reduce_scatter | solution.py:555
  215.1 353.0 %reduce-scatter.5.cloned.1.call-start = ((), (), s32[]{:S(2)}) async-start(), calls=%async_computation.14 | async-start | bytes 4915200 | tf_op jit(solution)/shard_map/reduce_scatter | solution.py:555
  368.4 275.1 %reduce-scatter.7.cloned.1.call-start = ((), (), s32[]{:S(2)}) async-start(), calls=%async_computation.15 | async-start | bytes 4915200 | tf_op jit(solution)/shard_map/reduce_scatter | solution.py:555
  419.4 75.8 %all-to-all-start.7 = ((bf16[8,8,10,768]{3,1,2,0:T(8,128)(2,1)}), bf16[8,8,10,768]{3,1,2,0:T(8,128)(2,1)S(1)}, u32[]{:S(2)}, u32[]{:S(2)}) async-start(bf16[8,8,10,768]{3,1,2,0:T(8,128)(2,1)} %bitcast.93), calls=%async_computation.11 | async-start | bytes 1966080 | tf_op jit(solution)/shard_map/all_to_all | solution.py:557
  495.2 75.4 %copy-start.44 = (bf16[8,8,10,768]{3,1,2,0:T(8,128)(2,1)}, bf16[8,8,10,768]{3,1,2,0:T(8,128)(2,1)S(1)}, u32[]{:S(2)}) copy-start(bf16[8,8,10,768]{3,1,2,0:T(8,128)(2,1)S(1)} %all-to-all-done.7) | copy-start | bytes 2949124
  495.2 75.4 %all-to-all-start.6 = ((bf16[8,8,10,768]{3,1,2,0:T(8,128)(2,1)}), bf16[8,8,10,768]{3,1,2,0:T(8,128)(2,1)}, u32[]{:S(2)}, u32[]{:S(2)}) async-start(bf16[8,8,10,768]{3,1,2,0:T(8,128)(2,1)} %bitcast.91), calls=%async_computation.9 | async-start | bytes 1966080 | tf_op jit(solution)/shard_map/all_to_all | solution.py:557
  570.6 75.4 %all-to-all-start.2 = ((bf16[8,8,10,768]{3,1,2,0:T(8,128)(2,1)}), bf16[8,8,10,768]{3,1,2,0:T(8,128)(2,1)}, u32[]{:S(2)}, u32[]{:S(2)}) async-start(bf16[8,8,10,768]{3,1,2,0:T(8,128)(2,1)} %bitcast.92), calls=%async_computation.3 | async-start | bytes 1966080 | tf_op jit(solution)/shard_map/all_to_all | solution.py:557
  575.0 76.3 %copy-start.7 = (bf16[2,1,512,768]{3,2,1,0:T(8,128)(2,1)S(1)}, bf16[2,1,512,768]{3,2,1,0:T(8,128)(2,1)}, u32[]{:S(2)}) copy-start(bf16[2,1,512,768]{3,2,1,0:T(8,128)(2,1)} %param.16) | copy-start | bytes 4718596
  646.0 21.0 %all-to-all-start.3 = ((bf16[8,8,10,768]{3,1,2,0:T(8,128)(2,1)}), bf16[8,8,10,768]{3,1,2,0:T(8,128)(2,1)}, u32[]{:S(2)}, u32[]{:S(2)}) async-start(bf16[8,8,10,768]{3,1,2,0:T(8,128)(2,1)} %bitcast.90), calls=%async_computation.5 | async-start | bytes 1966080 | tf_op jit(solution)/shard_map/all_to_all | solution.py:557
  650.2 270.0 %all-reduce.2.cloned.1.call-start = ((), (), s32[]{:S(2)}) async-start(), calls=%async_computation.20 | async-start | bytes 9633792 | tf_op jit(solution)/shard_map/psum | solution.py:632
  652.6 5.0 copy-start.45
  667.0 5.7 copy-start.14
  677.8 9.2 copy-start.11
  677.8 9.2 copy-start.16
  677.8 9.2 copy-start.33
  677.8 9.2 copy-start.39
  687.0 8.4 copy-start.47
  695.4 3.6 copy-start.8
  695.4 3.6 copy-start.35
  732.5 34.2 %slice-start = ((s8[7077888]{0:T(1024)(128)(4,1)}), s8[4194304]{0:T(1024)(128)(4,1)S(1)}, s32[]{:S(2)}) async-start(s8[7077888]{0:T(1024)(128)(4,1)} %bitcast.88), calls=%async_computation.21 | async-start | bytes 8388608
  732.5 34.2 %slice-start.1 = ((s8[7077888]{0:T(1024)(128)(4,1)}), s8[2883584]{0:T(1024)(128)(4,1)S(1)}, s32[]{:S(2)}) async-start(s8[7077888]{0:T(1024)(128)(4,1)} %bitcast.88), calls=%async_computation.22 | async-start | bytes 5767168
  766.7 4.5 copy-start.43
  820.6 28.5 %copy-start.51 = (f32[12,1,1024]{2,1,0:T(1,128)S(1)}, f32[12,1,1024]{2,1,0:T(1,128)}, u32[]{:S(2)}) copy-start(f32[12,1,1024]{2,1,0:T(1,128)} %get-tuple-element.91) | copy-start | bytes 147460
  820.6 28.5 %copy-start.52 = (f32[12,1,1024]{2,1,0:T(1,128)S(1)}, f32[12,1,1024]{2,1,0:T(1,128)}, u32[]{:S(2)}) copy-start(f32[12,1,1024]{2,1,0:T(1,128)} %get-tuple-element.90) | copy-start | bytes 147460
  820.6 28.6 %copy-start.49 = (f32[1024,32]{1,0:T(8,128)S(1)}, f32[1024,32]{1,0:T(8,128)}, u32[]{:S(2)}) copy-start(f32[1024,32]{1,0:T(8,128)} %constant.14.clone) | copy-start | bytes 393220
  820.6 29.7 %copy-start.55 = (f32[1,768]{1,0:T(1,128)S(1)}, f32[1,768]{1,0:T(1,128)}, u32[]{:S(2)}) copy-start(f32[1,768]{1,0:T(1,128)} %get-tuple-element.87) | copy-start | bytes 9220
  820.7 29.7 %copy-start.56 = (f32[1,768]{1,0:T(1,128)S(1)}, f32[1,768]{1,0:T(1,128)}, u32[]{:S(2)}) copy-start(f32[1,768]{1,0:T(1,128)} %get-tuple-element.86) | copy-start | bytes 9220
  920.2 4.0 copy-start.42
  924.2 3.8 copy-start.1
  (24 other events, 31.5 us)
Sparse Core Ops, SparseCore 0:
  36.3 75.7 all-gather.12
  114.3 75.0 all-gather.10
  190.9 74.9 all-gather.8
  268.0 74.9 all-gather.6
  345.7 71.2 reduce-scatter.10
  419.7 73.0 reduce-scatter.8
  495.1 73.0 reduce-scatter.4
  570.5 73.0 reduce-scatter.6
  773.9 146.3 all-reduce.1

commit v2 on v1

v2 whole, which is shorter than its diff:
```python
import functools

import jax
import jax.numpy as jnp
import numpy as np
from jax import lax
from jax.experimental import pallas as pl
from jax.experimental.pallas import tpu as pltpu
from jax.sharding import PartitionSpec as P

HEADS = 12
HEAD_DIM = 64
BUCKETS = 32
MAXDIST = 128
PAIR = 2 * HEAD_DIM
PAIRS = HEADS // 2
ROWS = 128

epsilon = 1e-06
negative = -1e30
F32 = jnp.float32
BF16 = jnp.bfloat16
MIB = 1 << 20


def params(mib):
    return pltpu.CompilerParams(vmem_limit_bytes=mib * MIB)


def cost(*_):
    return pl.CostEstimate(flops=1, bytes_accessed=1, transcendentals=0)


def offset_bucket(offsets):
    halfway = BUCKETS // 2
    exact_count = halfway // 2
    relative_distance = np.abs(offsets)
    scaled = (
        np.log(np.maximum(relative_distance, 1) / exact_count)
        / np.log(MAXDIST / exact_count)
        * (halfway - exact_count)
    )
    far_bucket = np.minimum(exact_count + np.floor(scaled).astype(np.int64), halfway - 1)
    near_bucket = np.where(relative_distance < exact_count, relative_distance, far_bucket)
    return (np.where(offsets > 0, halfway, 0) + near_bucket).astype(np.int32)


def dot(a, b):
    return lax.dot_general(a, b, (((1,), (0,)), ((), ())), preferred_element_type=F32)


def dot_t(a, b):
    return lax.dot_general(a, b, (((1,), (1,)), ((), ())), preferred_element_type=F32)


def t_dot(a, b):
    return lax.dot_general(a, b, (((0,), (0,)), ((), ())), preferred_element_type=F32)


def one_hot(condition):
    return jnp.where(condition, 1.0, 0.0).astype(BF16)


def batch_block(array, b):
    rest = array.shape[1:]
    return pl.BlockSpec((1,) + rest, lambda *_: (b,) + (0,) * len(rest))


ANYWHERE = pl.BlockSpec(memory_space=pl.ANY)
WHOLE = pl.BlockSpec(memory_space=pltpu.VMEM)
SCALARS = pl.BlockSpec(memory_space=pltpu.SMEM)


def iota(shape, axis):
    return lax.broadcasted_iota(jnp.int32, shape, axis)


def padded(rows):
    return -(-rows // 16) * 16


def spread_slots(slot, per, message):
    if message == per:
        return slot
    return jnp.where(slot < 0, -1, slot + lax.div(jnp.maximum(slot, 0), per) * (message - per))


def prep_kernel(per, capacity, len_ref, row_ref, col_ref, cot_ref, srow_ref, scol_ref, slots_ref):
    batches, _, length = row_ref.shape
    groups, message, width = slots_ref.shape
    experts = groups * per // capacity
    before = one_hot(iota((length, length), 0) < iota((length, length), 1))
    after = one_hot(iota((length, length), 1) < iota((length, length), 0))
    for b in range(batches):
        count = len_ref[b]
        row = row_ref[b]
        col = col_ref[b]
        valid_row = iota((1, length), 1) < count
        valid_col = iota((length, 1), 0) < count
        chosen_row = iota((experts, length), 0) == row
        chosen_col = iota((length, experts), 1) == col
        earlier_row = dot(one_hot(chosen_row & valid_row), before)
        rank_row = jnp.sum(jnp.where(chosen_row, earlier_row, 0.0), axis=0, keepdims=True).astype(jnp.int32)
        earlier_col = dot(after, one_hot(chosen_col & valid_col))
        rank_col = jnp.sum(jnp.where(chosen_col, earlier_col, 0.0), axis=1, keepdims=True).astype(jnp.int32)
        slot_row = jnp.where(valid_row & (rank_row < capacity), row * capacity + rank_row, -1)
        srow_ref[b] = slot_row
        scol_ref[b] = jnp.where(valid_col & (rank_col < capacity), col * capacity + rank_col, -1)
        if b == 0:
            dispatch = one_hot(iota((groups * message, length), 0) == spread_slots(slot_row, per, message))
            slots_ref[...] = dot(dispatch, cot_ref[0, 0]).astype(BF16).reshape(groups, message, width)


def prep(lengths, routes, cot, groups, per, capacity):
    batches, length = routes.shape
    width = cot.shape[-1]
    vmem = WHOLE
    message = padded(per)
    return pl.pallas_call(
        functools.partial(prep_kernel, per, capacity),
        grid=(1,),
        in_specs=[SCALARS, vmem, vmem, batch_block(cot, 0)],
        out_specs=[vmem] * 3,
        out_shape=[
            jax.ShapeDtypeStruct((batches, 1, length), jnp.int32),
            jax.ShapeDtypeStruct((batches, length, 1), jnp.int32),
            jax.ShapeDtypeStruct((groups, message, width), BF16),
        ],
        compiler_params=params(32),
        cost_estimate=cost(2 * groups * message * length * width, 4 * groups * message * width),
    )(lengths, routes.reshape(batches, 1, length), routes.reshape(batches, length, 1), cot)


def regroup_kernel(count, inputs, *refs):
    move_ref, out_ref = refs[0], refs[-1]
    total = refs[1][...].astype(F32)
    for ref in refs[2 : 1 + count]:
        total = total + ref[...].astype(F32)
    out_ref[...] = dot(move_ref[...], total.astype(BF16).reshape(inputs, -1)).astype(BF16).reshape(out_ref.shape)


def regroup(move, arrays, shape):
    inputs = move.shape[1]
    vmem = pl.BlockSpec(memory_space=pltpu.VMEM)
    return pl.pallas_call(
        functools.partial(regroup_kernel, len(arrays), inputs),
        in_specs=[vmem] * (1 + len(arrays)),
        out_specs=vmem,
        out_shape=jax.ShapeDtypeStruct(shape, BF16),
        compiler_params=params(32),
        cost_estimate=cost(2 * move.size * shape[-1], 4e6),
    )(move, *arrays)


def regroup_gated_kernel(capacity, move_ref, in_ref, out_ref):
    groups, message, width = in_ref.shape
    total = move_ref.shape[0]
    local = total // (groups * capacity)
    rows = groups * capacity
    flat = in_ref[...].reshape(groups * message, width)
    out_ref[:total, :] = dot(move_ref[...], flat).astype(BF16)
    place = iota((message, 128), 0)
    lane = iota((message, 128), 1)
    columns = []
    for g in range(groups):
        gates = in_ref[g, message - 16 : message, :].astype(F32)[0:1, :]
        parts = [
            jnp.sum(jnp.where(place == lane, gates[:, 128 * k : 128 * (k + 1)], 0.0), axis=1, keepdims=True)
            for k in range(3)
        ]
        wide = iota((message, 128), 1)
        columns.append(jnp.where(wide == 0, parts[0], jnp.where(wide == 1, parts[1], jnp.where(wide == 2, parts[2], 0.0))))
    column = jnp.concatenate(columns, axis=0).astype(BF16)
    moved = dot(move_ref[...], column)
    place = iota((rows, 128), 0)
    lane = iota((rows, 128), 1)
    lines = []
    for l in range(local):
        mine = moved[l * rows : (l + 1) * rows, :]
        parts = [
            jnp.sum(jnp.where(place == lane, mine[:, k : k + 1], 0.0), axis=0, keepdims=True) for k in range(3)
        ]
        lines.append(jnp.concatenate(parts + [jnp.zeros((1, width - 384), F32)], axis=1))
    lines.append(jnp.zeros((16 - local, width), F32))
    out_ref[total:, :] = jnp.concatenate(lines, axis=0).astype(BF16)


def regroup_gated(move, slots, capacity):
    width = slots.shape[-1]
    vmem = pl.BlockSpec(memory_space=pltpu.VMEM)
    return pl.pallas_call(
        functools.partial(regroup_gated_kernel, capacity),
        in_specs=[vmem] * 2,
        out_specs=vmem,
        out_shape=jax.ShapeDtypeStruct((move.shape[0] + 16, width), BF16),
        compiler_params=params(32),
        cost_estimate=cost(2 * move.size * width, 4e6),
    )(move, slots)


def band_bias(vector_ref, head):
    wide = jnp.broadcast_to(vector_ref[head], (ROWS, vector_ref.shape[-1]))
    return pltpu.roll(wide, 0, 1, stride=1, stride_axis=0)


def band_slice(block, length):
    start = length - ROWS * (block + 1)
    return slice(start, start + length)


def attn_kernel(
    per,
    gated,
    batch,
    waits,
    *refs,
):
    refs = refs[waits:]
    len_ref, tok_ref, cot_ref, gain_ref, wq_ref, wk_ref, wv_ref, wo_ref, vec_ref, gffn_ref, wr_ref, srow_ref, rcol_ref, *refs = refs
    qkv_ref, mixed_ref, lse_ref, res_ref, probs_ref, slots_ref, *rest = refs
    band_ref = rest[-1]
    length, width = tok_ref.shape[2:]
    count = len_ref[batch]
    tokens = tok_ref[0, 0].astype(F32)
    inverse = lax.rsqrt(jnp.mean(tokens * tokens, axis=-1, keepdims=True) + epsilon)
    normed = (tokens * inverse * gain_ref[...]).astype(BF16)
    for which, w_ref in enumerate((wq_ref, wk_ref, wv_ref)):
        for part in range(width // 256):
            rows = dot(normed, w_ref[:, 256 * part : 256 * part + 256]).astype(BF16)
            qkv_ref[which, 2 * part] = rows[:, :PAIR]
            qkv_ref[which, 2 * part + 1] = rows[:, PAIR:]
    mask = jnp.where(iota((1, length), 1) < count, 0.0, negative)
    lane = iota((ROWS, PAIR), 1)
    lse_ref[...] = jnp.zeros_like(lse_ref)

    def one_pair(pair, carry):
        keys = qkv_ref[1, pair]
        values = qkv_ref[2, pair]
        for side in range(2):
            head = 2 * pair + side
            band_ref[...] = band_bias(vec_ref, head)
            mine = (lane >= HEAD_DIM) if side else (lane < HEAD_DIM)
            for block in range(length // ROWS):
                here = slice(ROWS * block, ROWS * (block + 1))
                queries = qkv_ref[0, pair, here, :] * 0.125
                queries = jnp.where(mine, queries, jnp.zeros_like(queries))
                scores = dot_t(queries, keys) + band_ref[:, band_slice(block, length)] + mask
                highest = jnp.max(scores, axis=-1, keepdims=True)
                powers = jnp.exp(scores - highest)
                total = jnp.sum(powers, axis=-1, keepdims=True)
                mixed = (dot(powers.astype(BF16), values) / total).astype(BF16)
                column = iota((ROWS, lse_ref.shape[1]), 1)
                lse_ref[here, :] = jnp.where(column == head, highest + jnp.log(total), lse_ref[here, :])
                if side:
                    mixed = jnp.where(mine, mixed, mixed_ref[pair, here, :])
                mixed_ref[pair, here, :] = mixed
        return carry

    lax.fori_loop(0, PAIRS, one_pair, 0)
    mixed_all = jnp.concatenate([mixed_ref[p] for p in range(PAIRS)], axis=1)
    residual = tokens + dot(mixed_all, wo_ref[...])
    res_ref[...] = residual
    inverse = lax.rsqrt(jnp.mean(residual * residual, axis=-1, keepdims=True) + epsilon)
    routed = (residual * inverse * gffn_ref[...]).astype(BF16)
    logits = dot(routed, wr_ref[...])
    powers = jnp.exp(logits - jnp.max(logits, axis=-1, keepdims=True))
    probs = powers / jnp.sum(powers, axis=-1, keepdims=True)
    probs_ref[...] = probs
    gate = jnp.sum(jnp.where(iota(probs.shape, 1) == rcol_ref[0], probs, 0.0), axis=-1, keepdims=True)
    groups, message, _ = slots_ref.shape
    places = iota((groups * message, length), 0)
    dispatch = one_hot(places == spread_slots(srow_ref[0], per, message))
    slots_ref[...] = dot(dispatch, routed).astype(BF16).reshape(slots_ref.shape)
    if gated:
        grad_ref = rest[0]
        if grad_ref.shape[1] != message:
            dispatch = one_hot(
                iota((groups * grad_ref.shape[1], length), 0) == spread_slots(srow_ref[0], per, grad_ref.shape[1])
            )
        grads = (gate * cot_ref[0, 0].astype(F32)).astype(BF16)
        grad_ref[...] = dot(dispatch, grads).astype(BF16).reshape(grad_ref.shape)
        return
    first = gate.astype(BF16).astype(F32)
    second = (gate - first).astype(BF16).astype(F32)
    third = gate - first - second
    column = iota((length, PAIR), 1)
    pieces = jnp.where(column == 0, first, jnp.where(column == 1, second, jnp.where(column == 2, third, 0.0)))
    sorted_gates = dot(dispatch, pieces.astype(BF16))
    data = message - 16
    place = iota((data, 128), 0)
    lane = iota((data, 128), 1)
    for g in range(groups):
        mine = sorted_gates[g * message : g * message + data, :]
        parts = [
            jnp.sum(jnp.where(place == lane, mine[:, k : k + 1], 0.0), axis=0, keepdims=True) for k in range(3)
        ]
        line = jnp.concatenate(parts + [jnp.zeros((1, width - 384), F32)], axis=1)
        slots_ref[g, data:message, :] = jnp.broadcast_to(line, (16, width)).astype(BF16)


def attention_forward(
    batch, after, counts, tokens, cot, gain, wq, wk, wv, wo, vector, gain_ffn, w_router, srow, rcol, groups, per, gated
):
    length, width = tokens.shape[2:]
    experts = w_router.shape[1]
    message = padded(per) if gated else padded(per) + 16
    slabs = [jax.ShapeDtypeStruct((groups, message, width), BF16)]
    if gated:
        slabs = slabs + slabs
    return pl.pallas_call(
        functools.partial(attn_kernel, per, gated, batch, len(after)),
        grid=(1,),
        in_specs=[ANYWHERE] * len(after)
        + [SCALARS, batch_block(tokens, batch), batch_block(cot, batch)]
        + [WHOLE] * 8
        + [batch_block(srow, batch), batch_block(rcol, batch)],
        out_specs=[WHOLE] * (5 + len(slabs)),
        out_shape=[
            jax.ShapeDtypeStruct((3, PAIRS, length, PAIR), BF16),
            jax.ShapeDtypeStruct((PAIRS, length, PAIR), BF16),
            jax.ShapeDtypeStruct((length, 128), F32),
            jax.ShapeDtypeStruct((length, width), F32),
            jax.ShapeDtypeStruct((length, experts), F32),
            *slabs,
        ],
        scratch_shapes=[pltpu.VMEM((ROWS, vector.shape[-1]), F32)],
        compiler_params=params(48),
        cost_estimate=cost(20e9, 14e6, HEADS * length * length),
    )(*after, counts, tokens, cot, gain, wq, wk, wv, wo, vector, gain_ffn, w_router, srow, rcol)


GELU_SCALE = 0.7978845608028654
GELU_CUBIC = 0.044715


def expert_kernel(planes, gated, waits, *refs):
    pieces = 2 * planes - 1
    refs = refs[waits:]
    plane = refs[0][0]
    x_refs, refs = refs[1 : 1 + pieces], refs[1 + pieces :]
    c_refs, refs = refs[:pieces], refs[pieces:]
    gate_refs = ()
    if not gated:
        gate_refs, refs = refs[:pieces], refs[pieces:]
    wi_ref, wo_ref, *refs = refs
    out_refs, in_refs = refs[:planes], refs[planes : 2 * planes]
    act_ref, pre_ref, x_ref, c_ref = refs[2 * planes :]
    rows = x_refs[0].shape[0]

    def assemble(parts):
        found = [parts[0][...]]
        for k in range(1, planes):
            from_above = plane + k < planes
            found.append(jnp.where(from_above, parts[k][...], parts[2 * planes - 1 - k][...]))
        return found

    inputs = jnp.concatenate(assemble(x_refs), axis=0)
    grads = assemble(c_refs)
    if not gated:
        place = iota((rows, 128), 0)
        lane = iota((rows, 128), 1)
        expert = pl.program_id(0)
        for k, lines in enumerate(assemble(gate_refs)):
            lines = jnp.where(iota(lines.shape, 0) == expert, lines.astype(F32), 0.0)
            line = jnp.sum(lines, axis=0, keepdims=True)
            line = line[:, :128] + line[:, 128:256] + line[:, 256:384]
            gate = jnp.sum(jnp.where(place == lane, line, 0.0), axis=1, keepdims=True)
            grads[k] = (grads[k].astype(F32) * gate).astype(BF16)
    grads = jnp.concatenate(grads, axis=0)
    x_ref[0] = inputs
    c_ref[0] = grads
    pre = dot(inputs, wi_ref[0])
    square = pre * pre
    curve = jnp.tanh(GELU_SCALE * pre * (1.0 + GELU_CUBIC * square))
    half = 0.5 * (1.0 + curve)
    act = (pre * half).astype(BF16)
    slope = half + 0.5 * pre * (1.0 - curve * curve) * (GELU_SCALE * (1.0 + 3.0 * GELU_CUBIC * square))
    act_ref[0] = act
    outs = dot(act, wo_ref[0]).astype(BF16)
    pre_grad = (slope * dot_t(grads, wo_ref[0])).astype(BF16)
    pre_ref[0] = pre_grad
    ins = dot_t(pre_grad, wi_ref[0]).astype(BF16)
    for k in range(planes):
        out_refs[k][...] = outs[k * rows : (k + 1) * rows]
        in_refs[k][...] = ins[k * rows : (k + 1) * rows]


def experts_both(after, plane, xs, cs, w_inner, w_outer, gated):
    local, width, hidden = w_inner.shape
    pieces = len(xs)
    planes = (pieces + 1) // 2
    rows = cs[0].shape[0] // local
    slab = pl.BlockSpec((rows, width), lambda e: (e, 0))
    lines = pl.BlockSpec((16, width), lambda e: (local * rows // 16, 0))
    mat = lambda a, b: pl.BlockSpec((1, a, b), lambda e: (e, 0, 0))
    total = planes * rows
    part = jax.ShapeDtypeStruct((local * rows, width), BF16)
    kept = lambda n: jax.ShapeDtypeStruct((local, total, n), BF16)
    return pl.pallas_call(
        functools.partial(expert_kernel, planes, gated, len(after)),
        grid=(local,),
        in_specs=[ANYWHERE] * len(after)
        + [SCALARS]
        + [slab] * (2 * pieces)
        + ([] if gated else [lines] * pieces)
        + [mat(width, hidden), mat(hidden, width)],
        out_specs=[slab] * (2 * planes)
        + [mat(total, hidden), mat(total, hidden), mat(total, width), mat(total, width)],
        out_shape=[part] * (2 * planes) + [kept(hidden), kept(hidden), kept(width), kept(width)],
        compiler_params=params(48),
        cost_estimate=cost(
            8 * local * total * width * hidden, 4 * local * hidden * width + 24 * local * total * width, local * total * hidden
        ),
    )(*after, plane, *xs, *cs, *(() if gated else xs), w_inner, w_outer)


def expert_grad_kernel(batches, *refs):
    xs, cs, acts, pres = (refs[k * batches : (k + 1) * batches] for k in range(4))
    outer_ref, inner_ref = refs[4 * batches :]
    outer = inner = None
    for b in range(batches):
        outer_part = t_dot(acts[b][0], cs[b][0])
        inner_part = t_dot(xs[b][0], pres[b][0])
        outer = outer_part if outer is None else outer + outer_part
        inner = inner_part if inner is None else inner + inner_part
    outer_ref[0] = outer
    inner_ref[0] = inner


def expert_grads(xs, cs, acts, pres):
    batches = len(xs)
    local, total, width = xs[0].shape
    hidden = acts[0].shape[2]
    mat = lambda a, b: pl.BlockSpec((1, a, b), lambda e: (e, 0, 0))
    return pl.pallas_call(
        functools.partial(expert_grad_kernel, batches),
        grid=(local,),
        in_specs=[mat(total, width)] * (2 * batches) + [mat(total, hidden)] * (2 * batches),
        out_specs=[mat(hidden, width), mat(width, hidden)],
        out_shape=[
            jax.ShapeDtypeStruct((local, hidden, width), F32),
            jax.ShapeDtypeStruct((local, width, hidden), F32),
        ],
        compiler_params=params(48),
        cost_estimate=cost(
            4 * batches * local * total * width * hidden, 8 * local * hidden * width + 8 * batches * local * total * width
        ),
    )(*xs, *cs, *acts, *pres)


def combine_kernel(per, batch, waits, *refs):
    refs = refs[waits:]
    len_ref, out_ref, in_ref, scol_ref, rcol_ref, res_ref, probs_ref, cot_ref, gffn_ref, wr_ref, wo_ref, mixed_ref, *refs = refs
    past_ref = refs.pop(0) if batch else None
    layer_ref, resgrad_ref, mgrad_ref, shared_ref = refs
    length, width = cot_ref.shape[2:]
    experts = wr_ref.shape[1]
    groups, message, _ = out_ref.shape
    valid = iota((length, 1), 0) < len_ref[batch]
    collect = one_hot(iota((length, groups * message), 1) == spread_slots(scol_ref[0], per, message))
    returned = dot(collect, out_ref[...].reshape(groups * message, width))
    residual = res_ref[...]
    probs = probs_ref[...]
    chosen = iota(probs.shape, 1) == rcol_ref[0]
    gate = jnp.sum(jnp.where(chosen, probs, 0.0), axis=-1, keepdims=True)
    layer_ref[...] = jnp.where(valid, residual + gate * returned, 0.0).astype(BF16)
    out_grad = jnp.where(valid, cot_ref[0, 0].astype(F32), 0.0)
    gate_grad = jnp.sum(out_grad * returned, axis=-1, keepdims=True)
    prob_grad = jnp.where(chosen, gate_grad, 0.0)
    logit_grad = (probs * (prob_grad - jnp.sum(probs * prob_grad, axis=-1, keepdims=True))).astype(BF16)
    inverse = lax.rsqrt(jnp.mean(residual * residual, axis=-1, keepdims=True) + epsilon)
    gain = gffn_ref[...]
    scaled = residual * inverse
    routed = (scaled * gain).astype(BF16)

    def share(first, rows):
        if past_ref is not None:
            rows = rows + past_ref[first : first + rows.shape[0], :]
        shared_ref[first : first + rows.shape[0], :] = rows.astype(shared_ref.dtype)

    share(width, t_dot(logit_grad, routed))
    routed_grad = dot_t(logit_grad, wr_ref[...]) + dot(collect, in_ref[...].reshape(groups * message, width))
    gain_part = jnp.sum(routed_grad * scaled, axis=0, keepdims=True)
    left = shared_ref.shape[0] - width - experts
    share(width + experts, jnp.where(iota((left, width), 0) == 0, gain_part, 0.0))
    upstream = routed_grad * gain
    middle = jnp.mean(upstream * scaled, axis=-1, keepdims=True)
    residual_grad = out_grad + inverse * (upstream - scaled * middle)
    resgrad_ref[...] = residual_grad
    attended = residual_grad.astype(BF16)
    mixed_all = jnp.concatenate([mixed_ref[p] for p in range(PAIRS)], axis=1)
    share(0, t_dot(mixed_all, attended))
    mixed_grad = dot_t(attended, wo_ref[...]).astype(BF16)
    for pair in range(PAIRS):
        mgrad_ref[pair] = mixed_grad[:, pair * PAIR : (pair + 1) * PAIR]


def combine(
    batch, last, after, counts, outs, ins, scol, rcol, residual, probs, cot, gain_ffn, w_router, w_output, mixed, past, per, shared
):
    length, width = cot.shape[2:]
    return pl.pallas_call(
        functools.partial(combine_kernel, per, batch, len(after)),
        grid=(1,),
        in_specs=[ANYWHERE] * len(after)
        + [SCALARS, WHOLE, WHOLE, batch_block(scol, batch), batch_block(rcol, batch), WHOLE, WHOLE, batch_block(cot, batch)]
        + [WHOLE] * (5 if batch else 4),
        out_specs=[WHOLE] * 4,
        out_shape=[
            jax.ShapeDtypeStruct((length, width), BF16),
            jax.ShapeDtypeStruct((length, width), F32),
            jax.ShapeDtypeStruct((PAIRS, length, PAIR), BF16),
            jax.ShapeDtypeStruct((shared, width), BF16 if last else F32),
        ],
        compiler_params=params(48),
        cost_estimate=cost(8e9, 12e6),
    )(
        *after, counts, outs, ins, scol, rcol, residual, probs, cot, gain_ffn, w_router, w_output, mixed, *([past] if batch else [])
    )


def attn_back_kernel(batch, waits, *refs):
    refs = refs[waits:]
    len_ref, qkv_ref, lse_ref, vec_ref, sel_ref, mgrad_ref, tok_ref, gain_ref, wq_ref, wk_ref, wv_ref, resgrad_ref, *refs = refs
    past_ref = refs.pop(0) if batch else None
    shared_ref, tgrad_ref, band_ref, probs_ref, sgrad_ref, spread_ref, low_ref, kt_ref, vt_ref, diag_ref = refs
    length, width = tok_ref.shape[2:]
    mask = jnp.where(iota((1, length), 1) < len_ref[batch], 0.0, negative)
    lane = iota((ROWS, PAIR), 1)
    diag_ref[...] = jnp.zeros_like(diag_ref)

    def one_pair(pair, carry):
        keys = qkv_ref[1, pair]
        values = qkv_ref[2, pair]
        queries_t = qkv_ref[0, pair].T
        grads_t = mgrad_ref[pair].T
        for side in range(2):
            head = 2 * pair + side
            band_ref[...] = band_bias(vec_ref, head)
            spread_ref[...] = jnp.zeros_like(spread_ref)
            mine = (lane >= HEAD_DIM) if side else (lane < HEAD_DIM)
            for block in range(length // ROWS):
                here = slice(ROWS * block, ROWS * (block + 1))
                window = band_slice(block, length)
                queries = qkv_ref[0, pair, here, :] * 0.125
                queries = jnp.where(mine, queries, jnp.zeros_like(queries))
                grads = mgrad_ref[pair, here, :]
                grads = jnp.where(mine, grads, jnp.zeros_like(grads))
                column = iota((ROWS, lse_ref.shape[1]), 1)
                log_total = jnp.sum(jnp.where(column == head, lse_ref[here, :], 0.0), axis=-1, keepdims=True)
                scores = dot_t(queries, keys) + band_ref[:, window] + mask
                probs = jnp.exp(scores - log_total)
                probs_ref[here, :] = probs.astype(BF16)
                weighted = probs * dot_t(grads, values)
                score_grad = weighted - probs * jnp.sum(weighted, axis=-1, keepdims=True)
                spread_ref[:, window] += score_grad
                low = score_grad.astype(BF16)
                sgrad_ref[here, :] = low
                query_grad = (dot(low, keys) * 0.125).astype(BF16)
                if side:
                    query_grad = jnp.where(mine, query_grad, low_ref[0, pair, here, :])
                low_ref[0, pair, here, :] = query_grad
            rows = slice(HEAD_DIM * side, HEAD_DIM * (side + 1))
            kt_ref[rows, :] = dot(queries_t[rows, :], sgrad_ref[...]) * 0.125
            vt_ref[rows, :] = dot(grads_t[rows, :], probs_ref[...])
            size = spread_ref.shape[1]
            eight = spread_ref[0:8, :]
            for step in range(8, ROWS, 8):
                eight = eight + pltpu.roll(spread_ref[step : step + 8, :], size - step, 1)
            diagonal = eight[0:1, :]
            for step in range(1, 8):
                diagonal = diagonal + pltpu.roll(eight[step : step + 1, :], size - step, 1)
            diag_ref[...] = jnp.where(iota(diag_ref.shape, 0) == head, diagonal, diag_ref[...])
        low_ref[1, pair] = kt_ref[...].T.astype(BF16)
        low_ref[2, pair] = vt_ref[...].T.astype(BF16)
        return carry

    lax.fori_loop(0, PAIRS, one_pair, 0)

    def share(first, rows):
        if past_ref is not None:
            rows = rows + past_ref[first : first + rows.shape[0], :]
        shared_ref[first : first + rows.shape[0], :] = rows.astype(shared_ref.dtype)

    tokens = tok_ref[0, 0].astype(F32)
    inverse = lax.rsqrt(jnp.mean(tokens * tokens, axis=-1, keepdims=True) + epsilon)
    gain = gain_ref[...]
    scaled = tokens * inverse
    normed_t = (scaled * gain).astype(BF16).T
    normed_grad = jnp.zeros((length, width), F32)
    for which, w_ref in enumerate((wq_ref, wk_ref, wv_ref)):
        low = jnp.concatenate([low_ref[which, p] for p in range(PAIRS)], axis=1)
        share(which * width, dot(normed_t, low))
        normed_grad = normed_grad + dot_t(low, w_ref[...])
    gain_part = jnp.sum(normed_grad * scaled, axis=0, keepdims=True)
    bias_part = lax.dot_general(
        diag_ref[...], sel_ref[...], (((1,), (0,)), ((), ())), precision=lax.Precision.HIGHEST, preferred_element_type=F32
    )
    left = shared_ref.shape[0] - 3 * width - 24
    first = jnp.where(iota((8, width), 0) == 0, gain_part, 0.0)
    wide = jnp.concatenate([bias_part, jnp.zeros((16, width - bias_part.shape[1]), F32)], axis=1)
    share(3 * width, jnp.concatenate([first, wide, jnp.zeros((left, width), F32)], axis=0))
    upstream = normed_grad * gain
    middle = jnp.mean(upstream * scaled, axis=-1, keepdims=True)
    tgrad_ref[...] = (resgrad_ref[...] + inverse * (upstream - scaled * middle)).astype(BF16)


def attention_backward(
    batch, last, after, counts, qkv, lse, vector, selector, mixed_grad, tokens, gain, wq, wk, wv, residual_grad, past, shared
):
    length, width = tokens.shape[2:]
    size = vector.shape[-1]
    return pl.pallas_call(
        functools.partial(attn_back_kernel, batch, len(after)),
        grid=(1,),
        in_specs=[ANYWHERE] * len(after)
        + [SCALARS]
        + [WHOLE] * 5
        + [batch_block(tokens, batch)]
        + [WHOLE] * (6 if batch else 5),
        out_specs=[WHOLE] * 2,
        out_shape=[
            jax.ShapeDtypeStruct((shared, width), BF16 if last else F32),
            jax.ShapeDtypeStruct((length, width), BF16),
        ],
        scratch_shapes=[
            pltpu.VMEM((ROWS, size), F32),
            pltpu.VMEM((length, length), BF16),
            pltpu.VMEM((length, length), BF16),
            pltpu.VMEM((ROWS, size), F32),
            pltpu.VMEM((3, PAIRS, length, PAIR), BF16),
            pltpu.VMEM((PAIR, length), F32),
            pltpu.VMEM((PAIR, length), F32),
            pltpu.VMEM((16, size), F32),
        ],
        compiler_params=params(56),
        cost_estimate=cost(32e9, 20e6, HEADS * length * length),
    )(
        *after, counts, qkv, lse, vector, selector, mixed_grad, tokens, gain, wq, wk, wv, residual_grad, *([past] if batch else [])
    )


def upward(planes, first, last):
    return [(k, k + 1) for k in range(first, last)]


def downward(planes, first, last):
    return [(planes - 1 - k, planes - 2 - k) for k in range(first, last)]


def mix_kernel(both, planes, step, waits, here_ref, up_ref, down_ref, upsum_ref, downsum_ref, *refs):
    to_up, to_down = refs[waits:]
    for moving, sums, out, place in (
        (up_ref, upsum_ref, to_up, here_ref[0]),
        (down_ref, downsum_ref, to_down, planes - 1 - here_ref[0]),
    ):
        total = moving[...] + sums[...]
        out[...] = jnp.where(place <= step, total, moving[...]) if both else total


def mix(both, planes, step, here, up, down, upsum, downsum, after):
    rows, width = up.shape
    block = pl.BlockSpec((rows // 4, width), lambda i: (i, 0))
    return pl.pallas_call(
        functools.partial(mix_kernel, both, planes, step, len(after)),
        grid=(4,),
        in_specs=[SCALARS] + [block] * 4 + [ANYWHERE] * len(after),
        out_specs=[block] * 2,
        out_shape=[jax.ShapeDtypeStruct((rows, width), BF16)] * 2,
        compiler_params=params(32),
        cost_estimate=cost(),
    )(here, up, down, upsum, downsum, *after)


class Chain:
    def __init__(self, planes, own=None, sums=None):
        self.planes, self.own, self.sums = planes, own, sums
        self.here = lax.axis_index("hidden")[None]
        self.from_below, self.from_above = [], []
        if own is not None:
            self.up = self.down = own
        else:
            self.up, self.down = sums[planes - 1], sums[1]
        self.count = 0
        self.steps = planes if own is not None and sums is not None else planes - 1

    def send(self):
        planes, s = self.planes, self.count
        if self.own is not None and self.sums is not None:
            first, last = 0, planes - 1
        elif self.own is not None:
            first, last = s, planes - 1
        else:
            first, last = 0, s + 1
        self.up = lax.ppermute(self.up, "hidden", upward(planes, first, last))
        self.down = lax.ppermute(self.down, "hidden", downward(planes, first, last))
        self.count += 1
        if self.own is not None and s < planes - 1:
            self.from_below.append(self.up)
            self.from_above.append(self.down)

    def mix(self, *after):
        planes, s = self.planes, self.count - 1
        both = self.own is not None
        offset = 1 if both else 2
        self.up, self.down = mix(
            both, planes, s, self.here, self.up, self.down, self.sums[planes - offset - s], self.sums[s + offset], after
        )

    def run(self):
        while self.count < self.steps:
            self.send()
        return self

    def gathered(self):
        return (self.own, *self.from_above, *self.from_below)

    def scattered(self):
        return (self.sums[0], self.up, self.down)


def exchange_sum(values, axis_bits):
    me = lax.axis_index("expert")
    size = lax.axis_size("expert")
    for bit in axis_bits:
        halves = values.reshape(2, values.shape[0] // 2, values.shape[1])
        side = (me // bit) % 2
        mine = lax.dynamic_index_in_dim(halves, side, 0, keepdims=False)
        other = lax.dynamic_index_in_dim(halves, 1 - side, 0, keepdims=False)
        values = mine + lax.ppermute(other, "expert", [(k, k ^ bit) for k in range(size)])
    return values


def exchange_join(values, axis_bits):
    me = lax.axis_index("expert")
    size = lax.axis_size("expert")
    for bit in reversed(axis_bits):
        other = lax.ppermute(values, "expert", [(k, k ^ bit) for k in range(size)])
        second = (me // bit) % 2 == 1
        values = jnp.concatenate([jnp.where(second, other, values), jnp.where(second, values, other)])
    return values


def sum_everywhere(values):
    size = lax.axis_size("expert")
    planes = lax.axis_size("hidden")
    bits = [1 << k for k in range(size.bit_length() - 1)]
    count = values.shape[0]
    unit = 16 * size
    values = jnp.pad(values.astype(BF16), ((0, -count % unit), (0, 0)))
    near, far = bits[:1], bits[1:]
    values = exchange_sum(values, near)
    half = values.shape[0] // 2
    done = []
    for part, order in ((values[:half], far), (values[half:], far[::-1])):
        part = exchange_sum(part, order)
        total = part.astype(F32)
        for k in range(1, planes):
            total = total + lax.ppermute(part, "hidden", [(p, p ^ k) for p in range(planes)]).astype(F32)
        done.append(exchange_join(total.astype(BF16), order))
    return exchange_join(jnp.concatenate(done), near)[:count].astype(F32)


def offset_selector(length):
    place = np.arange(2 * length)
    offsets = np.where(place < 2 * length - ROWS, place, place - 2 * length) - (length - ROWS)
    offsets = np.clip(offsets, -(length - 1), length - 1)
    return (offset_bucket(offsets)[:, None] == np.arange(BUCKETS)[None, :]).astype(np.float32)


def moves(groups, local, capacity, message):
    expert, group, slot = np.meshgrid(np.arange(local), np.arange(groups), np.arange(capacity), indexing="ij")
    source = (group * message + expert * capacity + slot).reshape(-1)
    return (source[:, None] == np.arange(groups * message)[None, :]).astype(jnp.bfloat16)


def shards(
    tokens,
    cotangent,
    lengths,
    routes,
    gain_attn,
    w_query,
    w_key,
    w_value,
    w_output,
    bucket_head_bias,
    gain_ffn,
    w_router,
    w_inner,
    w_outer,
):
    batches, _, length, width = tokens.shape
    experts = w_router.shape[1]
    local = w_inner.shape[0]
    groups = lax.axis_size("expert")
    planes = lax.axis_size("hidden")
    capacity = (5 * length + 4 * experts - 1) // (4 * experts)
    per = local * capacity
    rows = groups * capacity
    message = padded(per)
    move = jnp.asarray(moves(groups, local, capacity, message))
    move_gated = jnp.asarray(moves(groups, local, capacity, message + 16))
    move_back = jnp.asarray(moves(groups, local, capacity, message).T)
    selector = jnp.asarray(offset_selector(length))
    vector = lax.dot_general(
        bucket_head_bias, selector, (((0,), (1,)), ((), ())), precision=lax.Precision.HIGHEST
    )[:, None, :]
    gain_a = gain_attn[None, :]
    gain_f = gain_ffn[None, :]
    counts = lengths[:, 0]
    plane = lax.axis_index("hidden")[None]

    def to_groups(values):
        return lax.all_to_all(values, "expert", split_axis=0, concat_axis=0, tiled=True)

    def leaving(values):
        sent = to_groups(values)
        if values.shape[1] != message:
            return regroup_gated(move_gated, sent, capacity)
        return regroup(move, [sent], (local * rows, width))

    def arriving(parts):
        return to_groups(regroup(move_back, parts, (groups, message, width)))

    def attend(b, *after):
        return attention_forward(
            b,
            after,
            counts,
            tokens,
            cotangent,
            gain_a,
            w_query,
            w_key,
            w_value,
            w_output,
            vector,
            gain_f,
            w_router,
            srow,
            rcol,
            groups,
            per,
            b > 0,
        )

    srow, scol, cot_slots = prep(counts, routes.reshape(batches, length), cotangent, groups, per, capacity)
    rcol = routes.reshape(batches, length, 1)
    each = range(batches)
    grads = leaving(cot_slots)
    forward = [attend(0, grads)]
    inputs = leaving(forward[0][5])
    grad_chain = Chain(planes, grads).run()
    input_chain = Chain(planes, inputs).run()
    early = width + experts + 16
    early = early + -early % (16 * groups)
    late = 3 * width + 24
    late = late + -late % (16 * groups)
    kept, layer_rows, token_grads = [], [], []
    early_part = late_part = None

    def finish(b, after, outs, ins):
        qkv, mixed, lse, residual, probs = forward[b][:5]
        last = b + 1 == batches
        layer, res_grad, mixed_grad, early_part_b = combine(
            b,
            last,
            after,
            counts,
            outs,
            ins,
            scol,
            rcol,
            residual,
            probs,
            cotangent,
            gain_f,
            w_router,
            w_output,
            mixed,
            early_part,
            per,
            early,
        )
        late_part_b, token_grad = attention_backward(
            b,
            last,
            (),
            counts,
            qkv,
            lse,
            vector,
            selector,
            mixed_grad,
            tokens,
            gain_a,
            w_query,
            w_key,
            w_value,
            res_grad,
            late_part,
            late,
        )
        layer_rows.append(layer)
        token_grads.append(token_grad)
        return early_part_b, late_part_b

    for b in each:
        xs, cs = input_chain.gathered(), grad_chain.gathered()
        last = b + 1 == batches
        if last:
            grads = inputs = None
            after = () if b == 0 else (grad_chain.up, input_chain.up)
        else:
            forward.append(attend(b + 1, inputs))
            grads, inputs = leaving(forward[b + 1][6]), leaving(forward[b + 1][5])
            after = (grads, inputs)
        worked = experts_both(after, plane, xs, cs, w_inner, w_outer, b > 0)
        kept.append(worked[2 * planes :])
        if b:
            grad_chain.send()
            input_chain.send()
            outs, ins = arriving(grad_chain.scattered()), arriving(input_chain.scattered())
        grad_chain = Chain(planes, grads, worked[:planes])
        input_chain = Chain(planes, inputs, worked[planes : 2 * planes])
        grad_chain.send()
        input_chain.send()
        if b:
            early_part, late_part = finish(b - 1, (), outs, ins)
        while grad_chain.count < grad_chain.steps - (0 if last else 1):
            held = (late_part,) if b and grad_chain.count == grad_chain.steps - 1 else ()
            grad_chain.mix(*held)
            grad_chain.send()
            input_chain.mix(*held)
            input_chain.send()
        if not last:
            grad_chain.mix()
            input_chain.mix()
    outer_total, inner_total = expert_grads(
        [k[2] for k in kept], [k[3] for k in kept], [k[0] for k in kept], [k[1] for k in kept]
    )
    outs, ins = arriving(grad_chain.scattered()), arriving(input_chain.scattered())
    early_part, late_part = finish(batches - 1, (inner_total,), outs, ins)
    early_sum = sum_everywhere(early_part)
    late_sum = sum_everywhere(late_part)
    bias = late_sum[3 * width + 8 : 3 * width + 8 + HEADS, :BUCKETS]
    return (
        jnp.stack(layer_rows)[:, None],
        jnp.stack(token_grads)[:, None],
        late_sum[3 * width],
        late_sum[:width],
        late_sum[width : 2 * width],
        late_sum[2 * width : 3 * width],
        early_sum[:width],
        bias.T,
        early_sum[width + experts],
        early_sum[width : width + experts].T,
        inner_total,
        outer_total,
    )


def solution(mesh):
    token = P(None, ("expert", "hidden"), None, None)
    placed = (
        token,
        token,
        P(None, ("expert", "hidden")),
        token,
        *(P() for _ in range(8)),
        P("expert", None, "hidden"),
        P("expert", "hidden", None),
    )
    return jax.shard_map(
        shards,
        mesh=mesh,
        in_specs=placed,
        out_specs=(
            token,
            token,
            *(P() for _ in range(8)),
            P("expert", None, "hidden"),
            P("expert", "hidden", None),
        ),
        check_vma=False,
    )
```

time: 944 us -> 773 us (0.82)
  waiting for transfers between devices: 444 us -> 284 us
  blocking collectives: 151 us -> 0 us
  starting transfers between devices: 17.4 us -> 162 us
  Pallas kernels: 199 us -> 240 us
  local copies, waits for them, and re-layouts: 87.9 us -> 54.1 us
  between operations: 15 us -> 1.97 us
    reduce_scatter x4 -> x0, waiting for transfers between devices: 255 us -> none  [to_tokens(): summed = lax.psum_scatter(values, 'hidden', scatter_dimension=0)]
    ppermute x0 -> x72, waiting for transfers between devices: none -> 251 us  [the longest x20 96.2 us: send(): self.down = lax.ppermute(self.down, 'hidden', downward(planes, first, last))]
    all_gather x4 -> x0, waiting for transfers between devices: 161 us -> none  [to_experts(): return lax.all_gather(mine, 'hidden', axis=0)]
    ppermute x0 -> x72, starting transfers between devices: none -> 129 us  [the longest x20 67.7 us: send(): self.up = lax.ppermute(self.up, 'hidden', upward(planes, first, last))]
    all_to_all x4 -> x0, blocking collectives: 71.1 us -> none  [to_experts(): lax.all_to_all(values.reshape(groups, local, capacity, width), 'expert',...]
    pallas_call x9 -> x27, Pallas kernels: 171 us -> 213 us  [the longest x2 68.7 us: attention_backward(): pl.pallas_call(functools.partial(attn_back_kernel, batch, len(after)), gr...]
    all_gather x1 -> x0, blocking collectives: 42.1 us -> none  [shards(): gates = lax.all_gather(gates, ('hidden', 'expert'), axis=0)]
    psum x1 -> x0, blocking collectives: 37.5 us -> none  [shards(): lax.psum(jnp.concatenate([gain_a_part[0], gain_f_part[0], bias_part.resha...]
  transfers between devices with their start and end apart: 13 -> 80, of which waited for: 8 -> 42; matrix products, arithmetic and copies ran while one was open for 6% -> 3% of each run, Pallas kernels for 12% -> 27%
where the time goes in v2:
time: 773 us; the launch traced here: 761 us
  waiting for transfers between devices  284 us (37%)
  Pallas kernels  240 us (31%)
  starting transfers between devices  162 us (21%)
  local copies, waits for them, and re-layouts  54.1 us (7%)
  other arithmetic  16.3 us (2%)
    ppermute x20, waiting for transfers between devices, send(): self.down = lax.ppermute(self.down, 'hidden', downward(planes, first, last))  96.2 us
    ppermute x20, waiting for transfers between devices, send(): self.up = lax.ppermute(self.up, 'hidden', upward(planes, first, last))  85.2 us
    pallas_call x2, Pallas kernels, attention_backward(): pl.pallas_call(functools.partial(attn_back_kernel, batch, len(after)), gr...  68.7 us
    ppermute x20, starting transfers between devices, send(): self.up = lax.ppermute(self.up, 'hidden', upward(planes, first, last))  67.7 us
    pallas_call x2, Pallas kernels, experts_both(): pl.pallas_call(functools.partial(expert_kernel, planes, gated, len(after)...  44.5 us
    unnamed x171, local copies, waits for them, and re-layouts  44 us
    pallas_call x2, Pallas kernels, attention_forward(): pl.pallas_call(functools.partial(attn_kernel, per, gated, batch, len(afte...  43.7 us
    ppermute x12, waiting for transfers between devices, sum_everywhere(): lax.ppermute(part, 'hidden', [(p, p ^ k) for p in range(planes)])  39.3 us
  transfers between devices with their start and end apart: 80, of which 42 were waited for; matrix products, arithmetic and copies ran while one was open for 3% of the time, Pallas kernels for 27%

profile of v2, /device:TPU:0, one launch (start us, length us, event | category | flops | bytes accessed | tf_op | source)
XLA Modules:
  0.0 760.7 jit_solution(9489086749846570589)
XLA Ops:
  7.7 5.3 all-to-all-start
  17.1 10.6 %all-to-all-done.refs_1_ = bf16[8,80,768]{2,1,0:T(8,128)(2,1)S(1)} async-done(((bf16[8,80,768]{2,1,0:T(8,128)(2,1)}), bf16[8,80,768]{2,1,0:T(8,128)(2,1)S(1)}, u32[]{:S(2)}, u32[]{:S(2)}) %all-to-all-start) | async-done | bytes 983072 | tf_op jit(solution)/shard_map/all_to_all | solution.py:815
  30.8 21.6 %shard_map.267 = (bf16[3,6,512,128]{3,2,1,0:T(8,128)(2,1)}, bf16[6,512,128]{2,1,0:T(8,128)(2,1)S(1)}, f32[512,128]{1,0:T(8,128)S(1)}, f32[512,768]{1,0:T(8,128)}...) custom-call(bf16[640,768]{1,0:T(8,128)(2,1)S(1)} %shard_map.266.refs_0_.refs_10_, s32[2]{0:T(128)S(1)} %bitcast.78, ...), custom_call_target="tpu_custom_call" | custom-call | flops 1 | bytes 1 | tf_op jit(solution)/shard_map/pallas_call | solution.py:310
  59.3 4.4 collective-permute-start.9
  63.7 12.3 %all-to-all-done.1.in_ref = bf16[8,96,768]{2,1,0:T(8,128)(2,1)S(1)} async-done(((bf16[8,96,768]{2,1,0:T(8,128)(2,1)}), bf16[8,96,768]{2,1,0:T(8,128)(2,1)S(1)}, u32[]{:S(2)}, u32[]{:S(2)}) %all-to-all-start.1) | async-done | bytes 1179680 | tf_op jit(solution)/shard_map/all_to_all | solution.py:815
  83.6 6.1 collective-permute-start.3
  91.4 16.7 %collective-permute-done.refs_4_.refs_18_ = bf16[656,768]{1,0:T(8,128)(2,1)S(1)} collective-permute-done((bf16[656,768]{1,0:T(8,128)(2,1)S(1)}, bf16[656,768]{1,0:T(8,128)(2,1)S(1)}, u32[]{:S(2)}, u32[]{:S(2)}) %collective-permute-start) | collective-permute-done | bytes 1007648 | tf_op jit(solution)/shard_map/ppermute | solution.py:696
  109.4 19.9 %collective-permute-done.6.refs_11_ = bf16[640,768]{1,0:T(8,128)(2,1)} collective-permute-done((bf16[640,768]{1,0:T(8,128)(2,1)S(1)}, bf16[640,768]{1,0:T(8,128)(2,1)}, u32[]{:S(2)}, u32[]{:S(2)}) %collective-permute-start.6) | collective-permute-done | bytes 983072 | tf_op jit(solution)/shard_map/ppermute | solution.py:696
  135.4 22.1 %shard_map.269 = (bf16[3,6,512,128]{3,2,1,0:T(8,128)(2,1)}, bf16[6,512,128]{2,1,0:T(8,128)(2,1)S(1)}, f32[512,128]{1,0:T(8,128)S(1)}, f32[512,768]{1,0:T(8,128)}...) custom-call(bf16[656,768]{1,0:T(8,128)(2,1)S(1)} %shard_map.268.refs_0_.refs_3_.refs_17_, ...), custom_call_target="tpu_custom_call" | custom-call | flops 1 | bytes 1 | tf_op jit(solution)/shard_map/pallas_call | solution.py:310
  169.2 8.8 %all-to-all-done.3.refs_1_ = bf16[8,80,768]{2,1,0:T(8,128)(2,1)S(1)} async-done(((bf16[8,80,768]{2,1,0:T(8,128)(2,1)}), bf16[8,80,768]{2,1,0:T(8,128)(2,1)S(1)}, u32[]{:S(2)}, u32[]{:S(2)}) %all-to-all-start.3) | async-done | bytes 983072 | tf_op jit(solution)/shard_map/all_to_all | solution.py:815
  178.0 4.2 all-to-all-start.2
  184.8 9.3 %collective-permute-start.20 = (bf16[640,768]{1,0:T(8,128)(2,1)S(1)}, bf16[640,768]{1,0:T(8,128)(2,1)}, u32[]{:S(2)}, u32[]{:S(2)}) collective-permute-start(bf16[640,768]{1,0:T(8,128)(2,1)S(1)} %shard_map.271.refs_1_.refs_3_), channel_id=1, source_target_pairs={{0,1},{1,2},{2,3},{4,5},{5,6},{6,7},{8,9},{9,10},{10,11},{12,13},{... | collective-permute-start | bytes 2949128 | tf_op jit(solution)/shard_map/ppermute | solution.py:695
  199.1 16.4 %collective-permute-done.8.refs_13_ = bf16[640,768]{1,0:T(8,128)(2,1)} collective-permute-done((bf16[640,768]{1,0:T(8,128)(2,1)}, bf16[640,768]{1,0:T(8,128)(2,1)}, u32[]{:S(2)}, u32[]{:S(2)}) %collective-permute-start.8) | collective-permute-done | bytes 983072 | tf_op jit(solution)/shard_map/ppermute | solution.py:696
  219.2 21.5 %shard_map.272 = (bf16[640,768]{1,0:T(8,128)(2,1)S(1)}, bf16[640,768]{1,0:T(8,128)(2,1)S(1)}, bf16[640,768]{1,0:T(8,128)(2,1)S(1)}, bf16[640,768]{1,0:T(8,128)(2...) custom-call(bf16[640,768]{1,0:T(8,128)(2,1)} %copy-done.8, ...), custom_call_target="tpu_custom_call" | custom-call | flops 1 | bytes 1 | tf_op jit(solution)/shard_map/pallas_call | solution.py:399
  245.6 4.6 collective-permute-start.22
  251.5 6.1 collective-permute-done.13.down_ref.refs_11_
  263.0 9.3 %collective-permute-done.22.up_ref.refs_8_ = bf16[640,768]{1,0:T(8,128)(2,1)S(1)} collective-permute-done((bf16[640,768]{1,0:T(8,128)(2,1)S(1)}, bf16[640,768]{1,0:T(8,128)(2,1)S(1)}, u32[]{:S(2)}, u32[]{:S(2)}) %collective-permute-start.22) | collective-permute-done | bytes 983072 | tf_op jit(solution)/shard_map/ppermute | solution.py:695
  272.3 6.2 collective-permute-done.23.down_ref.refs_5_
  282.3 11.1 %collective-permute-done.14.up_ref.refs_15_ = bf16[640,768]{1,0:T(8,128)(2,1)S(1)} collective-permute-done((bf16[640,768]{1,0:T(8,128)(2,1)S(1)}, bf16[640,768]{1,0:T(8,128)(2,1)S(1)}, u32[]{:S(2)}, u32[]{:S(2)}) %collective-permute-start.14) | collective-permute-done | bytes 983072 | tf_op jit(solution)/shard_map/ppermute | solution.py:695
  293.4 6.2 collective-permute-done.15.down_ref.refs_12_
  303.4 11.0 %collective-permute-done.24.up_ref.refs_9_ = bf16[640,768]{1,0:T(8,128)(2,1)S(1)} collective-permute-done((bf16[640,768]{1,0:T(8,128)(2,1)S(1)}, bf16[640,768]{1,0:T(8,128)(2,1)S(1)}, u32[]{:S(2)}, u32[]{:S(2)}) %collective-permute-start.24) | collective-permute-done | bytes 983072 | tf_op jit(solution)/shard_map/ppermute | solution.py:695
  314.5 6.2 collective-permute-done.25.down_ref.refs_6_
  324.7 10.9 %collective-permute-done.16.up_ref.refs_16_ = bf16[640,768]{1,0:T(8,128)(2,1)S(1)} collective-permute-done((bf16[640,768]{1,0:T(8,128)(2,1)S(1)}, bf16[640,768]{1,0:T(8,128)(2,1)S(1)}, u32[]{:S(2)}, u32[]{:S(2)}) %collective-permute-start.16) | collective-permute-done | bytes 983072 | tf_op jit(solution)/shard_map/ppermute | solution.py:695
  335.5 6.2 collective-permute-done.17.down_ref.refs_13_
  343.8 23.0 %shard_map.282 = (bf16[640,768]{1,0:T(8,128)(2,1)S(1)}, bf16[640,768]{1,0:T(8,128)(2,1)S(1)}, bf16[640,768]{1,0:T(8,128)(2,1)S(1)}, bf16[640,768]{1,0:T(8,128)(2...) custom-call(bf16[640,768]{1,0:T(8,128)(2,1)} %get-tuple-element.99.r, ...), custom_call_target="tpu_custom_call" | custom-call | flops 1 | bytes 1 | tf_op jit(solution)/shard_map/pallas_call | solution.py:399
  385.4 5.5 collective-permute-start.28
  390.9 4.7 collective-permute-done.34.up_ref
  401.2 5.3 collective-permute-start.36
  406.5 10.1 %collective-permute-done.18.refs_2_ = bf16[640,768]{1,0:T(8,128)(2,1)} collective-permute-done((bf16[640,768]{1,0:T(8,128)(2,1)}, bf16[640,768]{1,0:T(8,128)(2,1)}, u32[]{:S(2)}, u32[]{:S(2)}) %collective-permute-start.18) | collective-permute-done | bytes 983072 | tf_op jit(solution)/shard_map/ppermute | solution.py:695
  425.8 11.9 %collective-permute-done.28.up_ref = bf16[640,768]{1,0:T(8,128)(2,1)} collective-permute-done((bf16[640,768]{1,0:T(8,128)(2,1)}, bf16[640,768]{1,0:T(8,128)(2,1)}, u32[]{:S(2)}, u32[]{:S(2)}) %collective-permute-start.28) | collective-permute-done | bytes 983072 | tf_op jit(solution)/shard_map/ppermute | solution.py:695
  442.8 5.4 collective-permute-start.30
  452.9 7.9 %shard_map.281 = (bf16[512,768]{1,0:T(8,128)(2,1)S(1)}, f32[512,768]{1,0:T(8,128)}, bf16[6,512,128]{2,1,0:T(8,128)(2,1)S(1)}, f32[896,768]{1,0:T(8,128)}) custom-call(s32[2]{0:T(128)S(1)} %bitcast.80, bf16[8,80,768]{2,1,0:T(8,128)(2,1)S(1)} %all-to-all-done.4.refs_1_, bf16[8,80,768]{2,1,0:T(8,128)(2,1)S(1)} %all-to-all-done.5.refs_2_, ...), custom_call_target="tpu_custom_call" | custom-call | flops 1 | bytes 1 | tf_op jit(solution)/shard_map/pallas_call | solution.py:502
  462.7 33.7 %shard_map.285 = (f32[2432,768]{1,0:T(8,128)}, bf16[512,768]{1,0:T(8,128)(2,1)}) custom-call(s32[2]{0:T(128)} %bitcast.75, bf16[3,6,512,128]{3,2,1,0:T(8,128)(2,1)} %get-tuple-element.131.refs_1_, f32[512,128]{1,0:T(8,128)} %copy-done.65, f32[12,1,1024]{2,1,0:T(1,128)} %broadcast_in_dim.23.refs_9_.refs_3_, f32[1024,32]{1,0:T(8,128)} %constant.192.clone.refs_4_, ...), custom_call_target="tpu_custom_call" | custom-call | flops 1 | bytes 1 | tf_op jit(solution)/shard_map/pallas_call | solution.py:613
  509.2 5.5 collective-permute-start.32
  516.0 9.9 %collective-permute-done.38.refs_2_ = bf16[640,768]{1,0:T(8,128)(2,1)S(1)} collective-permute-done((bf16[640,768]{1,0:T(8,128)(2,1)S(1)}, bf16[640,768]{1,0:T(8,128)(2,1)S(1)}, u32[]{:S(2)}, u32[]{:S(2)}) %collective-permute-start.38) | collective-permute-done | bytes 983072 | tf_op jit(solution)/shard_map/ppermute | solution.py:695
  525.9 4.6 collective-permute-done.39.refs_3_
  532.5 4.6 all-to-all-start.7
  537.1 6.3 collective-permute-done.32.refs_2_
  543.4 4.3 collective-permute-done.33.refs_3_
  557.5 27.0 %shard_map.283 = (f32[8,768,768]{2,1,0:T(8,128)}, f32[8,768,768]{2,1,0:T(8,128)}) custom-call(bf16[8,320,768]{2,1,0:T(8,128)(2,1)S(1)} %copy-done.15, bf16[8,320,768]{2,1,0:T(8,128)(2,1)} %get-tuple-element.117.refs_1_, bf16[8,320,768]{2,1,0:T(8,128)(2,1)} %get-tuple-element.118.refs_2_, bf16[8,320,768]{2,1,0:T(8,128)(2,1)} %get-tuple-element.119.refs_3_, ...), custom_call_target="tpu_custom_call" | custom-call | flops 1 | bytes 1 | tf_op jit(solution)/shard_map/pallas_call | solution.py:435
  586.5 8.4 %shard_map.291 = (bf16[512,768]{1,0:T(8,128)(2,1)S(1)}, f32[512,768]{1,0:T(8,128)}, bf16[6,512,128]{2,1,0:T(8,128)(2,1)S(1)}, bf16[896,768]{1,0:T(8,128)(2,1)}) custom-call(f32[8,768,768]{2,1,0:T(8,128)} %get-tuple-element.182.refs_0_, s32[2]{0:T(128)S(1)} %bitcast.81, bf16[8,80,768]{2,1,0:T(8,128)(2,1)S(1)} %all-to-all-done.6.refs_2_, ...), custom_call_target="tpu_custom_call" | custom-call | flops 1 | bytes 1 | tf_op jit(solution)/shard_map/pallas_call | solution.py:502
  598.3 35.0 %shard_map.292 = (bf16[2432,768]{1,0:T(8,128)(2,1)}, bf16[512,768]{1,0:T(8,128)(2,1)}) custom-call(s32[2]{0:T(128)} %bitcast.76, bf16[3,6,512,128]{3,2,1,0:T(8,128)(2,1)} %get-tuple-element.152.refs_1_, f32[512,128]{1,0:T(8,128)} %copy-done.62, f32[12,1,1024]{2,1,0:T(1,128)} %broadcast_in_dim.23.refs_9_.refs_3_, f32[1024,32]{1,0:T(8,128)} %constant.192.clone.refs_4_, ...), custom_call_target="tpu_custom_call" | custom-call | flops 1 | bytes 1 | tf_op jit(solution)/shard_map/pallas_call | solution.py:613
  654.9 5.9 collective-permute-done.60
  674.7 8.2 %collective-permute-done.41 = bf16[304,768]{1,0:T(8,128)(2,1)S(1)} collective-permute-done((bf16[304,768]{1,0:T(8,128)(2,1)S(1)}, bf16[304,768]{1,0:T(8,128)(2,1)S(1)}, u32[]{:S(2)}, u32[]{:S(2)}) %collective-permute-start.41) | collective-permute-done | bytes 466976 | tf_op jit(solution)/shard_map/ppermute | solution.py:730
  693.7 7.9 %collective-permute-done.43 = bf16[152,768]{1,0:T(8,128)(2,1)S(1)} collective-permute-done((bf16[152,768]{1,0:T(8,128)(2,1)S(1)}, bf16[152,768]{1,0:T(8,128)(2,1)S(1)}, u32[]{:S(2)}, u32[]{:S(2)}) %collective-permute-start.43) | collective-permute-done | bytes 233504 | tf_op jit(solution)/shard_map/ppermute | solution.py:759
  701.6 7.4 collective-permute-done.44
  714.0 10.3 %collective-permute-done.51 = bf16[152,768]{1,0:T(8,128)(2,1)S(1)} collective-permute-done((bf16[152,768]{1,0:T(8,128)(2,1)S(1)}, bf16[152,768]{1,0:T(8,128)(2,1)S(1)}, u32[]{:S(2)}, u32[]{:S(2)}) %collective-permute-start.51) | collective-permute-done | bytes 233504 | tf_op jit(solution)/shard_map/ppermute | solution.py:759
  726.7 6.5 collective-permute-done.53
  (368 shorter events, 242.1 us)
Async XLA Ops:
  55.7 20.3 %all-to-all-start.1 = ((bf16[8,96,768]{2,1,0:T(8,128)(2,1)}), bf16[8,96,768]{2,1,0:T(8,128)(2,1)S(1)}, u32[]{:S(2)}, u32[]{:S(2)}) async-start(bf16[8,96,768]{2,1,0:T(8,128)(2,1)} %copy-done.38), calls=%async_computation.1 | async-start | bytes 2359296 | tf_op jit(solution)/shard_map/all_to_all | solution.py:815
  59.3 30.5 %collective-permute-start.9 = (bf16[640,768]{1,0:T(8,128)(2,1)S(1)}, bf16[640,768]{1,0:T(8,128)(2,1)}, u32[]{:S(2)}, u32[]{:S(2)}) collective-permute-start(bf16[640,768]{1,0:T(8,128)(2,1)S(1)} %shard_map.266.refs_0_.refs_10_), channel_id=1, source_target_pairs={{0,1},{1,2},{2,3},{4,5},{5,6},{6,7},{8,9},{9,10},{10,11},{12,13},{... | collective-permute-start | bytes 2949128 | tf_op jit(solution)/shard_map/ppermute | solution.py:695
  81.0 27.1 %collective-permute-start = (bf16[656,768]{1,0:T(8,128)(2,1)S(1)}, bf16[656,768]{1,0:T(8,128)(2,1)S(1)}, u32[]{:S(2)}, u32[]{:S(2)}) collective-permute-start(bf16[656,768]{1,0:T(8,128)(2,1)S(1)} %shard_map.268.refs_0_.refs_3_.refs_17_), channel_id=1, source_target_pairs={{3,2},{2,1},{1,0},{7,6},{6,5},{5,4},{11,10},{10,9},{9,8},{15,14},{... | collective-permute-start | bytes 3022856 | tf_op jit(solution)/shard_map/ppermute | solution.py:696
  82.3 47.0 %collective-permute-start.6 = (bf16[640,768]{1,0:T(8,128)(2,1)S(1)}, bf16[640,768]{1,0:T(8,128)(2,1)}, u32[]{:S(2)}, u32[]{:S(2)}) collective-permute-start(bf16[640,768]{1,0:T(8,128)(2,1)S(1)} %shard_map.266.refs_0_.refs_10_), channel_id=1, source_target_pairs={{3,2},{2,1},{1,0},{7,6},{6,5},{5,4},{11,10},{10,9},{9,8},{15,14},{... | collective-permute-start | bytes 2949128 | tf_op jit(solution)/shard_map/ppermute | solution.py:696
  83.6 47.0 %collective-permute-start.3 = (bf16[656,768]{1,0:T(8,128)(2,1)S(1)}, bf16[656,768]{1,0:T(8,128)(2,1)}, u32[]{:S(2)}, u32[]{:S(2)}) collective-permute-start(bf16[656,768]{1,0:T(8,128)(2,1)S(1)} %shard_map.268.refs_0_.refs_3_.refs_17_), channel_id=1, source_target_pairs={{0,1},{1,2},{2,3},{4,5},{5,6},{6,7},{8,9},{9,10},{10,11},{12,13},{... | collective-permute-start | bytes 3022856 | tf_op jit(solution)/shard_map/ppermute | solution.py:695
  89.7 42.5 %collective-permute-start.10 = (bf16[640,768]{1,0:T(8,128)(2,1)}, bf16[640,768]{1,0:T(8,128)(2,1)}, u32[]{:S(2)}, u32[]{:S(2)}) collective-permute-start(bf16[640,768]{1,0:T(8,128)(2,1)} %collective-permute-done.9.refs_14_), channel_id=1, source_target_pairs={{1,2},{2,3},{5,6},{6,7},{9,10},{10,11},{13,14},{14,15},{17,18},{18... | collective-permute-start | bytes 2949128 | tf_op jit(solution)/shard_map/ppermute | solution.py:695
  108.1 55.2 %collective-permute-start.1 = (bf16[656,768]{1,0:T(8,128)(2,1)S(1)}, bf16[656,768]{1,0:T(8,128)(2,1)}, u32[]{:S(2)}, u32[]{:S(2)}) collective-permute-start(bf16[656,768]{1,0:T(8,128)(2,1)S(1)} %collective-permute-done.refs_4_.refs_18_), channel_id=1, source_target_pairs={{2,1},{1,0},{6,5},{5,4},{10,9},{9,8},{14,13},{13,12},{18,17},{17,1... | collective-permute-start | bytes 3022856 | tf_op jit(solution)/shard_map/ppermute | solution.py:696
  129.3 38.6 %collective-permute-start.7 = (bf16[640,768]{1,0:T(8,128)(2,1)}, bf16[640,768]{1,0:T(8,128)(2,1)}, u32[]{:S(2)}, u32[]{:S(2)}) collective-permute-start(bf16[640,768]{1,0:T(8,128)(2,1)} %collective-permute-done.6.refs_11_), channel_id=1, source_target_pairs={{2,1},{1,0},{6,5},{5,4},{10,9},{9,8},{14,13},{13,12},{18,17},{17,1... | collective-permute-start | bytes 2949128 | tf_op jit(solution)/shard_map/ppermute | solution.py:696
  130.6 51.6 %collective-permute-start.4 = (bf16[656,768]{1,0:T(8,128)(2,1)}, bf16[656,768]{1,0:T(8,128)(2,1)}, u32[]{:S(2)}, u32[]{:S(2)}) collective-permute-start(bf16[656,768]{1,0:T(8,128)(2,1)} %collective-permute-done.3.refs_7_.refs_21_), channel_id=1, source_target_pairs={{1,2},{2,3},{5,6},{6,7},{9,10},{10,11},{13,14},{14,15},{17,18},{18... | collective-permute-start | bytes 3022856 | tf_op jit(solution)/shard_map/ppermute | solution.py:695
  132.3 61.8 %collective-permute-start.11 = (bf16[640,768]{1,0:T(8,128)(2,1)}, bf16[640,768]{1,0:T(8,128)(2,1)}, u32[]{:S(2)}, u32[]{:S(2)}) collective-permute-start(bf16[640,768]{1,0:T(8,128)(2,1)} %collective-permute-done.10.refs_15_), channel_id=1, source_target_pairs={{2,3},{6,7},{10,11},{14,15},{18,19},{22,23},{26,27},{30,31}} | collective-permute-start | bytes 2949128 | tf_op jit(solution)/shard_map/ppermute | solution.py:695
  163.3 54.6 %collective-permute-start.2 = (bf16[656,768]{1,0:T(8,128)(2,1)}, bf16[656,768]{1,0:T(8,128)(2,1)}, u32[]{:S(2)}, u32[]{:S(2)}) collective-permute-start(bf16[656,768]{1,0:T(8,128)(2,1)} %collective-permute-done.1.refs_5_.refs_19_), channel_id=1, source_target_pairs={{1,0},{5,4},{9,8},{13,12},{17,16},{21,20},{25,24},{29,28}} | collective-permute-start | bytes 3022856 | tf_op jit(solution)/shard_map/ppermute | solution.py:696
  167.9 47.6 %collective-permute-start.8 = (bf16[640,768]{1,0:T(8,128)(2,1)}, bf16[640,768]{1,0:T(8,128)(2,1)}, u32[]{:S(2)}, u32[]{:S(2)}) collective-permute-start(bf16[640,768]{1,0:T(8,128)(2,1)} %collective-permute-done.7.refs_12_), channel_id=1, source_target_pairs={{1,0},{5,4},{9,8},{13,12},{17,16},{21,20},{25,24},{29,28}} | collective-permute-start | bytes 2949128 | tf_op jit(solution)/shard_map/ppermute | solution.py:696
  182.2 37.0 %collective-permute-start.5 = (bf16[656,768]{1,0:T(8,128)(2,1)}, bf16[656,768]{1,0:T(8,128)(2,1)}, u32[]{:S(2)}, u32[]{:S(2)}) collective-permute-start(bf16[656,768]{1,0:T(8,128)(2,1)} %collective-permute-done.4.refs_8_.refs_22_), channel_id=1, source_target_pairs={{2,3},{6,7},{10,11},{14,15},{18,19},{22,23},{26,27},{30,31}} | collective-permute-start | bytes 3022856 | tf_op jit(solution)/shard_map/ppermute | solution.py:695
  184.8 57.0 %collective-permute-start.20 = (bf16[640,768]{1,0:T(8,128)(2,1)S(1)}, bf16[640,768]{1,0:T(8,128)(2,1)}, u32[]{:S(2)}, u32[]{:S(2)}) collective-permute-start(bf16[640,768]{1,0:T(8,128)(2,1)S(1)} %shard_map.271.refs_1_.refs_3_), channel_id=1, source_target_pairs={{0,1},{1,2},{2,3},{4,5},{5,6},{6,7},{8,9},{9,10},{10,11},{12,13},{... | collective-permute-start | bytes 2949128 | tf_op jit(solution)/shard_map/ppermute | solution.py:695
  194.1 47.7 %collective-permute-start.21 = (bf16[640,768]{1,0:T(8,128)(2,1)S(1)}, bf16[640,768]{1,0:T(8,128)(2,1)}, u32[]{:S(2)}, u32[]{:S(2)}) collective-permute-start(bf16[640,768]{1,0:T(8,128)(2,1)S(1)} %shard_map.271.refs_1_.refs_3_), channel_id=1, source_target_pairs={{3,2},{2,1},{1,0},{7,6},{6,5},{5,4},{11,10},{10,9},{9,8},{15,14},{... | collective-permute-start | bytes 2949128 | tf_op jit(solution)/shard_map/ppermute | solution.py:696
  215.5 36.0 %collective-permute-start.12 = (bf16[640,768]{1,0:T(8,128)(2,1)S(1)}, bf16[640,768]{1,0:T(8,128)(2,1)}, u32[]{:S(2)}, u32[]{:S(2)}) collective-permute-start(bf16[640,768]{1,0:T(8,128)(2,1)S(1)} %shard_map.270.refs_0_.refs_10_), channel_id=1, source_target_pairs={{0,1},{1,2},{2,3},{4,5},{5,6},{6,7},{8,9},{9,10},{10,11},{12,13},{... | collective-permute-start | bytes 2949128 | tf_op jit(solution)/shard_map/ppermute | solution.py:695
  217.9 39.7 %collective-permute-start.13 = (bf16[640,768]{1,0:T(8,128)(2,1)S(1)}, bf16[640,768]{1,0:T(8,128)(2,1)}, u32[]{:S(2)}, u32[]{:S(2)}) collective-permute-start(bf16[640,768]{1,0:T(8,128)(2,1)S(1)} %shard_map.270.refs_0_.refs_10_), channel_id=1, source_target_pairs={{3,2},{2,1},{1,0},{7,6},{6,5},{5,4},{11,10},{10,9},{9,8},{15,14},{... | collective-permute-start | bytes 2949128 | tf_op jit(solution)/shard_map/ppermute | solution.py:696
  245.6 26.8 %collective-permute-start.22 = (bf16[640,768]{1,0:T(8,128)(2,1)S(1)}, bf16[640,768]{1,0:T(8,128)(2,1)S(1)}, u32[]{:S(2)}, u32[]{:S(2)}) collective-permute-start(bf16[640,768]{1,0:T(8,128)(2,1)S(1)} %get-tuple-element.104), channel_id=1, source_target_pairs={{0,1},{1,2},{2,3},{4,5},{5,6},{6,7},{8,9},{9,10},{10,11},{12,13},{... | collective-permute-start | bytes 2949128 | tf_op jit(solution)/shard_map/ppermute | solution.py:695
  250.2 28.4 %collective-permute-start.23 = (bf16[640,768]{1,0:T(8,128)(2,1)S(1)}, bf16[640,768]{1,0:T(8,128)(2,1)S(1)}, u32[]{:S(2)}, u32[]{:S(2)}) collective-permute-start(bf16[640,768]{1,0:T(8,128)(2,1)S(1)} %get-tuple-element.105), channel_id=1, source_target_pairs={{3,2},{2,1},{1,0},{7,6},{6,5},{5,4},{11,10},{10,9},{9,8},{15,14},{... | collective-permute-start | bytes 2949128 | tf_op jit(solution)/shard_map/ppermute | solution.py:696
  260.3 33.1 %collective-permute-start.14 = (bf16[640,768]{1,0:T(8,128)(2,1)S(1)}, bf16[640,768]{1,0:T(8,128)(2,1)S(1)}, u32[]{:S(2)}, u32[]{:S(2)}) collective-permute-start(bf16[640,768]{1,0:T(8,128)(2,1)S(1)} %get-tuple-element.94), channel_id=1, source_target_pairs={{0,1},{1,2},{2,3},{4,5},{5,6},{6,7},{8,9},{9,10},{10,11},{12,13},{... | collective-permute-start | bytes 2949128 | tf_op jit(solution)/shard_map/ppermute | solution.py:695
  261.7 37.9 %collective-permute-start.15 = (bf16[640,768]{1,0:T(8,128)(2,1)S(1)}, bf16[640,768]{1,0:T(8,128)(2,1)S(1)}, u32[]{:S(2)}, u32[]{:S(2)}) collective-permute-start(bf16[640,768]{1,0:T(8,128)(2,1)S(1)} %get-tuple-element.95), channel_id=1, source_target_pairs={{3,2},{2,1},{1,0},{7,6},{6,5},{5,4},{11,10},{10,9},{9,8},{15,14},{... | collective-permute-start | bytes 2949128 | tf_op jit(solution)/shard_map/ppermute | solution.py:696
  279.5 34.9 %collective-permute-start.24 = (bf16[640,768]{1,0:T(8,128)(2,1)S(1)}, bf16[640,768]{1,0:T(8,128)(2,1)S(1)}, u32[]{:S(2)}, u32[]{:S(2)}) collective-permute-start(bf16[640,768]{1,0:T(8,128)(2,1)S(1)} %get-tuple-element.107), channel_id=1, source_target_pairs={{0,1},{1,2},{2,3},{4,5},{5,6},{6,7},{8,9},{9,10},{10,11},{12,13},{... | collective-permute-start | bytes 2949128 | tf_op jit(solution)/shard_map/ppermute | solution.py:695
  281.0 39.7 %collective-permute-start.25 = (bf16[640,768]{1,0:T(8,128)(2,1)S(1)}, bf16[640,768]{1,0:T(8,128)(2,1)S(1)}, u32[]{:S(2)}, u32[]{:S(2)}) collective-permute-start(bf16[640,768]{1,0:T(8,128)(2,1)S(1)} %get-tuple-element.108), channel_id=1, source_target_pairs={{3,2},{2,1},{1,0},{7,6},{6,5},{5,4},{11,10},{10,9},{9,8},{15,14},{... | collective-permute-start | bytes 2949128 | tf_op jit(solution)/shard_map/ppermute | solution.py:696
  300.6 34.9 %collective-permute-start.16 = (bf16[640,768]{1,0:T(8,128)(2,1)S(1)}, bf16[640,768]{1,0:T(8,128)(2,1)S(1)}, u32[]{:S(2)}, u32[]{:S(2)}) collective-permute-start(bf16[640,768]{1,0:T(8,128)(2,1)S(1)} %get-tuple-element.97), channel_id=1, source_target_pairs={{0,1},{1,2},{2,3},{4,5},{5,6},{6,7},{8,9},{9,10},{10,11},{12,13},{... | collective-permute-start | bytes 2949128 | tf_op jit(solution)/shard_map/ppermute | solution.py:695
  302.1 39.6 %collective-permute-start.17 = (bf16[640,768]{1,0:T(8,128)(2,1)S(1)}, bf16[640,768]{1,0:T(8,128)(2,1)S(1)}, u32[]{:S(2)}, u32[]{:S(2)}) collective-permute-start(bf16[640,768]{1,0:T(8,128)(2,1)S(1)} %get-tuple-element.98), channel_id=1, source_target_pairs={{3,2},{2,1},{1,0},{7,6},{6,5},{5,4},{11,10},{10,9},{9,8},{15,14},{... | collective-permute-start | bytes 2949128 | tf_op jit(solution)/shard_map/ppermute | solution.py:696
  321.7 56.2 %collective-permute-start.26 = (bf16[640,768]{1,0:T(8,128)(2,1)S(1)}, bf16[640,768]{1,0:T(8,128)(2,1)S(1)}, u32[]{:S(2)}, u32[]{:S(2)}) collective-permute-start(bf16[640,768]{1,0:T(8,128)(2,1)S(1)} %get-tuple-element.109.refs_1_), channel_id=1, source_target_pairs={{0,1},{1,2},{2,3},{4,5},{5,6},{6,7},{8,9},{9,10},{10,11},{12,13},{... | collective-permute-start | bytes 2949128 | tf_op jit(solution)/shard_map/ppermute | solution.py:695
  323.2 56.0 %collective-permute-start.27 = (bf16[640,768]{1,0:T(8,128)(2,1)S(1)}, bf16[640,768]{1,0:T(8,128)(2,1)S(1)}, u32[]{:S(2)}, u32[]{:S(2)}) collective-permute-start(bf16[640,768]{1,0:T(8,128)(2,1)S(1)} %get-tuple-element.110), channel_id=1, source_target_pairs={{3,2},{2,1},{1,0},{7,6},{6,5},{5,4},{11,10},{10,9},{9,8},{15,14},{... | collective-permute-start | bytes 2949128 | tf_op jit(solution)/shard_map/ppermute | solution.py:696
  371.6 23.9 %collective-permute-start.34 = (bf16[640,768]{1,0:T(8,128)(2,1)}, bf16[640,768]{1,0:T(8,128)(2,1)}, u32[]{:S(2)}, u32[]{:S(2)}) collective-permute-start(bf16[640,768]{1,0:T(8,128)(2,1)} %get-tuple-element.139.downsum_ref), channel_id=1, source_target_pairs={{0,1},{4,5},{8,9},{12,13},{16,17},{20,21},{24,25},{28,29}} | collective-permute-start | bytes 2949128 | tf_op jit(solution)/shard_map/ppermute | solution.py:695
  374.0 23.2 %collective-permute-start.35 = (bf16[640,768]{1,0:T(8,128)(2,1)}, bf16[640,768]{1,0:T(8,128)(2,1)}, u32[]{:S(2)}, u32[]{:S(2)}) collective-permute-start(bf16[640,768]{1,0:T(8,128)(2,1)} %get-tuple-element.140.upsum_ref), channel_id=1, source_target_pairs={{3,2},{7,6},{11,10},{15,14},{19,18},{23,22},{27,26},{31,30}} | collective-permute-start | bytes 2949128 | tf_op jit(solution)/shard_map/ppermute | solution.py:696
  375.6 41.0 %collective-permute-start.18 = (bf16[640,768]{1,0:T(8,128)(2,1)}, bf16[640,768]{1,0:T(8,128)(2,1)}, u32[]{:S(2)}, u32[]{:S(2)}) collective-permute-start(bf16[640,768]{1,0:T(8,128)(2,1)} %get-tuple-element.99.refs_0_), channel_id=1, source_target_pairs={{0,1},{1,2},{2,3},{4,5},{5,6},{6,7},{8,9},{9,10},{10,11},{12,13},{... | collective-permute-start | bytes 2949128 | tf_op jit(solution)/shard_map/ppermute | solution.py:695
  377.9 40.3 %collective-permute-start.19 = (bf16[640,768]{1,0:T(8,128)(2,1)}, bf16[640,768]{1,0:T(8,128)(2,1)}, u32[]{:S(2)}, u32[]{:S(2)}) collective-permute-start(bf16[640,768]{1,0:T(8,128)(2,1)} %get-tuple-element.100), channel_id=1, source_target_pairs={{3,2},{2,1},{1,0},{7,6},{6,5},{5,4},{11,10},{10,9},{9,8},{15,14},{... | collective-permute-start | bytes 2949128 | tf_op jit(solution)/shard_map/ppermute | solution.py:696
  381.2 40.5 %all-to-all-start.5 = ((bf16[8,80,768]{2,1,0:T(8,128)(2,1)}), bf16[8,80,768]{2,1,0:T(8,128)(2,1)S(1)}, u32[]{:S(2)}, u32[]{:S(2)}) async-start(bf16[8,80,768]{2,1,0:T(8,128)(2,1)} %shard_map.280), calls=%async_computation.5 | async-start | bytes 1966080 | tf_op jit(solution)/shard_map/all_to_all | solution.py:815
  385.4 52.3 %collective-permute-start.28 = (bf16[640,768]{1,0:T(8,128)(2,1)}, bf16[640,768]{1,0:T(8,128)(2,1)}, u32[]{:S(2)}, u32[]{:S(2)}) collective-permute-start(bf16[640,768]{1,0:T(8,128)(2,1)} %copy-done.47), channel_id=1, source_target_pairs={{0,1},{4,5},{8,9},{12,13},{16,17},{20,21},{24,25},{28,29}} | collective-permute-start | bytes 2949128 | tf_op jit(solution)/shard_map/ppermute | solution.py:695
  395.5 42.1 %collective-permute-start.29 = (bf16[640,768]{1,0:T(8,128)(2,1)}, bf16[640,768]{1,0:T(8,128)(2,1)}, u32[]{:S(2)}, u32[]{:S(2)}) collective-permute-start(bf16[640,768]{1,0:T(8,128)(2,1)} %copy-done.45), channel_id=1, source_target_pairs={{3,2},{7,6},{11,10},{15,14},{19,18},{23,22},{27,26},{31,30}} | collective-permute-start | bytes 2949128 | tf_op jit(solution)/shard_map/ppermute | solution.py:696
  401.2 95.2 %collective-permute-start.36 = (bf16[640,768]{1,0:T(8,128)(2,1)}, bf16[640,768]{1,0:T(8,128)(2,1)}, u32[]{:S(2)}, u32[]{:S(2)}) collective-permute-start(bf16[640,768]{1,0:T(8,128)(2,1)} %get-tuple-element.142), channel_id=1, source_target_pairs={{0,1},{1,2},{4,5},{5,6},{8,9},{9,10},{12,13},{13,14},{16,17},{17,1... | collective-permute-start | bytes 2949128 | tf_op jit(solution)/shard_map/ppermute | solution.py:695
  416.6 79.8 %collective-permute-start.37 = (bf16[640,768]{1,0:T(8,128)(2,1)}, bf16[640,768]{1,0:T(8,128)(2,1)}, u32[]{:S(2)}, u32[]{:S(2)}) collective-permute-start(bf16[640,768]{1,0:T(8,128)(2,1)} %get-tuple-element.143), channel_id=1, source_target_pairs={{3,2},{2,1},{7,6},{6,5},{11,10},{10,9},{15,14},{14,13},{19,18},{18... | collective-permute-start | bytes 2949128 | tf_op jit(solution)/shard_map/ppermute | solution.py:696
  421.7 28.1 %all-to-all-start.4 = ((bf16[8,80,768]{2,1,0:T(8,128)(2,1)}), bf16[8,80,768]{2,1,0:T(8,128)(2,1)S(1)}, u32[]{:S(2)}, u32[]{:S(2)}) async-start(bf16[8,80,768]{2,1,0:T(8,128)(2,1)} %copy-done.17), calls=%async_computation.4 | async-start | bytes 1966080 | tf_op jit(solution)/shard_map/all_to_all | solution.py:815
  442.8 62.4 %collective-permute-start.30 = (bf16[640,768]{1,0:T(8,128)(2,1)}, bf16[640,768]{1,0:T(8,128)(2,1)}, u32[]{:S(2)}, u32[]{:S(2)}) collective-permute-start(bf16[640,768]{1,0:T(8,128)(2,1)} %get-tuple-element.129), channel_id=1, source_target_pairs={{0,1},{1,2},{4,5},{5,6},{8,9},{9,10},{12,13},{13,14},{16,17},{17,1... | collective-permute-start | bytes 2949128 | tf_op jit(solution)/shard_map/ppermute | solution.py:695
  448.2 57.0 %collective-permute-start.31 = (bf16[640,768]{1,0:T(8,128)(2,1)}, bf16[640,768]{1,0:T(8,128)(2,1)}, u32[]{:S(2)}, u32[]{:S(2)}) collective-permute-start(bf16[640,768]{1,0:T(8,128)(2,1)} %get-tuple-element.130), channel_id=1, source_target_pairs={{3,2},{2,1},{7,6},{6,5},{11,10},{10,9},{15,14},{14,13},{19,18},{18... | collective-permute-start | bytes 2949128 | tf_op jit(solution)/shard_map/ppermute | solution.py:696
  502.4 23.5 %collective-permute-start.38 = (bf16[640,768]{1,0:T(8,128)(2,1)S(1)}, bf16[640,768]{1,0:T(8,128)(2,1)S(1)}, u32[]{:S(2)}, u32[]{:S(2)}) collective-permute-start(bf16[640,768]{1,0:T(8,128)(2,1)S(1)} %get-tuple-element.144), channel_id=1, source_target_pairs={{0,1},{1,2},{2,3},{4,5},{5,6},{6,7},{8,9},{9,10},{10,11},{12,13},{... | collective-permute-start | bytes 2949128 | tf_op jit(solution)/shard_map/ppermute | solution.py:695
  503.8 26.7 %collective-permute-start.39 = (bf16[640,768]{1,0:T(8,128)(2,1)S(1)}, bf16[640,768]{1,0:T(8,128)(2,1)S(1)}, u32[]{:S(2)}, u32[]{:S(2)}) collective-permute-start(bf16[640,768]{1,0:T(8,128)(2,1)S(1)} %get-tuple-element.145), channel_id=1, source_target_pairs={{3,2},{2,1},{1,0},{7,6},{6,5},{5,4},{11,10},{10,9},{9,8},{15,14},{... | collective-permute-start | bytes 2949128 | tf_op jit(solution)/shard_map/ppermute | solution.py:696
  509.2 34.2 %collective-permute-start.32 = (bf16[640,768]{1,0:T(8,128)(2,1)}, bf16[640,768]{1,0:T(8,128)(2,1)}, u32[]{:S(2)}, u32[]{:S(2)}) collective-permute-start(bf16[640,768]{1,0:T(8,128)(2,1)} %get-tuple-element.136), channel_id=1, source_target_pairs={{0,1},{1,2},{2,3},{4,5},{5,6},{6,7},{8,9},{9,10},{10,11},{12,13},{... | collective-permute-start | bytes 2949128 | tf_op jit(solution)/shard_map/ppermute | solution.py:695
  514.7 33.0 %collective-permute-start.33 = (bf16[640,768]{1,0:T(8,128)(2,1)}, bf16[640,768]{1,0:T(8,128)(2,1)}, u32[]{:S(2)}, u32[]{:S(2)}) collective-permute-start(bf16[640,768]{1,0:T(8,128)(2,1)} %get-tuple-element.137), channel_id=1, source_target_pairs={{3,2},{2,1},{1,0},{7,6},{6,5},{5,4},{11,10},{10,9},{9,8},{15,14},{... | collective-permute-start | bytes 2949128 | tf_op jit(solution)/shard_map/ppermute | solution.py:696
  551.8 32.7 %all-to-all-start.6 = ((bf16[8,80,768]{2,1,0:T(8,128)(2,1)}), bf16[8,80,768]{2,1,0:T(8,128)(2,1)S(1)}, u32[]{:S(2)}, u32[]{:S(2)}) async-start(bf16[8,80,768]{2,1,0:T(8,128)(2,1)} %copy-done.16), calls=%async_computation.6 | async-start | bytes 1966080 | tf_op jit(solution)/shard_map/all_to_all | solution.py:815
  597.8 38.5 %collective-permute-start.56 = (bf16[448,768]{1,0:T(8,128)(2,1)S(1)}, bf16[448,768]{1,0:T(8,128)(2,1)S(1)}, u32[]{:S(2)}, u32[]{:S(2)}) collective-permute-start(bf16[448,768]{1,0:T(8,128)(2,1)S(1)} %dynamic-slice_bitcast_fusion.1), channel_id=1, source_target_pairs={{0,4},{4,0},{8,12},{12,8},{16,20},{20,16},{24,28},{28,24},{1,5},{5... | collective-permute-start | bytes 2064392 | tf_op jit(solution)/shard_map/ppermute | solution.py:730
  636.2 32.7 %collective-permute-start.40 = (bf16[1216,768]{1,0:T(8,128)(2,1)}, bf16[1216,768]{1,0:T(8,128)(2,1)S(1)}, u32[]{:S(2)}, u32[]{:S(2)}) collective-permute-start(bf16[1216,768]{1,0:T(8,128)(2,1)} %dynamic-slice_bitcast_fusion), channel_id=1, source_target_pairs={{0,4},{4,0},{8,12},{12,8},{16,20},{20,16},{24,28},{28,24},{1,5},{5... | collective-permute-start | bytes 5603336 | tf_op jit(solution)/shard_map/ppermute | solution.py:730
  667.2 67.1 %collective-permute-start.69 = (bf16[56,768]{1,0:T(8,128)(2,1)S(1)}, bf16[56,768]{1,0:T(8,128)(2,1)S(1)}, u32[]{:S(2)}, u32[]{:S(2)}) collective-permute-start(bf16[56,768]{1,0:T(8,128)(2,1)S(1)} %add_convert_fusion.2), channel_id=1, source_target_pairs={{0,8},{4,12},{8,0},{12,4},{16,24},{20,28},{24,16},{28,20},{1,9},{5... | collective-permute-start | bytes 258056 | tf_op jit(solution)/shard_map/ppermute | solution.py:738
  673.2 70.2 %collective-permute-start.63 = (bf16[112,768]{1,0:T(8,128)(2,1)S(1)}, bf16[112,768]{1,0:T(8,128)(2,1)S(1)}, u32[]{:S(2)}, u32[]{:S(2)}) collective-permute-start(bf16[112,768]{1,0:T(8,128)(2,1)S(1)} %pad_maximum_fusion.4), channel_id=1, source_target_pairs={{0,8},{4,12},{8,0},{12,4},{16,24},{20,28},{24,16},{28,20},{1,9},{5... | collective-permute-start | bytes 516104 | tf_op jit(solution)/shard_map/ppermute | solution.py:738
  (117 other events, 1198.7 us)

commit v3 on v2

v3 whole, which is shorter than its diff:
```python
import functools

import jax
import jax.numpy as jnp
import numpy as np
from jax import lax
from jax.experimental import pallas as pl
from jax.experimental.pallas import tpu as pltpu
from jax.sharding import PartitionSpec as P

HEADS = 12
HEAD_DIM = 64
BUCKETS = 32
MAXDIST = 128
PAIR = 2 * HEAD_DIM
PAIRS = HEADS // 2
ROWS = 128

epsilon = 1e-06
negative = -1e30
F32 = jnp.float32
BF16 = jnp.bfloat16
MIB = 1 << 20


def params(mib):
    return pltpu.CompilerParams(vmem_limit_bytes=mib * MIB)


def cost():
    return pl.CostEstimate(flops=1, bytes_accessed=1, transcendentals=0)


def offset_bucket(offsets):
    halfway = BUCKETS // 2
    exact_count = halfway // 2
    relative_distance = np.abs(offsets)
    scaled = (
        np.log(np.maximum(relative_distance, 1) / exact_count)
        / np.log(MAXDIST / exact_count)
        * (halfway - exact_count)
    )
    far_bucket = np.minimum(exact_count + np.floor(scaled).astype(np.int64), halfway - 1)
    near_bucket = np.where(relative_distance < exact_count, relative_distance, far_bucket)
    return (np.where(offsets > 0, halfway, 0) + near_bucket).astype(np.int32)


def dot(a, b):
    return lax.dot_general(a, b, (((1,), (0,)), ((), ())), preferred_element_type=F32)


def dot_t(a, b):
    return lax.dot_general(a, b, (((1,), (1,)), ((), ())), preferred_element_type=F32)


def t_dot(a, b):
    return lax.dot_general(a, b, (((0,), (0,)), ((), ())), preferred_element_type=F32)


def one_hot(condition):
    return jnp.where(condition, 1.0, 0.0).astype(BF16)


def batch_block(array, b):
    rest = array.shape[1:]
    return pl.BlockSpec((1,) + rest, lambda *_: (b,) + (0,) * len(rest))


ANYWHERE = pl.BlockSpec(memory_space=pl.ANY)
WHOLE = pl.BlockSpec(memory_space=pltpu.VMEM)
SCALARS = pl.BlockSpec(memory_space=pltpu.SMEM)


def iota(shape, axis):
    return lax.broadcasted_iota(jnp.int32, shape, axis)


def padded(rows):
    return -(-rows // 16) * 16


def spread_slots(slot, per, message, first=0, last=None):
    last = per if last is None else last
    group = lax.div(jnp.maximum(slot, 0), per)
    inside = slot - group * per
    held = (slot >= 0) & (inside >= first) & (inside < last)
    return jnp.where(held, group * message + inside - first, -1)


def prep_kernel(per, capacity, len_ref, row_ref, col_ref, cot_ref, srow_ref, scol_ref, slots_ref):
    batches, _, length = row_ref.shape
    groups, message, width = slots_ref.shape
    experts = groups * per // capacity
    before = one_hot(iota((length, length), 0) < iota((length, length), 1))
    after = one_hot(iota((length, length), 1) < iota((length, length), 0))
    for b in range(batches):
        count = len_ref[b]
        row = row_ref[b]
        col = col_ref[b]
        valid_row = iota((1, length), 1) < count
        valid_col = iota((length, 1), 0) < count
        chosen_row = iota((experts, length), 0) == row
        chosen_col = iota((length, experts), 1) == col
        earlier_row = dot(one_hot(chosen_row & valid_row), before)
        rank_row = jnp.sum(jnp.where(chosen_row, earlier_row, 0.0), axis=0, keepdims=True).astype(jnp.int32)
        earlier_col = dot(after, one_hot(chosen_col & valid_col))
        rank_col = jnp.sum(jnp.where(chosen_col, earlier_col, 0.0), axis=1, keepdims=True).astype(jnp.int32)
        slot_row = jnp.where(valid_row & (rank_row < capacity), row * capacity + rank_row, -1)
        srow_ref[b] = slot_row
        scol_ref[b] = jnp.where(valid_col & (rank_col < capacity), col * capacity + rank_col, -1)
        if b == 0:
            dispatch = one_hot(iota((groups * message, length), 0) == spread_slots(slot_row, per, message))
            slots_ref[...] = dot(dispatch, cot_ref[0, 0]).astype(BF16).reshape(groups, message, width)


def prep(lengths, routes, cot, groups, per, capacity):
    batches, length = routes.shape
    width = cot.shape[-1]
    vmem = WHOLE
    message = padded(per)
    return pl.pallas_call(
        functools.partial(prep_kernel, per, capacity),
        grid=(1,),
        in_specs=[SCALARS, vmem, vmem, batch_block(cot, 0)],
        out_specs=[vmem] * 3,
        out_shape=[
            jax.ShapeDtypeStruct((batches, 1, length), jnp.int32),
            jax.ShapeDtypeStruct((batches, length, 1), jnp.int32),
            jax.ShapeDtypeStruct((groups, message, width), BF16),
        ],
        compiler_params=params(32),
        cost_estimate=cost(),
    )(lengths, routes.reshape(batches, 1, length), routes.reshape(batches, length, 1), cot)


def regroup_kernel(count, inputs, waits, *refs):
    refs = refs[waits:]
    move_ref, out_ref = refs[0], refs[-1]
    total = refs[1][...].astype(F32)
    for ref in refs[2 : 1 + count]:
        total = total + ref[...].astype(F32)
    out_ref[...] = dot(move_ref[...], total.astype(BF16).reshape(inputs, -1)).astype(BF16).reshape(out_ref.shape)


def regroup(move, arrays, shape, after=()):
    inputs = move.shape[1]
    vmem = pl.BlockSpec(memory_space=pltpu.VMEM)
    return pl.pallas_call(
        functools.partial(regroup_kernel, len(arrays), inputs, len(after)),
        in_specs=[ANYWHERE] * len(after) + [vmem] * (1 + len(arrays)),
        out_specs=vmem,
        out_shape=jax.ShapeDtypeStruct(shape, BF16),
        compiler_params=params(32),
        cost_estimate=cost(),
    )(*after, move, *arrays)


def regroup_gated_kernel(capacity, *refs):
    move_ref, in_ref, out_ref = refs[-3:]
    groups, message, width = in_ref.shape
    total = move_ref.shape[0]
    local = total // (groups * capacity)
    rows = groups * capacity
    flat = in_ref[...].reshape(groups * message, width)
    out_ref[:total, :] = dot(move_ref[...], flat).astype(BF16)
    place = iota((message, 128), 0)
    lane = iota((message, 128), 1)
    columns = []
    for g in range(groups):
        gates = in_ref[g, message - 16 : message, :].astype(F32)[0:1, :]
        parts = [
            jnp.sum(jnp.where(place == lane, gates[:, 128 * k : 128 * (k + 1)], 0.0), axis=1, keepdims=True)
            for k in range(3)
        ]
        wide = iota((message, 128), 1)
        columns.append(jnp.where(wide == 0, parts[0], jnp.where(wide == 1, parts[1], jnp.where(wide == 2, parts[2], 0.0))))
    column = jnp.concatenate(columns, axis=0).astype(BF16)
    moved = dot(move_ref[...], column)
    place = iota((rows, 128), 0)
    lane = iota((rows, 128), 1)
    lines = []
    for l in range(local):
        mine = moved[l * rows : (l + 1) * rows, :]
        parts = [
            jnp.sum(jnp.where(place == lane, mine[:, k : k + 1], 0.0), axis=0, keepdims=True) for k in range(3)
        ]
        lines.append(jnp.concatenate(parts + [jnp.zeros((1, width - 384), F32)], axis=1))
    lines.append(jnp.zeros((16 - local, width), F32))
    out_ref[total:, :] = jnp.concatenate(lines, axis=0).astype(BF16)


def regroup_gated(move, slots, capacity, after=()):
    width = slots.shape[-1]
    vmem = pl.BlockSpec(memory_space=pltpu.VMEM)
    return pl.pallas_call(
        functools.partial(regroup_gated_kernel, capacity),
        in_specs=[ANYWHERE] * len(after) + [vmem] * 2,
        out_specs=vmem,
        out_shape=jax.ShapeDtypeStruct((move.shape[0] + 16, width), BF16),
        compiler_params=params(32),
        cost_estimate=cost(),
    )(*after, move, slots)


def band_bias(vector_ref, head):
    wide = jnp.broadcast_to(vector_ref[head], (ROWS, vector_ref.shape[-1]))
    return pltpu.roll(wide, 0, 1, stride=1, stride_axis=0)


def band_slice(block, length):
    start = length - ROWS * (block + 1)
    return slice(start, start + length)


def attn_kernel(batch, waits, *refs):
    refs = refs[waits:]
    len_ref, tok_ref, gain_ref, wq_ref, wk_ref, wv_ref, vec_ref, qkv_ref, mixed_ref, lse_ref, band_ref, probs_ref, mixed_t_ref = refs
    length, width = tok_ref.shape[2:]
    count = len_ref[batch]
    tokens = tok_ref[0, 0].astype(F32)
    inverse = lax.rsqrt(jnp.mean(tokens * tokens, axis=-1, keepdims=True) + epsilon)
    normed = (tokens * inverse * gain_ref[...]).astype(BF16)
    for which, w_ref in enumerate((wq_ref, wk_ref, wv_ref)):
        for part in range(width // 256):
            rows = dot(normed, w_ref[:, 256 * part : 256 * part + 256]).astype(BF16)
            qkv_ref[which, 2 * part] = rows[:, :PAIR]
            qkv_ref[which, 2 * part + 1] = rows[:, PAIR:]
    mask = jnp.where(iota((1, length), 1) < count, 0.0, negative)
    lane = iota((ROWS, PAIR), 1)
    lse_ref[...] = jnp.zeros_like(lse_ref)

    def one_pair(pair, carry):
        keys = qkv_ref[1, pair]
        values_t = qkv_ref[2, pair].T
        for side in range(2):
            head = 2 * pair + side
            band_ref[...] = band_bias(vec_ref, head)
            mine = (lane >= HEAD_DIM) if side else (lane < HEAD_DIM)
            for block in range(length // ROWS):
                here = slice(ROWS * block, ROWS * (block + 1))
                queries = qkv_ref[0, pair, here, :] * 0.125
                queries = jnp.where(mine, queries, jnp.zeros_like(queries))
                scores = dot_t(queries, keys) + band_ref[:, band_slice(block, length)] + mask
                highest = jnp.max(scores, axis=-1, keepdims=True)
                powers = jnp.exp(scores - highest)
                total = jnp.sum(powers, axis=-1, keepdims=True)
                probs_ref[here, :] = (powers * (1.0 / total)).astype(BF16)
                column = iota((ROWS, lse_ref.shape[1]), 1)
                lse_ref[here, :] = jnp.where(column == head, highest + jnp.log(total), lse_ref[here, :])
            rows = slice(HEAD_DIM * side, HEAD_DIM * (side + 1))
            mixed_t_ref[rows, :] = dot_t(values_t[rows, :], probs_ref[...])
        mixed_ref[pair] = mixed_t_ref[...].T.astype(BF16)
        return carry

    lax.fori_loop(0, PAIRS, one_pair, 0)


def attention_forward(batch, after, counts, tokens, gain, wq, wk, wv, vector):
    length = tokens.shape[2]
    return pl.pallas_call(
        functools.partial(attn_kernel, batch, len(after)),
        grid=(1,),
        in_specs=[ANYWHERE] * len(after) + [SCALARS, batch_block(tokens, batch)] + [WHOLE] * 5,
        out_specs=[WHOLE] * 3,
        out_shape=[
            jax.ShapeDtypeStruct((3, PAIRS, length, PAIR), BF16),
            jax.ShapeDtypeStruct((PAIRS, length, PAIR), BF16),
            jax.ShapeDtypeStruct((length, 128), F32),
        ],
        scratch_shapes=[
            pltpu.VMEM((ROWS, vector.shape[-1]), F32),
            pltpu.VMEM((length, length), BF16),
            pltpu.VMEM((PAIR, length), F32),
        ],
        compiler_params=params(48),
        cost_estimate=cost(),
    )(*after, counts, tokens, gain, wq, wk, wv, vector)


def route_kernel(per, gated, waits, *refs):
    refs = refs[waits:]
    tok_ref, cot_ref, mixed_ref, wo_ref, gffn_ref, wr_ref, srow_ref, rcol_ref, res_ref, probs_ref, *out_refs = refs
    length, width = tok_ref.shape[2:]
    mixed_all = jnp.concatenate([mixed_ref[p] for p in range(PAIRS)], axis=1)
    residual = tok_ref[0, 0].astype(F32) + dot(mixed_all, wo_ref[...])
    res_ref[...] = residual
    inverse = lax.rsqrt(jnp.mean(residual * residual, axis=-1, keepdims=True) + epsilon)
    routed = (residual * inverse * gffn_ref[...]).astype(BF16)
    logits = dot(routed, wr_ref[...])
    powers = jnp.exp(logits - jnp.max(logits, axis=-1, keepdims=True))
    probs = powers / jnp.sum(powers, axis=-1, keepdims=True)
    probs_ref[...] = probs
    gate = jnp.sum(jnp.where(iota(probs.shape, 1) == rcol_ref[0], probs, 0.0), axis=-1, keepdims=True)
    groups, message, _ = out_refs[0].shape
    places = iota((groups * message, length), 0)
    if gated:
        grads = (gate * cot_ref[0, 0].astype(F32)).astype(BF16)
        half = per // 2
        for which, out_ref in enumerate(out_refs):
            place = spread_slots(srow_ref[0], per, message, which * half, (which + 1) * half)
            rows = dot(one_hot(places == place), grads)
            rows = rows + dot(one_hot(places == jnp.where(place < 0, -1, place + half)), routed)
            out_ref[...] = rows.astype(BF16).reshape(out_ref.shape)
        return
    slots_ref = out_refs[0]
    dispatch = one_hot(places == spread_slots(srow_ref[0], per, message))
    slots_ref[...] = dot(dispatch, routed).astype(BF16).reshape(slots_ref.shape)
    first = gate.astype(BF16).astype(F32)
    second = (gate - first).astype(BF16).astype(F32)
    third = gate - first - second
    column = iota((length, PAIR), 1)
    pieces = jnp.where(column == 0, first, jnp.where(column == 1, second, jnp.where(column == 2, third, 0.0)))
    sorted_gates = dot(dispatch, pieces.astype(BF16))
    data = message - 16
    place = iota((data, 128), 0)
    lane = iota((data, 128), 1)
    for g in range(groups):
        mine = sorted_gates[g * message : g * message + data, :]
        parts = [
            jnp.sum(jnp.where(place == lane, mine[:, k : k + 1], 0.0), axis=0, keepdims=True) for k in range(3)
        ]
        line = jnp.concatenate(parts + [jnp.zeros((1, width - 384), F32)], axis=1)
        slots_ref[g, data:message, :] = jnp.broadcast_to(line, (16, width)).astype(BF16)


def route(batch, after, tokens, cot, mixed, wo, gain_ffn, w_router, srow, rcol, groups, per, gated):
    length, width = tokens.shape[2:]
    experts = w_router.shape[1]
    message = padded(per) if gated else padded(per) + 16
    return pl.pallas_call(
        functools.partial(route_kernel, per, gated, len(after)),
        grid=(1,),
        in_specs=[ANYWHERE] * len(after)
        + [batch_block(tokens, batch), batch_block(cot, batch)]
        + [WHOLE] * 4
        + [batch_block(srow, batch), batch_block(rcol, batch)],
        out_specs=[WHOLE] * (4 if gated else 3),
        out_shape=[
            jax.ShapeDtypeStruct((length, width), F32),
            jax.ShapeDtypeStruct((length, experts), F32),
        ]
        + [jax.ShapeDtypeStruct((groups, message, width), BF16)] * (2 if gated else 1),
        compiler_params=params(48),
        cost_estimate=cost(),
    )(*after, tokens, cot, mixed, wo, gain_ffn, w_router, srow, rcol)


GELU_SCALE = 0.7978845608028654
GELU_CUBIC = 0.044715


def expert_kernel(planes, gated, first_expert, waits, *refs):
    pieces = 2 * planes - 1
    refs = refs[waits:]
    plane = refs[0][0]
    x_refs, refs = refs[1 : 1 + pieces], refs[1 + pieces :]
    c_refs, refs = refs[:pieces], refs[pieces:]
    gate_refs = ()
    if not gated:
        gate_refs, refs = refs[:pieces], refs[pieces:]
    wi_ref, wo_ref, *refs = refs
    sum_refs = refs[:planes]
    act_ref, pre_ref, x_ref, c_ref = refs[planes:]
    rows = x_refs[0].shape[0]

    def assemble(parts):
        found = [parts[0][...]]
        for k in range(1, planes):
            from_above = plane + k < planes
            found.append(jnp.where(from_above, parts[k][...], parts[2 * planes - 1 - k][...]))
        return found

    inputs = jnp.concatenate(assemble(x_refs), axis=0)
    grads = assemble(c_refs)
    if not gated:
        place = iota((rows, 128), 0)
        lane = iota((rows, 128), 1)
        expert = first_expert + pl.program_id(0)
        for k, lines in enumerate(assemble(gate_refs)):
            lines = jnp.where(iota(lines.shape, 0) == expert, lines.astype(F32), 0.0)
            line = jnp.sum(lines, axis=0, keepdims=True)
            line = line[:, :128] + line[:, 128:256] + line[:, 256:384]
            gate = jnp.sum(jnp.where(place == lane, line, 0.0), axis=1, keepdims=True)
            grads[k] = (grads[k].astype(F32) * gate).astype(BF16)
    grads = jnp.concatenate(grads, axis=0)
    x_ref[0] = inputs
    c_ref[0] = grads
    pre = dot(inputs, wi_ref[0])
    square = pre * pre
    curve = jnp.tanh(GELU_SCALE * pre * (1.0 + GELU_CUBIC * square))
    half = 0.5 * (1.0 + curve)
    act = (pre * half).astype(BF16)
    slope = half + 0.5 * pre * (1.0 - curve * curve) * (GELU_SCALE * (1.0 + 3.0 * GELU_CUBIC * square))
    act_ref[0] = act
    outs = dot(act, wo_ref[0]).astype(BF16)
    pre_grad = (slope * dot_t(grads, wo_ref[0])).astype(BF16)
    pre_ref[0] = pre_grad
    ins = dot_t(pre_grad, wi_ref[0]).astype(BF16)
    for k in range(planes):
        sum_refs[k][0] = outs[k * rows : (k + 1) * rows]
        sum_refs[k][1] = ins[k * rows : (k + 1) * rows]


def experts_half(which, after, plane, messages, w_inner, w_outer, xs=None, cs=None):
    local, width, hidden = w_inner.shape
    mine = local // 2
    first = which * mine
    gated = messages is not None
    pieces = len(messages if gated else xs)
    planes = (pieces + 1) // 2
    if gated:
        rows = messages[0].shape[1] // mine
        x_block = pl.BlockSpec((None, rows, width), lambda e: (1, e, 0))
        c_block = pl.BlockSpec((None, rows, width), lambda e: (0, e, 0))
        arrays = (*messages, *messages)
        blocks = [x_block] * pieces + [c_block] * pieces
    else:
        rows = cs[0].shape[0] // local
        slab = pl.BlockSpec((rows, width), lambda e: (first + e, 0))
        lines = pl.BlockSpec((16, width), lambda e: (local * rows // 16, 0))
        arrays = (*xs, *cs, *xs)
        blocks = [slab] * (2 * pieces) + [lines] * pieces
    weight = lambda a, b: pl.BlockSpec((1, a, b), lambda e: (first + e, 0, 0))
    mat = lambda a, b: pl.BlockSpec((1, a, b), lambda e: (e, 0, 0))
    total = planes * rows
    kept = lambda n: jax.ShapeDtypeStruct((mine, total, n), BF16)
    return pl.pallas_call(
        functools.partial(expert_kernel, planes, gated, first, len(after)),
        grid=(mine,),
        in_specs=[ANYWHERE] * len(after) + [SCALARS] + blocks + [weight(width, hidden), weight(hidden, width)],
        out_specs=[pl.BlockSpec((2, rows, width), lambda e: (0, e, 0))] * planes
        + [mat(total, hidden), mat(total, hidden), mat(total, width), mat(total, width)],
        out_shape=[jax.ShapeDtypeStruct((2, mine * rows, width), BF16)] * planes
        + [kept(hidden), kept(hidden), kept(width), kept(width)],
        compiler_params=params(48),
        cost_estimate=cost(),
    )(*after, plane, *arrays, w_inner, w_outer)


def expert_grad_kernel(batches, waits, *refs):
    xs, cs, acts, pres = (refs[waits + k * batches : waits + (k + 1) * batches] for k in range(4))
    outer_ref, inner_ref = refs[-2:]
    whole = lambda refs: jnp.concatenate([ref[0] for ref in refs], axis=0)
    outer_ref[0] = t_dot(whole(acts), whole(cs))
    inner_ref[0] = t_dot(whole(xs), whole(pres))


def expert_grads(which, after, past, local, xs, cs, acts, pres):
    batches = len(xs)
    mine, total, width = xs[0].shape
    hidden = acts[0].shape[2]
    first = which * mine
    mat = lambda a, b: pl.BlockSpec((1, a, b), lambda e: (e, 0, 0))
    out = lambda a, b: pl.BlockSpec((1, a, b), lambda e: (first + e, 0, 0))
    behind = len(after) + 4 * batches
    return pl.pallas_call(
        functools.partial(expert_grad_kernel, batches, len(after)),
        grid=(mine,),
        in_specs=[ANYWHERE] * len(after)
        + [mat(total, width)] * (2 * batches)
        + [mat(total, hidden)] * (2 * batches)
        + [ANYWHERE] * len(past),
        out_specs=[out(hidden, width), out(width, hidden)],
        out_shape=[
            jax.ShapeDtypeStruct((local, hidden, width), F32),
            jax.ShapeDtypeStruct((local, width, hidden), F32),
        ],
        input_output_aliases={behind + k: k for k in range(len(past))},
        compiler_params=params(48),
        cost_estimate=cost(),
    )(*after, *xs, *cs, *acts, *pres, *past)


def combine_kernel(per, batch, waits, *refs):
    refs = refs[waits:]
    len_ref, low_ref, high_ref, scol_ref, rcol_ref, res_ref, probs_ref, cot_ref, gffn_ref, wr_ref, wo_ref, mixed_ref, *refs = refs
    past_ref = refs.pop(0) if batch else None
    layer_ref, resgrad_ref, mgrad_ref, shared_ref = refs
    length, width = cot_ref.shape[2:]
    experts = wr_ref.shape[1]
    groups, message, _ = low_ref.shape
    valid = iota((length, 1), 0) < len_ref[batch]
    places = iota((length, groups * message), 1)
    half = per // 2
    returned = input_grad = None
    for which, ref in enumerate((low_ref, high_ref)):
        place = spread_slots(scol_ref[0], per, message, which * half, (which + 1) * half)
        rows = ref[...].reshape(groups * message, width)
        out_part = dot(one_hot(places == place), rows)
        in_part = dot(one_hot(places == jnp.where(place < 0, -1, place + half)), rows)
        returned = out_part if returned is None else returned + out_part
        input_grad = in_part if input_grad is None else input_grad + in_part
    residual = res_ref[...]
    probs = probs_ref[...]
    chosen = iota(probs.shape, 1) == rcol_ref[0]
    gate = jnp.sum(jnp.where(chosen, probs, 0.0), axis=-1, keepdims=True)
    layer_ref[...] = jnp.where(valid, residual + gate * returned, 0.0).astype(BF16)
    out_grad = jnp.where(valid, cot_ref[0, 0].astype(F32), 0.0)
    gate_grad = jnp.sum(out_grad * returned, axis=-1, keepdims=True)
    prob_grad = jnp.where(chosen, gate_grad, 0.0)
    logit_grad = (probs * (prob_grad - jnp.sum(probs * prob_grad, axis=-1, keepdims=True))).astype(BF16)
    inverse = lax.rsqrt(jnp.mean(residual * residual, axis=-1, keepdims=True) + epsilon)
    gain = gffn_ref[...]
    scaled = residual * inverse
    routed = (scaled * gain).astype(BF16)

    def share(first, whole_rows):
        for side in range(2):
            rows = whole_rows[:, side * width // 2 : (side + 1) * width // 2]
            here = slice(side * shared_ref.shape[0] // 2 + first, side * shared_ref.shape[0] // 2 + first + rows.shape[0])
            if past_ref is not None:
                rows = rows + past_ref[here, :]
            shared_ref[here, :] = rows.astype(shared_ref.dtype)

    share(width, t_dot(logit_grad, routed))
    routed_grad = dot_t(logit_grad, wr_ref[...]) + input_grad
    gain_part = jnp.sum(routed_grad * scaled, axis=0, keepdims=True)
    left = shared_ref.shape[0] // 2 - width - experts
    share(width + experts, jnp.where(iota((left, width), 0) == 0, gain_part, 0.0))
    upstream = routed_grad * gain
    middle = jnp.mean(upstream * scaled, axis=-1, keepdims=True)
    residual_grad = out_grad + inverse * (upstream - scaled * middle)
    resgrad_ref[...] = residual_grad
    attended = residual_grad.astype(BF16)
    mixed_all = jnp.concatenate([mixed_ref[p] for p in range(PAIRS)], axis=1)
    share(0, t_dot(mixed_all, attended))
    mixed_grad = dot_t(attended, wo_ref[...]).astype(BF16)
    for pair in range(PAIRS):
        mgrad_ref[pair] = mixed_grad[:, pair * PAIR : (pair + 1) * PAIR]


def combine(
    batch, last, after, counts, low, high, scol, rcol, residual, probs, cot, gain_ffn, w_router, w_output, mixed, past, per, shared
):
    length, width = cot.shape[2:]
    return pl.pallas_call(
        functools.partial(combine_kernel, per, batch, len(after)),
        grid=(1,),
        in_specs=[ANYWHERE] * len(after)
        + [SCALARS, WHOLE, WHOLE, batch_block(scol, batch), batch_block(rcol, batch), WHOLE, WHOLE, batch_block(cot, batch)]
        + [WHOLE] * (4 + len(past)),
        out_specs=[WHOLE] * 4,
        out_shape=[
            jax.ShapeDtypeStruct((length, width), BF16),
            jax.ShapeDtypeStruct((length, width), F32),
            jax.ShapeDtypeStruct((PAIRS, length, PAIR), BF16),
            jax.ShapeDtypeStruct((shared, width // 2), BF16 if last else F32),
        ],
        compiler_params=params(48),
        cost_estimate=cost(),
    )(
        *after, counts, low, high, scol, rcol, residual, probs, cot, gain_ffn, w_router, w_output, mixed, *past
    )


def attn_back_kernel(batch, which, waits, *refs):
    refs = refs[waits:]
    len_ref, qkv_ref, lse_ref, vec_ref, sel_ref, mgrad_ref, tok_ref, gain_ref, wq_ref, wk_ref, wv_ref, *refs = refs
    past_ref = refs.pop(0) if batch else None
    if which:
        seen_ref, part_ref, resgrad_ref, *refs = refs
        shared_ref, tgrad_ref, *refs = refs
    else:
        early_ref = refs.pop(0) if batch else None
        shared_ref, diag_out_ref, part_out_ref, *refs = refs
    band_ref, probs_ref, sgrad_ref, spread_ref, low_ref, qt_ref, kt_ref, vt_ref, diag_ref, *buffers, sems = refs
    fetched = [tok_ref.at[batch, 0], wq_ref, wk_ref, wv_ref]
    if past_ref is not None:
        fetched.append(past_ref)
    if which:
        fetched += [part_ref, resgrad_ref]
    elif batch:
        fetched.append(early_ref)
    copies = [pltpu.make_async_copy(ref, buffer, sems.at[k]) for k, (ref, buffer) in enumerate(zip(fetched, buffers))]
    for copy in copies:
        copy.start()
    tok_ref, wq_ref, wk_ref, wv_ref, *buffers = buffers
    if past_ref is not None:
        past_ref = buffers.pop(0)
    if which:
        part_ref, resgrad_ref = buffers
    elif batch:
        early_ref = buffers[0]
    length, width = tok_ref.shape
    first_pair = which * (PAIRS // 2)
    mask = jnp.where(iota((1, length), 1) < len_ref[batch], 0.0, negative)
    lane = iota((ROWS, PAIR), 1)
    diag_ref[...] = seen_ref[...] if which else jnp.zeros_like(diag_ref)

    def one_pair(step, carry):
        pair = first_pair + step
        keys = qkv_ref[1, pair]
        values = qkv_ref[2, pair]
        queries_t = qkv_ref[0, pair].T
        keys_t = qkv_ref[1, pair].T
        grads_t = mgrad_ref[pair].T
        for side in range(2):
            head = 2 * pair + side
            band_ref[...] = band_bias(vec_ref, head)
            spread_ref[...] = jnp.zeros_like(spread_ref)
            mine = (lane >= HEAD_DIM) if side else (lane < HEAD_DIM)
            for block in range(length // ROWS):
                here = slice(ROWS * block, ROWS * (block + 1))
                window = band_slice(block, length)
                queries = qkv_ref[0, pair, here, :] * 0.125
                queries = jnp.where(mine, queries, jnp.zeros_like(queries))
                grads = mgrad_ref[pair, here, :]
                grads = jnp.where(mine, grads, jnp.zeros_like(grads))
                column = iota((ROWS, lse_ref.shape[1]), 1)
                log_total = jnp.sum(jnp.where(column == head, lse_ref[here, :], 0.0), axis=-1, keepdims=True)
                scores = dot_t(queries, keys) + band_ref[:, window] + mask
                probs = jnp.exp(scores - log_total)
                probs_ref[here, :] = probs.astype(BF16)
                weighted = probs * dot_t(grads, values)
                score_grad = weighted - probs * jnp.sum(weighted, axis=-1, keepdims=True)
                spread_ref[:, window] += score_grad
                sgrad_ref[here, :] = score_grad.astype(BF16)
            rows = slice(HEAD_DIM * side, HEAD_DIM * (side + 1))
            qt_ref[rows, :] = dot_t(keys_t[rows, :], sgrad_ref[...]) * 0.125
            kt_ref[rows, :] = dot(queries_t[rows, :], sgrad_ref[...]) * 0.125
            vt_ref[rows, :] = dot(grads_t[rows, :], probs_ref[...])
            size = spread_ref.shape[1]
            eight = spread_ref[0:8, :]
            for move in range(8, ROWS, 8):
                eight = eight + pltpu.roll(spread_ref[move : move + 8, :], size - move, 1)
            diagonal = eight[0:1, :]
            for move in range(1, 8):
                diagonal = diagonal + pltpu.roll(eight[move : move + 1, :], size - move, 1)
            diag_ref[...] = jnp.where(iota(diag_ref.shape, 0) == head, diagonal, diag_ref[...])
        low_ref[0, step] = qt_ref[...].T.astype(BF16)
        low_ref[1, step] = kt_ref[...].T.astype(BF16)
        low_ref[2, step] = vt_ref[...].T.astype(BF16)
        return carry

    lax.fori_loop(0, PAIRS // 2, one_pair, 0)
    for copy in copies:
        copy.wait()
    offset = 0 if which or shared_ref.dtype == F32 else early_ref.shape[0]

    def share(first, rows):
        if past_ref is not None:
            rows = rows + past_ref[first : first + rows.shape[0], :]
        shared_ref[offset + first : offset + first + rows.shape[0], :] = rows.astype(shared_ref.dtype)

    tokens = tok_ref[...].astype(F32)
    inverse = lax.rsqrt(jnp.mean(tokens * tokens, axis=-1, keepdims=True) + epsilon)
    gain = gain_ref[...]
    scaled = tokens * inverse
    normed_t = (scaled * gain).astype(BF16).T
    normed_grad = part_ref[...] if which else jnp.zeros((length, width), F32)
    half = width // 2
    for matrix, w_ref in enumerate((wq_ref, wk_ref, wv_ref)):
        low = jnp.concatenate([low_ref[matrix, p] for p in range(PAIRS // 2)], axis=1)
        share(matrix * width, dot(normed_t, low))
        normed_grad = normed_grad + dot_t(low, w_ref[:, which * half : (which + 1) * half])
    if not which:
        if offset:
            shared_ref[:offset, :] = early_ref[...]
            done = offset + 3 * width
            if done < shared_ref.shape[0]:
                shared_ref[done:, :] = jnp.zeros((shared_ref.shape[0] - done, half), shared_ref.dtype)
        diag_out_ref[...] = diag_ref[...]
        part_out_ref[...] = normed_grad
        return
    gain_part = jnp.sum(normed_grad * scaled, axis=0, keepdims=True)
    bias_part = lax.dot_general(
        diag_ref[...], sel_ref[...], (((1,), (0,)), ((), ())), precision=lax.Precision.HIGHEST, preferred_element_type=F32
    )
    row = iota((8, half), 0)
    gains = jnp.where(row == 0, gain_part[:, :half], jnp.where(row == 1, gain_part[:, half:], 0.0))
    wide = jnp.concatenate([bias_part, jnp.zeros((16, half - bias_part.shape[1]), F32)], axis=1)
    left = shared_ref.shape[0] - 3 * width - 24
    last = [gains, wide] + ([jnp.zeros((left, half), F32)] if left else [])
    share(3 * width, jnp.concatenate(last, axis=0))
    upstream = normed_grad * gain
    middle = jnp.mean(upstream * scaled, axis=-1, keepdims=True)
    tgrad_ref[...] = (resgrad_ref[...] + inverse * (upstream - scaled * middle)).astype(BF16)


def attention_backward(batch, which, last, after, counts, qkv, lse, vector, selector, mixed_grad, tokens, gain, wq, wk, wv, past, more, rows):
    length, width = tokens.shape[2:]
    half = width // 2
    size = vector.shape[-1]
    late = (wq, wk, wv, *past, *(more[1:] if which else more))
    buffers = [((length, width), BF16)] + [(array.shape, array.dtype) for array in late]
    shared = jax.ShapeDtypeStruct((rows, half), BF16 if last else F32)
    if which:
        outs = [shared, jax.ShapeDtypeStruct((length, width), BF16)]
    else:
        outs = [shared, jax.ShapeDtypeStruct((16, size), F32), jax.ShapeDtypeStruct((length, width), F32)]
    return pl.pallas_call(
        functools.partial(attn_back_kernel, batch, which, len(after)),
        grid=(1,),
        in_specs=[ANYWHERE] * len(after)
        + [SCALARS]
        + [WHOLE] * 5
        + [ANYWHERE, WHOLE]
        + [ANYWHERE] * (3 + len(past))
        + [WHOLE if which and k == 0 else ANYWHERE for k in range(len(more))],
        out_specs=[WHOLE] * len(outs),
        out_shape=outs,
        scratch_shapes=[
            pltpu.VMEM((ROWS, size), F32),
            pltpu.VMEM((length, length), BF16),
            pltpu.VMEM((length, length), BF16),
            pltpu.VMEM((ROWS, size), F32),
            pltpu.VMEM((3, PAIRS // 2, length, PAIR), BF16),
            pltpu.VMEM((PAIR, length), F32),
            pltpu.VMEM((PAIR, length), F32),
            pltpu.VMEM((PAIR, length), F32),
            pltpu.VMEM((16, size), F32),
            *(pltpu.VMEM(shape, kind) for shape, kind in buffers),
            pltpu.SemaphoreType.DMA((len(buffers),)),
        ],
        compiler_params=params(56),
        cost_estimate=cost(),
    )(*after, counts, qkv, lse, vector, selector, mixed_grad, tokens, gain, wq, wk, wv, *past, *more)


def unpack_kernel(early, experts, side_ref, mine_ref, other_ref, *refs):
    mine, other = mine_ref[...], other_ref[...]
    second = side_ref[0] == 1
    rows = jnp.concatenate([jnp.where(second, other, mine), jnp.where(second, mine, other)], axis=0).astype(F32)
    half = rows.shape[1]
    width = 2 * half
    if not early:
        q_ref, k_ref, v_ref, gain_ref, bias_ref = refs[3:]
        offset = 0
        gain_ref[...] = jnp.concatenate([rows[3 * width : 3 * width + 1], rows[3 * width + 1 : 3 * width + 2]], axis=1)
        bias_ref[...] = rows[3 * width + 8 : 3 * width + 8 + HEADS, :BUCKETS].T
    else:
        q_ref, k_ref, v_ref, output_ref, router_ref, gain_ref = refs
        offset = 2 * early
        output_ref[...] = jnp.concatenate([rows[:width], rows[early : early + width]], axis=1)
        last = early - 16
        router_ref[...] = jnp.concatenate([rows[width:last], rows[early + width : early + last]], axis=1).T
        gain_ref[...] = jnp.concatenate([rows[last : last + 1], rows[early + last : early + last + 1]], axis=1)
    for k, ref in enumerate((q_ref, k_ref, v_ref)):
        ref[...] = rows[offset + k * width : offset + (k + 1) * width]


def unpack(early, experts, side, mine, other, past):
    half = mine.shape[1]
    width = 2 * half
    matrix = jax.ShapeDtypeStruct((width, width), F32)
    line = jax.ShapeDtypeStruct((1, width), F32)
    columns = pl.BlockSpec((width, half), lambda _: (0, 0 if early else 1))
    if early:
        more = [matrix, jax.ShapeDtypeStruct((width, experts), F32), line]
    else:
        more = [line, jax.ShapeDtypeStruct((BUCKETS, HEADS), F32)]
    return pl.pallas_call(
        functools.partial(unpack_kernel, early, experts),
        grid=(1,),
        in_specs=[SCALARS, WHOLE, WHOLE] + [ANYWHERE] * len(past),
        out_specs=[columns] * 3 + [WHOLE] * len(more),
        out_shape=[matrix] * 3 + more,
        input_output_aliases={3 + k: k for k in range(len(past))},
        compiler_params=params(56),
        cost_estimate=cost(),
    )(side, mine, other, *past)


def upward(planes, first, last):
    return [(k, k + 1) for k in range(first, last)]


def downward(planes, first, last):
    return [(planes - 1 - k, planes - 2 - k) for k in range(first, last)]


def mix_kernel(both, planes, step, waits, here_ref, up_ref, down_ref, upsum_ref, downsum_ref, *refs):
    to_up, to_down = refs[waits:]
    for moving, sums, out, place in (
        (up_ref, upsum_ref, to_up, here_ref[0]),
        (down_ref, downsum_ref, to_down, planes - 1 - here_ref[0]),
    ):
        total = moving[...] + sums[...]
        out[...] = jnp.where(place <= step, total, moving[...]) if both else total


def mix(both, planes, step, here, up, down, upsum, downsum, after):
    kinds, rows, width = up.shape
    block = pl.BlockSpec((1, rows // 2, width), lambda i, j: (i, j, 0))
    return pl.pallas_call(
        functools.partial(mix_kernel, both, planes, step, len(after)),
        grid=(kinds, 2),
        in_specs=[SCALARS] + [block] * 4 + [ANYWHERE] * len(after),
        out_specs=[block] * 2,
        out_shape=[jax.ShapeDtypeStruct(up.shape, BF16)] * 2,
        compiler_params=params(32),
        cost_estimate=cost(),
    )(here, up, down, upsum, downsum, *after)


def gate_kernel(*refs):
    pass


def gate(arrays, after):
    count = len(arrays)
    return pl.pallas_call(
        gate_kernel,
        in_specs=[ANYWHERE] * (count + len(after)),
        out_specs=[ANYWHERE] * count,
        out_shape=[jax.ShapeDtypeStruct(array.shape, array.dtype) for array in arrays],
        input_output_aliases={k: k for k in range(count)},
        cost_estimate=cost(),
    )(*arrays, *after)


class Chain:
    def __init__(self, planes, own=None, sums=None):
        self.planes, self.own, self.sums = planes, own, sums
        self.here = lax.axis_index("hidden")[None]
        self.from_below, self.from_above = [], []
        if own is not None:
            self.up = self.down = own
        else:
            self.up, self.down = sums[planes - 1], sums[1]
        self.count = 0
        self.steps = planes if own is not None and sums is not None else planes - 1

    def send(self):
        planes, s = self.planes, self.count
        if self.own is not None and self.sums is not None:
            first, last = 0, planes - 1
        elif self.own is not None:
            first, last = s, planes - 1
        else:
            first, last = 0, s + 1
        self.up = lax.ppermute(self.up, "hidden", upward(planes, first, last))
        self.down = lax.ppermute(self.down, "hidden", downward(planes, first, last))
        self.count += 1
        if self.own is not None and s < planes - 1:
            self.from_below.append(self.up)
            self.from_above.append(self.down)

    def mix(self, *after):
        planes, s = self.planes, self.count - 1
        both = self.own is not None
        offset = 1 if both else 2
        self.up, self.down = mix(
            both, planes, s, self.here, self.up, self.down, self.sums[planes - offset - s], self.sums[s + offset], after
        )
        self.mixed = self.up

    def gate(self, *after):
        self.up, self.down = gate((self.up, self.down), after)
        self.from_below[-1], self.from_above[-1] = self.up, self.down

    def run(self):
        while self.count < self.steps:
            self.send()
        return self

    def gathered(self):
        return (self.own, *self.from_above, *self.from_below)

    def scattered(self):
        return (self.sums[0], self.up, self.down)


def swap(values, axis, distance):
    return lax.ppermute(values, axis, [(k, k ^ distance) for k in range(lax.axis_size(axis))])


def share_sums(values, axis, near, count):
    me = lax.axis_index(axis) // near
    parts = values.reshape(count, values.shape[0] // count, values.shape[1])
    total = lax.dynamic_index_in_dim(parts, me, 0, keepdims=False).astype(F32)
    for k in range(1, count):
        part = lax.dynamic_index_in_dim(parts, me ^ k, 0, keepdims=False)
        total = total + swap(part, axis, k * near).astype(F32)
    return total.astype(BF16)


def join_sums(values, axis, near, count):
    me = lax.axis_index(axis) // near
    found = [values] + [swap(values, axis, k * near) for k in range(1, count)]
    joined = []
    for j in range(count):
        piece = found[count - 1]
        for k in range(count - 2, -1, -1):
            piece = jnp.where(me ^ k == j, found[k], piece)
        joined.append(piece)
    return jnp.concatenate(joined)


def sum_everywhere(values):
    size = lax.axis_size("expert")
    planes = lax.axis_size("hidden")
    values = share_sums(values, "expert", 2, size // 2)
    values = share_sums(values, "hidden", 1, planes)
    values = join_sums(values, "hidden", 1, planes)
    values = join_sums(values, "expert", 2, size // 2)
    return values, swap(values, "expert", 1)


def share_half(values):
    side = lax.axis_index("expert") % 2
    parts = values.reshape(2, values.shape[0] // 2, values.shape[1])
    mine = lax.dynamic_index_in_dim(parts, side, 0, keepdims=False)
    other = lax.dynamic_index_in_dim(parts, 1 - side, 0, keepdims=False)
    return mine + swap(other, "expert", 1)


def offset_selector(length):
    place = np.arange(2 * length)
    offsets = np.where(place < 2 * length - ROWS, place, place - 2 * length) - (length - ROWS)
    offsets = np.clip(offsets, -(length - 1), length - 1)
    return (offset_bucket(offsets)[:, None] == np.arange(BUCKETS)[None, :]).astype(np.float32)


def moves(groups, local, capacity, message, kinds=1):
    kind, expert, group, slot = np.meshgrid(
        np.arange(kinds), np.arange(local), np.arange(groups), np.arange(capacity), indexing="ij"
    )
    source = (group * message + (kind * local + expert) * capacity + slot).reshape(-1)
    return (source[:, None] == np.arange(groups * message)[None, :]).astype(jnp.bfloat16)


def shards(
    tokens,
    cotangent,
    lengths,
    routes,
    gain_attn,
    w_query,
    w_key,
    w_value,
    w_output,
    bucket_head_bias,
    gain_ffn,
    w_router,
    w_inner,
    w_outer,
):
    batches, _, length, width = tokens.shape
    experts = w_router.shape[1]
    local = w_inner.shape[0]
    groups = lax.axis_size("expert")
    planes = lax.axis_size("hidden")
    capacity = (5 * length + 4 * experts - 1) // (4 * experts)
    per = local * capacity
    rows = groups * capacity
    message = padded(per)
    move = jnp.asarray(moves(groups, local, capacity, message))
    move_gated = jnp.asarray(moves(groups, local, capacity, message + 16))
    move_pair = jnp.asarray(moves(groups, local // 2, capacity, message, 2))
    move_back = jnp.asarray(moves(groups, local // 2, capacity, message, 2).T)
    selector = jnp.asarray(offset_selector(length))
    vector = lax.dot_general(
        bucket_head_bias, selector, (((0,), (1,)), ((), ())), precision=lax.Precision.HIGHEST
    )[:, None, :]
    gain_a = gain_attn[None, :]
    gain_f = gain_ffn[None, :]
    counts = lengths[:, 0]
    plane = lax.axis_index("hidden")[None]

    def to_groups(values):
        return lax.all_to_all(values, "expert", split_axis=0, concat_axis=0, tiled=True)

    def leaving(values, *after):
        return regroup(move_pair, [to_groups(values)], (2, local // 2 * rows, width), after)

    def arriving(chain, *after):
        return to_groups(regroup(move_back, chain.scattered(), (groups, message, width), after))

    def attend(b, *after):
        return attention_forward(b, after, counts, tokens, gain_a, w_query, w_key, w_value, vector)

    def routing(b, *after):
        return route(
            b, after, tokens, cotangent, forward[b][1], w_output, gain_f, w_router, srow, rcol, groups, per, b > 0
        )

    srow, scol, cot_slots = prep(counts, routes.reshape(batches, length), cotangent, groups, per, capacity)
    rcol = routes.reshape(batches, length, 1)
    early_rows = width + experts + 16
    unit = 16 * groups * planes
    first_rows = 2 * early_rows + 3 * width
    first_rows = first_rows + -first_rows % unit
    second_rows = 3 * width + 24
    second_rows = second_rows + -second_rows % unit
    kept, layer_rows, token_grads = [], [], []
    early_part, first_part, second_part = (), (), ()

    def back_tokens(b, after, low, high):
        return combine(
            b,
            b + 1 == batches,
            after,
            counts,
            low,
            high,
            scol,
            rcol,
            *routed[b][:2],
            cotangent,
            gain_f,
            w_router,
            w_output,
            forward[b][1],
            early_part,
            per,
            2 * early_rows,
        )

    def back_half(b, which, after, mixed_grad, more):
        qkv, _, lse = forward[b]
        last = b + 1 == batches
        return attention_backward(
            b,
            which,
            last,
            after,
            counts,
            qkv,
            lse,
            vector,
            selector,
            mixed_grad,
            tokens,
            gain_a,
            w_query,
            w_key,
            w_value,
            second_part if which else first_part,
            more,
            second_rows if which else first_rows if last else 3 * width,
        )

    def grads_half(h, after, past):
        return expert_grads(h, after, past, local, *([k[h][part] for k in kept] for part in (2, 3, 0, 1)))

    grads = regroup(move, [to_groups(cot_slots)], (local * rows, width))
    grad_chain = Chain(planes, grads)
    grad_chain.send()
    forward = [attend(0, grads)]
    routed = [routing(0, grad_chain.up, grad_chain.down)]
    grad_chain.send()
    inputs = regroup_gated(move_gated, to_groups(routed[0][2]), capacity)
    grad_chain.gate(inputs)
    grad_chain.run()
    input_chain = Chain(planes, inputs)
    input_chain.send()
    forward.append(attend(1, inputs))
    routed.append(routing(1))
    input_chain.gate(forward[1][1])
    input_chain.send()
    held = (input_chain.up, input_chain.down, grad_chain.up, grad_chain.down)
    input_chain.run()
    halves = range(2)
    chains = [None, None]
    for b in range(batches):
        last = b + 1 == batches
        before = chains
        messages = [None, None]
        ready = ()
        if not last:
            if b:
                forward.append(attend(b + 1))
                routed.append(routing(b + 1))
            messages = [leaving(m, *held) for m in routed[b + 1][2:]]
            held = ()
            ready = tuple(messages)
        chains, worked = [], []
        for h in halves:
            if b == 0:
                done = experts_half(
                    h, ready, plane, None, w_inner, w_outer, input_chain.gathered(), grad_chain.gathered()
                )
            else:
                before[h].mix(*(w[0] for w in worked))
                tied = (before[h].up, before[h].down)
                if h:
                    tied += (before[0].up, before[0].down)
                done = experts_half(h, ready + tied, plane, before[h].gathered(), w_inner, w_outer)
                before[h].send()
            worked.append(done)
            chains.append(Chain(planes, messages[h], done[:planes]))
            chains[h].send()
        kept.append([w[planes:] for w in worked])
        low_chain, high_chain = chains
        if not last:
            for step in range(1, planes):
                for chain in chains:
                    if step > 1:
                        chain.send()
                    if step < planes - 1:
                        chain.mix()
            if b == 0:
                continue
            low, high = (arriving(chain) for chain in before)
            layer, res_grad, mixed_grad, early_part = back_tokens(b - 1, (), low, high)
            first_part, *more = back_half(b - 1, 0, (), mixed_grad, (early_part,) if b > 1 else ())
            second_part, token_grad = back_half(b - 1, 1, (), mixed_grad, (*more, res_grad))
        else:
            low = arriving(before[0], before[1].up, before[1].down)
            high = arriving(before[1])
            low_chain.mix()
            low_chain.send()
            totals = grads_half(0, (low_chain.mixed,), ())
            high_chain.mix(totals[0])
            high_chain.send()
            low_chain.mix(high)
            low_chain.send()
            layer, res_grad, mixed_grad, early_part = back_tokens(b - 1, (low_chain.mixed,), low, high)
            high_chain.mix(mixed_grad)
            high_chain.send()
            first_part, *more = back_half(
                b - 1, 0, (high_chain.mixed,), mixed_grad, (early_part,) if b > 1 else ()
            )
            low = regroup(move_back, low_chain.scattered(), (groups, message, width), (first_part,))
            second_part, token_grad = back_half(b - 1, 1, (low,), mixed_grad, (*more, res_grad))
            low = to_groups(low)
            high = regroup(move_back, high_chain.scattered(), (groups, message, width), (second_part, low))
            totals = grads_half(1, (high,), totals)
            high = to_groups(high)
        layer_rows.append(layer)
        token_grads.append(token_grad)
        early_part, first_part, second_part = (early_part,), (first_part,), (second_part,)
    layer, res_grad, mixed_grad, early_part = back_tokens(batches - 1, (totals[0],), low, high)
    first_part, *more = back_half(batches - 1, 0, (), mixed_grad, (early_part,))
    side = (lax.axis_index("expert") % 2)[None]
    first_half = share_half(first_part)
    second_part, token_grad = back_half(batches - 1, 1, (first_half,), mixed_grad, (*more, res_grad))
    first_sums = sum_everywhere(first_half)
    second_sums = sum_everywhere(share_half(second_part))
    layer_rows.append(layer)
    token_grads.append(token_grad)
    *attended, output_grad, router_grad, gain_f_grad = unpack(early_rows, experts, side, *first_sums, ())
    query_grad, key_grad, value_grad, gain_a_grad, bias_grad = unpack(0, experts, side, *second_sums, attended)
    return (
        jnp.stack(layer_rows)[:, None],
        jnp.stack(token_grads)[:, None],
        gain_a_grad[0],
        query_grad,
        key_grad,
        value_grad,
        output_grad,
        bias_grad,
        gain_f_grad[0],
        router_grad,
        totals[1],
        totals[0],
    )


def solution(mesh):
    token = P(None, ("expert", "hidden"), None, None)
    placed = (
        token,
        token,
        P(None, ("expert", "hidden")),
        token,
        *(P() for _ in range(8)),
        P("expert", None, "hidden"),
        P("expert", "hidden", None),
    )
    return jax.shard_map(
        shards,
        mesh=mesh,
        in_specs=placed,
        out_specs=(
            token,
            token,
            *(P() for _ in range(8)),
            P("expert", None, "hidden"),
            P("expert", "hidden", None),
        ),
        check_vma=False,
    )
```

time: 773 us -> 679 us (0.88)
  waiting for transfers between devices: 284 us -> 165 us
  blocking collectives: 0 us -> 39.1 us
  starting transfers between devices: 162 us -> 147 us
  Pallas kernels: 240 us -> 250 us
    ppermute x20, waiting for transfers between devices: 85.2 us -> 8.31 us  [send(): self.up = lax.ppermute(self.up, 'hidden', upward(planes, first, last))]
    all_to_all x0 -> x2, blocking collectives: none -> 39.1 us  [to_groups(): lax.all_to_all(values, 'expert', split_axis=0, concat_axis=0, tiled=True)]
    ppermute x32 -> x28, waiting for transfers between devices: 69.3 us -> 35.8 us  [swap(): lax.ppermute(values, axis, [(k, k ^ distance) for k in range(lax.axis_siz...]
    all_to_all x8 -> x6, waiting for transfers between devices: 33.8 us -> 7.49 us  [to_groups(): lax.all_to_all(values, 'expert', split_axis=0, concat_axis=0, tiled=True)]
    ppermute x20, waiting for transfers between devices: 96.2 us -> 113 us  [send(): self.down = lax.ppermute(self.down, 'hidden', downward(planes, first, last))]
    ppermute x20, starting transfers between devices: 67.7 us -> 57.9 us  [send(): self.up = lax.ppermute(self.up, 'hidden', upward(planes, first, last))]
    all_to_all x8 -> x6, starting transfers between devices: 33.1 us -> 24.6 us  [to_groups(): lax.all_to_all(values, 'expert', split_axis=0, concat_axis=0, tiled=True)]
    pallas_call x14 -> x25, Pallas kernels: 197 us -> 202 us  [the longest x4 60.8 us: attention_backward(): pl.pallas_call(functools.partial(attn_back_kernel, batch, which, len(afte...]
  transfers between devices with their start and end apart: 80 -> 74, of which waited for: 42 -> 35; matrix products, arithmetic and copies ran while one was open for 3% -> 2% of each run, Pallas kernels for 27% -> 31%
where the time goes in v3:
time: 679 us; the launch traced here: 668 us
  Pallas kernels  250 us (37%)
  waiting for transfers between devices  165 us (24%)
  starting transfers between devices  147 us (22%)
  local copies, waits for them, and re-layouts  51.9 us (8%)
  blocking collectives  39.1 us (6%)
  other arithmetic  12.5 us (2%)
    ppermute x20, waiting for transfers between devices, send(): self.down = lax.ppermute(self.down, 'hidden', downward(planes, first, last))  113 us
    pallas_call x4, Pallas kernels, attention_backward(): pl.pallas_call(functools.partial(attn_back_kernel, batch, which, len(afte...  60.8 us
    ppermute x20, starting transfers between devices, send(): self.up = lax.ppermute(self.up, 'hidden', upward(planes, first, last))  57.9 us
    pallas_call x4, Pallas kernels, experts_half(): pl.pallas_call(functools.partial(expert_kernel, planes, gated, first, len...  51.7 us
    unnamed x225, local copies, waits for them, and re-layouts  46.4 us
    all_to_all x2, blocking collectives, to_groups(): lax.all_to_all(values, 'expert', split_axis=0, concat_axis=0, tiled=True)  39.1 us
    ppermute x28, starting transfers between devices, swap(): lax.ppermute(values, axis, [(k, k ^ distance) for k in range(lax.axis_siz...  37 us
    ppermute x28, waiting for transfers between devices, swap(): lax.ppermute(values, axis, [(k, k ^ distance) for k in range(lax.axis_siz...  35.8 us
  transfers between devices with their start and end apart: 74, of which 35 were waited for; matrix products, arithmetic and copies ran while one was open for 2% of the time, Pallas kernels for 31%

profile of v3, /device:TPU:0, one launch (start us, length us, event | category | flops | bytes accessed | tf_op | source)
XLA Modules:
  0.0 668.2 jit_solution(8928343536489590325)
XLA Ops:
  7.2 19.7 %all_to_all.40.refs_1_ = bf16[8,80,768]{2,1,0:T(8,128)(2,1)S(1)} all-to-all(bf16[8,80,768]{2,1,0:T(8,128)(2,1)S(1)} %get-tuple-element.117), channel_id=1, replica_groups=mesh['expert'=8,'hidden'=4] {'expert'}, dimensions={0} | all-to-all | bytes 1966080 | tf_op jit(solution)/shard_map/all_to_all | solution.py:962
  28.9 4.4 collective-permute-start
  36.9 14.0 %shard_map.276 = (bf16[3,6,512,128]{3,2,1,0:T(8,128)(2,1)}, bf16[6,512,128]{2,1,0:T(8,128)(2,1)S(1)}, f32[512,128]{1,0:T(8,128)S(1)}) custom-call(bf16[640,768]{1,0:T(8,128)(2,1)} %shard_map.275.refs_0_.refs_10_, s32[2]{0:T(128)S(1)} %bitcast.77, bf16[2,1,512,768]{3,2,1,0:T(8,128)(2,1)} %refs_7_.6, f32[1,768]{1,0:T(1,128)S(1)} %broadcast_in_dim.26.refs_3_.refs_8_.refs_7_, ...), custom_call_target="tpu_custom_call" | custom-call | flops 1 | bytes 1 | tf_op jit(solution)/shard_map/pallas_call | solution.py:260
  53.4 5.1 collective-permute-done.1.refs_1_.refs_11_
  58.5 3.9 shard_map.277
  62.4 19.3 %all_to_all.41.refs_1_ = bf16[8,96,768]{2,1,0:T(8,128)(2,1)S(1)} all-to-all(bf16[8,96,768]{2,1,0:T(8,128)(2,1)S(1)} %get-tuple-element.120), channel_id=1, replica_groups=mesh['expert'=8,'hidden'=4] {'expert'}, dimensions={0} | all-to-all | bytes 2359296 | tf_op jit(solution)/shard_map/all_to_all | solution.py:962
  90.3 13.9 %shard_map.279 = (bf16[3,6,512,128]{3,2,1,0:T(8,128)(2,1)}, bf16[6,512,128]{2,1,0:T(8,128)(2,1)S(1)}, f32[512,128]{1,0:T(8,128)S(1)}) custom-call(bf16[656,768]{1,0:T(8,128)(2,1)S(1)} %shard_map.278.refs_0_.refs_2_.refs_3_.refs_17_, s32[2]{0:T(128)S(1)} %bitcast.78, bf16[2,1,512,768]{3,2,1,0:T(8,128)(2,1)} %refs_7_.6, ...), custom_call_target="tpu_custom_call" | custom-call | flops 1 | bytes 1 | tf_op jit(solution)/shard_map/pallas_call | solution.py:260
  107.1 5.9 collective-permute-done.3.refs_1_
  116.2 18.0 %collective-permute-done.7.refs_1_ = bf16[640,768]{1,0:T(8,128)(2,1)} collective-permute-done((bf16[640,768]{1,0:T(8,128)(2,1)}, bf16[640,768]{1,0:T(8,128)(2,1)}, u32[]{:S(2)}, u32[]{:S(2)}) %collective-permute-start.7) | collective-permute-done | bytes 983072 | tf_op jit(solution)/shard_map/ppermute | solution.py:833
  138.4 4.9 shard_map.282
  145.9 4.4 all-to-all-start.2
  150.3 5.3 collective-permute-done.5.refs_1_.refs_5_.refs_19_
  158.6 6.4 all-to-all-done.2.refs_5_
  165.0 4.2 all-to-all-start.3
  169.3 7.5 %collective-permute-done.9.refs_3_.refs_13_ = bf16[640,768]{1,0:T(8,128)(2,1)} collective-permute-done((bf16[640,768]{1,0:T(8,128)(2,1)}, bf16[640,768]{1,0:T(8,128)(2,1)}, u32[]{:S(2)}, u32[]{:S(2)}) %collective-permute-start.9) | collective-permute-done | bytes 983072 | tf_op jit(solution)/shard_map/ppermute | solution.py:833
  187.2 6.4 collective-permute-start.22
  193.6 4.8 collective-permute-done.12.refs_6_.refs_20_
  199.7 12.9 %shard_map.285 = (bf16[2,320,768]{2,1,0:T(8,128)(2,1)S(1)}, bf16[2,320,768]{2,1,0:T(8,128)(2,1)S(1)}, bf16[2,320,768]{2,1,0:T(8,128)(2,1)S(1)}, bf16[2,320,768]{...) custom-call(bf16[2,320,768]{2,1,0:T(8,128)(2,1)} %shard_map.283.refs, ...), custom_call_target="tpu_custom_call" | custom-call | flops 1 | bytes 1 | tf_op jit(solution)/shard_map/pallas_call | solution.py:427
  212.6 6.9 %collective-permute-done.11.down_ref.refs_4_.refs_11_ = bf16[2,320,768]{2,1,0:T(8,128)(2,1)} collective-permute-done((bf16[2,320,768]{2,1,0:T(8,128)(2,1)}, bf16[2,320,768]{2,1,0:T(8,128)(2,1)}, u32[]{:S(2)}, u32[]{:S(2)}) %collective-permute-start.11) | collective-permute-done | bytes 983072 | tf_op jit(solution)/shard_map/ppermute | solution.py:833
  226.4 12.9 %shard_map.291 = (bf16[2,320,768]{2,1,0:T(8,128)(2,1)S(1)}, bf16[2,320,768]{2,1,0:T(8,128)(2,1)S(1)}, bf16[2,320,768]{2,1,0:T(8,128)(2,1)S(1)}, bf16[2,320,768]{...) custom-call(bf16[2,320,768]{2,1,0:T(8,128)(2,1)} %shard_map.283.refs, ...), custom_call_target="tpu_custom_call" | custom-call | flops 1 | bytes 1 | tf_op jit(solution)/shard_map/pallas_call | solution.py:427
  248.1 13.4 %collective-permute-done.15.down_ref.refs_5_.refs_12_ = bf16[2,320,768]{2,1,0:T(8,128)(2,1)S(1)} collective-permute-done((bf16[2,320,768]{2,1,0:T(8,128)(2,1)S(1)}, bf16[2,320,768]{2,1,0:T(8,128)(2,1)S(1)}, u32[]{:S(2)}, u32[]{:S(2)}) %collective-permute-start.15) | collective-permute-done | bytes 983072 | tf_op jit(solution)/shard_map/ppermute | solution.py:833
  267.4 15.2 %collective-permute-done.25.down_ref.refs_7_.refs_14_ = bf16[2,320,768]{2,1,0:T(8,128)(2,1)S(1)} collective-permute-done((bf16[2,320,768]{2,1,0:T(8,128)(2,1)S(1)}, bf16[2,320,768]{2,1,0:T(8,128)(2,1)S(1)}, u32[]{:S(2)}, u32[]{:S(2)}) %collective-permute-start.25) | collective-permute-done | bytes 983072 | tf_op jit(solution)/shard_map/ppermute | solution.py:833
  287.5 16.1 %collective-permute-done.17.down_ref.refs_6_.refs_13_ = bf16[2,320,768]{2,1,0:T(8,128)(2,1)S(1)} collective-permute-done((bf16[2,320,768]{2,1,0:T(8,128)(2,1)S(1)}, bf16[2,320,768]{2,1,0:T(8,128)(2,1)S(1)}, u32[]{:S(2)}, u32[]{:S(2)}) %collective-permute-start.17) | collective-permute-done | bytes 983072 | tf_op jit(solution)/shard_map/ppermute | solution.py:833
  307.4 12.7 %shard_map.289 = (bf16[2,320,768]{2,1,0:T(8,128)(2,1)S(1)}, bf16[2,320,768]{2,1,0:T(8,128)(2,1)S(1)}, bf16[2,320,768]{2,1,0:T(8,128)(2,1)S(1)}, bf16[2,320,768]{...) custom-call(bf16[2,320,768]{2,1,0:T(8,128)(2,1)S(1)} %get-tuple-elem, ...), custom_call_target="tpu_custom_call" | custom-call | flops 1 | bytes 1 | tf_op jit(solution)/shard_map/pallas_call | solution.py:427
  320.1 5.6 collective-permute-start.18
  332.0 13.7 %collective-permute-done.31.refs_5_.refs_3_ = bf16[2,320,768]{2,1,0:T(8,128)(2,1)S(1)} collective-permute-done((bf16[2,320,768]{2,1,0:T(8,128)(2,1)S(1)}, bf16[2,320,768]{2,1,0:T(8,128)(2,1)S(1)}, u32[]{:S(2)}, u32[]{:S(2)}) %collective-permute-start.31) | collective-permute-done | bytes 983072 | tf_op jit(solution)/shard_map/ppermute | solution.py:833
  346.7 13.3 %shard_map.299 = (bf16[2,320,768]{2,1,0:T(8,128)(2,1)S(1)}, bf16[2,320,768]{2,1,0:T(8,128)(2,1)}, bf16[2,320,768]{2,1,0:T(8,128)(2,1)S(1)}, bf16[2,320,768]{2,1,...) custom-call(bf16[2,320,768]{2,1,0:T(8,128)(2,1)} %get-tuple-element., ...), custom_call_target="tpu_custom_call" | custom-call | flops 1 | bytes 1 | tf_op jit(solution)/shard_map/pallas_call | solution.py:427
  364.0 4.0 shard_map.290
  382.2 13.4 %shard_map.300 = (f32[8,768,768]{2,1,0:T(8,128)}, f32[8,768,768]{2,1,0:T(8,128)}) custom-call(bf16[2,320,768]{2,1,0:T(8,128)(2,1)} %get-tuple-element.140.refs_0_, bf16[4,320,768]{2,1,0:T(8,128)(2,1)S(1)} %copy-done.58, bf16[4,320,768]{2,1,0:T(8,128)(2,1)S(1)} %copy-done.59, bf16[4,320,768]{2,1,0:T(8,128)(2,1)} %get-tuple-element.164.refs_3_, ...), custom_call_target="tpu_custom_call" | custom-call | flops 1 | bytes 1 | tf_op jit(solution)/shard_map/pallas_call | solution.py:456
  395.7 4.3 shard_map.301
  400.0 4.9 collective-permute-start.34
  408.7 4.3 all-to-all-start.5
  420.3 5.4 collective-permute-start.36
  433.0 8.7 %shard_map.298 = (bf16[512,768]{1,0:T(8,128)(2,1)S(1)}, f32[512,768]{1,0:T(8,128)}, bf16[6,512,128]{2,1,0:T(8,128)(2,1)S(1)}, f32[1696,384]{1,0:T(8,128)}) custom-call(bf16[2,320,768]{2,1,0:T(8,128)(2,1)} %get-tuple-element.153.refs_0_, s32[2]{0:T(128)S(1)} %bitcast.79, bf16[8,80,768]{2,1,0:T(8,128)(2,1)S(1)} %copy-done.50, bf16[8,80,768]{2,1,0:T(8,128)(2,1)} %copy-done.28, ...), custom_call_target="tpu_custom_call" | custom-call | flops 1 | bytes 1 | tf_op jit(solution)/shard_map/pallas_call | solution.py:536
  441.7 4.8 shard_map.302
  446.5 4.8 collective-permute-start.38
  452.6 14.9 %shard_map.303 = (f32[2304,384]{1,0:T(8,128)}, f32[16,1024]{1,0:T(8,128)}, f32[512,768]{1,0:T(8,128)}) custom-call(bf16[2,320,768]{2,1,0:T(8,128)(2,1)} %get-tuple-element.174.refs_0_, s32[2]{0:T(128)} %bitcast.72, bf16[3,6,512,128]{3,2,1,0:T(8,128)(2,1)} %get-tuple-element.175.refs_2_, f32[512,128]{1,0:T(8,128)} %copy-done.63, f32[12,1,1024]{2,1,0:T(1,128)} %copy-done.54, ...), custom_call_target="tpu_custom_call" | custom-call | flops 1 | bytes 1 | tf_op jit(solution)/shard_map/pallas_call | solution.py:691
  473.0 4.0 all-to-all-start.6
  477.0 15.6 %shard_map.305 = (f32[2560,384]{1,0:T(8,128)}, bf16[512,768]{1,0:T(8,128)(2,1)}) custom-call(bf16[8,80,768]{2,1,0:T(8,128)(2,1)} %shard_map.304.refs_0_, s32[2]{0:T(128)} %bitcast.73, bf16[3,6,512,128]{3,2,1,0:T(8,128)(2,1)} %get-tuple-element.175.refs_2_, f32[512,128]{1,0:T(8,128)} %copy-done.63, f32[12,1,1024]{2,1,0:T(1,128)} %copy-done.54, ...), custom_call_target="tpu_custom_call" | custom-call | flops 1 | bytes 1 | tf_op jit(solution)/shard_map/pallas_call | solution.py:691
  498.2 4.2 all-to-all-start.7
  505.5 13.5 %shard_map.307 = (f32[8,768,768]{2,1,0:T(8,128)}, f32[8,768,768]{2,1,0:T(8,128)}) custom-call(bf16[8,80,768]{2,1,0:T(8,128)(2,1)} %shard_map.306.refs_0_, bf16[4,320,768]{2,1,0:T(8,128)(2,1)S(1)} %copy-done.60, bf16[4,320,768]{2,1,0:T(8,128)(2,1)S(1)} %copy-done.61, ...), custom_call_target="tpu_custom_call", output_to_operand_aliasing={{0}: (9, {}), {1}: (10, {})} | custom-call | flops 1 | bytes 1 | tf_op jit(solution)/shard_map/pallas_call | solution.py:456
  521.0 8.7 %shard_map.308 = (bf16[512,768]{1,0:T(8,128)(2,1)S(1)}, f32[512,768]{1,0:T(8,128)}, bf16[6,512,128]{2,1,0:T(8,128)(2,1)S(1)}, bf16[1696,384]{1,0:T(8,128)(2,1)}) custom-call(f32[8,768,768]{2,1,0:T(8,128)} %get-tuple-element.245.refs_0_, s32[2]{0:T(128)S(1)} %bitcast.80, bf16[8,80,768]{2,1,0:T(8,128)(2,1)S(1)} %all-to-all-done.6.refs_1_.refs_2_, ...), custom_call_target="tpu_custom_call" | custom-call | flops 1 | bytes 1 | tf_op jit(solution)/shard_map/pallas_call | solution.py:536
  531.5 15.2 %shard_map.309 = (bf16[4096,384]{1,0:T(8,128)(2,1)}, f32[16,1024]{1,0:T(8,128)}, f32[512,768]{1,0:T(8,128)}) custom-call(s32[2]{0:T(128)} %bitcast.74, bf16[3,6,512,128]{3,2,1,0:T(8,128)(2,1)} %get-tuple-element.200.refs_1_.refs_2_, f32[512,128]{1,0:T(8,128)} %copy-done.62, f32[12,1,1024]{2,1,0:T(1,128)} %copy-done.54, ...), custom_call_target="tpu_custom_call" | custom-call | flops 1 | bytes 1 | tf_op jit(solution)/shard_map/pallas_call | solution.py:691
  558.2 15.1 %shard_map.310 = (bf16[2560,384]{1,0:T(8,128)(2,1)}, bf16[512,768]{1,0:T(8,128)(2,1)}) custom-call(bf16[2048,384]{1,0:T(8,128)(2,1)} %copy-done.98, s32[2]{0:T(128)} %bitcast.75, bf16[3,6,512,128]{3,2,1,0:T(8,128)(2,1)} %get-tuple-element.200.refs_1_.refs_2_, f32[512,128]{1,0:T(8,128)} %copy-done.62, f32[12,1,1024]{2,1,0:T(1,128)} %copy-done.54, ...), custom_call_target="tpu_custom_call" | custom-call | flops 1 | bytes 1 | tf_op jit(solution)/shard_map/pallas_call | solution.py:691
  583.4 7.5 %collective-permute-done.59 = bf16[128,384]{1,0:T(8,128)(2,1)S(1)} collective-permute-done((bf16[128,384]{1,0:T(8,128)(2,1)S(1)}, bf16[128,384]{1,0:T(8,128)(2,1)S(1)}, u32[]{:S(2)}, u32[]{:S(2)}) %collective-permute-start.59) | collective-permute-done | bytes 98336 | tf_op jit(solution)/shard_map/ppermute | solution.py:865
  621.7 5.2 collective-permute-done.65
  642.8 4.5 collective-permute-done.52
  652.9 4.9 shard_map.311
  (397 shorter events, 227.3 us)
Async XLA Ops:
  28.9 24.5 %collective-permute-start = (bf16[640,768]{1,0:T(8,128)(2,1)}, bf16[640,768]{1,0:T(8,128)(2,1)}, u32[]{:S(2)}, u32[]{:S(2)}) collective-permute-start(bf16[640,768]{1,0:T(8,128)(2,1)} %shard_map.275.refs_0_.refs_10_), channel_id=1, source_target_pairs={{0,1},{1,2},{2,3},{4,5},{5,6},{6,7},{8,9},{9,10},{10,11},{12,13},{... | collective-permute-start | bytes 2949128 | tf_op jit(solution)/shard_map/ppermute | solution.py:832
  33.3 25.1 %collective-permute-start.1 = (bf16[640,768]{1,0:T(8,128)(2,1)}, bf16[640,768]{1,0:T(8,128)(2,1)}, u32[]{:S(2)}, u32[]{:S(2)}) collective-permute-start(bf16[640,768]{1,0:T(8,128)(2,1)} %shard_map.275.refs_0_.refs_10_), channel_id=1, source_target_pairs={{3,2},{2,1},{1,0},{7,6},{6,5},{5,4},{11,10},{10,9},{9,8},{15,14},{... | collective-permute-start | bytes 2949128 | tf_op jit(solution)/shard_map/ppermute | solution.py:833
  83.3 23.9 %collective-permute-start.2 = (bf16[656,768]{1,0:T(8,128)(2,1)S(1)}, bf16[656,768]{1,0:T(8,128)(2,1)S(1)}, u32[]{:S(2)}, u32[]{:S(2)}) collective-permute-start(bf16[656,768]{1,0:T(8,128)(2,1)S(1)} %shard_map.278.refs_0_.refs_2_.refs_3_.refs_17_), channel_id=1, source_target_pairs={{0,1},{1,2},{2,3},{4,5},{5,6},{6,7},{8,9},{9,10},{10,11},{12,13},{... | collective-permute-start | bytes 3022856 | tf_op jit(solution)/shard_map/ppermute | solution.py:832
  85.9 27.1 %collective-permute-start.3 = (bf16[656,768]{1,0:T(8,128)(2,1)S(1)}, bf16[656,768]{1,0:T(8,128)(2,1)S(1)}, u32[]{:S(2)}, u32[]{:S(2)}) collective-permute-start(bf16[656,768]{1,0:T(8,128)(2,1)S(1)} %shard_map.278.refs_0_.refs_2_.refs_3_.refs_17_), channel_id=1, source_target_pairs={{3,2},{2,1},{1,0},{7,6},{6,5},{5,4},{11,10},{10,9},{9,8},{15,14},{... | collective-permute-start | bytes 3022856 | tf_op jit(solution)/shard_map/ppermute | solution.py:833
  87.2 29.0 %collective-permute-start.6 = (bf16[640,768]{1,0:T(8,128)(2,1)}, bf16[640,768]{1,0:T(8,128)(2,1)}, u32[]{:S(2)}, u32[]{:S(2)}) collective-permute-start(bf16[640,768]{1,0:T(8,128)(2,1)} %collective-permute-done.refs_0_.refs_14_), channel_id=1, source_target_pairs={{1,2},{2,3},{5,6},{6,7},{9,10},{10,11},{13,14},{14,15},{17,18},{18... | collective-permute-start | bytes 2949128 | tf_op jit(solution)/shard_map/ppermute | solution.py:832
  88.8 45.4 %collective-permute-start.7 = (bf16[640,768]{1,0:T(8,128)(2,1)}, bf16[640,768]{1,0:T(8,128)(2,1)}, u32[]{:S(2)}, u32[]{:S(2)}) collective-permute-start(bf16[640,768]{1,0:T(8,128)(2,1)} %collective-permute-done.1.refs_1_.refs_11_), channel_id=1, source_target_pairs={{2,1},{1,0},{6,5},{5,4},{10,9},{9,8},{14,13},{13,12},{18,17},{17,1... | collective-permute-start | bytes 2949128 | tf_op jit(solution)/shard_map/ppermute | solution.py:833
  114.0 41.6 %collective-permute-start.5 = (bf16[656,768]{1,0:T(8,128)(2,1)}, bf16[656,768]{1,0:T(8,128)(2,1)S(1)}, u32[]{:S(2)}, u32[]{:S(2)}) collective-permute-start(bf16[656,768]{1,0:T(8,128)(2,1)} %get-tuple-element.123.refs_4_.refs_18_), channel_id=1, source_target_pairs={{2,1},{1,0},{6,5},{5,4},{10,9},{9,8},{14,13},{13,12},{18,17},{17,1... | collective-permute-start | bytes 3022856 | tf_op jit(solution)/shard_map/ppermute | solution.py:833
  115.4 41.5 %collective-permute-start.4 = (bf16[656,768]{1,0:T(8,128)(2,1)}, bf16[656,768]{1,0:T(8,128)(2,1)S(1)}, u32[]{:S(2)}, u32[]{:S(2)}) collective-permute-start(bf16[656,768]{1,0:T(8,128)(2,1)} %get-tuple-element.122.refs_7_.refs_21_), channel_id=1, source_target_pairs={{1,2},{2,3},{5,6},{6,7},{9,10},{10,11},{13,14},{14,15},{17,18},{18... | collective-permute-start | bytes 3022856 | tf_op jit(solution)/shard_map/ppermute | solution.py:832
  134.2 35.1 %collective-permute-start.8 = (bf16[640,768]{1,0:T(8,128)(2,1)}, bf16[640,768]{1,0:T(8,128)(2,1)}, u32[]{:S(2)}, u32[]{:S(2)}) collective-permute-start(bf16[640,768]{1,0:T(8,128)(2,1)} %get-tuple-element.124.refs_15_), channel_id=1, source_target_pairs={{2,3},{6,7},{10,11},{14,15},{18,19},{22,23},{26,27},{30,31}} | collective-permute-start | bytes 2949128 | tf_op jit(solution)/shard_map/ppermute | solution.py:832
  135.8 41.0 %collective-permute-start.9 = (bf16[640,768]{1,0:T(8,128)(2,1)}, bf16[640,768]{1,0:T(8,128)(2,1)}, u32[]{:S(2)}, u32[]{:S(2)}) collective-permute-start(bf16[640,768]{1,0:T(8,128)(2,1)} %get-tuple-element.125.refs_12_), channel_id=1, source_target_pairs={{1,0},{5,4},{9,8},{13,12},{17,16},{21,20},{25,24},{29,28}} | collective-permute-start | bytes 2949128 | tf_op jit(solution)/shard_map/ppermute | solution.py:833
  155.7 42.8 %collective-permute-start.12 = (bf16[656,768]{1,0:T(8,128)(2,1)S(1)}, bf16[656,768]{1,0:T(8,128)(2,1)}, u32[]{:S(2)}, u32[]{:S(2)}) collective-permute-start(bf16[656,768]{1,0:T(8,128)(2,1)S(1)} %collective-permute-done.5.refs_1_.refs_5_.refs_19_), channel_id=1, source_target_pairs={{1,0},{5,4},{9,8},{13,12},{17,16},{21,20},{25,24},{29,28}} | collective-permute-start | bytes 3022856 | tf_op jit(solution)/shard_map/ppermute | solution.py:833
  157.0 42.7 %collective-permute-start.13 = (bf16[656,768]{1,0:T(8,128)(2,1)S(1)}, bf16[656,768]{1,0:T(8,128)(2,1)}, u32[]{:S(2)}, u32[]{:S(2)}) collective-permute-start(bf16[656,768]{1,0:T(8,128)(2,1)S(1)} %collective-permute-done.4.refs_0_.refs_8_.refs_22_), channel_id=1, source_target_pairs={{2,3},{6,7},{10,11},{14,15},{18,19},{22,23},{26,27},{30,31}} | collective-permute-start | bytes 3022856 | tf_op jit(solution)/shard_map/ppermute | solution.py:832
  179.9 32.7 %collective-permute-start.10 = (bf16[2,320,768]{2,1,0:T(8,128)(2,1)}, bf16[2,320,768]{2,1,0:T(8,128)(2,1)}, u32[]{:S(2)}, u32[]{:S(2)}) collective-permute-start(bf16[2,320,768]{2,1,0:T(8,128)(2,1)} %shard_map.283.refs_0_.refs_3_.refs_10_), channel_id=1, source_target_pairs={{0,1},{1,2},{2,3},{4,5},{5,6},{6,7},{8,9},{9,10},{10,11},{12,13},{... | collective-permute-start | bytes 2949128 | tf_op jit(solution)/shard_map/ppermute | solution.py:832
  182.3 37.1 %collective-permute-start.11 = (bf16[2,320,768]{2,1,0:T(8,128)(2,1)}, bf16[2,320,768]{2,1,0:T(8,128)(2,1)}, u32[]{:S(2)}, u32[]{:S(2)}) collective-permute-start(bf16[2,320,768]{2,1,0:T(8,128)(2,1)} %shard_map.283.refs_0_.refs_3_.refs_10_), channel_id=1, source_target_pairs={{3,2},{2,1},{1,0},{7,6},{6,5},{5,4},{11,10},{10,9},{9,8},{15,14},{... | collective-permute-start | bytes 2949128 | tf_op jit(solution)/shard_map/ppermute | solution.py:833
  187.2 52.1 %collective-permute-start.22 = (bf16[2,320,768]{2,1,0:T(8,128)(2,1)}, bf16[2,320,768]{2,1,0:T(8,128)(2,1)}, u32[]{:S(2)}, u32[]{:S(2)}) collective-permute-start(bf16[2,320,768]{2,1,0:T(8,128)(2,1)} %shard_map.284.refs_1_.refs_5_.refs_12_), channel_id=1, source_target_pairs={{0,1},{1,2},{2,3},{4,5},{5,6},{6,7},{8,9},{9,10},{10,11},{12,13},{... | collective-permute-start | bytes 2949128 | tf_op jit(solution)/shard_map/ppermute | solution.py:832
  198.4 42.0 %collective-permute-start.23 = (bf16[2,320,768]{2,1,0:T(8,128)(2,1)}, bf16[2,320,768]{2,1,0:T(8,128)(2,1)S(1)}, u32[]{:S(2)}, u32[]{:S(2)}) collective-permute-start(bf16[2,320,768]{2,1,0:T(8,128)(2,1)} %shard_map.284.refs_1_.refs_5_.refs_12_), channel_id=1, source_target_pairs={{3,2},{2,1},{1,0},{7,6},{6,5},{5,4},{11,10},{10,9},{9,8},{15,14},{... | collective-permute-start | bytes 2949128 | tf_op jit(solution)/shard_map/ppermute | solution.py:833
  223.2 24.9 %collective-permute-start.14 = (bf16[2,320,768]{2,1,0:T(8,128)(2,1)}, bf16[2,320,768]{2,1,0:T(8,128)(2,1)S(1)}, u32[]{:S(2)}, u32[]{:S(2)}) collective-permute-start(bf16[2,320,768]{2,1,0:T(8,128)(2,1)} %get-tuple-element.130), channel_id=1, source_target_pairs={{0,1},{1,2},{2,3},{4,5},{5,6},{6,7},{8,9},{9,10},{10,11},{12,13},{... | collective-permute-start | bytes 2949128 | tf_op jit(solution)/shard_map/ppermute | solution.py:832
  224.7 36.8 %collective-permute-start.15 = (bf16[2,320,768]{2,1,0:T(8,128)(2,1)S(1)}, bf16[2,320,768]{2,1,0:T(8,128)(2,1)S(1)}, u32[]{:S(2)}, u32[]{:S(2)}) collective-permute-start(bf16[2,320,768]{2,1,0:T(8,128)(2,1)S(1)} %get-tuple-element.131), channel_id=1, source_target_pairs={{3,2},{2,1},{1,0},{7,6},{6,5},{5,4},{11,10},{10,9},{9,8},{15,14},{... | collective-permute-start | bytes 2949128 | tf_op jit(solution)/shard_map/ppermute | solution.py:833
  243.0 24.3 %collective-permute-start.24 = (bf16[2,320,768]{2,1,0:T(8,128)(2,1)S(1)}, bf16[2,320,768]{2,1,0:T(8,128)(2,1)S(1)}, u32[]{:S(2)}, u32[]{:S(2)}) collective-permute-start(bf16[2,320,768]{2,1,0:T(8,128)(2,1)S(1)} %get-tuple-element.145), channel_id=1, source_target_pairs={{0,1},{1,2},{2,3},{4,5},{5,6},{6,7},{8,9},{9,10},{10,11},{12,13},{... | collective-permute-start | bytes 2949128 | tf_op jit(solution)/shard_map/ppermute | solution.py:832
  246.8 35.8 %collective-permute-start.25 = (bf16[2,320,768]{2,1,0:T(8,128)(2,1)S(1)}, bf16[2,320,768]{2,1,0:T(8,128)(2,1)S(1)}, u32[]{:S(2)}, u32[]{:S(2)}) collective-permute-start(bf16[2,320,768]{2,1,0:T(8,128)(2,1)S(1)} %get-tuple-element.146), channel_id=1, source_target_pairs={{3,2},{2,1},{1,0},{7,6},{6,5},{5,4},{11,10},{10,9},{9,8},{15,14},{... | collective-permute-start | bytes 2949128 | tf_op jit(solution)/shard_map/ppermute | solution.py:833
  262.5 25.0 %collective-permute-start.16 = (bf16[2,320,768]{2,1,0:T(8,128)(2,1)S(1)}, bf16[2,320,768]{2,1,0:T(8,128)(2,1)S(1)}, u32[]{:S(2)}, u32[]{:S(2)}) collective-permute-start(bf16[2,320,768]{2,1,0:T(8,128)(2,1)S(1)} %get-tuple-element.133), channel_id=1, source_target_pairs={{0,1},{1,2},{2,3},{4,5},{5,6},{6,7},{8,9},{9,10},{10,11},{12,13},{... | collective-permute-start | bytes 2949128 | tf_op jit(solution)/shard_map/ppermute | solution.py:832
  264.0 39.6 %collective-permute-start.17 = (bf16[2,320,768]{2,1,0:T(8,128)(2,1)S(1)}, bf16[2,320,768]{2,1,0:T(8,128)(2,1)S(1)}, u32[]{:S(2)}, u32[]{:S(2)}) collective-permute-start(bf16[2,320,768]{2,1,0:T(8,128)(2,1)S(1)} %get-tuple-element.134), channel_id=1, source_target_pairs={{3,2},{2,1},{1,0},{7,6},{6,5},{5,4},{11,10},{10,9},{9,8},{15,14},{... | collective-permute-start | bytes 2949128 | tf_op jit(solution)/shard_map/ppermute | solution.py:833
  284.3 41.4 %collective-permute-start.26 = (bf16[2,320,768]{2,1,0:T(8,128)(2,1)}, bf16[2,320,768]{2,1,0:T(8,128)(2,1)S(1)}, u32[]{:S(2)}, u32[]{:S(2)}) collective-permute-start(bf16[2,320,768]{2,1,0:T(8,128)(2,1)} %get-tuple-element.148), channel_id=1, source_target_pairs={{0,1},{1,2},{2,3},{4,5},{5,6},{6,7},{8,9},{9,10},{10,11},{12,13},{... | collective-permute-start | bytes 2949128 | tf_op jit(solution)/shard_map/ppermute | solution.py:832
  285.8 41.6 %collective-permute-start.27 = (bf16[2,320,768]{2,1,0:T(8,128)(2,1)S(1)}, bf16[2,320,768]{2,1,0:T(8,128)(2,1)S(1)}, u32[]{:S(2)}, u32[]{:S(2)}) collective-permute-start(bf16[2,320,768]{2,1,0:T(8,128)(2,1)S(1)} %get-tuple-element.149), channel_id=1, source_target_pairs={{3,2},{2,1},{1,0},{7,6},{6,5},{5,4},{11,10},{10,9},{9,8},{15,14},{... | collective-permute-start | bytes 2949128 | tf_op jit(solution)/shard_map/ppermute | solution.py:833
  304.6 26.1 %collective-permute-start.30 = (bf16[2,320,768]{2,1,0:T(8,128)(2,1)S(1)}, bf16[2,320,768]{2,1,0:T(8,128)(2,1)S(1)}, u32[]{:S(2)}, u32[]{:S(2)}) collective-permute-start(bf16[2,320,768]{2,1,0:T(8,128)(2,1)S(1)} %get-tuple-element.135.refs_0_), channel_id=1, source_target_pairs={{0,1},{1,2},{2,3},{4,5},{5,6},{6,7},{8,9},{9,10},{10,11},{12,13},{... | collective-permute-start | bytes 2949128 | tf_op jit(solution)/shard_map/ppermute | solution.py:832
  306.1 39.7 %collective-permute-start.31 = (bf16[2,320,768]{2,1,0:T(8,128)(2,1)S(1)}, bf16[2,320,768]{2,1,0:T(8,128)(2,1)S(1)}, u32[]{:S(2)}, u32[]{:S(2)}) collective-permute-start(bf16[2,320,768]{2,1,0:T(8,128)(2,1)S(1)} %get-tuple-element.136.refs_1_), channel_id=1, source_target_pairs={{3,2},{2,1},{1,0},{7,6},{6,5},{5,4},{11,10},{10,9},{9,8},{15,14},{... | collective-permute-start | bytes 2949128 | tf_op jit(solution)/shard_map/ppermute | solution.py:833
  320.1 42.3 %collective-permute-start.18 = (bf16[2,320,768]{2,1,0:T(8,128)(2,1)S(1)}, bf16[2,320,768]{2,1,0:T(8,128)(2,1)}, u32[]{:S(2)}, u32[]{:S(2)}) collective-permute-start(bf16[2,320,768]{2,1,0:T(8,128)(2,1)S(1)} %get-tuple-element.137.downsum_ref), channel_id=1, source_target_pairs={{0,1},{4,5},{8,9},{12,13},{16,17},{20,21},{24,25},{28,29}} | collective-permute-start | bytes 2949128 | tf_op jit(solution)/shard_map/ppermute | solution.py:832
  325.7 38.3 %collective-permute-start.19 = (bf16[2,320,768]{2,1,0:T(8,128)(2,1)S(1)}, bf16[2,320,768]{2,1,0:T(8,128)(2,1)}, u32[]{:S(2)}, u32[]{:S(2)}) collective-permute-start(bf16[2,320,768]{2,1,0:T(8,128)(2,1)S(1)} %get-tuple-element.138.upsum_ref), channel_id=1, source_target_pairs={{3,2},{7,6},{11,10},{15,14},{19,18},{23,22},{27,26},{31,30}} | collective-permute-start | bytes 2949128 | tf_op jit(solution)/shard_map/ppermute | solution.py:833
  329.4 42.5 %collective-permute-start.28 = (bf16[2,320,768]{2,1,0:T(8,128)(2,1)}, bf16[2,320,768]{2,1,0:T(8,128)(2,1)S(1)}, u32[]{:S(2)}, u32[]{:S(2)}) collective-permute-start(bf16[2,320,768]{2,1,0:T(8,128)(2,1)} %get-tuple-element.151.refs_0_), channel_id=1, source_target_pairs={{0,1},{1,2},{2,3},{4,5},{5,6},{6,7},{8,9},{9,10},{10,11},{12,13},{... | collective-permute-start | bytes 2949128 | tf_op jit(solution)/shard_map/ppermute | solution.py:832
  330.7 42.8 %collective-permute-start.29 = (bf16[2,320,768]{2,1,0:T(8,128)(2,1)}, bf16[2,320,768]{2,1,0:T(8,128)(2,1)S(1)}, u32[]{:S(2)}, u32[]{:S(2)}) collective-permute-start(bf16[2,320,768]{2,1,0:T(8,128)(2,1)} %get-tuple-element.152.refs_1_), channel_id=1, source_target_pairs={{3,2},{2,1},{1,0},{7,6},{6,5},{5,4},{11,10},{10,9},{9,8},{15,14},{... | collective-permute-start | bytes 2949128 | tf_op jit(solution)/shard_map/ppermute | solution.py:833
  360.0 35.6 %collective-permute-start.32 = (bf16[2,320,768]{2,1,0:T(8,128)(2,1)}, bf16[2,320,768]{2,1,0:T(8,128)(2,1)}, u32[]{:S(2)}, u32[]{:S(2)}) collective-permute-start(bf16[2,320,768]{2,1,0:T(8,128)(2,1)} %get-tuple-element.159.downsum_ref), channel_id=1, source_target_pairs={{0,1},{4,5},{8,9},{12,13},{16,17},{20,21},{24,25},{28,29}} | collective-permute-start | bytes 2949128 | tf_op jit(solution)/shard_map/ppermute | solution.py:832
  362.4 33.2 %collective-permute-start.33 = (bf16[2,320,768]{2,1,0:T(8,128)(2,1)}, bf16[2,320,768]{2,1,0:T(8,128)(2,1)}, u32[]{:S(2)}, u32[]{:S(2)}) collective-permute-start(bf16[2,320,768]{2,1,0:T(8,128)(2,1)} %get-tuple-element.160.upsum_ref), channel_id=1, source_target_pairs={{3,2},{7,6},{11,10},{15,14},{19,18},{23,22},{27,26},{31,30}} | collective-permute-start | bytes 2949128 | tf_op jit(solution)/shard_map/ppermute | solution.py:833
  368.0 46.0 %collective-permute-start.20 = (bf16[2,320,768]{2,1,0:T(8,128)(2,1)}, bf16[2,320,768]{2,1,0:T(8,128)(2,1)}, u32[]{:S(2)}, u32[]{:S(2)}) collective-permute-start(bf16[2,320,768]{2,1,0:T(8,128)(2,1)} %get-tuple-element.140.refs_0_), channel_id=1, source_target_pairs={{0,1},{1,2},{4,5},{5,6},{8,9},{9,10},{12,13},{13,14},{16,17},{17,1... | collective-permute-start | bytes 2949128 | tf_op jit(solution)/shard_map/ppermute | solution.py:832
  371.9 42.1 %collective-permute-start.21 = (bf16[2,320,768]{2,1,0:T(8,128)(2,1)}, bf16[2,320,768]{2,1,0:T(8,128)(2,1)}, u32[]{:S(2)}, u32[]{:S(2)}) collective-permute-start(bf16[2,320,768]{2,1,0:T(8,128)(2,1)} %get-tuple-element.141), channel_id=1, source_target_pairs={{3,2},{2,1},{7,6},{6,5},{11,10},{10,9},{15,14},{14,13},{19,18},{18... | collective-permute-start | bytes 2949128 | tf_op jit(solution)/shard_map/ppermute | solution.py:833
  375.6 33.1 %all-to-all-start.4 = ((bf16[8,80,768]{2,1,0:T(8,128)(2,1)}), bf16[8,80,768]{2,1,0:T(8,128)(2,1)S(1)}, u32[]{:S(2)}, u32[]{:S(2)}) async-start(bf16[8,80,768]{2,1,0:T(8,128)(2,1)} %copy-done.46), calls=%async_computation.4 | async-start | bytes 1966080 | tf_op jit(solution)/shard_map/all_to_all | solution.py:962
  400.0 41.7 %collective-permute-start.34 = (bf16[2,320,768]{2,1,0:T(8,128)(2,1)}, bf16[2,320,768]{2,1,0:T(8,128)(2,1)}, u32[]{:S(2)}, u32[]{:S(2)}) collective-permute-start(bf16[2,320,768]{2,1,0:T(8,128)(2,1)} %get-tuple-element.171), channel_id=1, source_target_pairs={{0,1},{1,2},{4,5},{5,6},{8,9},{9,10},{12,13},{13,14},{16,17},{17,1... | collective-permute-start | bytes 2949128 | tf_op jit(solution)/shard_map/ppermute | solution.py:832
  404.9 36.8 %collective-permute-start.35 = (bf16[2,320,768]{2,1,0:T(8,128)(2,1)}, bf16[2,320,768]{2,1,0:T(8,128)(2,1)}, u32[]{:S(2)}, u32[]{:S(2)}) collective-permute-start(bf16[2,320,768]{2,1,0:T(8,128)(2,1)} %get-tuple-element.172), channel_id=1, source_target_pairs={{3,2},{2,1},{7,6},{6,5},{11,10},{10,9},{15,14},{14,13},{19,18},{18... | collective-permute-start | bytes 2949128 | tf_op jit(solution)/shard_map/ppermute | solution.py:833
  420.3 47.2 %collective-permute-start.36 = (bf16[2,320,768]{2,1,0:T(8,128)(2,1)}, bf16[2,320,768]{2,1,0:T(8,128)(2,1)}, u32[]{:S(2)}, u32[]{:S(2)}) collective-permute-start(bf16[2,320,768]{2,1,0:T(8,128)(2,1)} %get-tuple-element.153.refs_0_), channel_id=1, source_target_pairs={{0,1},{1,2},{2,3},{4,5},{5,6},{6,7},{8,9},{9,10},{10,11},{12,13},{... | collective-permute-start | bytes 2949128 | tf_op jit(solution)/shard_map/ppermute | solution.py:832
  425.7 41.9 %collective-permute-start.37 = (bf16[2,320,768]{2,1,0:T(8,128)(2,1)}, bf16[2,320,768]{2,1,0:T(8,128)(2,1)}, u32[]{:S(2)}, u32[]{:S(2)}) collective-permute-start(bf16[2,320,768]{2,1,0:T(8,128)(2,1)} %get-tuple-element.178), channel_id=1, source_target_pairs={{3,2},{2,1},{1,0},{7,6},{6,5},{5,4},{11,10},{10,9},{9,8},{15,14},{... | collective-permute-start | bytes 2949128 | tf_op jit(solution)/shard_map/ppermute | solution.py:833
  446.5 46.1 %collective-permute-start.38 = (bf16[2,320,768]{2,1,0:T(8,128)(2,1)}, bf16[2,320,768]{2,1,0:T(8,128)(2,1)}, u32[]{:S(2)}, u32[]{:S(2)}) collective-permute-start(bf16[2,320,768]{2,1,0:T(8,128)(2,1)} %get-tuple-element.174.refs_0_), channel_id=1, source_target_pairs={{0,1},{1,2},{2,3},{4,5},{5,6},{6,7},{8,9},{9,10},{10,11},{12,13},{... | collective-permute-start | bytes 2949128 | tf_op jit(solution)/shard_map/ppermute | solution.py:832
  451.3 41.3 %collective-permute-start.39 = (bf16[2,320,768]{2,1,0:T(8,128)(2,1)}, bf16[2,320,768]{2,1,0:T(8,128)(2,1)}, u32[]{:S(2)}, u32[]{:S(2)}) collective-permute-start(bf16[2,320,768]{2,1,0:T(8,128)(2,1)} %get-tuple-element.184), channel_id=1, source_target_pairs={{3,2},{2,1},{1,0},{7,6},{6,5},{5,4},{11,10},{10,9},{9,8},{15,14},{... | collective-permute-start | bytes 2949128 | tf_op jit(solution)/shard_map/ppermute | solution.py:833
  473.0 19.6 %all-to-all-start.6 = ((bf16[8,80,768]{2,1,0:T(8,128)(2,1)}), bf16[8,80,768]{2,1,0:T(8,128)(2,1)S(1)}, u32[]{:S(2)}, u32[]{:S(2)}) async-start(bf16[8,80,768]{2,1,0:T(8,128)(2,1)} %shard_map.304.refs_0_), calls=%async_computation.6 | async-start | bytes 1966080 | tf_op jit(solution)/shard_map/all_to_all | solution.py:962
  498.2 20.8 %all-to-all-start.7 = ((bf16[8,80,768]{2,1,0:T(8,128)(2,1)}), bf16[8,80,768]{2,1,0:T(8,128)(2,1)S(1)}, u32[]{:S(2)}, u32[]{:S(2)}) async-start(bf16[8,80,768]{2,1,0:T(8,128)(2,1)} %shard_map.306.refs_0_), calls=%async_computation.7 | async-start | bytes 1966080 | tf_op jit(solution)/shard_map/all_to_all | solution.py:962
  554.7 20.8 %collective-permute-start.55 = (bf16[512,384]{1,0:T(8,128)(2,1)}, bf16[512,384]{1,0:T(8,128)(2,1)}, u32[]{:S(2)}, u32[]{:S(2)}) collective-permute-start(bf16[512,384]{1,0:T(8,128)(2,1)} %get-tuple-element.250), channel_id=1, source_target_pairs={{0,8},{4,12},{8,0},{12,4},{16,24},{20,28},{24,16},{28,20},{1,9},{5... | collective-permute-start | bytes 1179656 | tf_op jit(solution)/shard_map/ppermute | solution.py:865
  556.6 19.6 %collective-permute-start.56 = (bf16[512,384]{1,0:T(8,128)(2,1)}, bf16[512,384]{1,0:T(8,128)(2,1)}, u32[]{:S(2)}, u32[]{:S(2)}) collective-permute-start(bf16[512,384]{1,0:T(8,128)(2,1)} %get-tuple-element.252), channel_id=1, source_target_pairs={{0,16},{4,20},{8,24},{12,28},{16,0},{20,4},{24,8},{28,12},{1,17},{... | collective-permute-start | bytes 1179656 | tf_op jit(solution)/shard_map/ppermute | solution.py:865
  575.6 19.8 %collective-permute-start.41 = (bf16[1280,384]{1,0:T(8,128)(2,1)}, bf16[1280,384]{1,0:T(8,128)(2,1)}, u32[]{:S(2)}, u32[]{:S(2)}) collective-permute-start(bf16[1280,384]{1,0:T(8,128)(2,1)} %dynamic-slice_bitcast_fusion.1), channel_id=1, source_target_pairs={{0,4},{4,0},{8,12},{12,8},{16,20},{20,16},{24,28},{28,24},{1,5},{5... | collective-permute-start | bytes 2949128 | tf_op jit(solution)/shard_map/ppermute | solution.py:865
  604.6 22.3 %collective-permute-start.65 = (bf16[512,384]{1,0:T(8,128)(2,1)S(1)}, bf16[512,384]{1,0:T(8,128)(2,1)S(1)}, u32[]{:S(2)}, u32[]{:S(2)}) collective-permute-start(bf16[512,384]{1,0:T(8,128)(2,1)S(1)} %pad_maximum_fusion.2), channel_id=1, source_target_pairs={{0,16},{4,20},{8,24},{12,28},{16,0},{20,4},{24,8},{28,12},{1,17},{... | collective-permute-start | bytes 1179656 | tf_op jit(solution)/shard_map/ppermute | solution.py:865
  606.8 20.1 %collective-permute-start.66 = (bf16[512,384]{1,0:T(8,128)(2,1)S(1)}, bf16[512,384]{1,0:T(8,128)(2,1)S(1)}, u32[]{:S(2)}, u32[]{:S(2)}) collective-permute-start(bf16[512,384]{1,0:T(8,128)(2,1)S(1)} %pad_maximum_fusion.2), channel_id=1, source_target_pairs={{0,24},{4,28},{8,16},{12,20},{16,8},{20,12},{24,0},{28,4},{1,25},{... | collective-permute-start | bytes 1179656 | tf_op jit(solution)/shard_map/ppermute | solution.py:865
  (137 other events, 1399.5 us)

commit v4 on v3

--- a/solution.py
+++ b/solution.py
@@ -214,7 +214,7 @@
 
 def attn_kernel(batch, waits, *refs):
     refs = refs[waits:]
-    len_ref, tok_ref, gain_ref, wq_ref, wk_ref, wv_ref, vec_ref, qkv_ref, mixed_ref, lse_ref, band_ref, probs_ref, mixed_t_ref = refs
+    len_ref, tok_ref, gain_ref, wq_ref, wk_ref, wv_ref, vec_ref, qkv_ref, mixed_ref, lse_ref, bands_ref, probs_ref, mixed_t_ref = refs
     length, width = tok_ref.shape[2:]
     count = len_ref[batch]
     tokens = tok_ref[0, 0].astype(F32)
@@ -234,21 +234,21 @@
         values_t = qkv_ref[2, pair].T
         for side in range(2):
             head = 2 * pair + side
-            band_ref[...] = band_bias(vec_ref, head)
+            bands_ref[side] = band_bias(vec_ref, head)
             mine = (lane >= HEAD_DIM) if side else (lane < HEAD_DIM)
             for block in range(length // ROWS):
                 here = slice(ROWS * block, ROWS * (block + 1))
                 queries = qkv_ref[0, pair, here, :] * 0.125
                 queries = jnp.where(mine, queries, jnp.zeros_like(queries))
-                scores = dot_t(queries, keys) + band_ref[:, band_slice(block, length)] + mask
+                scores = dot_t(queries, keys) + bands_ref[side, :, band_slice(block, length)] + mask
                 highest = jnp.max(scores, axis=-1, keepdims=True)
                 powers = jnp.exp(scores - highest)
                 total = jnp.sum(powers, axis=-1, keepdims=True)
-                probs_ref[here, :] = (powers * (1.0 / total)).astype(BF16)
+                probs_ref[side, here, :] = (powers * (1.0 / total)).astype(BF16)
                 column = iota((ROWS, lse_ref.shape[1]), 1)
                 lse_ref[here, :] = jnp.where(column == head, highest + jnp.log(total), lse_ref[here, :])
             rows = slice(HEAD_DIM * side, HEAD_DIM * (side + 1))
-            mixed_t_ref[rows, :] = dot_t(values_t[rows, :], probs_ref[...])
+            mixed_t_ref[rows, :] = dot_t(values_t[rows, :], probs_ref[side])
         mixed_ref[pair] = mixed_t_ref[...].T.astype(BF16)
         return carry
 
@@ -268,8 +268,8 @@
             jax.ShapeDtypeStruct((length, 128), F32),
         ],
         scratch_shapes=[
-            pltpu.VMEM((ROWS, vector.shape[-1]), F32),
-            pltpu.VMEM((length, length), BF16),
+            pltpu.VMEM((2, ROWS, vector.shape[-1]), F32),
+            pltpu.VMEM((2, length, length), BF16),
             pltpu.VMEM((PAIR, length), F32),
         ],
         compiler_params=params(48),
@@ -286,7 +286,7 @@
     res_ref[...] = residual
     inverse = lax.rsqrt(jnp.mean(residual * residual, axis=-1, keepdims=True) + epsilon)
     routed = (residual * inverse * gffn_ref[...]).astype(BF16)
-    logits = dot(routed, wr_ref[...])
+    logits = dot_t(routed, wr_ref[...])
     powers = jnp.exp(logits - jnp.max(logits, axis=-1, keepdims=True))
     probs = powers / jnp.sum(powers, axis=-1, keepdims=True)
     probs_ref[...] = probs
@@ -325,7 +325,7 @@
 
 def route(batch, after, tokens, cot, mixed, wo, gain_ffn, w_router, srow, rcol, groups, per, gated):
     length, width = tokens.shape[2:]
-    experts = w_router.shape[1]
+    experts = w_router.shape[0]
     message = padded(per) if gated else padded(per) + 16
     return pl.pallas_call(
         functools.partial(route_kernel, per, gated, len(after)),
@@ -477,7 +477,7 @@
     past_ref = refs.pop(0) if batch else None
     layer_ref, resgrad_ref, mgrad_ref, shared_ref = refs
     length, width = cot_ref.shape[2:]
-    experts = wr_ref.shape[1]
+    experts = wr_ref.shape[0]
     groups, message, _ = low_ref.shape
     valid = iota((length, 1), 0) < len_ref[batch]
     places = iota((length, groups * message), 1)
@@ -513,7 +513,7 @@
             shared_ref[here, :] = rows.astype(shared_ref.dtype)
 
     share(width, t_dot(logit_grad, routed))
-    routed_grad = dot_t(logit_grad, wr_ref[...]) + input_grad
+    routed_grad = dot(logit_grad, wr_ref[...]) + input_grad
     gain_part = jnp.sum(routed_grad * scaled, axis=0, keepdims=True)
     left = shared_ref.shape[0] // 2 - width - experts
     share(width + experts, jnp.where(iota((left, width), 0) == 0, gain_part, 0.0))
@@ -563,8 +563,11 @@
     else:
         early_ref = refs.pop(0) if batch else None
         shared_ref, diag_out_ref, part_out_ref, *refs = refs
-    band_ref, probs_ref, sgrad_ref, spread_ref, low_ref, qt_ref, kt_ref, vt_ref, diag_ref, *buffers, sems = refs
-    fetched = [tok_ref.at[batch, 0], wq_ref, wk_ref, wv_ref]
+    bands_ref, probs_ref, sgrad_ref, spread_ref, low_ref, qt_ref, kt_ref, vt_ref, diag_ref, stage_ref, rest_ref, *buffers = refs
+    *buffers, sems, out_sems = buffers
+    half = wq_ref.shape[0] // 2
+    columns = pl.ds(which * half, half)
+    fetched = [tok_ref.at[batch, 0]] + [ref.at[:, columns] for ref in (wq_ref, wk_ref, wv_ref)]
     if past_ref is not None:
         fetched.append(past_ref)
     if which:
@@ -574,6 +577,8 @@
     copies = [pltpu.make_async_copy(ref, buffer, sems.at[k]) for k, (ref, buffer) in enumerate(zip(fetched, buffers))]
     for copy in copies:
         copy.start()
+    going = []
+    offset = 0 if which or shared_ref.dtype == F32 else early_ref.shape[0]
     tok_ref, wq_ref, wk_ref, wv_ref, *buffers = buffers
     if past_ref is not None:
         past_ref = buffers.pop(0)
@@ -589,40 +594,40 @@
 
     def one_pair(step, carry):
         pair = first_pair + step
-        keys = qkv_ref[1, pair]
-        values = qkv_ref[2, pair]
-        queries_t = qkv_ref[0, pair].T
-        keys_t = qkv_ref[1, pair].T
-        grads_t = mgrad_ref[pair].T
+        keys = qkv_ref[1, step]
+        values = qkv_ref[2, step]
+        queries_t = qkv_ref[0, step].T
+        keys_t = qkv_ref[1, step].T
+        grads_t = mgrad_ref[step].T
         for side in range(2):
             head = 2 * pair + side
-            band_ref[...] = band_bias(vec_ref, head)
-            spread_ref[...] = jnp.zeros_like(spread_ref)
+            bands_ref[side] = band_bias(vec_ref, head)
+            spread_ref[side] = jnp.zeros(spread_ref.shape[1:], F32)
             mine = (lane >= HEAD_DIM) if side else (lane < HEAD_DIM)
             for block in range(length // ROWS):
                 here = slice(ROWS * block, ROWS * (block + 1))
                 window = band_slice(block, length)
-                queries = qkv_ref[0, pair, here, :] * 0.125
+                queries = qkv_ref[0, step, here, :] * 0.125
                 queries = jnp.where(mine, queries, jnp.zeros_like(queries))
-                grads = mgrad_ref[pair, here, :]
+                grads = mgrad_ref[step, here, :]
                 grads = jnp.where(mine, grads, jnp.zeros_like(grads))
                 column = iota((ROWS, lse_ref.shape[1]), 1)
                 log_total = jnp.sum(jnp.where(column == head, lse_ref[here, :], 0.0), axis=-1, keepdims=True)
-                scores = dot_t(queries, keys) + band_ref[:, window] + mask
+                scores = dot_t(queries, keys) + bands_ref[side, :, window] + mask
                 probs = jnp.exp(scores - log_total)
-                probs_ref[here, :] = probs.astype(BF16)
+                probs_ref[side, here, :] = probs.astype(BF16)
                 weighted = probs * dot_t(grads, values)
                 score_grad = weighted - probs * jnp.sum(weighted, axis=-1, keepdims=True)
-                spread_ref[:, window] += score_grad
-                sgrad_ref[here, :] = score_grad.astype(BF16)
+                spread_ref[side, :, window] += score_grad
+                sgrad_ref[side, here, :] = score_grad.astype(BF16)
             rows = slice(HEAD_DIM * side, HEAD_DIM * (side + 1))
-            qt_ref[rows, :] = dot_t(keys_t[rows, :], sgrad_ref[...]) * 0.125
-            kt_ref[rows, :] = dot(queries_t[rows, :], sgrad_ref[...]) * 0.125
-            vt_ref[rows, :] = dot(grads_t[rows, :], probs_ref[...])
-            size = spread_ref.shape[1]
-            eight = spread_ref[0:8, :]
+            qt_ref[rows, :] = dot_t(keys_t[rows, :], sgrad_ref[side]) * 0.125
+            kt_ref[rows, :] = dot(queries_t[rows, :], sgrad_ref[side]) * 0.125
+            vt_ref[rows, :] = dot(grads_t[rows, :], probs_ref[side])
+            size = spread_ref.shape[2]
+            eight = spread_ref[side, 0:8, :]
             for move in range(8, ROWS, 8):
-                eight = eight + pltpu.roll(spread_ref[move : move + 8, :], size - move, 1)
+                eight = eight + pltpu.roll(spread_ref[side, move : move + 8, :], size - move, 1)
             diagonal = eight[0:1, :]
             for move in range(1, 8):
                 diagonal = diagonal + pltpu.roll(eight[move : move + 1, :], size - move, 1)
@@ -635,12 +640,18 @@
     lax.fori_loop(0, PAIRS // 2, one_pair, 0)
     for copy in copies:
         copy.wait()
-    offset = 0 if which or shared_ref.dtype == F32 else early_ref.shape[0]
-
-    def share(first, rows):
-        if past_ref is not None:
-            rows = rows + past_ref[first : first + rows.shape[0], :]
-        shared_ref[offset + first : offset + first + rows.shape[0], :] = rows.astype(shared_ref.dtype)
+
+    def send(source, first, place):
+        target = shared_ref.at[pl.ds(offset + first, source.shape[0])]
+        going.append(pltpu.make_async_copy(source, target, out_sems.at[place]))
+        going[-1].start()
+
+    if offset:
+        going.append(pltpu.make_async_copy(early_ref, shared_ref.at[pl.ds(0, offset)], out_sems.at[0]))
+        going[0].start()
+
+    def past(first, count):
+        return 0.0 if past_ref is None else past_ref[first : first + count, :]
 
     tokens = tok_ref[...].astype(F32)
     inverse = lax.rsqrt(jnp.mean(tokens * tokens, axis=-1, keepdims=True) + epsilon)
@@ -648,41 +659,48 @@
     scaled = tokens * inverse
     normed_t = (scaled * gain).astype(BF16).T
     normed_grad = part_ref[...] if which else jnp.zeros((length, width), F32)
-    half = width // 2
     for matrix, w_ref in enumerate((wq_ref, wk_ref, wv_ref)):
         low = jnp.concatenate([low_ref[matrix, p] for p in range(PAIRS // 2)], axis=1)
-        share(matrix * width, dot(normed_t, low))
-        normed_grad = normed_grad + dot_t(low, w_ref[:, which * half : (which + 1) * half])
-    if not which:
-        if offset:
-            shared_ref[:offset, :] = early_ref[...]
-            done = offset + 3 * width
-            if done < shared_ref.shape[0]:
-                shared_ref[done:, :] = jnp.zeros((shared_ref.shape[0] - done, half), shared_ref.dtype)
+        stage_ref[matrix] = (dot(normed_t, low) + past(matrix * width, width)).astype(stage_ref.dtype)
+        send(stage_ref.at[matrix], matrix * width, 1 + matrix)
+        normed_grad = normed_grad + dot_t(low, w_ref[...])
+    left = rest_ref.shape[0]
+    if which:
+        gain_part = jnp.sum(normed_grad * scaled, axis=0, keepdims=True)
+        bias_part = lax.dot_general(
+            diag_ref[...],
+            sel_ref[...],
+            (((1,), (0,)), ((), ())),
+            precision=lax.Precision.HIGHEST,
+            preferred_element_type=F32,
+        )
+        row = iota((8, half), 0)
+        gains = jnp.where(row == 0, gain_part[:, :half], jnp.where(row == 1, gain_part[:, half:], 0.0))
+        wide = jnp.concatenate([bias_part, jnp.zeros((16, half - bias_part.shape[1]), F32)], axis=1)
+        last = [gains, wide] + ([jnp.zeros((left - 24, half), F32)] if left > 24 else [])
+        rest_ref[...] = (jnp.concatenate(last, axis=0) + past(3 * width, left)).astype(rest_ref.dtype)
+        send(rest_ref, 3 * width, 4)
+        upstream = normed_grad * gain
+        middle = jnp.mean(upstream * scaled, axis=-1, keepdims=True)
+        tgrad_ref[...] = (resgrad_ref[...] + inverse * (upstream - scaled * middle)).astype(BF16)
+    else:
+        if offset and offset + 3 * width < shared_ref.shape[0]:
+            rest_ref[...] = jnp.zeros_like(rest_ref)
+            send(rest_ref, 3 * width, 4)
         diag_out_ref[...] = diag_ref[...]
         part_out_ref[...] = normed_grad
-        return
-    gain_part = jnp.sum(normed_grad * scaled, axis=0, keepdims=True)
-    bias_part = lax.dot_general(
-        diag_ref[...], sel_ref[...], (((1,), (0,)), ((), ())), precision=lax.Precision.HIGHEST, preferred_element_type=F32
-    )
-    row = iota((8, half), 0)
-    gains = jnp.where(row == 0, gain_part[:, :half], jnp.where(row == 1, gain_part[:, half:], 0.0))
-    wide = jnp.concatenate([bias_part, jnp.zeros((16, half - bias_part.shape[1]), F32)], axis=1)
-    left = shared_ref.shape[0] - 3 * width - 24
-    last = [gains, wide] + ([jnp.zeros((left, half), F32)] if left else [])
-    share(3 * width, jnp.concatenate(last, axis=0))
-    upstream = normed_grad * gain
-    middle = jnp.mean(upstream * scaled, axis=-1, keepdims=True)
-    tgrad_ref[...] = (resgrad_ref[...] + inverse * (upstream - scaled * middle)).astype(BF16)
+    for copy in going:
+        copy.wait()
 
 
 def attention_backward(batch, which, last, after, counts, qkv, lse, vector, selector, mixed_grad, tokens, gain, wq, wk, wv, past, more, rows):
     length, width = tokens.shape[2:]
     half = width // 2
     size = vector.shape[-1]
-    late = (wq, wk, wv, *past, *(more[1:] if which else more))
-    buffers = [((length, width), BF16)] + [(array.shape, array.dtype) for array in late]
+    late = (*past, *(more[1:] if which else more))
+    buffers = [((length, width), BF16)] + [((width, half), BF16)] * 3 + [(array.shape, array.dtype) for array in late]
+    sent = 0 if which or not last else more[0].shape[0]
+    rest = max(rows - sent - 3 * width, 16)
     shared = jax.ShapeDtypeStruct((rows, half), BF16 if last else F32)
     if which:
         outs = [shared, jax.ShapeDtypeStruct((length, width), BF16)]
@@ -692,25 +710,29 @@
         functools.partial(attn_back_kernel, batch, which, len(after)),
         grid=(1,),
         in_specs=[ANYWHERE] * len(after)
-        + [SCALARS]
-        + [WHOLE] * 5
+        + [SCALARS, pl.BlockSpec((3, PAIRS // 2, length, PAIR), lambda _: (0, which, 0, 0))]
+        + [WHOLE] * 3
+        + [pl.BlockSpec((PAIRS // 2, length, PAIR), lambda _: (which, 0, 0))]
         + [ANYWHERE, WHOLE]
         + [ANYWHERE] * (3 + len(past))
         + [WHOLE if which and k == 0 else ANYWHERE for k in range(len(more))],
-        out_specs=[WHOLE] * len(outs),
+        out_specs=[ANYWHERE] + [WHOLE] * (len(outs) - 1),
         out_shape=outs,
         scratch_shapes=[
-            pltpu.VMEM((ROWS, size), F32),
-            pltpu.VMEM((length, length), BF16),
-            pltpu.VMEM((length, length), BF16),
-            pltpu.VMEM((ROWS, size), F32),
+            pltpu.VMEM((2, ROWS, size), F32),
+            pltpu.VMEM((2, length, length), BF16),
+            pltpu.VMEM((2, length, length), BF16),
+            pltpu.VMEM((2, ROWS, size), F32),
             pltpu.VMEM((3, PAIRS // 2, length, PAIR), BF16),
             pltpu.VMEM((PAIR, length), F32),
             pltpu.VMEM((PAIR, length), F32),
             pltpu.VMEM((PAIR, length), F32),
             pltpu.VMEM((16, size), F32),
+            pltpu.VMEM((3, width, half), shared.dtype),
+            pltpu.VMEM((rest, half), shared.dtype),
             *(pltpu.VMEM(shape, kind) for shape, kind in buffers),
             pltpu.SemaphoreType.DMA((len(buffers),)),
+            pltpu.SemaphoreType.DMA((5,)),
         ],
         compiler_params=params(56),
         cost_estimate=cost(),
@@ -727,13 +749,13 @@
         q_ref, k_ref, v_ref, gain_ref, bias_ref = refs[3:]
         offset = 0
         gain_ref[...] = jnp.concatenate([rows[3 * width : 3 * width + 1], rows[3 * width + 1 : 3 * width + 2]], axis=1)
-        bias_ref[...] = rows[3 * width + 8 : 3 * width + 8 + HEADS, :BUCKETS].T
+        bias_ref[...] = rows[3 * width + 8 : 3 * width + 8 + HEADS, :BUCKETS]
     else:
         q_ref, k_ref, v_ref, output_ref, router_ref, gain_ref = refs
         offset = 2 * early
         output_ref[...] = jnp.concatenate([rows[:width], rows[early : early + width]], axis=1)
         last = early - 16
-        router_ref[...] = jnp.concatenate([rows[width:last], rows[early + width : early + last]], axis=1).T
+        router_ref[...] = jnp.concatenate([rows[width:last], rows[early + width : early + last]], axis=1)
         gain_ref[...] = jnp.concatenate([rows[last : last + 1], rows[early + last : early + last + 1]], axis=1)
     for k, ref in enumerate((q_ref, k_ref, v_ref)):
         ref[...] = rows[offset + k * width : offset + (k + 1) * width]
@@ -746,9 +768,9 @@
     line = jax.ShapeDtypeStruct((1, width), F32)
     columns = pl.BlockSpec((width, half), lambda _: (0, 0 if early else 1))
     if early:
-        more = [matrix, jax.ShapeDtypeStruct((width, experts), F32), line]
+        more = [matrix, jax.ShapeDtypeStruct((experts, width), F32), line]
     else:
-        more = [line, jax.ShapeDtypeStruct((BUCKETS, HEADS), F32)]
+        more = [line, jax.ShapeDtypeStruct((HEADS, BUCKETS), F32)]
     return pl.pallas_call(
         functools.partial(unpack_kernel, early, experts),
         grid=(1,),
@@ -955,6 +977,7 @@
     )[:, None, :]
     gain_a = gain_attn[None, :]
     gain_f = gain_ffn[None, :]
+    router_rows = w_router.T
     counts = lengths[:, 0]
     plane = lax.axis_index("hidden")[None]
 
@@ -972,7 +995,7 @@
 
     def routing(b, *after):
         return route(
-            b, after, tokens, cotangent, forward[b][1], w_output, gain_f, w_router, srow, rcol, groups, per, b > 0
+            b, after, tokens, cotangent, forward[b][1], w_output, gain_f, router_rows, srow, rcol, groups, per, b > 0
         )
 
     srow, scol, cot_slots = prep(counts, routes.reshape(batches, length), cotangent, groups, per, capacity)
@@ -999,7 +1022,7 @@
             *routed[b][:2],
             cotangent,
             gain_f,
-            w_router,
+            router_rows,
             w_output,
             forward[b][1],
             early_part,
@@ -1034,19 +1057,18 @@
     def grads_half(h, after, past):
         return expert_grads(h, after, past, local, *([k[h][part] for k in kept] for part in (2, 3, 0, 1)))
 
-    grads = regroup(move, [to_groups(cot_slots)], (local * rows, width))
+    forward = [attend(0, cot_slots)]
+    routed = [routing(0)]
+    grads = regroup(move, [to_groups(cot_slots)], (local * rows, width), (routed[0][2],))
     grad_chain = Chain(planes, grads)
     grad_chain.send()
-    forward = [attend(0, grads)]
-    routed = [routing(0, grad_chain.up, grad_chain.down)]
-    grad_chain.send()
-    inputs = regroup_gated(move_gated, to_groups(routed[0][2]), capacity)
-    grad_chain.gate(inputs)
-    grad_chain.run()
+    inputs = regroup_gated(move_gated, to_groups(routed[0][2]), capacity, (grads,))
     input_chain = Chain(planes, inputs)
     input_chain.send()
-    forward.append(attend(1, inputs))
-    routed.append(routing(1))
+    forward.append(attend(1, inputs, grad_chain.up, grad_chain.down))
+    grad_chain.send()
+    routed.append(routing(1, grad_chain.up, grad_chain.down))
+    grad_chain.run()
     input_chain.gate(forward[1][1])
     input_chain.send()
     held = (input_chain.up, input_chain.down, grad_chain.up, grad_chain.down)
@@ -1126,12 +1148,15 @@
     side = (lax.axis_index("expert") % 2)[None]
     first_half = share_half(first_part)
     second_part, token_grad = back_half(batches - 1, 1, (first_half,), mixed_grad, (*more, res_grad))
-    first_sums = sum_everywhere(first_half)
-    second_sums = sum_everywhere(share_half(second_part))
+    mine, other = sum_everywhere(first_half)
+    mine_second, other_second = sum_everywhere(share_half(second_part))
+    early_done = unpack(early_rows, experts, side, mine, other, ())
     layer_rows.append(layer)
     token_grads.append(token_grad)
-    *attended, output_grad, router_grad, gain_f_grad = unpack(early_rows, experts, side, *first_sums, ())
-    query_grad, key_grad, value_grad, gain_a_grad, bias_grad = unpack(0, experts, side, *second_sums, attended)
+    *attended, output_grad, router_grad, gain_f_grad = early_done
+    query_grad, key_grad, value_grad, gain_a_grad, bias_grad = unpack(
+        0, experts, side, mine_second, other_second, attended
+    )
     return (
         jnp.stack(layer_rows)[:, None],
         jnp.stack(token_grads)[:, None],
@@ -1140,9 +1165,9 @@
         key_grad,
         value_grad,
         output_grad,
-        bias_grad,
+        bias_grad.T,
         gain_f_grad[0],
-        router_grad,
+        router_grad.T,
         totals[1],
         totals[0],
     )

time: 679 us -> 662 us (0.975)
  blocking collectives: 39.1 us -> 0 us
  starting transfers between devices: 147 us -> 158 us
  waiting for transfers between devices: 165 us -> 173 us
    all_to_all x2 -> x0, blocking collectives: 39.1 us -> none  [to_groups(): lax.all_to_all(values, 'expert', split_axis=0, concat_axis=0, tiled=True)]
    all_to_all x6 -> x8, starting transfers between devices: 24.6 us -> 34 us  [to_groups(): lax.all_to_all(values, 'expert', split_axis=0, concat_axis=0, tiled=True)]
    all_to_all x6 -> x8, waiting for transfers between devices: 7.49 us -> 14.8 us  [to_groups(): lax.all_to_all(values, 'expert', split_axis=0, concat_axis=0, tiled=True)]
    unnamed x225 -> x210, local copies, waits for them, and re-layouts: 46.4 us -> 46.5 us
  transfers between devices with their start and end apart: 74 -> 76, of which waited for: 35 -> 33; matrix products, arithmetic and copies ran while one was open for 2% -> 2% of each run, Pallas kernels for 31% -> 34%
where the time goes in v4:
time: 662 us; the launch traced here: 651 us
  Pallas kernels  252 us (38%)
  waiting for transfers between devices  173 us (26%)
  starting transfers between devices  158 us (24%)
  local copies, waits for them, and re-layouts  52.6 us (8%)
  other arithmetic  12.5 us (2%)
    ppermute x20, waiting for transfers between devices, send(): self.down = lax.ppermute(self.down, 'hidden', downward(planes, first, last))  110 us
    ppermute x20, starting transfers between devices, send(): self.up = lax.ppermute(self.up, 'hidden', upward(planes, first, last))  58.4 us
    pallas_call x4, Pallas kernels, attention_backward(): pl.pallas_call(functools.partial(attn_back_kernel, batch, which, len(afte...  58 us
    pallas_call x4, Pallas kernels, experts_half(): pl.pallas_call(functools.partial(expert_kernel, planes, gated, first, len...  51.6 us
    unnamed x210, local copies, waits for them, and re-layouts  46.5 us
    ppermute x28, starting transfers between devices, swap(): lax.ppermute(values, axis, [(k, k ^ distance) for k in range(lax.axis_siz...  37.4 us
    ppermute x28, waiting for transfers between devices, swap(): lax.ppermute(values, axis, [(k, k ^ distance) for k in range(lax.axis_siz...  36 us
    all_to_all x8, starting transfers between devices, to_groups(): lax.all_to_all(values, 'expert', split_axis=0, concat_axis=0, tiled=True)  34 us
  transfers between devices with their start and end apart: 76, of which 33 were waited for; matrix products, arithmetic and copies ran while one was open for 2% of the time, Pallas kernels for 34%

profile of v4, /device:TPU:0, one launch (start us, length us, event | category | flops | bytes accessed | tf_op | source)
XLA Modules:
  0.0 651.3 jit_solution(3001426833800181958)
XLA Ops:
  8.7 5.2 all-to-all-start
  17.6 14.0 %shard_map.275 = (bf16[3,6,512,128]{3,2,1,0:T(8,128)(2,1)}, bf16[6,512,128]{2,1,0:T(8,128)(2,1)S(1)}, f32[512,128]{1,0:T(8,128)S(1)}) custom-call(bf16[8,80,768]{2,1,0:T(8,128)(2,1)S(1)} %copy-done.40, s32[2]{0:T(128)S(1)} %bitcast.84, bf16[2,1,512,768]{3,2,1,0:T(8,128)(2,1)} %refs_7_.7, f32[1,768]{1,0:T(1,128)S(1)} %broadcast_in_dim.26.refs_3_.refs_5_.refs_8_.refs_7_, ...), custom_call_target="tpu_custom_call" | custom-call | flops 1 | bytes 1 | tf_op jit(solution)/shard_map/pallas_call | solution.py:260
  32.3 4.9 shard_map.276
  40.1 4.4 all-to-all-start.1
  46.7 5.1 collective-permute-start.2
  53.1 8.3 %all-to-all-done.1.refs_2_ = bf16[8,96,768]{2,1,0:T(8,128)(2,1)} async-done(((bf16[8,96,768]{2,1,0:T(8,128)(2,1)}), bf16[8,96,768]{2,1,0:T(8,128)(2,1)}, u32[]{:S(2)}, u32[]{:S(2)}) %all-to-all-start.1) | async-done | bytes 1179680 | tf_op jit(solution)/shard_map/all_to_all | solution.py:985
  65.3 5.0 collective-permute-start
  79.9 14.6 %shard_map.279 = (bf16[3,6,512,128]{3,2,1,0:T(8,128)(2,1)}, bf16[6,512,128]{2,1,0:T(8,128)(2,1)S(1)}, f32[512,128]{1,0:T(8,128)S(1)}) custom-call(bf16[656,768]{1,0:T(8,128)(2,1)S(1)} %shard_map.278.refs_0_.refs_3_.refs_17_, bf16[640,768]{1,0:T(8,128)(2,1)} %collective-permute-done.2.refs_1_.refs_14_, ...), custom_call_target="tpu_custom_call" | custom-call | flops 1 | bytes 1 | tf_op jit(solution)/shard_map/pallas_call | solution.py:260
  95.4 4.4 collective-permute-done.1.refs_1_
  104.5 16.5 %collective-permute-done.8.refs_1_.refs_12_ = bf16[640,768]{1,0:T(8,128)(2,1)} collective-permute-done((bf16[640,768]{1,0:T(8,128)(2,1)}, bf16[640,768]{1,0:T(8,128)(2,1)}, u32[]{:S(2)}, u32[]{:S(2)}) %collective-permute-start.8) | collective-permute-done | bytes 983072 | tf_op jit(solution)/shard_map/ppermute | solution.py:855
  123.5 5.3 shard_map.281
  131.4 4.2 all-to-all-start.2
  135.7 6.8 %collective-permute-done.5.refs_1_.refs_5_.refs_19_ = bf16[656,768]{1,0:T(8,128)(2,1)S(1)} collective-permute-done((bf16[656,768]{1,0:T(8,128)(2,1)}, bf16[656,768]{1,0:T(8,128)(2,1)S(1)}, u32[]{:S(2)}, u32[]{:S(2)}) %collective-permute-start.5) | collective-permute-done | bytes 1007648 | tf_op jit(solution)/shard_map/ppermute | solution.py:855
  145.5 4.9 all-to-all-done.2.refs_5_
  150.4 4.2 all-to-all-start.3
  154.7 9.0 %collective-permute-done.9.refs_3_.refs_13_ = bf16[640,768]{1,0:T(8,128)(2,1)} collective-permute-done((bf16[640,768]{1,0:T(8,128)(2,1)}, bf16[640,768]{1,0:T(8,128)(2,1)}, u32[]{:S(2)}, u32[]{:S(2)}) %collective-permute-start.9) | collective-permute-done | bytes 983072 | tf_op jit(solution)/shard_map/ppermute | solution.py:855
  173.6 5.5 collective-permute-start.22
  179.1 6.2 collective-permute-done.12.refs_6_.refs_20_
  186.6 12.9 %shard_map.284 = (bf16[2,320,768]{2,1,0:T(8,128)(2,1)S(1)}, bf16[2,320,768]{2,1,0:T(8,128)(2,1)S(1)}, bf16[2,320,768]{2,1,0:T(8,128)(2,1)S(1)}, bf16[2,320,768]{...) custom-call(bf16[2,320,768]{2,1,0:T(8,128)(2,1)} %shard_map.282.refs, ...), custom_call_target="tpu_custom_call" | custom-call | flops 1 | bytes 1 | tf_op jit(solution)/shard_map/pallas_call | solution.py:427
  199.5 6.9 %collective-permute-done.11.down_ref.refs_4_.refs_11_ = bf16[2,320,768]{2,1,0:T(8,128)(2,1)} collective-permute-done((bf16[2,320,768]{2,1,0:T(8,128)(2,1)}, bf16[2,320,768]{2,1,0:T(8,128)(2,1)}, u32[]{:S(2)}, u32[]{:S(2)}) %collective-permute-start.11) | collective-permute-done | bytes 983072 | tf_op jit(solution)/shard_map/ppermute | solution.py:855
  213.3 12.8 %shard_map.290 = (bf16[2,320,768]{2,1,0:T(8,128)(2,1)S(1)}, bf16[2,320,768]{2,1,0:T(8,128)(2,1)S(1)}, bf16[2,320,768]{2,1,0:T(8,128)(2,1)S(1)}, bf16[2,320,768]{...) custom-call(bf16[2,320,768]{2,1,0:T(8,128)(2,1)} %shard_map.282.refs, ...), custom_call_target="tpu_custom_call" | custom-call | flops 1 | bytes 1 | tf_op jit(solution)/shard_map/pallas_call | solution.py:427
  235.0 13.4 %collective-permute-done.15.down_ref.refs_5_.refs_12_ = bf16[2,320,768]{2,1,0:T(8,128)(2,1)S(1)} collective-permute-done((bf16[2,320,768]{2,1,0:T(8,128)(2,1)S(1)}, bf16[2,320,768]{2,1,0:T(8,128)(2,1)S(1)}, u32[]{:S(2)}, u32[]{:S(2)}) %collective-permute-start.15) | collective-permute-done | bytes 983072 | tf_op jit(solution)/shard_map/ppermute | solution.py:855
  255.8 13.7 %collective-permute-done.25.down_ref.refs_7_.refs_14_ = bf16[2,320,768]{2,1,0:T(8,128)(2,1)S(1)} collective-permute-done((bf16[2,320,768]{2,1,0:T(8,128)(2,1)S(1)}, bf16[2,320,768]{2,1,0:T(8,128)(2,1)S(1)}, u32[]{:S(2)}, u32[]{:S(2)}) %collective-permute-start.25) | collective-permute-done | bytes 983072 | tf_op jit(solution)/shard_map/ppermute | solution.py:855
  276.0 14.5 %collective-permute-done.17.down_ref.refs_6_.refs_13_ = bf16[2,320,768]{2,1,0:T(8,128)(2,1)S(1)} collective-permute-done((bf16[2,320,768]{2,1,0:T(8,128)(2,1)S(1)}, bf16[2,320,768]{2,1,0:T(8,128)(2,1)S(1)}, u32[]{:S(2)}, u32[]{:S(2)}) %collective-permute-start.17) | collective-permute-done | bytes 983072 | tf_op jit(solution)/shard_map/ppermute | solution.py:855
  294.3 12.7 %shard_map.288 = (bf16[2,320,768]{2,1,0:T(8,128)(2,1)S(1)}, bf16[2,320,768]{2,1,0:T(8,128)(2,1)S(1)}, bf16[2,320,768]{2,1,0:T(8,128)(2,1)S(1)}, bf16[2,320,768]{...) custom-call(bf16[2,320,768]{2,1,0:T(8,128)(2,1)S(1)} %get-tuple-elem, ...), custom_call_target="tpu_custom_call" | custom-call | flops 1 | bytes 1 | tf_op jit(solution)/shard_map/pallas_call | solution.py:427
  307.0 5.5 collective-permute-start.18
  319.4 13.2 %collective-permute-done.31.refs_5_.refs_3_ = bf16[2,320,768]{2,1,0:T(8,128)(2,1)S(1)} collective-permute-done((bf16[2,320,768]{2,1,0:T(8,128)(2,1)S(1)}, bf16[2,320,768]{2,1,0:T(8,128)(2,1)S(1)}, u32[]{:S(2)}, u32[]{:S(2)}) %collective-permute-start.31) | collective-permute-done | bytes 983072 | tf_op jit(solution)/shard_map/ppermute | solution.py:855
  333.6 13.2 %shard_map.298 = (bf16[2,320,768]{2,1,0:T(8,128)(2,1)S(1)}, bf16[2,320,768]{2,1,0:T(8,128)(2,1)}, bf16[2,320,768]{2,1,0:T(8,128)(2,1)S(1)}, bf16[2,320,768]{2,1,...) custom-call(bf16[2,320,768]{2,1,0:T(8,128)(2,1)} %get-tuple-element., ...), custom_call_target="tpu_custom_call" | custom-call | flops 1 | bytes 1 | tf_op jit(solution)/shard_map/pallas_call | solution.py:427
  356.2 4.1 collective-permute-done.28.refs_2_.refs_0_
  371.8 13.4 %shard_map.299 = (f32[8,768,768]{2,1,0:T(8,128)}, f32[8,768,768]{2,1,0:T(8,128)}) custom-call(bf16[2,320,768]{2,1,0:T(8,128)(2,1)} %get-tuple-element.136.refs_0_, bf16[4,320,768]{2,1,0:T(8,128)(2,1)S(1)} %copy-done.55, bf16[4,320,768]{2,1,0:T(8,128)(2,1)S(1)} %copy-done.56, bf16[4,320,768]{2,1,0:T(8,128)(2,1)} %get-tuple-element.160.refs_3_, ...), custom_call_target="tpu_custom_call" | custom-call | flops 1 | bytes 1 | tf_op jit(solution)/shard_map/pallas_call | solution.py:456
  385.2 4.1 shard_map.300
  389.3 4.9 collective-permute-start.34
  398.0 4.2 all-to-all-start.5
  408.8 5.3 collective-permute-start.36
  422.2 8.6 %shard_map.297 = (bf16[512,768]{1,0:T(8,128)(2,1)S(1)}, f32[512,768]{1,0:T(8,128)}, bf16[6,512,128]{2,1,0:T(8,128)(2,1)S(1)}, f32[1696,384]{1,0:T(8,128)}) custom-call(bf16[2,320,768]{2,1,0:T(8,128)(2,1)} %get-tuple-element.149.refs_0_, s32[2]{0:T(128)S(1)} %bitcast.86, bf16[8,80,768]{2,1,0:T(8,128)(2,1)S(1)} %copy-done.46, bf16[8,80,768]{2,1,0:T(8,128)(2,1)} %copy-done.26, ...), custom_call_target="tpu_custom_call" | custom-call | flops 1 | bytes 1 | tf_op jit(solution)/shard_map/pallas_call | solution.py:536
  430.9 4.8 shard_map.301
  435.7 4.3 collective-permute-start.38
  441.2 14.3 %shard_map.302 = (f32[2304,384]{1,0:T(8,128)}, f32[16,1024]{1,0:T(8,128)}, f32[512,768]{1,0:T(8,128)}) custom-call(bf16[2,320,768]{2,1,0:T(8,128)(2,1)} %get-tuple-element.170.refs_0_, s32[2]{0:T(128)} %bitcast.79, bf16[3,6,512,128]{3,2,1,0:T(8,128)(2,1)} %get-tuple-element.171.refs_2_, f32[512,128]{1,0:T(8,128)} %copy-done.64, f32[12,1,1024]{2,1,0:T(1,128)} %copy-done.50, ...), custom_call_target="tpu_custom_call" | custom-call | flops 1 | bytes 1 | tf_op jit(solution)/shard_map/pallas_call | solution.py:709
  465.1 14.8 %shard_map.304 = (f32[2560,384]{1,0:T(8,128)}, bf16[512,768]{1,0:T(8,128)(2,1)}) custom-call(bf16[8,80,768]{2,1,0:T(8,128)(2,1)} %shard_map.303.refs_0_, s32[2]{0:T(128)} %bitcast.80, bf16[3,6,512,128]{3,2,1,0:T(8,128)(2,1)} %get-tuple-element.171.refs_2_, f32[512,128]{1,0:T(8,128)} %copy-done.64, f32[12,1,1024]{2,1,0:T(1,128)} %copy-done.50, ...), custom_call_target="tpu_custom_call" | custom-call | flops 1 | bytes 1 | tf_op jit(solution)/shard_map/pallas_call | solution.py:709
  485.5 4.2 all-to-all-start.7
  492.8 13.5 %shard_map.306 = (f32[8,768,768]{2,1,0:T(8,128)}, f32[8,768,768]{2,1,0:T(8,128)}) custom-call(bf16[8,80,768]{2,1,0:T(8,128)(2,1)} %shard_map.305.refs_0_, bf16[4,320,768]{2,1,0:T(8,128)(2,1)S(1)} %copy-done.57, bf16[4,320,768]{2,1,0:T(8,128)(2,1)S(1)} %copy-done.58, ...), custom_call_target="tpu_custom_call", output_to_operand_aliasing={{0}: (9, {}), {1}: (10, {})} | custom-call | flops 1 | bytes 1 | tf_op jit(solution)/shard_map/pallas_call | solution.py:456
  508.3 8.8 %shard_map.307 = (bf16[512,768]{1,0:T(8,128)(2,1)S(1)}, f32[512,768]{1,0:T(8,128)}, bf16[6,512,128]{2,1,0:T(8,128)(2,1)S(1)}, bf16[1696,384]{1,0:T(8,128)(2,1)}) custom-call(f32[8,768,768]{2,1,0:T(8,128)} %get-tuple-element.241.refs_0_, s32[2]{0:T(128)S(1)} %bitcast.87, bf16[8,80,768]{2,1,0:T(8,128)(2,1)S(1)} %all-to-all-done.6.refs_1_.refs_2_, ...), custom_call_target="tpu_custom_call" | custom-call | flops 1 | bytes 1 | tf_op jit(solution)/shard_map/pallas_call | solution.py:536
  518.9 14.1 %shard_map.308 = (bf16[4096,384]{1,0:T(8,128)(2,1)}, f32[16,1024]{1,0:T(8,128)}, f32[512,768]{1,0:T(8,128)}) custom-call(s32[2]{0:T(128)} %bitcast.81, bf16[3,6,512,128]{3,2,1,0:T(8,128)(2,1)} %get-tuple-element.196.refs_1_.refs_2_, f32[512,128]{1,0:T(8,128)} %copy-done.63, f32[12,1,1024]{2,1,0:T(1,128)} %copy-done.50, ...), custom_call_target="tpu_custom_call" | custom-call | flops 1 | bytes 1 | tf_op jit(solution)/shard_map/pallas_call | solution.py:709
  544.4 14.8 %shard_map.309 = (bf16[2560,384]{1,0:T(8,128)(2,1)}, bf16[512,768]{1,0:T(8,128)(2,1)}) custom-call(bf16[2048,384]{1,0:T(8,128)(2,1)} %copy-done.95, s32[2]{0:T(128)} %bitcast.82, bf16[3,6,512,128]{3,2,1,0:T(8,128)(2,1)} %get-tuple-element.196.refs_1_.refs_2_, f32[512,128]{1,0:T(8,128)} %copy-done.63, f32[12,1,1024]{2,1,0:T(1,128)} %copy-done.50, ...), custom_call_target="tpu_custom_call" | custom-call | flops 1 | bytes 1 | tf_op jit(solution)/shard_map/pallas_call | solution.py:709
  569.3 7.5 %collective-permute-done.59 = bf16[128,384]{1,0:T(8,128)(2,1)S(1)} collective-permute-done((bf16[128,384]{1,0:T(8,128)(2,1)S(1)}, bf16[128,384]{1,0:T(8,128)(2,1)S(1)}, u32[]{:S(2)}, u32[]{:S(2)}) %collective-permute-start.59) | collective-permute-done | bytes 98336 | tf_op jit(solution)/shard_map/ppermute | solution.py:887
  608.0 4.9 collective-permute-done.65
  629.2 4.6 collective-permute-done.52
  639.4 4.8 shard_map.310
  (383 shorter events, 241.5 us)
Async XLA Ops:
  8.7 31.3 %all-to-all-start = ((bf16[8,80,768]{2,1,0:T(8,128)(2,1)}), bf16[8,80,768]{2,1,0:T(8,128)(2,1)}, u32[]{:S(2)}, u32[]{:S(2)}) async-start(bf16[8,80,768]{2,1,0:T(8,128)(2,1)} %copy-done.39), calls=%async_computation | async-start | bytes 1966080 | tf_op jit(solution)/shard_map/all_to_all | solution.py:985
  40.1 21.3 %all-to-all-start.1 = ((bf16[8,96,768]{2,1,0:T(8,128)(2,1)}), bf16[8,96,768]{2,1,0:T(8,128)(2,1)}, u32[]{:S(2)}, u32[]{:S(2)}) async-start(bf16[8,96,768]{2,1,0:T(8,128)(2,1)} %get-tuple-element.118.refs_0_), calls=%async_computation.1 | async-start | bytes 2359296 | tf_op jit(solution)/shard_map/all_to_all | solution.py:985
  46.7 26.2 %collective-permute-start.2 = (bf16[640,768]{1,0:T(8,128)(2,1)S(1)}, bf16[640,768]{1,0:T(8,128)(2,1)}, u32[]{:S(2)}, u32[]{:S(2)}) collective-permute-start(bf16[640,768]{1,0:T(8,128)(2,1)S(1)} %shard_map.277.refs_0_.refs_10_), channel_id=1, source_target_pairs={{0,1},{1,2},{2,3},{4,5},{5,6},{6,7},{8,9},{9,10},{10,11},{12,13},{... | collective-permute-start | bytes 2949128 | tf_op jit(solution)/shard_map/ppermute | solution.py:854
  51.8 26.6 %collective-permute-start.3 = (bf16[640,768]{1,0:T(8,128)(2,1)S(1)}, bf16[640,768]{1,0:T(8,128)(2,1)}, u32[]{:S(2)}, u32[]{:S(2)}) collective-permute-start(bf16[640,768]{1,0:T(8,128)(2,1)S(1)} %shard_map.277.refs_0_.refs_10_), channel_id=1, source_target_pairs={{3,2},{2,1},{1,0},{7,6},{6,5},{5,4},{11,10},{10,9},{9,8},{15,14},{... | collective-permute-start | bytes 2949128 | tf_op jit(solution)/shard_map/ppermute | solution.py:855
  65.3 30.1 %collective-permute-start = (bf16[656,768]{1,0:T(8,128)(2,1)S(1)}, bf16[656,768]{1,0:T(8,128)(2,1)}, u32[]{:S(2)}, u32[]{:S(2)}) collective-permute-start(bf16[656,768]{1,0:T(8,128)(2,1)S(1)} %shard_map.278.refs_0_.refs_3_.refs_17_), channel_id=1, source_target_pairs={{0,1},{1,2},{2,3},{4,5},{5,6},{6,7},{8,9},{9,10},{10,11},{12,13},{... | collective-permute-start | bytes 3022856 | tf_op jit(solution)/shard_map/ppermute | solution.py:854
  70.3 29.5 %collective-permute-start.1 = (bf16[656,768]{1,0:T(8,128)(2,1)S(1)}, bf16[656,768]{1,0:T(8,128)(2,1)S(1)}, u32[]{:S(2)}, u32[]{:S(2)}) collective-permute-start(bf16[656,768]{1,0:T(8,128)(2,1)S(1)} %shard_map.278.refs_0_.refs_3_.refs_17_), channel_id=1, source_target_pairs={{3,2},{2,1},{1,0},{7,6},{6,5},{5,4},{11,10},{10,9},{9,8},{15,14},{... | collective-permute-start | bytes 3022856 | tf_op jit(solution)/shard_map/ppermute | solution.py:855
  72.9 30.0 %collective-permute-start.6 = (bf16[640,768]{1,0:T(8,128)(2,1)}, bf16[640,768]{1,0:T(8,128)(2,1)}, u32[]{:S(2)}, u32[]{:S(2)}) collective-permute-start(bf16[640,768]{1,0:T(8,128)(2,1)} %collective-permute-done.2.refs_1_.refs_14_), channel_id=1, source_target_pairs={{1,2},{2,3},{5,6},{6,7},{9,10},{10,11},{13,14},{14,15},{17,18},{18... | collective-permute-start | bytes 2949128 | tf_op jit(solution)/shard_map/ppermute | solution.py:854
  78.4 42.7 %collective-permute-start.8 = (bf16[640,768]{1,0:T(8,128)(2,1)}, bf16[640,768]{1,0:T(8,128)(2,1)}, u32[]{:S(2)}, u32[]{:S(2)}) collective-permute-start(bf16[640,768]{1,0:T(8,128)(2,1)} %collective-permute-done.3.refs_2_.refs_11_), channel_id=1, source_target_pairs={{2,1},{1,0},{6,5},{5,4},{10,9},{9,8},{14,13},{13,12},{18,17},{17,1... | collective-permute-start | bytes 2949128 | tf_op jit(solution)/shard_map/ppermute | solution.py:855
  100.8 41.7 %collective-permute-start.5 = (bf16[656,768]{1,0:T(8,128)(2,1)}, bf16[656,768]{1,0:T(8,128)(2,1)S(1)}, u32[]{:S(2)}, u32[]{:S(2)}) collective-permute-start(bf16[656,768]{1,0:T(8,128)(2,1)} %get-tuple-element.121.refs_4_.refs_18_), channel_id=1, source_target_pairs={{2,1},{1,0},{6,5},{5,4},{10,9},{9,8},{14,13},{13,12},{18,17},{17,1... | collective-permute-start | bytes 3022856 | tf_op jit(solution)/shard_map/ppermute | solution.py:855
  102.1 41.7 %collective-permute-start.4 = (bf16[656,768]{1,0:T(8,128)(2,1)}, bf16[656,768]{1,0:T(8,128)(2,1)S(1)}, u32[]{:S(2)}, u32[]{:S(2)}) collective-permute-start(bf16[656,768]{1,0:T(8,128)(2,1)} %get-tuple-element.120.refs_7_.refs_21_), channel_id=1, source_target_pairs={{1,2},{2,3},{5,6},{6,7},{9,10},{10,11},{13,14},{14,15},{17,18},{18... | collective-permute-start | bytes 3022856 | tf_op jit(solution)/shard_map/ppermute | solution.py:854
  102.9 51.8 %collective-permute-start.7 = (bf16[640,768]{1,0:T(8,128)(2,1)}, bf16[640,768]{1,0:T(8,128)(2,1)}, u32[]{:S(2)}, u32[]{:S(2)}) collective-permute-start(bf16[640,768]{1,0:T(8,128)(2,1)} %collective-permute-done.6.refs_0_.refs_15_), channel_id=1, source_target_pairs={{2,3},{6,7},{10,11},{14,15},{18,19},{22,23},{26,27},{30,31}} | collective-permute-start | bytes 2949128 | tf_op jit(solution)/shard_map/ppermute | solution.py:854
  121.0 42.7 %collective-permute-start.9 = (bf16[640,768]{1,0:T(8,128)(2,1)}, bf16[640,768]{1,0:T(8,128)(2,1)}, u32[]{:S(2)}, u32[]{:S(2)}) collective-permute-start(bf16[640,768]{1,0:T(8,128)(2,1)} %collective-permute-done.8.refs_1_.refs_12_), channel_id=1, source_target_pairs={{1,0},{5,4},{9,8},{13,12},{17,16},{21,20},{25,24},{29,28}} | collective-permute-start | bytes 2949128 | tf_op jit(solution)/shard_map/ppermute | solution.py:855
  142.5 42.8 %collective-permute-start.12 = (bf16[656,768]{1,0:T(8,128)(2,1)S(1)}, bf16[656,768]{1,0:T(8,128)(2,1)}, u32[]{:S(2)}, u32[]{:S(2)}) collective-permute-start(bf16[656,768]{1,0:T(8,128)(2,1)S(1)} %collective-permute-done.5.refs_1_.refs_5_.refs_19_), channel_id=1, source_target_pairs={{1,0},{5,4},{9,8},{13,12},{17,16},{21,20},{25,24},{29,28}} | collective-permute-start | bytes 3022856 | tf_op jit(solution)/shard_map/ppermute | solution.py:855
  143.8 42.8 %collective-permute-start.13 = (bf16[656,768]{1,0:T(8,128)(2,1)S(1)}, bf16[656,768]{1,0:T(8,128)(2,1)}, u32[]{:S(2)}, u32[]{:S(2)}) collective-permute-start(bf16[656,768]{1,0:T(8,128)(2,1)S(1)} %collective-permute-done.4.refs_0_.refs_8_.refs_22_), channel_id=1, source_target_pairs={{2,3},{6,7},{10,11},{14,15},{18,19},{22,23},{26,27},{30,31}} | collective-permute-start | bytes 3022856 | tf_op jit(solution)/shard_map/ppermute | solution.py:854
  150.4 20.1 %all-to-all-start.3 = ((bf16[8,80,768]{2,1,0:T(8,128)(2,1)}), bf16[8,80,768]{2,1,0:T(8,128)(2,1)}, u32[]{:S(2)}, u32[]{:S(2)}) async-start(bf16[8,80,768]{2,1,0:T(8,128)(2,1)} %copy-done.75), calls=%async_computation.3 | async-start | bytes 1966080 | tf_op jit(solution)/shard_map/all_to_all | solution.py:985
  166.8 32.7 %collective-permute-start.10 = (bf16[2,320,768]{2,1,0:T(8,128)(2,1)}, bf16[2,320,768]{2,1,0:T(8,128)(2,1)}, u32[]{:S(2)}, u32[]{:S(2)}) collective-permute-start(bf16[2,320,768]{2,1,0:T(8,128)(2,1)} %shard_map.282.refs_0_.refs_3_.refs_10_), channel_id=1, source_target_pairs={{0,1},{1,2},{2,3},{4,5},{5,6},{6,7},{8,9},{9,10},{10,11},{12,13},{... | collective-permute-start | bytes 2949128 | tf_op jit(solution)/shard_map/ppermute | solution.py:854
  169.2 37.2 %collective-permute-start.11 = (bf16[2,320,768]{2,1,0:T(8,128)(2,1)}, bf16[2,320,768]{2,1,0:T(8,128)(2,1)}, u32[]{:S(2)}, u32[]{:S(2)}) collective-permute-start(bf16[2,320,768]{2,1,0:T(8,128)(2,1)} %shard_map.282.refs_0_.refs_3_.refs_10_), channel_id=1, source_target_pairs={{3,2},{2,1},{1,0},{7,6},{6,5},{5,4},{11,10},{10,9},{9,8},{15,14},{... | collective-permute-start | bytes 2949128 | tf_op jit(solution)/shard_map/ppermute | solution.py:855
  173.6 52.5 %collective-permute-start.22 = (bf16[2,320,768]{2,1,0:T(8,128)(2,1)}, bf16[2,320,768]{2,1,0:T(8,128)(2,1)}, u32[]{:S(2)}, u32[]{:S(2)}) collective-permute-start(bf16[2,320,768]{2,1,0:T(8,128)(2,1)} %shard_map.283.refs_1_.refs_5_.refs_12_), channel_id=1, source_target_pairs={{0,1},{1,2},{2,3},{4,5},{5,6},{6,7},{8,9},{9,10},{10,11},{12,13},{... | collective-permute-start | bytes 2949128 | tf_op jit(solution)/shard_map/ppermute | solution.py:854
  185.3 42.0 %collective-permute-start.23 = (bf16[2,320,768]{2,1,0:T(8,128)(2,1)}, bf16[2,320,768]{2,1,0:T(8,128)(2,1)S(1)}, u32[]{:S(2)}, u32[]{:S(2)}) collective-permute-start(bf16[2,320,768]{2,1,0:T(8,128)(2,1)} %shard_map.283.refs_1_.refs_5_.refs_12_), channel_id=1, source_target_pairs={{3,2},{2,1},{1,0},{7,6},{6,5},{5,4},{11,10},{10,9},{9,8},{15,14},{... | collective-permute-start | bytes 2949128 | tf_op jit(solution)/shard_map/ppermute | solution.py:855
  210.1 24.8 %collective-permute-start.14 = (bf16[2,320,768]{2,1,0:T(8,128)(2,1)}, bf16[2,320,768]{2,1,0:T(8,128)(2,1)S(1)}, u32[]{:S(2)}, u32[]{:S(2)}) collective-permute-start(bf16[2,320,768]{2,1,0:T(8,128)(2,1)} %get-tuple-element.126), channel_id=1, source_target_pairs={{0,1},{1,2},{2,3},{4,5},{5,6},{6,7},{8,9},{9,10},{10,11},{12,13},{... | collective-permute-start | bytes 2949128 | tf_op jit(solution)/shard_map/ppermute | solution.py:854
  211.6 36.8 %collective-permute-start.15 = (bf16[2,320,768]{2,1,0:T(8,128)(2,1)S(1)}, bf16[2,320,768]{2,1,0:T(8,128)(2,1)S(1)}, u32[]{:S(2)}, u32[]{:S(2)}) collective-permute-start(bf16[2,320,768]{2,1,0:T(8,128)(2,1)S(1)} %get-tuple-element.127), channel_id=1, source_target_pairs={{3,2},{2,1},{1,0},{7,6},{6,5},{5,4},{11,10},{10,9},{9,8},{15,14},{... | collective-permute-start | bytes 2949128 | tf_op jit(solution)/shard_map/ppermute | solution.py:855
  229.9 25.8 %collective-permute-start.24 = (bf16[2,320,768]{2,1,0:T(8,128)(2,1)S(1)}, bf16[2,320,768]{2,1,0:T(8,128)(2,1)S(1)}, u32[]{:S(2)}, u32[]{:S(2)}) collective-permute-start(bf16[2,320,768]{2,1,0:T(8,128)(2,1)S(1)} %get-tuple-element.141), channel_id=1, source_target_pairs={{0,1},{1,2},{2,3},{4,5},{5,6},{6,7},{8,9},{9,10},{10,11},{12,13},{... | collective-permute-start | bytes 2949128 | tf_op jit(solution)/shard_map/ppermute | solution.py:854
  233.6 35.8 %collective-permute-start.25 = (bf16[2,320,768]{2,1,0:T(8,128)(2,1)S(1)}, bf16[2,320,768]{2,1,0:T(8,128)(2,1)S(1)}, u32[]{:S(2)}, u32[]{:S(2)}) collective-permute-start(bf16[2,320,768]{2,1,0:T(8,128)(2,1)S(1)} %get-tuple-element.142), channel_id=1, source_target_pairs={{3,2},{2,1},{1,0},{7,6},{6,5},{5,4},{11,10},{10,9},{9,8},{15,14},{... | collective-permute-start | bytes 2949128 | tf_op jit(solution)/shard_map/ppermute | solution.py:855
  249.3 26.7 %collective-permute-start.16 = (bf16[2,320,768]{2,1,0:T(8,128)(2,1)S(1)}, bf16[2,320,768]{2,1,0:T(8,128)(2,1)S(1)}, u32[]{:S(2)}, u32[]{:S(2)}) collective-permute-start(bf16[2,320,768]{2,1,0:T(8,128)(2,1)S(1)} %get-tuple-element.129), channel_id=1, source_target_pairs={{0,1},{1,2},{2,3},{4,5},{5,6},{6,7},{8,9},{9,10},{10,11},{12,13},{... | collective-permute-start | bytes 2949128 | tf_op jit(solution)/shard_map/ppermute | solution.py:854
  250.8 39.7 %collective-permute-start.17 = (bf16[2,320,768]{2,1,0:T(8,128)(2,1)S(1)}, bf16[2,320,768]{2,1,0:T(8,128)(2,1)S(1)}, u32[]{:S(2)}, u32[]{:S(2)}) collective-permute-start(bf16[2,320,768]{2,1,0:T(8,128)(2,1)S(1)} %get-tuple-element.130), channel_id=1, source_target_pairs={{3,2},{2,1},{1,0},{7,6},{6,5},{5,4},{11,10},{10,9},{9,8},{15,14},{... | collective-permute-start | bytes 2949128 | tf_op jit(solution)/shard_map/ppermute | solution.py:855
  271.1 41.4 %collective-permute-start.26 = (bf16[2,320,768]{2,1,0:T(8,128)(2,1)}, bf16[2,320,768]{2,1,0:T(8,128)(2,1)S(1)}, u32[]{:S(2)}, u32[]{:S(2)}) collective-permute-start(bf16[2,320,768]{2,1,0:T(8,128)(2,1)} %get-tuple-element.144), channel_id=1, source_target_pairs={{0,1},{1,2},{2,3},{4,5},{5,6},{6,7},{8,9},{9,10},{10,11},{12,13},{... | collective-permute-start | bytes 2949128 | tf_op jit(solution)/shard_map/ppermute | solution.py:854
  272.7 41.5 %collective-permute-start.27 = (bf16[2,320,768]{2,1,0:T(8,128)(2,1)S(1)}, bf16[2,320,768]{2,1,0:T(8,128)(2,1)S(1)}, u32[]{:S(2)}, u32[]{:S(2)}) collective-permute-start(bf16[2,320,768]{2,1,0:T(8,128)(2,1)S(1)} %get-tuple-element.145), channel_id=1, source_target_pairs={{3,2},{2,1},{1,0},{7,6},{6,5},{5,4},{11,10},{10,9},{9,8},{15,14},{... | collective-permute-start | bytes 2949128 | tf_op jit(solution)/shard_map/ppermute | solution.py:855
  291.5 26.7 %collective-permute-start.30 = (bf16[2,320,768]{2,1,0:T(8,128)(2,1)S(1)}, bf16[2,320,768]{2,1,0:T(8,128)(2,1)S(1)}, u32[]{:S(2)}, u32[]{:S(2)}) collective-permute-start(bf16[2,320,768]{2,1,0:T(8,128)(2,1)S(1)} %get-tuple-element.131.refs_0_), channel_id=1, source_target_pairs={{0,1},{1,2},{2,3},{4,5},{5,6},{6,7},{8,9},{9,10},{10,11},{12,13},{... | collective-permute-start | bytes 2949128 | tf_op jit(solution)/shard_map/ppermute | solution.py:854
  293.0 39.7 %collective-permute-start.31 = (bf16[2,320,768]{2,1,0:T(8,128)(2,1)S(1)}, bf16[2,320,768]{2,1,0:T(8,128)(2,1)S(1)}, u32[]{:S(2)}, u32[]{:S(2)}) collective-permute-start(bf16[2,320,768]{2,1,0:T(8,128)(2,1)S(1)} %get-tuple-element.132.refs_1_), channel_id=1, source_target_pairs={{3,2},{2,1},{1,0},{7,6},{6,5},{5,4},{11,10},{10,9},{9,8},{15,14},{... | collective-permute-start | bytes 2949128 | tf_op jit(solution)/shard_map/ppermute | solution.py:855
  307.0 41.4 %collective-permute-start.18 = (bf16[2,320,768]{2,1,0:T(8,128)(2,1)S(1)}, bf16[2,320,768]{2,1,0:T(8,128)(2,1)}, u32[]{:S(2)}, u32[]{:S(2)}) collective-permute-start(bf16[2,320,768]{2,1,0:T(8,128)(2,1)S(1)} %get-tuple-element.133.downsum_ref), channel_id=1, source_target_pairs={{0,1},{4,5},{8,9},{12,13},{16,17},{20,21},{24,25},{28,29}} | collective-permute-start | bytes 2949128 | tf_op jit(solution)/shard_map/ppermute | solution.py:854
  312.5 37.5 %collective-permute-start.19 = (bf16[2,320,768]{2,1,0:T(8,128)(2,1)S(1)}, bf16[2,320,768]{2,1,0:T(8,128)(2,1)}, u32[]{:S(2)}, u32[]{:S(2)}) collective-permute-start(bf16[2,320,768]{2,1,0:T(8,128)(2,1)S(1)} %get-tuple-element.134.upsum_ref), channel_id=1, source_target_pairs={{3,2},{7,6},{11,10},{15,14},{19,18},{23,22},{27,26},{31,30}} | collective-permute-start | bytes 2949128 | tf_op jit(solution)/shard_map/ppermute | solution.py:855
  316.1 44.2 %collective-permute-start.28 = (bf16[2,320,768]{2,1,0:T(8,128)(2,1)}, bf16[2,320,768]{2,1,0:T(8,128)(2,1)S(1)}, u32[]{:S(2)}, u32[]{:S(2)}) collective-permute-start(bf16[2,320,768]{2,1,0:T(8,128)(2,1)} %get-tuple-element.147.refs_0_), channel_id=1, source_target_pairs={{0,1},{1,2},{2,3},{4,5},{5,6},{6,7},{8,9},{9,10},{10,11},{12,13},{... | collective-permute-start | bytes 2949128 | tf_op jit(solution)/shard_map/ppermute | solution.py:854
  318.1 43.9 %collective-permute-start.29 = (bf16[2,320,768]{2,1,0:T(8,128)(2,1)}, bf16[2,320,768]{2,1,0:T(8,128)(2,1)S(1)}, u32[]{:S(2)}, u32[]{:S(2)}) collective-permute-start(bf16[2,320,768]{2,1,0:T(8,128)(2,1)} %get-tuple-element.148.refs_1_), channel_id=1, source_target_pairs={{3,2},{2,1},{1,0},{7,6},{6,5},{5,4},{11,10},{10,9},{9,8},{15,14},{... | collective-permute-start | bytes 2949128 | tf_op jit(solution)/shard_map/ppermute | solution.py:855
  346.9 38.3 %collective-permute-start.32 = (bf16[2,320,768]{2,1,0:T(8,128)(2,1)}, bf16[2,320,768]{2,1,0:T(8,128)(2,1)S(1)}, u32[]{:S(2)}, u32[]{:S(2)}) collective-permute-start(bf16[2,320,768]{2,1,0:T(8,128)(2,1)} %get-tuple-element.155.downsum_ref), channel_id=1, source_target_pairs={{0,1},{4,5},{8,9},{12,13},{16,17},{20,21},{24,25},{28,29}} | collective-permute-start | bytes 2949128 | tf_op jit(solution)/shard_map/ppermute | solution.py:854
  348.4 36.8 %collective-permute-start.33 = (bf16[2,320,768]{2,1,0:T(8,128)(2,1)}, bf16[2,320,768]{2,1,0:T(8,128)(2,1)}, u32[]{:S(2)}, u32[]{:S(2)}) collective-permute-start(bf16[2,320,768]{2,1,0:T(8,128)(2,1)} %get-tuple-element.156.upsum_ref), channel_id=1, source_target_pairs={{3,2},{7,6},{11,10},{15,14},{19,18},{23,22},{27,26},{31,30}} | collective-permute-start | bytes 2949128 | tf_op jit(solution)/shard_map/ppermute | solution.py:855
  354.0 48.5 %collective-permute-start.20 = (bf16[2,320,768]{2,1,0:T(8,128)(2,1)}, bf16[2,320,768]{2,1,0:T(8,128)(2,1)}, u32[]{:S(2)}, u32[]{:S(2)}) collective-permute-start(bf16[2,320,768]{2,1,0:T(8,128)(2,1)} %get-tuple-element.136.refs_0_), channel_id=1, source_target_pairs={{0,1},{1,2},{4,5},{5,6},{8,9},{9,10},{12,13},{13,14},{16,17},{17,1... | collective-permute-start | bytes 2949128 | tf_op jit(solution)/shard_map/ppermute | solution.py:854
  360.4 42.1 %collective-permute-start.21 = (bf16[2,320,768]{2,1,0:T(8,128)(2,1)}, bf16[2,320,768]{2,1,0:T(8,128)(2,1)}, u32[]{:S(2)}, u32[]{:S(2)}) collective-permute-start(bf16[2,320,768]{2,1,0:T(8,128)(2,1)} %get-tuple-element.137), channel_id=1, source_target_pairs={{3,2},{2,1},{7,6},{6,5},{11,10},{10,9},{15,14},{14,13},{19,18},{18... | collective-permute-start | bytes 2949128 | tf_op jit(solution)/shard_map/ppermute | solution.py:855
  365.0 33.0 %all-to-all-start.4 = ((bf16[8,80,768]{2,1,0:T(8,128)(2,1)}), bf16[8,80,768]{2,1,0:T(8,128)(2,1)S(1)}, u32[]{:S(2)}, u32[]{:S(2)}) async-start(bf16[8,80,768]{2,1,0:T(8,128)(2,1)} %shard_map.294), calls=%async_computation.4 | async-start | bytes 1966080 | tf_op jit(solution)/shard_map/all_to_all | solution.py:985
  389.3 41.6 %collective-permute-start.34 = (bf16[2,320,768]{2,1,0:T(8,128)(2,1)}, bf16[2,320,768]{2,1,0:T(8,128)(2,1)}, u32[]{:S(2)}, u32[]{:S(2)}) collective-permute-start(bf16[2,320,768]{2,1,0:T(8,128)(2,1)} %get-tuple-element.167), channel_id=1, source_target_pairs={{0,1},{1,2},{4,5},{5,6},{8,9},{9,10},{12,13},{13,14},{16,17},{17,1... | collective-permute-start | bytes 2949128 | tf_op jit(solution)/shard_map/ppermute | solution.py:854
  394.2 36.7 %collective-permute-start.35 = (bf16[2,320,768]{2,1,0:T(8,128)(2,1)}, bf16[2,320,768]{2,1,0:T(8,128)(2,1)}, u32[]{:S(2)}, u32[]{:S(2)}) collective-permute-start(bf16[2,320,768]{2,1,0:T(8,128)(2,1)} %get-tuple-element.168), channel_id=1, source_target_pairs={{3,2},{2,1},{7,6},{6,5},{11,10},{10,9},{15,14},{14,13},{19,18},{18... | collective-permute-start | bytes 2949128 | tf_op jit(solution)/shard_map/ppermute | solution.py:855
  408.8 46.8 %collective-permute-start.36 = (bf16[2,320,768]{2,1,0:T(8,128)(2,1)}, bf16[2,320,768]{2,1,0:T(8,128)(2,1)}, u32[]{:S(2)}, u32[]{:S(2)}) collective-permute-start(bf16[2,320,768]{2,1,0:T(8,128)(2,1)} %get-tuple-element.149.refs_0_), channel_id=1, source_target_pairs={{0,1},{1,2},{2,3},{4,5},{5,6},{6,7},{8,9},{9,10},{10,11},{12,13},{... | collective-permute-start | bytes 2949128 | tf_op jit(solution)/shard_map/ppermute | solution.py:854
  414.1 41.5 %collective-permute-start.37 = (bf16[2,320,768]{2,1,0:T(8,128)(2,1)}, bf16[2,320,768]{2,1,0:T(8,128)(2,1)}, u32[]{:S(2)}, u32[]{:S(2)}) collective-permute-start(bf16[2,320,768]{2,1,0:T(8,128)(2,1)} %get-tuple-element.174), channel_id=1, source_target_pairs={{3,2},{2,1},{1,0},{7,6},{6,5},{5,4},{11,10},{10,9},{9,8},{15,14},{... | collective-permute-start | bytes 2949128 | tf_op jit(solution)/shard_map/ppermute | solution.py:855
  435.7 44.2 %collective-permute-start.38 = (bf16[2,320,768]{2,1,0:T(8,128)(2,1)}, bf16[2,320,768]{2,1,0:T(8,128)(2,1)}, u32[]{:S(2)}, u32[]{:S(2)}) collective-permute-start(bf16[2,320,768]{2,1,0:T(8,128)(2,1)} %get-tuple-element.170.refs_0_), channel_id=1, source_target_pairs={{0,1},{1,2},{2,3},{4,5},{5,6},{6,7},{8,9},{9,10},{10,11},{12,13},{... | collective-permute-start | bytes 2949128 | tf_op jit(solution)/shard_map/ppermute | solution.py:854
  439.9 40.0 %collective-permute-start.39 = (bf16[2,320,768]{2,1,0:T(8,128)(2,1)}, bf16[2,320,768]{2,1,0:T(8,128)(2,1)}, u32[]{:S(2)}, u32[]{:S(2)}) collective-permute-start(bf16[2,320,768]{2,1,0:T(8,128)(2,1)} %get-tuple-element.180), channel_id=1, source_target_pairs={{3,2},{2,1},{1,0},{7,6},{6,5},{5,4},{11,10},{10,9},{9,8},{15,14},{... | collective-permute-start | bytes 2949128 | tf_op jit(solution)/shard_map/ppermute | solution.py:855
  485.5 20.8 %all-to-all-start.7 = ((bf16[8,80,768]{2,1,0:T(8,128)(2,1)}), bf16[8,80,768]{2,1,0:T(8,128)(2,1)S(1)}, u32[]{:S(2)}, u32[]{:S(2)}) async-start(bf16[8,80,768]{2,1,0:T(8,128)(2,1)} %shard_map.305.refs_0_), calls=%async_computation.7 | async-start | bytes 1966080 | tf_op jit(solution)/shard_map/all_to_all | solution.py:985
  540.9 20.5 %collective-permute-start.55 = (bf16[512,384]{1,0:T(8,128)(2,1)}, bf16[512,384]{1,0:T(8,128)(2,1)}, u32[]{:S(2)}, u32[]{:S(2)}) collective-permute-start(bf16[512,384]{1,0:T(8,128)(2,1)} %get-tuple-element.246), channel_id=1, source_target_pairs={{0,8},{4,12},{8,0},{12,4},{16,24},{20,28},{24,16},{28,20},{1,9},{5... | collective-permute-start | bytes 1179656 | tf_op jit(solution)/shard_map/ppermute | solution.py:887
  590.6 22.4 %collective-permute-start.65 = (bf16[512,384]{1,0:T(8,128)(2,1)S(1)}, bf16[512,384]{1,0:T(8,128)(2,1)S(1)}, u32[]{:S(2)}, u32[]{:S(2)}) collective-permute-start(bf16[512,384]{1,0:T(8,128)(2,1)S(1)} %pad_maximum_fusion.2), channel_id=1, source_target_pairs={{0,16},{4,20},{8,24},{12,28},{16,0},{20,4},{24,8},{28,12},{1,17},{... | collective-permute-start | bytes 1179656 | tf_op jit(solution)/shard_map/ppermute | solution.py:887
  592.8 20.2 %collective-permute-start.66 = (bf16[512,384]{1,0:T(8,128)(2,1)S(1)}, bf16[512,384]{1,0:T(8,128)(2,1)S(1)}, u32[]{:S(2)}, u32[]{:S(2)}) collective-permute-start(bf16[512,384]{1,0:T(8,128)(2,1)S(1)} %pad_maximum_fusion.2), channel_id=1, source_target_pairs={{0,24},{4,28},{8,16},{12,20},{16,8},{20,12},{24,0},{28,4},{1,25},{... | collective-permute-start | bytes 1179656 | tf_op jit(solution)/shard_map/ppermute | solution.py:887
  (133 other events, 1152.7 us)

commit v5 on v4

--- a/solution.py
+++ b/solution.py
@@ -128,41 +128,55 @@
             jax.ShapeDtypeStruct((batches, length, 1), jnp.int32),
             jax.ShapeDtypeStruct((groups, message, width), BF16),
         ],
-        compiler_params=params(32),
+        compiler_params=params(60),
         cost_estimate=cost(),
     )(lengths, routes.reshape(batches, 1, length), routes.reshape(batches, length, 1), cot)
 
 
-def regroup_kernel(count, inputs, waits, *refs):
+def slot_places(kinds, local, groups, capacity, message):
+    row = iota((1, kinds * local * groups * capacity), 1)
+    slot = lax.rem(row, capacity)
+    row = lax.div(row, capacity)
+    group = lax.rem(row, groups)
+    return group * message + lax.div(row, groups) * capacity + slot
+
+
+def regroup_kernel(back, kinds, local, groups, capacity, message, waits, *refs):
     refs = refs[waits:]
-    move_ref, out_ref = refs[0], refs[-1]
-    total = refs[1][...].astype(F32)
-    for ref in refs[2 : 1 + count]:
+    out_ref = refs[-1]
+    total = refs[0][...].astype(F32)
+    for ref in refs[1:-1]:
         total = total + ref[...].astype(F32)
-    out_ref[...] = dot(move_ref[...], total.astype(BF16).reshape(inputs, -1)).astype(BF16).reshape(out_ref.shape)
-
-
-def regroup(move, arrays, shape, after=()):
-    inputs = move.shape[1]
-    vmem = pl.BlockSpec(memory_space=pltpu.VMEM)
+    places = slot_places(kinds, local, groups, capacity, message)
+    move = one_hot(iota((groups * message, places.shape[1]), 0) == places)
+    if back:
+        rows = dot(move, total.astype(BF16).reshape(places.shape[1], -1))
+    else:
+        rows = t_dot(move, total.astype(BF16).reshape(groups * message, -1))
+    out_ref[...] = rows.astype(BF16).reshape(out_ref.shape)
+
+
+def regroup(back, arrays, shape, kinds, local, groups, capacity, message, after=()):
     return pl.pallas_call(
-        functools.partial(regroup_kernel, len(arrays), inputs, len(after)),
-        in_specs=[ANYWHERE] * len(after) + [vmem] * (1 + len(arrays)),
-        out_specs=vmem,
+        functools.partial(regroup_kernel, back, kinds, local, groups, capacity, message, len(after)),
+        in_specs=[ANYWHERE] * len(after) + [WHOLE] * len(arrays),
+        out_specs=WHOLE,
         out_shape=jax.ShapeDtypeStruct(shape, BF16),
-        compiler_params=params(32),
+        compiler_params=params(60),
         cost_estimate=cost(),
-    )(*after, move, *arrays)
+    )(*after, *arrays)
 
 
 def regroup_gated_kernel(capacity, *refs):
-    move_ref, in_ref, out_ref = refs[-3:]
+    in_ref, out_ref = refs[-2:]
     groups, message, width = in_ref.shape
-    total = move_ref.shape[0]
+    total = out_ref.shape[0] - 16
     local = total // (groups * capacity)
     rows = groups * capacity
     flat = in_ref[...].reshape(groups * message, width)
-    out_ref[:total, :] = dot(move_ref[...], flat).astype(BF16)
+    places = slot_places(1, local, groups, capacity, message)
+    move = one_hot(iota((groups * message, total), 0) == places)
+    out_ref[:total, :] = t_dot(move, flat).astype(BF16)
     place = iota((message, 128), 0)
     lane = iota((message, 128), 1)
     columns = []
@@ -175,7 +189,7 @@
         wide = iota((message, 128), 1)
         columns.append(jnp.where(wide == 0, parts[0], jnp.where(wide == 1, parts[1], jnp.where(wide == 2, parts[2], 0.0))))
     column = jnp.concatenate(columns, axis=0).astype(BF16)
-    moved = dot(move_ref[...], column)
+    moved = t_dot(move, column)
     place = iota((rows, 128), 0)
     lane = iota((rows, 128), 1)
     lines = []
@@ -189,17 +203,16 @@
     out_ref[total:, :] = jnp.concatenate(lines, axis=0).astype(BF16)
 
 
-def regroup_gated(move, slots, capacity, after=()):
+def regroup_gated(slots, rows, capacity, after=()):
     width = slots.shape[-1]
-    vmem = pl.BlockSpec(memory_space=pltpu.VMEM)
     return pl.pallas_call(
         functools.partial(regroup_gated_kernel, capacity),
-        in_specs=[ANYWHERE] * len(after) + [vmem] * 2,
-        out_specs=vmem,
-        out_shape=jax.ShapeDtypeStruct((move.shape[0] + 16, width), BF16),
-        compiler_params=params(32),
+        in_specs=[ANYWHERE] * len(after) + [WHOLE],
+        out_specs=WHOLE,
+        out_shape=jax.ShapeDtypeStruct((rows + 16, width), BF16),
+        compiler_params=params(60),
         cost_estimate=cost(),
-    )(*after, move, slots)
+    )(*after, slots)
 
 
 def band_bias(vector_ref, head):
@@ -272,7 +285,7 @@
             pltpu.VMEM((2, length, length), BF16),
             pltpu.VMEM((PAIR, length), F32),
         ],
-        compiler_params=params(48),
+        compiler_params=params(60),
         cost_estimate=cost(),
     )(*after, counts, tokens, gain, wq, wk, wv, vector)
 
@@ -340,7 +353,7 @@
             jax.ShapeDtypeStruct((length, experts), F32),
         ]
         + [jax.ShapeDtypeStruct((groups, message, width), BF16)] * (2 if gated else 1),
-        compiler_params=params(48),
+        compiler_params=params(60),
         cost_estimate=cost(),
     )(*after, tokens, cot, mixed, wo, gain_ffn, w_router, srow, rcol)
 
@@ -432,7 +445,7 @@
         + [mat(total, hidden), mat(total, hidden), mat(total, width), mat(total, width)],
         out_shape=[jax.ShapeDtypeStruct((2, mine * rows, width), BF16)] * planes
         + [kept(hidden), kept(hidden), kept(width), kept(width)],
-        compiler_params=params(48),
+        compiler_params=params(60),
         cost_estimate=cost(),
     )(*after, plane, *arrays, w_inner, w_outer)
 
@@ -466,7 +479,7 @@
             jax.ShapeDtypeStruct((local, width, hidden), F32),
         ],
         input_output_aliases={behind + k: k for k in range(len(past))},
-        compiler_params=params(48),
+        compiler_params=params(60),
         cost_estimate=cost(),
     )(*after, *xs, *cs, *acts, *pres, *past)
 
@@ -475,8 +488,15 @@
     refs = refs[waits:]
     len_ref, low_ref, high_ref, scol_ref, rcol_ref, res_ref, probs_ref, cot_ref, gffn_ref, wr_ref, wo_ref, mixed_ref, *refs = refs
     past_ref = refs.pop(0) if batch else None
-    layer_ref, resgrad_ref, mgrad_ref, shared_ref = refs
-    length, width = cot_ref.shape[2:]
+    layer_ref, resgrad_ref, mgrad_ref, shared_ref, *buffers, sems = refs
+    fetched = [res_ref, cot_ref.at[batch, 0], mixed_ref, wo_ref] + ([past_ref] if batch else [])
+    copies = [pltpu.make_async_copy(ref, buffer, sems.at[k]) for k, (ref, buffer) in enumerate(zip(fetched, buffers))]
+    for copy in copies:
+        copy.start()
+    res_ref, cot_ref, mixed_ref, wo_ref = buffers[:4]
+    if batch:
+        past_ref = buffers[4]
+    length, width = cot_ref.shape
     experts = wr_ref.shape[0]
     groups, message, _ = low_ref.shape
     valid = iota((length, 1), 0) < len_ref[batch]
@@ -490,12 +510,14 @@
         in_part = dot(one_hot(places == jnp.where(place < 0, -1, place + half)), rows)
         returned = out_part if returned is None else returned + out_part
         input_grad = in_part if input_grad is None else input_grad + in_part
+    copies[0].wait()
+    copies[1].wait()
     residual = res_ref[...]
     probs = probs_ref[...]
     chosen = iota(probs.shape, 1) == rcol_ref[0]
     gate = jnp.sum(jnp.where(chosen, probs, 0.0), axis=-1, keepdims=True)
     layer_ref[...] = jnp.where(valid, residual + gate * returned, 0.0).astype(BF16)
-    out_grad = jnp.where(valid, cot_ref[0, 0].astype(F32), 0.0)
+    out_grad = jnp.where(valid, cot_ref[...].astype(F32), 0.0)
     gate_grad = jnp.sum(out_grad * returned, axis=-1, keepdims=True)
     prob_grad = jnp.where(chosen, gate_grad, 0.0)
     logit_grad = (probs * (prob_grad - jnp.sum(probs * prob_grad, axis=-1, keepdims=True))).astype(BF16)
@@ -512,6 +534,8 @@
                 rows = rows + past_ref[here, :]
             shared_ref[here, :] = rows.astype(shared_ref.dtype)
 
+    for copy in copies[2:]:
+        copy.wait()
     share(width, t_dot(logit_grad, routed))
     routed_grad = dot(logit_grad, wr_ref[...]) + input_grad
     gain_part = jnp.sum(routed_grad * scaled, axis=0, keepdims=True)
@@ -537,8 +561,9 @@
         functools.partial(combine_kernel, per, batch, len(after)),
         grid=(1,),
         in_specs=[ANYWHERE] * len(after)
-        + [SCALARS, WHOLE, WHOLE, batch_block(scol, batch), batch_block(rcol, batch), WHOLE, WHOLE, batch_block(cot, batch)]
-        + [WHOLE] * (4 + len(past)),
+        + [SCALARS, WHOLE, WHOLE, batch_block(scol, batch), batch_block(rcol, batch), ANYWHERE, WHOLE, ANYWHERE]
+        + [WHOLE] * 2
+        + [ANYWHERE] * (2 + len(past)),
         out_specs=[WHOLE] * 4,
         out_shape=[
             jax.ShapeDtypeStruct((length, width), BF16),
@@ -546,7 +571,13 @@
             jax.ShapeDtypeStruct((PAIRS, length, PAIR), BF16),
             jax.ShapeDtypeStruct((shared, width // 2), BF16 if last else F32),
         ],
-        compiler_params=params(48),
+        scratch_shapes=[
+            pltpu.VMEM(residual.shape, residual.dtype),
+            pltpu.VMEM((length, width), BF16),
+            *(pltpu.VMEM(array.shape, array.dtype) for array in (mixed, w_output, *past)),
+            pltpu.SemaphoreType.DMA((4 + len(past),)),
+        ],
+        compiler_params=params(60),
         cost_estimate=cost(),
     )(
         *after, counts, low, high, scol, rcol, residual, probs, cot, gain_ffn, w_router, w_output, mixed, *past
@@ -734,53 +765,49 @@
             pltpu.SemaphoreType.DMA((len(buffers),)),
             pltpu.SemaphoreType.DMA((5,)),
         ],
-        compiler_params=params(56),
+        compiler_params=params(60),
         cost_estimate=cost(),
     )(*after, counts, qkv, lse, vector, selector, mixed_grad, tokens, gain, wq, wk, wv, *past, *more)
 
 
-def unpack_kernel(early, experts, side_ref, mine_ref, other_ref, *refs):
-    mine, other = mine_ref[...], other_ref[...]
-    second = side_ref[0] == 1
-    rows = jnp.concatenate([jnp.where(second, other, mine), jnp.where(second, mine, other)], axis=0).astype(F32)
+def unpack_kernel(early, side_ref, first_ref, first_other_ref, second_ref, second_other_ref, *refs):
+    q_ref, k_ref, v_ref, output_ref, router_ref, gain_f_ref, gain_a_ref, bias_ref = refs
+    swapped = side_ref[0] == 1
+
+    def whole(mine_ref, other_ref):
+        mine, other = mine_ref[...], other_ref[...]
+        parts = [jnp.where(swapped, other, mine), jnp.where(swapped, mine, other)]
+        return jnp.concatenate(parts, axis=0).astype(F32)
+
+    rows = whole(first_ref, first_other_ref)
+    width = 2 * rows.shape[1]
     half = rows.shape[1]
-    width = 2 * half
-    if not early:
-        q_ref, k_ref, v_ref, gain_ref, bias_ref = refs[3:]
-        offset = 0
-        gain_ref[...] = jnp.concatenate([rows[3 * width : 3 * width + 1], rows[3 * width + 1 : 3 * width + 2]], axis=1)
-        bias_ref[...] = rows[3 * width + 8 : 3 * width + 8 + HEADS, :BUCKETS]
-    else:
-        q_ref, k_ref, v_ref, output_ref, router_ref, gain_ref = refs
-        offset = 2 * early
-        output_ref[...] = jnp.concatenate([rows[:width], rows[early : early + width]], axis=1)
-        last = early - 16
-        router_ref[...] = jnp.concatenate([rows[width:last], rows[early + width : early + last]], axis=1)
-        gain_ref[...] = jnp.concatenate([rows[last : last + 1], rows[early + last : early + last + 1]], axis=1)
+    last = early - 16
+    output_ref[...] = jnp.concatenate([rows[:width], rows[early : early + width]], axis=1)
+    router_ref[...] = jnp.concatenate([rows[width:last], rows[early + width : early + last]], axis=1)
+    gain_f_ref[...] = jnp.concatenate([rows[last], rows[early + last]])
     for k, ref in enumerate((q_ref, k_ref, v_ref)):
-        ref[...] = rows[offset + k * width : offset + (k + 1) * width]
-
-
-def unpack(early, experts, side, mine, other, past):
-    half = mine.shape[1]
-    width = 2 * half
+        ref[:, :half] = rows[2 * early + k * width : 2 * early + (k + 1) * width]
+    rows = whole(second_ref, second_other_ref)
+    gain_a_ref[...] = jnp.concatenate([rows[3 * width], rows[3 * width + 1]])
+    bias_ref[...] = rows[3 * width + 8 : 3 * width + 8 + HEADS, :BUCKETS]
+    for k, ref in enumerate((q_ref, k_ref, v_ref)):
+        ref[:, half:] = rows[k * width : (k + 1) * width]
+
+
+def unpack(early, experts, side, first, first_other, second, second_other):
+    width = 2 * first.shape[1]
     matrix = jax.ShapeDtypeStruct((width, width), F32)
-    line = jax.ShapeDtypeStruct((1, width), F32)
-    columns = pl.BlockSpec((width, half), lambda _: (0, 0 if early else 1))
-    if early:
-        more = [matrix, jax.ShapeDtypeStruct((experts, width), F32), line]
-    else:
-        more = [line, jax.ShapeDtypeStruct((HEADS, BUCKETS), F32)]
+    line = jax.ShapeDtypeStruct((width,), F32)
     return pl.pallas_call(
-        functools.partial(unpack_kernel, early, experts),
-        grid=(1,),
-        in_specs=[SCALARS, WHOLE, WHOLE] + [ANYWHERE] * len(past),
-        out_specs=[columns] * 3 + [WHOLE] * len(more),
-        out_shape=[matrix] * 3 + more,
-        input_output_aliases={3 + k: k for k in range(len(past))},
-        compiler_params=params(56),
+        functools.partial(unpack_kernel, early),
+        in_specs=[SCALARS] + [WHOLE] * 4,
+        out_specs=[WHOLE] * 8,
+        out_shape=[matrix] * 4
+        + [jax.ShapeDtypeStruct((experts, width), F32), line, line, jax.ShapeDtypeStruct((HEADS, BUCKETS), F32)],
+        compiler_params=params(60),
         cost_estimate=cost(),
-    )(side, mine, other, *past)
+    )(side, first, first_other, second, second_other)
 
 
 def upward(planes, first, last):
@@ -932,14 +959,6 @@
     offsets = np.where(place < 2 * length - ROWS, place, place - 2 * length) - (length - ROWS)
     offsets = np.clip(offsets, -(length - 1), length - 1)
     return (offset_bucket(offsets)[:, None] == np.arange(BUCKETS)[None, :]).astype(np.float32)
-
-
-def moves(groups, local, capacity, message, kinds=1):
-    kind, expert, group, slot = np.meshgrid(
-        np.arange(kinds), np.arange(local), np.arange(groups), np.arange(capacity), indexing="ij"
-    )
-    source = (group * message + (kind * local + expert) * capacity + slot).reshape(-1)
-    return (source[:, None] == np.arange(groups * message)[None, :]).astype(jnp.bfloat16)
 
 
 def shards(
@@ -967,10 +986,7 @@
     per = local * capacity
     rows = groups * capacity
     message = padded(per)
-    move = jnp.asarray(moves(groups, local, capacity, message))
-    move_gated = jnp.asarray(moves(groups, local, capacity, message + 16))
-    move_pair = jnp.asarray(moves(groups, local // 2, capacity, message, 2))
-    move_back = jnp.asarray(moves(groups, local // 2, capacity, message, 2).T)
+    in_groups = (groups, capacity, message)
     selector = jnp.asarray(offset_selector(length))
     vector = lax.dot_general(
         bucket_head_bias, selector, (((0,), (1,)), ((), ())), precision=lax.Precision.HIGHEST
@@ -985,10 +1001,14 @@
         return lax.all_to_all(values, "expert", split_axis=0, concat_axis=0, tiled=True)
 
     def leaving(values, *after):
-        return regroup(move_pair, [to_groups(values)], (2, local // 2 * rows, width), after)
+        return regroup(False, [to_groups(values)], (2, local // 2 * rows, width), 2, local // 2, *in_groups, after)
+
+    def returning(chain, *after):
+        shape = (groups, message, width)
+        return regroup(True, chain.scattered(), shape, 2, local // 2, *in_groups, after)
 
     def arriving(chain, *after):
-        return to_groups(regroup(move_back, chain.scattered(), (groups, message, width), after))
+        return to_groups(returning(chain, *after))
 
     def attend(b, *after):
         return attention_forward(b, after, counts, tokens, gain_a, w_query, w_key, w_value, vector)
@@ -1059,10 +1079,10 @@
 
     forward = [attend(0, cot_slots)]
     routed = [routing(0)]
-    grads = regroup(move, [to_groups(cot_slots)], (local * rows, width), (routed[0][2],))
+    grads = regroup(False, [to_groups(cot_slots)], (local * rows, width), 1, local, *in_groups, (routed[0][2],))
     grad_chain = Chain(planes, grads)
     grad_chain.send()
-    inputs = regroup_gated(move_gated, to_groups(routed[0][2]), capacity, (grads,))
+    inputs = regroup_gated(to_groups(routed[0][2]), local * rows, capacity, (grads,))
     input_chain = Chain(planes, inputs)
     input_chain.send()
     forward.append(attend(1, inputs, grad_chain.up, grad_chain.down))
@@ -1134,10 +1154,10 @@
             first_part, *more = back_half(
                 b - 1, 0, (high_chain.mixed,), mixed_grad, (early_part,) if b > 1 else ()
             )
-            low = regroup(move_back, low_chain.scattered(), (groups, message, width), (first_part,))
+            low = returning(low_chain, first_part)
             second_part, token_grad = back_half(b - 1, 1, (low,), mixed_grad, (*more, res_grad))
             low = to_groups(low)
-            high = regroup(move_back, high_chain.scattered(), (groups, message, width), (second_part, low))
+            high = returning(high_chain, second_part, low)
             totals = grads_half(1, (high,), totals)
             high = to_groups(high)
         layer_rows.append(layer)
@@ -1150,23 +1170,21 @@
     second_part, token_grad = back_half(batches - 1, 1, (first_half,), mixed_grad, (*more, res_grad))
     mine, other = sum_everywhere(first_half)
     mine_second, other_second = sum_everywhere(share_half(second_part))
-    early_done = unpack(early_rows, experts, side, mine, other, ())
     layer_rows.append(layer)
     token_grads.append(token_grad)
-    *attended, output_grad, router_grad, gain_f_grad = early_done
-    query_grad, key_grad, value_grad, gain_a_grad, bias_grad = unpack(
-        0, experts, side, mine_second, other_second, attended
+    query_grad, key_grad, value_grad, output_grad, router_grad, gain_f_grad, gain_a_grad, bias_grad = unpack(
+        early_rows, experts, side, mine, other, mine_second, other_second
     )
     return (
         jnp.stack(layer_rows)[:, None],
         jnp.stack(token_grads)[:, None],
-        gain_a_grad[0],
+        gain_a_grad,
         query_grad,
         key_grad,
         value_grad,
         output_grad,
         bias_grad.T,
-        gain_f_grad[0],
+        gain_f_grad,
         router_grad.T,
         totals[1],
         totals[0],

time: 662 us -> 649 us (0.980); the launches traced: 651 us -> 645 us
  local copies, waits for them, and re-layouts: 52.6 us -> 25.7 us
  starting transfers between devices: 158 us -> 176 us
  Pallas kernels: 252 us -> 266 us
  waiting for transfers between devices: 173 us -> 165 us
    ppermute x20, waiting for transfers between devices: 110 us -> 68.3 us  [send(): self.down = lax.ppermute(self.down, 'hidden', downward(planes, first, last))]
    ppermute x20, waiting for transfers between devices: 12 us -> 44 us  [send(): self.up = lax.ppermute(self.up, 'hidden', upward(planes, first, last))]
    unnamed x210 -> x114, local copies, waits for them, and re-layouts: 46.5 us -> 17.7 us
    ppermute x20, starting transfers between devices: 27.9 us -> 40.6 us  [send(): self.down = lax.ppermute(self.down, 'hidden', downward(planes, first, last))]
    pallas_call x9 -> x8, Pallas kernels: 27.6 us -> 31.1 us  [the longest x7 24.8 us: regroup(): pl.pallas_call(functools.partial(regroup_kernel, back, kinds, local, grou...]
  transfers between devices with their start and end apart: 76 -> 76, of which waited for: 33 -> 33; matrix products, arithmetic and copies ran while one was open for 2% -> 2% of each run, Pallas kernels for 34% -> 36%
where the time goes in v5:
time: 649 us; the launch traced here: 645 us
  Pallas kernels  266 us (41%)
  starting transfers between devices  176 us (27%)
  waiting for transfers between devices  165 us (25%)
  local copies, waits for them, and re-layouts  25.7 us (4%)
  other arithmetic  9.92 us (2%)
    ppermute x20, waiting for transfers between devices, send(): self.down = lax.ppermute(self.down, 'hidden', downward(planes, first, last))  68.3 us
    ppermute x20, starting transfers between devices, send(): self.up = lax.ppermute(self.up, 'hidden', upward(planes, first, last))  64.5 us
    pallas_call x4, Pallas kernels, attention_backward(): pl.pallas_call(functools.partial(attn_back_kernel, batch, which, len(afte...  57.8 us
    pallas_call x4, Pallas kernels, experts_half(): pl.pallas_call(functools.partial(expert_kernel, planes, gated, first, len...  56 us
    ppermute x20, waiting for transfers between devices, send(): self.up = lax.ppermute(self.up, 'hidden', upward(planes, first, last))  44 us
    ppermute x20, starting transfers between devices, send(): self.down = lax.ppermute(self.down, 'hidden', downward(planes, first, last))  40.6 us
    ppermute x28, waiting for transfers between devices, swap(): lax.ppermute(values, axis, [(k, k ^ distance) for k in range(lax.axis_siz...  36.7 us
    ppermute x28, starting transfers between devices, swap(): lax.ppermute(values, axis, [(k, k ^ distance) for k in range(lax.axis_siz...  36.3 us
  transfers between devices with their start and end apart: 76, of which 33 were waited for; matrix products, arithmetic and copies ran while one was open for 2% of the time, Pallas kernels for 36%

profile of v5, /device:TPU:0, one launch (start us, length us, event | category | flops | bytes accessed | tf_op | source)
XLA Modules:
  0.0 645.3 jit_solution(10859022553491082995)
XLA Ops:
  6.2 5.2 all-to-all-start
  13.2 15.3 %shard_map.239 = (bf16[3,6,512,128]{3,2,1,0:T(8,128)(2,1)}, bf16[6,512,128]{2,1,0:T(8,128)(2,1)}, f32[512,128]{1,0:T(8,128)}) custom-call(bf16[8,80,768]{2,1,0:T(8,128)(2,1)} %get-tuple-element.112.refs_0_, s32[2]{0:T(128)} %bitcast.94, bf16[2,1,512,768]{3,2,1,0:T(8,128)(2,1)} %refs_7_.7, f32[1,768]{1,0:T(1,128)} %broadcast_in_dim.26.refs_3_.refs_5_.refs_8_.refs_7_, ...), custom_call_target="tpu_custom_call" | custom-call | flops 1 | bytes 1 | tf_op jit(solution)/shard_map/pallas_call | solution.py:273
  29.0 5.6 shard_map.240
  34.6 4.2 all-to-all-start.1
  46.8 8.8 %all-to-all-done.1.refs_1_ = bf16[8,96,768]{2,1,0:T(8,128)(2,1)S(1)} async-done(((bf16[8,96,768]{2,1,0:T(8,128)(2,1)}), bf16[8,96,768]{2,1,0:T(8,128)(2,1)S(1)}, u32[]{:S(2)}, u32[]{:S(2)}) %all-to-all-start.1) | async-done | bytes 1179680 | tf_op jit(solution)/shard_map/all_to_all | solution.py:1001
  73.9 15.3 %shard_map.243 = (bf16[3,6,512,128]{3,2,1,0:T(8,128)(2,1)}, bf16[6,512,128]{2,1,0:T(8,128)(2,1)}, f32[512,128]{1,0:T(8,128)}) custom-call(bf16[656,768]{1,0:T(8,128)(2,1)} %shard_map.242.refs_0_.refs_3_.refs_17_, bf16[640,768]{1,0:T(8,128)(2,1)} %copy-done.39, bf16[640,768]{1,0:T(8,128)(2,1)} %collective-permute-done.3.refs_2_.refs_11_, s32[2]{0:T(128)} %bitcast.95, ...), custom_call_target="tpu_custom_call" | custom-call | flops 1 | bytes 1 | tf_op jit(solution)/shard_map/pallas_call | solution.py:273
  89.2 4.8 collective-permute-done.1.refs_1_
  97.6 17.4 %collective-permute-done.8.refs_1_.refs_12_ = bf16[640,768]{1,0:T(8,128)(2,1)} collective-permute-done((bf16[640,768]{1,0:T(8,128)(2,1)}, bf16[640,768]{1,0:T(8,128)(2,1)}, u32[]{:S(2)}, u32[]{:S(2)}) %collective-permute-start.8) | collective-permute-done | bytes 983072 | tf_op jit(solution)/shard_map/ppermute | solution.py:882
  116.3 6.6 %shard_map.245 = (f32[512,768]{1,0:T(8,128)}, f32[512,64]{1,0:T(8,128)}, bf16[8,80,768]{2,1,0:T(8,128)(2,1)}, bf16[8,80,768]{2,1,0:T(8,128)(2,1)}) custom-call(bf16[640,768]{1,0:T(8,128)(2,1)} %collective-permute-done.6.refs_0_.refs_15_, bf16[640,768]{1,0:T(8,128)(2,1)} %collective-permute-done.8.refs_1_.refs_12_, bf16[2,1,512,768]{3,2,1,0:T(8,128)(2,1)} %refs_7_.7, ...), custom_call_target="tpu_custom_call" | custom-call | flops 1 | bytes 1 | tf_op jit(solution)/shard_map/pallas_call | solution.py:343
  122.9 4.3 all-to-all-start.2
  127.1 9.4 %collective-permute-done.5.refs_1_.refs_5_.refs_19_ = bf16[656,768]{1,0:T(8,128)(2,1)S(1)} collective-permute-done((bf16[656,768]{1,0:T(8,128)(2,1)}, bf16[656,768]{1,0:T(8,128)(2,1)S(1)}, u32[]{:S(2)}, u32[]{:S(2)}) %collective-permute-start.5) | collective-permute-done | bytes 1007648 | tf_op jit(solution)/shard_map/ppermute | solution.py:882
  141.9 4.2 all-to-all-start.3
  146.2 11.3 %collective-permute-done.9.refs_3_.refs_13_ = bf16[640,768]{1,0:T(8,128)(2,1)S(1)} collective-permute-done((bf16[640,768]{1,0:T(8,128)(2,1)}, bf16[640,768]{1,0:T(8,128)(2,1)S(1)}, u32[]{:S(2)}, u32[]{:S(2)}) %collective-permute-start.9) | collective-permute-done | bytes 983072 | tf_op jit(solution)/shard_map/ppermute | solution.py:882
  167.8 4.6 collective-permute-start.22
  172.4 6.8 %collective-permute-done.12.refs_6_.refs_20_ = bf16[656,768]{1,0:T(8,128)(2,1)} collective-permute-done((bf16[656,768]{1,0:T(8,128)(2,1)S(1)}, bf16[656,768]{1,0:T(8,128)(2,1)}, u32[]{:S(2)}, u32[]{:S(2)}) %collective-permute-start.12) | collective-permute-done | bytes 1007648 | tf_op jit(solution)/shard_map/ppermute | solution.py:882
  180.5 14.0 %shard_map.248 = (bf16[2,320,768]{2,1,0:T(8,128)(2,1)}, bf16[2,320,768]{2,1,0:T(8,128)(2,1)}, bf16[2,320,768]{2,1,0:T(8,128)(2,1)}, bf16[2,320,768]{2,1,0:T(8,12...) custom-call(bf16[2,320,768]{2,1,0:T(8,128)(2,1)} %shard_map.246.refs, ...), custom_call_target="tpu_custom_call" | custom-call | flops 1 | bytes 1 | tf_op jit(solution)/shard_map/pallas_call | solution.py:440
  194.6 5.7 collective-permute-done.11.down_ref.refs_4_.refs_11_
  207.9 13.9 %collective-permute-start.15 = (bf16[2,320,768]{2,1,0:T(8,128)(2,1)}, bf16[2,320,768]{2,1,0:T(8,128)(2,1)S(1)}, u32[]{:S(2)}, u32[]{:S(2)}) collective-permute-start(bf16[2,320,768]{2,1,0:T(8,128)(2,1)} %get-tuple-element.124), channel_id=1, source_target_pairs={{3,2},{2,1},{1,0},{7,6},{6,5},{5,4},{11,10},{10,9},{9,8},{15,14},{... | collective-permute-start | bytes 2949128 | tf_op jit(solution)/shard_map/ppermute | solution.py:882
  221.8 13.9 %shard_map.254 = (bf16[2,320,768]{2,1,0:T(8,128)(2,1)}, bf16[2,320,768]{2,1,0:T(8,128)(2,1)}, bf16[2,320,768]{2,1,0:T(8,128)(2,1)}, bf16[2,320,768]{2,1,0:T(8,12...) custom-call(bf16[2,320,768]{2,1,0:T(8,128)(2,1)} %shard_map.246.refs, ...), custom_call_target="tpu_custom_call" | custom-call | flops 1 | bytes 1 | tf_op jit(solution)/shard_map/pallas_call | solution.py:440
  239.3 4.6 collective-permute-start.24
  246.5 4.6 collective-permute-start.16
  252.4 13.6 %collective-permute-done.24.up_ref.refs_10_.refs_17_ = bf16[2,320,768]{2,1,0:T(8,128)(2,1)S(1)} collective-permute-done((bf16[2,320,768]{2,1,0:T(8,128)(2,1)S(1)}, bf16[2,320,768]{2,1,0:T(8,128)(2,1)S(1)}, u32[]{:S(2)}, u32[]{:S(2)}) %collective-permute-start.24) | collective-permute-done | bytes 983072 | tf_op jit(solution)/shard_map/ppermute | solution.py:881
  266.0 4.5 collective-permute-done.25.down_ref.refs_7_.refs_14_
  275.6 11.5 %collective-permute-done.16.up_ref.refs_9_.refs_16_ = bf16[2,320,768]{2,1,0:T(8,128)(2,1)S(1)} collective-permute-done((bf16[2,320,768]{2,1,0:T(8,128)(2,1)S(1)}, bf16[2,320,768]{2,1,0:T(8,128)(2,1)S(1)}, u32[]{:S(2)}, u32[]{:S(2)}) %collective-permute-start.16) | collective-permute-done | bytes 983072 | tf_op jit(solution)/shard_map/ppermute | solution.py:881
  287.1 4.5 collective-permute-done.17.down_ref.refs_6_.refs_13_
  297.8 14.1 %shard_map.252 = (bf16[2,320,768]{2,1,0:T(8,128)(2,1)}, bf16[2,320,768]{2,1,0:T(8,128)(2,1)}, bf16[2,320,768]{2,1,0:T(8,128)(2,1)}, bf16[2,320,768]{2,1,0:T(8,12...) custom-call(bf16[2,320,768]{2,1,0:T(8,128)(2,1)} %get-tuple-element., ...), custom_call_target="tpu_custom_call" | custom-call | flops 1 | bytes 1 | tf_op jit(solution)/shard_map/pallas_call | solution.py:440
  311.9 5.5 collective-permute-start.18
  323.7 5.6 collective-permute-done.30.refs_3_.refs_2_
  331.8 14.1 %shard_map.262 = (bf16[2,320,768]{2,1,0:T(8,128)(2,1)}, bf16[2,320,768]{2,1,0:T(8,128)(2,1)}, bf16[2,320,768]{2,1,0:T(8,128)(2,1)}, bf16[2,320,768]{2,1,0:T(8,12...) custom-call(bf16[2,320,768]{2,1,0:T(8,128)(2,1)} %get-tuple-element., ...), custom_call_target="tpu_custom_call" | custom-call | flops 1 | bytes 1 | tf_op jit(solution)/shard_map/pallas_call | solution.py:440
  355.9 5.3 collective-permute-start.20
  361.2 10.2 %collective-permute-done.28.refs_1_.refs_0_ = bf16[2,320,768]{2,1,0:T(8,128)(2,1)S(1)} collective-permute-done((bf16[2,320,768]{2,1,0:T(8,128)(2,1)}, bf16[2,320,768]{2,1,0:T(8,128)(2,1)S(1)}, u32[]{:S(2)}, u32[]{:S(2)}) %collective-permute-start.28) | collective-permute-done | bytes 983072 | tf_op jit(solution)/shard_map/ppermute | solution.py:881
  376.9 4.2 all-to-all-start.4
  381.1 14.5 %shard_map.263 = (f32[8,768,768]{2,1,0:T(8,128)}, f32[8,768,768]{2,1,0:T(8,128)}) custom-call(bf16[2,320,768]{2,1,0:T(8,128)(2,1)} %get-tuple-element.133.refs_0_, bf16[4,320,768]{2,1,0:T(8,128)(2,1)} %get-tuple-element.155.refs_1_, bf16[4,320,768]{2,1,0:T(8,128)(2,1)} %get-tuple-element.156.refs_2_, bf16[4,320,768]{2,1,0:T(8,128)(2,1)} %get-tuple-element.157.refs_3_, ...), custom_call_target="tpu_custom_call" | custom-call | flops 1 | bytes 1 | tf_op jit(solution)/shard_map/pallas_call | solution.py:469
  399.2 5.0 collective-permute-start.34
  409.7 4.5 all-to-all-start.5
  418.1 4.7 collective-permute-start.36
  424.1 4.8 all-to-all-done.5.refs_2_
  429.0 9.2 %shard_map.261 = (bf16[512,768]{1,0:T(8,128)(2,1)}, f32[512,768]{1,0:T(8,128)}, bf16[6,512,128]{2,1,0:T(8,128)(2,1)}, f32[1696,384]{1,0:T(8,128)}) custom-call(bf16[2,320,768]{2,1,0:T(8,128)(2,1)} %get-tuple-element.146.refs_0_, s32[2]{0:T(128)} %bitcast.96, bf16[8,80,768]{2,1,0:T(8,128)(2,1)} %all-to-all-done.5.refs_2_, bf16[8,80,768]{2,1,0:T(8,128)(2,1)} %copy-done.13, ...), custom_call_target="tpu_custom_call" | custom-call | flops 1 | bytes 1 | tf_op jit(solution)/shard_map/pallas_call | solution.py:560
  447.9 14.3 %shard_map.266 = (f32[2304,384]{1,0:T(8,128)}, f32[16,1024]{1,0:T(8,128)}, f32[512,768]{1,0:T(8,128)}) custom-call(bf16[2,320,768]{2,1,0:T(8,128)(2,1)} %copy-done.32, s32[2]{0:T(128)} %bitcast.97, bf16[3,6,512,128]{3,2,1,0:T(8,128)(2,1)} %get-tuple-element.168.refs_2_, f32[512,128]{1,0:T(8,128)} %get-tuple-element.169.refs_3_, ...), custom_call_target="tpu_custom_call" | custom-call | flops 1 | bytes 1 | tf_op jit(solution)/shard_map/pallas_call | solution.py:740
  469.6 14.7 %shard_map.268 = (f32[2560,384]{1,0:T(8,128)}, bf16[512,768]{1,0:T(8,128)(2,1)}) custom-call(bf16[8,80,768]{2,1,0:T(8,128)(2,1)} %shard_map.267.refs_0_, s32[2]{0:T(128)} %bitcast.98, bf16[3,6,512,128]{3,2,1,0:T(8,128)(2,1)} %get-tuple-element.168.refs_2_, f32[512,128]{1,0:T(8,128)} %get-tuple-element.169.refs_3_, ...), custom_call_target="tpu_custom_call" | custom-call | flops 1 | bytes 1 | tf_op jit(solution)/shard_map/pallas_call | solution.py:740
  493.1 14.4 %shard_map.270 = (f32[8,768,768]{2,1,0:T(8,128)}, f32[8,768,768]{2,1,0:T(8,128)}) custom-call(bf16[8,80,768]{2,1,0:T(8,128)(2,1)} %shard_map.269.refs_0_, bf16[4,320,768]{2,1,0:T(8,128)(2,1)} %get-tuple-element.178.refs_1_, bf16[4,320,768]{2,1,0:T(8,128)(2,1)} %get-tuple-element.179.refs_2_, ...), custom_call_target="tpu_custom_call", output_to_operand_aliasing={{0}: (9, {}), {1}: (10, {})} | custom-call | flops 1 | bytes 1 | tf_op jit(solution)/shard_map/pallas_call | solution.py:469
  508.8 8.7 %shard_map.271 = (bf16[512,768]{1,0:T(8,128)(2,1)}, f32[512,768]{1,0:T(8,128)}, bf16[6,512,128]{2,1,0:T(8,128)(2,1)}, bf16[1696,384]{1,0:T(8,128)(2,1)}) custom-call(f32[8,768,768]{2,1,0:T(8,128)} %get-tuple-element.235.refs_0_, s32[2]{0:T(128)} %bitcast.99, bf16[8,80,768]{2,1,0:T(8,128)(2,1)} %copy-done.40, bf16[8,80,768]{2,1,0:T(8,128)(2,1)} %copy-done.43, ...), custom_call_target="tpu_custom_call" | custom-call | flops 1 | bytes 1 | tf_op jit(solution)/shard_map/pallas_call | solution.py:560
  517.5 14.1 %shard_map.272 = (bf16[4096,384]{1,0:T(8,128)(2,1)}, f32[16,1024]{1,0:T(8,128)}, f32[512,768]{1,0:T(8,128)}) custom-call(s32[2]{0:T(128)} %bitcast.100, bf16[3,6,512,128]{3,2,1,0:T(8,128)(2,1)} %get-tuple-element.193.refs_1_.refs_2_, f32[512,128]{1,0:T(8,128)} %get-tuple-element.194.refs_2_.refs_3_, ...), custom_call_target="tpu_custom_call" | custom-call | flops 1 | bytes 1 | tf_op jit(solution)/shard_map/pallas_call | solution.py:740
  542.8 14.8 %shard_map.273 = (bf16[2560,384]{1,0:T(8,128)(2,1)}, bf16[512,768]{1,0:T(8,128)(2,1)}) custom-call(bf16[2048,384]{1,0:T(8,128)(2,1)} %copy-done.37, s32[2]{0:T(128)} %bitcast.101, bf16[3,6,512,128]{3,2,1,0:T(8,128)(2,1)} %get-tuple-element.193.refs_1_.refs_2_, f32[512,128]{1,0:T(8,128)} %get-tuple-element.194.refs_2_.refs_3_, ...), custom_call_target="tpu_custom_call" | custom-call | flops 1 | bytes 1 | tf_op jit(solution)/shard_map/pallas_call | solution.py:740
  567.7 7.6 %collective-permute-done.45 = bf16[128,384]{1,0:T(8,128)(2,1)S(1)} collective-permute-done((bf16[128,384]{1,0:T(8,128)(2,1)S(1)}, bf16[128,384]{1,0:T(8,128)(2,1)S(1)}, u32[]{:S(2)}, u32[]{:S(2)}) %collective-permute-start.45) | collective-permute-done | bytes 98336 | tf_op jit(solution)/shard_map/ppermute | solution.py:914
  606.4 4.8 collective-permute-done.51
  627.4 4.7 collective-permute-done.65
  638.7 6.4 shard_map.274
  (284 shorter events, 222.7 us)
Async XLA Ops:
  6.2 28.5 %all-to-all-start = ((bf16[8,80,768]{2,1,0:T(8,128)(2,1)}), bf16[8,80,768]{2,1,0:T(8,128)(2,1)S(1)}, u32[]{:S(2)}, u32[]{:S(2)}) async-start(bf16[8,80,768]{2,1,0:T(8,128)(2,1)} %get-tuple-element.112.refs_0_), calls=%async_computation | async-start | bytes 1966080 | tf_op jit(solution)/shard_map/all_to_all | solution.py:1001
  34.6 21.0 %all-to-all-start.1 = ((bf16[8,96,768]{2,1,0:T(8,128)(2,1)}), bf16[8,96,768]{2,1,0:T(8,128)(2,1)S(1)}, u32[]{:S(2)}, u32[]{:S(2)}) async-start(bf16[8,96,768]{2,1,0:T(8,128)(2,1)} %get-tuple-element.115.refs_0_), calls=%async_computation.1 | async-start | bytes 2359296 | tf_op jit(solution)/shard_map/all_to_all | solution.py:1001
  42.0 25.8 %collective-permute-start.2 = (bf16[640,768]{1,0:T(8,128)(2,1)}, bf16[640,768]{1,0:T(8,128)(2,1)S(1)}, u32[]{:S(2)}, u32[]{:S(2)}) collective-permute-start(bf16[640,768]{1,0:T(8,128)(2,1)} %shard_map.241.refs_0_.refs_10_), channel_id=1, source_target_pairs={{0,1},{1,2},{2,3},{4,5},{5,6},{6,7},{8,9},{9,10},{10,11},{12,13},{... | collective-permute-start | bytes 2949128 | tf_op jit(solution)/shard_map/ppermute | solution.py:881
  45.5 26.8 %collective-permute-start.3 = (bf16[640,768]{1,0:T(8,128)(2,1)}, bf16[640,768]{1,0:T(8,128)(2,1)}, u32[]{:S(2)}, u32[]{:S(2)}) collective-permute-start(bf16[640,768]{1,0:T(8,128)(2,1)} %shard_map.241.refs_0_.refs_10_), channel_id=1, source_target_pairs={{3,2},{2,1},{1,0},{7,6},{6,5},{5,4},{11,10},{10,9},{9,8},{15,14},{... | collective-permute-start | bytes 2949128 | tf_op jit(solution)/shard_map/ppermute | solution.py:882
  60.4 28.7 %collective-permute-start = (bf16[656,768]{1,0:T(8,128)(2,1)}, bf16[656,768]{1,0:T(8,128)(2,1)S(1)}, u32[]{:S(2)}, u32[]{:S(2)}) collective-permute-start(bf16[656,768]{1,0:T(8,128)(2,1)} %shard_map.242.refs_0_.refs_3_.refs_17_), channel_id=1, source_target_pairs={{0,1},{1,2},{2,3},{4,5},{5,6},{6,7},{8,9},{9,10},{10,11},{12,13},{... | collective-permute-start | bytes 3022856 | tf_op jit(solution)/shard_map/ppermute | solution.py:881
  64.0 29.9 %collective-permute-start.1 = (bf16[656,768]{1,0:T(8,128)(2,1)}, bf16[656,768]{1,0:T(8,128)(2,1)}, u32[]{:S(2)}, u32[]{:S(2)}) collective-permute-start(bf16[656,768]{1,0:T(8,128)(2,1)} %shard_map.242.refs_0_.refs_3_.refs_17_), channel_id=1, source_target_pairs={{3,2},{2,1},{1,0},{7,6},{6,5},{5,4},{11,10},{10,9},{9,8},{15,14},{... | collective-permute-start | bytes 3022856 | tf_op jit(solution)/shard_map/ppermute | solution.py:882
  67.8 29.0 %collective-permute-start.6 = (bf16[640,768]{1,0:T(8,128)(2,1)S(1)}, bf16[640,768]{1,0:T(8,128)(2,1)}, u32[]{:S(2)}, u32[]{:S(2)}) collective-permute-start(bf16[640,768]{1,0:T(8,128)(2,1)S(1)} %collective-permute-done.2.refs_1_.refs_14_), channel_id=1, source_target_pairs={{1,2},{2,3},{5,6},{6,7},{9,10},{10,11},{13,14},{14,15},{17,18},{18... | collective-permute-start | bytes 2949128 | tf_op jit(solution)/shard_map/ppermute | solution.py:881
  72.3 42.7 %collective-permute-start.8 = (bf16[640,768]{1,0:T(8,128)(2,1)}, bf16[640,768]{1,0:T(8,128)(2,1)}, u32[]{:S(2)}, u32[]{:S(2)}) collective-permute-start(bf16[640,768]{1,0:T(8,128)(2,1)} %collective-permute-done.3.refs_2_.refs_11_), channel_id=1, source_target_pairs={{2,1},{1,0},{6,5},{5,4},{10,9},{9,8},{14,13},{13,12},{18,17},{17,1... | collective-permute-start | bytes 2949128 | tf_op jit(solution)/shard_map/ppermute | solution.py:882
  93.9 42.5 %collective-permute-start.5 = (bf16[656,768]{1,0:T(8,128)(2,1)}, bf16[656,768]{1,0:T(8,128)(2,1)S(1)}, u32[]{:S(2)}, u32[]{:S(2)}) collective-permute-start(bf16[656,768]{1,0:T(8,128)(2,1)} %get-tuple-element.118.refs_4_.refs_18_), channel_id=1, source_target_pairs={{2,1},{1,0},{6,5},{5,4},{10,9},{9,8},{14,13},{13,12},{18,17},{17,1... | collective-permute-start | bytes 3022856 | tf_op jit(solution)/shard_map/ppermute | solution.py:882
  95.2 42.6 %collective-permute-start.4 = (bf16[656,768]{1,0:T(8,128)(2,1)}, bf16[656,768]{1,0:T(8,128)(2,1)}, u32[]{:S(2)}, u32[]{:S(2)}) collective-permute-start(bf16[656,768]{1,0:T(8,128)(2,1)} %get-tuple-element.117.refs_7_.refs_21_), channel_id=1, source_target_pairs={{1,2},{2,3},{5,6},{6,7},{9,10},{10,11},{13,14},{14,15},{17,18},{18... | collective-permute-start | bytes 3022856 | tf_op jit(solution)/shard_map/ppermute | solution.py:881
  96.8 49.3 %collective-permute-start.7 = (bf16[640,768]{1,0:T(8,128)(2,1)}, bf16[640,768]{1,0:T(8,128)(2,1)S(1)}, u32[]{:S(2)}, u32[]{:S(2)}) collective-permute-start(bf16[640,768]{1,0:T(8,128)(2,1)} %collective-permute-done.6.refs_0_.refs_15_), channel_id=1, source_target_pairs={{2,3},{6,7},{10,11},{14,15},{18,19},{22,23},{26,27},{30,31}} | collective-permute-start | bytes 2949128 | tf_op jit(solution)/shard_map/ppermute | solution.py:881
  115.0 42.6 %collective-permute-start.9 = (bf16[640,768]{1,0:T(8,128)(2,1)}, bf16[640,768]{1,0:T(8,128)(2,1)S(1)}, u32[]{:S(2)}, u32[]{:S(2)}) collective-permute-start(bf16[640,768]{1,0:T(8,128)(2,1)} %collective-permute-done.8.refs_1_.refs_12_), channel_id=1, source_target_pairs={{1,0},{5,4},{9,8},{13,12},{17,16},{21,20},{25,24},{29,28}} | collective-permute-start | bytes 2949128 | tf_op jit(solution)/shard_map/ppermute | solution.py:882
  136.5 42.8 %collective-permute-start.12 = (bf16[656,768]{1,0:T(8,128)(2,1)S(1)}, bf16[656,768]{1,0:T(8,128)(2,1)}, u32[]{:S(2)}, u32[]{:S(2)}) collective-permute-start(bf16[656,768]{1,0:T(8,128)(2,1)S(1)} %collective-permute-done.5.refs_1_.refs_5_.refs_19_), channel_id=1, source_target_pairs={{1,0},{5,4},{9,8},{13,12},{17,16},{21,20},{25,24},{29,28}} | collective-permute-start | bytes 3022856 | tf_op jit(solution)/shard_map/ppermute | solution.py:882
  137.8 42.8 %collective-permute-start.13 = (bf16[656,768]{1,0:T(8,128)(2,1)}, bf16[656,768]{1,0:T(8,128)(2,1)}, u32[]{:S(2)}, u32[]{:S(2)}) collective-permute-start(bf16[656,768]{1,0:T(8,128)(2,1)} %collective-permute-done.4.refs_0_.refs_8_.refs_22_), channel_id=1, source_target_pairs={{2,3},{6,7},{10,11},{14,15},{18,19},{22,23},{26,27},{30,31}} | collective-permute-start | bytes 3022856 | tf_op jit(solution)/shard_map/ppermute | solution.py:881
  141.9 22.7 %all-to-all-start.3 = ((bf16[8,80,768]{2,1,0:T(8,128)(2,1)}), bf16[8,80,768]{2,1,0:T(8,128)(2,1)}, u32[]{:S(2)}, u32[]{:S(2)}) async-start(bf16[8,80,768]{2,1,0:T(8,128)(2,1)} %get-tuple-element.120), calls=%async_computation.3 | async-start | bytes 1966080 | tf_op jit(solution)/shard_map/all_to_all | solution.py:1001
  161.7 32.8 %collective-permute-start.10 = (bf16[2,320,768]{2,1,0:T(8,128)(2,1)}, bf16[2,320,768]{2,1,0:T(8,128)(2,1)S(1)}, u32[]{:S(2)}, u32[]{:S(2)}) collective-permute-start(bf16[2,320,768]{2,1,0:T(8,128)(2,1)} %shard_map.246.refs_0_.refs_3_.refs_10_), channel_id=1, source_target_pairs={{0,1},{1,2},{2,3},{4,5},{5,6},{6,7},{8,9},{9,10},{10,11},{12,13},{... | collective-permute-start | bytes 2949128 | tf_op jit(solution)/shard_map/ppermute | solution.py:881
  163.3 37.0 %collective-permute-start.11 = (bf16[2,320,768]{2,1,0:T(8,128)(2,1)}, bf16[2,320,768]{2,1,0:T(8,128)(2,1)}, u32[]{:S(2)}, u32[]{:S(2)}) collective-permute-start(bf16[2,320,768]{2,1,0:T(8,128)(2,1)} %shard_map.246.refs_0_.refs_3_.refs_10_), channel_id=1, source_target_pairs={{3,2},{2,1},{1,0},{7,6},{6,5},{5,4},{11,10},{10,9},{9,8},{15,14},{... | collective-permute-start | bytes 2949128 | tf_op jit(solution)/shard_map/ppermute | solution.py:882
  167.8 68.0 %collective-permute-start.22 = (bf16[2,320,768]{2,1,0:T(8,128)(2,1)}, bf16[2,320,768]{2,1,0:T(8,128)(2,1)S(1)}, u32[]{:S(2)}, u32[]{:S(2)}) collective-permute-start(bf16[2,320,768]{2,1,0:T(8,128)(2,1)} %shard_map.247.refs_1_.refs_5_.refs_12_), channel_id=1, source_target_pairs={{0,1},{1,2},{2,3},{4,5},{5,6},{6,7},{8,9},{9,10},{10,11},{12,13},{... | collective-permute-start | bytes 2949128 | tf_op jit(solution)/shard_map/ppermute | solution.py:881
  179.2 56.5 %collective-permute-start.23 = (bf16[2,320,768]{2,1,0:T(8,128)(2,1)}, bf16[2,320,768]{2,1,0:T(8,128)(2,1)S(1)}, u32[]{:S(2)}, u32[]{:S(2)}) collective-permute-start(bf16[2,320,768]{2,1,0:T(8,128)(2,1)} %shard_map.247.refs_1_.refs_5_.refs_12_), channel_id=1, source_target_pairs={{3,2},{2,1},{1,0},{7,6},{6,5},{5,4},{11,10},{10,9},{9,8},{15,14},{... | collective-permute-start | bytes 2949128 | tf_op jit(solution)/shard_map/ppermute | solution.py:882
  206.4 38.8 %collective-permute-start.14 = (bf16[2,320,768]{2,1,0:T(8,128)(2,1)}, bf16[2,320,768]{2,1,0:T(8,128)(2,1)S(1)}, u32[]{:S(2)}, u32[]{:S(2)}) collective-permute-start(bf16[2,320,768]{2,1,0:T(8,128)(2,1)} %get-tuple-element.123), channel_id=1, source_target_pairs={{0,1},{1,2},{2,3},{4,5},{5,6},{6,7},{8,9},{9,10},{10,11},{12,13},{... | collective-permute-start | bytes 2949128 | tf_op jit(solution)/shard_map/ppermute | solution.py:881
  207.9 37.3 %collective-permute-start.15 = (bf16[2,320,768]{2,1,0:T(8,128)(2,1)}, bf16[2,320,768]{2,1,0:T(8,128)(2,1)S(1)}, u32[]{:S(2)}, u32[]{:S(2)}) collective-permute-start(bf16[2,320,768]{2,1,0:T(8,128)(2,1)} %get-tuple-element.124), channel_id=1, source_target_pairs={{3,2},{2,1},{1,0},{7,6},{6,5},{5,4},{11,10},{10,9},{9,8},{15,14},{... | collective-permute-start | bytes 2949128 | tf_op jit(solution)/shard_map/ppermute | solution.py:882
  239.3 26.7 %collective-permute-start.24 = (bf16[2,320,768]{2,1,0:T(8,128)(2,1)S(1)}, bf16[2,320,768]{2,1,0:T(8,128)(2,1)S(1)}, u32[]{:S(2)}, u32[]{:S(2)}) collective-permute-start(bf16[2,320,768]{2,1,0:T(8,128)(2,1)S(1)} %get-tuple-element.138), channel_id=1, source_target_pairs={{0,1},{1,2},{2,3},{4,5},{5,6},{6,7},{8,9},{9,10},{10,11},{12,13},{... | collective-permute-start | bytes 2949128 | tf_op jit(solution)/shard_map/ppermute | solution.py:881
  243.9 26.6 %collective-permute-start.25 = (bf16[2,320,768]{2,1,0:T(8,128)(2,1)S(1)}, bf16[2,320,768]{2,1,0:T(8,128)(2,1)S(1)}, u32[]{:S(2)}, u32[]{:S(2)}) collective-permute-start(bf16[2,320,768]{2,1,0:T(8,128)(2,1)S(1)} %get-tuple-element.139), channel_id=1, source_target_pairs={{3,2},{2,1},{1,0},{7,6},{6,5},{5,4},{11,10},{10,9},{9,8},{15,14},{... | collective-permute-start | bytes 2949128 | tf_op jit(solution)/shard_map/ppermute | solution.py:882
  246.5 40.6 %collective-permute-start.16 = (bf16[2,320,768]{2,1,0:T(8,128)(2,1)S(1)}, bf16[2,320,768]{2,1,0:T(8,128)(2,1)S(1)}, u32[]{:S(2)}, u32[]{:S(2)}) collective-permute-start(bf16[2,320,768]{2,1,0:T(8,128)(2,1)S(1)} %get-tuple-element.126), channel_id=1, source_target_pairs={{0,1},{1,2},{2,3},{4,5},{5,6},{6,7},{8,9},{9,10},{10,11},{12,13},{... | collective-permute-start | bytes 2949128 | tf_op jit(solution)/shard_map/ppermute | solution.py:881
  251.1 40.4 %collective-permute-start.17 = (bf16[2,320,768]{2,1,0:T(8,128)(2,1)S(1)}, bf16[2,320,768]{2,1,0:T(8,128)(2,1)S(1)}, u32[]{:S(2)}, u32[]{:S(2)}) collective-permute-start(bf16[2,320,768]{2,1,0:T(8,128)(2,1)S(1)} %get-tuple-element.127), channel_id=1, source_target_pairs={{3,2},{2,1},{1,0},{7,6},{6,5},{5,4},{11,10},{10,9},{9,8},{15,14},{... | collective-permute-start | bytes 2949128 | tf_op jit(solution)/shard_map/ppermute | solution.py:882
  272.4 45.0 %collective-permute-start.26 = (bf16[2,320,768]{2,1,0:T(8,128)(2,1)}, bf16[2,320,768]{2,1,0:T(8,128)(2,1)S(1)}, u32[]{:S(2)}, u32[]{:S(2)}) collective-permute-start(bf16[2,320,768]{2,1,0:T(8,128)(2,1)} %get-tuple-element.141), channel_id=1, source_target_pairs={{0,1},{1,2},{2,3},{4,5},{5,6},{6,7},{8,9},{9,10},{10,11},{12,13},{... | collective-permute-start | bytes 2949128 | tf_op jit(solution)/shard_map/ppermute | solution.py:881
  274.3 44.7 %collective-permute-start.27 = (bf16[2,320,768]{2,1,0:T(8,128)(2,1)}, bf16[2,320,768]{2,1,0:T(8,128)(2,1)S(1)}, u32[]{:S(2)}, u32[]{:S(2)}) collective-permute-start(bf16[2,320,768]{2,1,0:T(8,128)(2,1)} %get-tuple-element.142), channel_id=1, source_target_pairs={{3,2},{2,1},{1,0},{7,6},{6,5},{5,4},{11,10},{10,9},{9,8},{15,14},{... | collective-permute-start | bytes 2949128 | tf_op jit(solution)/shard_map/ppermute | solution.py:882
  293.6 35.8 %collective-permute-start.30 = (bf16[2,320,768]{2,1,0:T(8,128)(2,1)}, bf16[2,320,768]{2,1,0:T(8,128)(2,1)}, u32[]{:S(2)}, u32[]{:S(2)}) collective-permute-start(bf16[2,320,768]{2,1,0:T(8,128)(2,1)} %get-tuple-element.128.refs_0_), channel_id=1, source_target_pairs={{0,1},{1,2},{2,3},{4,5},{5,6},{6,7},{8,9},{9,10},{10,11},{12,13},{... | collective-permute-start | bytes 2949128 | tf_op jit(solution)/shard_map/ppermute | solution.py:881
  296.4 35.4 %collective-permute-start.31 = (bf16[2,320,768]{2,1,0:T(8,128)(2,1)}, bf16[2,320,768]{2,1,0:T(8,128)(2,1)}, u32[]{:S(2)}, u32[]{:S(2)}) collective-permute-start(bf16[2,320,768]{2,1,0:T(8,128)(2,1)} %get-tuple-element.129.refs_1_), channel_id=1, source_target_pairs={{3,2},{2,1},{1,0},{7,6},{6,5},{5,4},{11,10},{10,9},{9,8},{15,14},{... | collective-permute-start | bytes 2949128 | tf_op jit(solution)/shard_map/ppermute | solution.py:882
  311.9 38.5 %collective-permute-start.18 = (bf16[2,320,768]{2,1,0:T(8,128)(2,1)}, bf16[2,320,768]{2,1,0:T(8,128)(2,1)}, u32[]{:S(2)}, u32[]{:S(2)}) collective-permute-start(bf16[2,320,768]{2,1,0:T(8,128)(2,1)} %get-tuple-element.130.downsum_ref), channel_id=1, source_target_pairs={{0,1},{4,5},{8,9},{12,13},{16,17},{20,21},{24,25},{28,29}} | collective-permute-start | bytes 2949128 | tf_op jit(solution)/shard_map/ppermute | solution.py:881
  317.4 34.6 %collective-permute-start.19 = (bf16[2,320,768]{2,1,0:T(8,128)(2,1)}, bf16[2,320,768]{2,1,0:T(8,128)(2,1)}, u32[]{:S(2)}, u32[]{:S(2)}) collective-permute-start(bf16[2,320,768]{2,1,0:T(8,128)(2,1)} %get-tuple-element.131.upsum_ref), channel_id=1, source_target_pairs={{3,2},{7,6},{11,10},{15,14},{19,18},{23,22},{27,26},{31,30}} | collective-permute-start | bytes 2949128 | tf_op jit(solution)/shard_map/ppermute | solution.py:882
  322.4 49.1 %collective-permute-start.28 = (bf16[2,320,768]{2,1,0:T(8,128)(2,1)}, bf16[2,320,768]{2,1,0:T(8,128)(2,1)S(1)}, u32[]{:S(2)}, u32[]{:S(2)}) collective-permute-start(bf16[2,320,768]{2,1,0:T(8,128)(2,1)} %get-tuple-element.144.refs_0_), channel_id=1, source_target_pairs={{0,1},{1,2},{2,3},{4,5},{5,6},{6,7},{8,9},{9,10},{10,11},{12,13},{... | collective-permute-start | bytes 2949128 | tf_op jit(solution)/shard_map/ppermute | solution.py:881
  329.3 43.8 %collective-permute-start.29 = (bf16[2,320,768]{2,1,0:T(8,128)(2,1)}, bf16[2,320,768]{2,1,0:T(8,128)(2,1)}, u32[]{:S(2)}, u32[]{:S(2)}) collective-permute-start(bf16[2,320,768]{2,1,0:T(8,128)(2,1)} %get-tuple-element.145.refs_1_), channel_id=1, source_target_pairs={{3,2},{2,1},{1,0},{7,6},{6,5},{5,4},{11,10},{10,9},{9,8},{15,14},{... | collective-permute-start | bytes 2949128 | tf_op jit(solution)/shard_map/ppermute | solution.py:882
  345.9 49.7 %collective-permute-start.32 = (bf16[2,320,768]{2,1,0:T(8,128)(2,1)}, bf16[2,320,768]{2,1,0:T(8,128)(2,1)S(1)}, u32[]{:S(2)}, u32[]{:S(2)}) collective-permute-start(bf16[2,320,768]{2,1,0:T(8,128)(2,1)} %get-tuple-element.152.downsum_ref), channel_id=1, source_target_pairs={{0,1},{4,5},{8,9},{12,13},{16,17},{20,21},{24,25},{28,29}} | collective-permute-start | bytes 2949128 | tf_op jit(solution)/shard_map/ppermute | solution.py:881
  350.4 45.2 %collective-permute-start.33 = (bf16[2,320,768]{2,1,0:T(8,128)(2,1)}, bf16[2,320,768]{2,1,0:T(8,128)(2,1)}, u32[]{:S(2)}, u32[]{:S(2)}) collective-permute-start(bf16[2,320,768]{2,1,0:T(8,128)(2,1)} %get-tuple-element.153.upsum_ref), channel_id=1, source_target_pairs={{3,2},{7,6},{11,10},{15,14},{19,18},{23,22},{27,26},{31,30}} | collective-permute-start | bytes 2949128 | tf_op jit(solution)/shard_map/ppermute | solution.py:882
  355.9 58.3 %collective-permute-start.20 = (bf16[2,320,768]{2,1,0:T(8,128)(2,1)}, bf16[2,320,768]{2,1,0:T(8,128)(2,1)}, u32[]{:S(2)}, u32[]{:S(2)}) collective-permute-start(bf16[2,320,768]{2,1,0:T(8,128)(2,1)} %get-tuple-element.133.refs_0_), channel_id=1, source_target_pairs={{0,1},{1,2},{4,5},{5,6},{8,9},{9,10},{12,13},{13,14},{16,17},{17,1... | collective-permute-start | bytes 2949128 | tf_op jit(solution)/shard_map/ppermute | solution.py:881
  371.5 42.8 %collective-permute-start.21 = (bf16[2,320,768]{2,1,0:T(8,128)(2,1)}, bf16[2,320,768]{2,1,0:T(8,128)(2,1)}, u32[]{:S(2)}, u32[]{:S(2)}) collective-permute-start(bf16[2,320,768]{2,1,0:T(8,128)(2,1)} %get-tuple-element.134), channel_id=1, source_target_pairs={{3,2},{2,1},{7,6},{6,5},{11,10},{10,9},{15,14},{14,13},{19,18},{18... | collective-permute-start | bytes 2949128 | tf_op jit(solution)/shard_map/ppermute | solution.py:882
  376.9 32.8 %all-to-all-start.4 = ((bf16[8,80,768]{2,1,0:T(8,128)(2,1)}), bf16[8,80,768]{2,1,0:T(8,128)(2,1)S(1)}, u32[]{:S(2)}, u32[]{:S(2)}) async-start(bf16[8,80,768]{2,1,0:T(8,128)(2,1)} %shard_map.258), calls=%async_computation.4 | async-start | bytes 1966080 | tf_op jit(solution)/shard_map/all_to_all | solution.py:1001
  399.2 39.0 %collective-permute-start.34 = (bf16[2,320,768]{2,1,0:T(8,128)(2,1)}, bf16[2,320,768]{2,1,0:T(8,128)(2,1)}, u32[]{:S(2)}, u32[]{:S(2)}) collective-permute-start(bf16[2,320,768]{2,1,0:T(8,128)(2,1)} %get-tuple-element.164), channel_id=1, source_target_pairs={{0,1},{1,2},{4,5},{5,6},{8,9},{9,10},{12,13},{13,14},{16,17},{17,1... | collective-permute-start | bytes 2949128 | tf_op jit(solution)/shard_map/ppermute | solution.py:881
  404.2 34.0 %collective-permute-start.35 = (bf16[2,320,768]{2,1,0:T(8,128)(2,1)}, bf16[2,320,768]{2,1,0:T(8,128)(2,1)}, u32[]{:S(2)}, u32[]{:S(2)}) collective-permute-start(bf16[2,320,768]{2,1,0:T(8,128)(2,1)} %get-tuple-element.165), channel_id=1, source_target_pairs={{3,2},{2,1},{7,6},{6,5},{11,10},{10,9},{15,14},{14,13},{19,18},{18... | collective-permute-start | bytes 2949128 | tf_op jit(solution)/shard_map/ppermute | solution.py:882
  418.1 44.0 %collective-permute-start.36 = (bf16[2,320,768]{2,1,0:T(8,128)(2,1)}, bf16[2,320,768]{2,1,0:T(8,128)(2,1)}, u32[]{:S(2)}, u32[]{:S(2)}) collective-permute-start(bf16[2,320,768]{2,1,0:T(8,128)(2,1)} %get-tuple-element.146.refs_0_), channel_id=1, source_target_pairs={{0,1},{1,2},{2,3},{4,5},{5,6},{6,7},{8,9},{9,10},{10,11},{12,13},{... | collective-permute-start | bytes 2949128 | tf_op jit(solution)/shard_map/ppermute | solution.py:881
  422.9 39.3 %collective-permute-start.37 = (bf16[2,320,768]{2,1,0:T(8,128)(2,1)}, bf16[2,320,768]{2,1,0:T(8,128)(2,1)}, u32[]{:S(2)}, u32[]{:S(2)}) collective-permute-start(bf16[2,320,768]{2,1,0:T(8,128)(2,1)} %get-tuple-element.171), channel_id=1, source_target_pairs={{3,2},{2,1},{1,0},{7,6},{6,5},{5,4},{11,10},{10,9},{9,8},{15,14},{... | collective-permute-start | bytes 2949128 | tf_op jit(solution)/shard_map/ppermute | solution.py:882
  442.0 42.3 %collective-permute-start.38 = (bf16[2,320,768]{2,1,0:T(8,128)(2,1)S(1)}, bf16[2,320,768]{2,1,0:T(8,128)(2,1)}, u32[]{:S(2)}, u32[]{:S(2)}) collective-permute-start(bf16[2,320,768]{2,1,0:T(8,128)(2,1)S(1)} %get-tuple-element.167.refs_0_), channel_id=1, source_target_pairs={{0,1},{1,2},{2,3},{4,5},{5,6},{6,7},{8,9},{9,10},{10,11},{12,13},{... | collective-permute-start | bytes 2949128 | tf_op jit(solution)/shard_map/ppermute | solution.py:881
  446.2 38.1 %collective-permute-start.39 = (bf16[2,320,768]{2,1,0:T(8,128)(2,1)S(1)}, bf16[2,320,768]{2,1,0:T(8,128)(2,1)}, u32[]{:S(2)}, u32[]{:S(2)}) collective-permute-start(bf16[2,320,768]{2,1,0:T(8,128)(2,1)S(1)} %get-tuple-element.177), channel_id=1, source_target_pairs={{3,2},{2,1},{1,0},{7,6},{6,5},{5,4},{11,10},{10,9},{9,8},{15,14},{... | collective-permute-start | bytes 2949128 | tf_op jit(solution)/shard_map/ppermute | solution.py:882
  539.3 20.5 %collective-permute-start.41 = (bf16[512,384]{1,0:T(8,128)(2,1)}, bf16[512,384]{1,0:T(8,128)(2,1)}, u32[]{:S(2)}, u32[]{:S(2)}) collective-permute-start(bf16[512,384]{1,0:T(8,128)(2,1)} %get-tuple-element.240), channel_id=1, source_target_pairs={{0,8},{4,12},{8,0},{12,4},{16,24},{20,28},{24,16},{28,20},{1,9},{5... | collective-permute-start | bytes 1179656 | tf_op jit(solution)/shard_map/ppermute | solution.py:914
  559.9 20.0 %collective-permute-start.54 = (bf16[1280,384]{1,0:T(8,128)(2,1)}, bf16[1280,384]{1,0:T(8,128)(2,1)}, u32[]{:S(2)}, u32[]{:S(2)}) collective-permute-start(bf16[1280,384]{1,0:T(8,128)(2,1)} %dynamic-slice_bitcast_fusion.1), channel_id=1, source_target_pairs={{0,4},{4,0},{8,12},{12,8},{16,20},{20,16},{24,28},{28,24},{1,5},{5... | collective-permute-start | bytes 2949128 | tf_op jit(solution)/shard_map/ppermute | solution.py:914
  588.8 22.4 %collective-permute-start.51 = (bf16[512,384]{1,0:T(8,128)(2,1)S(1)}, bf16[512,384]{1,0:T(8,128)(2,1)S(1)}, u32[]{:S(2)}, u32[]{:S(2)}) collective-permute-start(bf16[512,384]{1,0:T(8,128)(2,1)S(1)} %pad_maximum_fusion.2), channel_id=1, source_target_pairs={{0,16},{4,20},{8,24},{12,28},{16,0},{20,4},{24,8},{28,12},{1,17},{... | collective-permute-start | bytes 1179656 | tf_op jit(solution)/shard_map/ppermute | solution.py:914
  591.1 20.1 %collective-permute-start.52 = (bf16[512,384]{1,0:T(8,128)(2,1)S(1)}, bf16[512,384]{1,0:T(8,128)(2,1)S(1)}, u32[]{:S(2)}, u32[]{:S(2)}) collective-permute-start(bf16[512,384]{1,0:T(8,128)(2,1)S(1)} %pad_maximum_fusion.2), channel_id=1, source_target_pairs={{0,24},{4,28},{8,16},{12,20},{16,8},{20,12},{24,0},{28,4},{1,25},{... | collective-permute-start | bytes 1179656 | tf_op jit(solution)/shard_map/ppermute | solution.py:914
  (85 other events, 714.4 us)

commit v6 on v5

--- a/solution.py
+++ b/solution.py
@@ -516,7 +516,7 @@
     probs = probs_ref[...]
     chosen = iota(probs.shape, 1) == rcol_ref[0]
     gate = jnp.sum(jnp.where(chosen, probs, 0.0), axis=-1, keepdims=True)
-    layer_ref[...] = jnp.where(valid, residual + gate * returned, 0.0).astype(BF16)
+    layer_ref[0, 0] = jnp.where(valid, residual + gate * returned, 0.0).astype(BF16)
     out_grad = jnp.where(valid, cot_ref[...].astype(F32), 0.0)
     gate_grad = jnp.sum(out_grad * returned, axis=-1, keepdims=True)
     prob_grad = jnp.where(chosen, gate_grad, 0.0)
@@ -554,19 +554,19 @@
 
 
 def combine(
-    batch, last, after, counts, low, high, scol, rcol, residual, probs, cot, gain_ffn, w_router, w_output, mixed, past, per, shared
+    batch, last, after, layers, counts, low, high, scol, rcol, residual, probs, cot, gain_ffn, w_router, w_output, mixed, past, per, shared
 ):
     length, width = cot.shape[2:]
     return pl.pallas_call(
-        functools.partial(combine_kernel, per, batch, len(after)),
+        functools.partial(combine_kernel, per, batch, len(after) + len(layers)),
         grid=(1,),
-        in_specs=[ANYWHERE] * len(after)
+        in_specs=[ANYWHERE] * (len(after) + len(layers))
         + [SCALARS, WHOLE, WHOLE, batch_block(scol, batch), batch_block(rcol, batch), ANYWHERE, WHOLE, ANYWHERE]
         + [WHOLE] * 2
         + [ANYWHERE] * (2 + len(past)),
-        out_specs=[WHOLE] * 4,
+        out_specs=[batch_block(cot, batch)] + [WHOLE] * 3,
         out_shape=[
-            jax.ShapeDtypeStruct((length, width), BF16),
+            jax.ShapeDtypeStruct(cot.shape, BF16),
             jax.ShapeDtypeStruct((length, width), F32),
             jax.ShapeDtypeStruct((PAIRS, length, PAIR), BF16),
             jax.ShapeDtypeStruct((shared, width // 2), BF16 if last else F32),
@@ -577,23 +577,25 @@
             *(pltpu.VMEM(array.shape, array.dtype) for array in (mixed, w_output, *past)),
             pltpu.SemaphoreType.DMA((4 + len(past),)),
         ],
+        input_output_aliases={len(after): 0} if layers else {},
         compiler_params=params(60),
         cost_estimate=cost(),
     )(
-        *after, counts, low, high, scol, rcol, residual, probs, cot, gain_ffn, w_router, w_output, mixed, *past
+        *after, *layers, counts, low, high, scol, rcol, residual, probs, cot, gain_ffn, w_router, w_output, mixed, *past
     )
 
 
-def attn_back_kernel(batch, which, waits, *refs):
+def attn_back_kernel(batch, which, last, waits, *refs):
     refs = refs[waits:]
-    len_ref, qkv_ref, lse_ref, vec_ref, sel_ref, mgrad_ref, tok_ref, gain_ref, wq_ref, wk_ref, wv_ref, *refs = refs
+    side_ref, len_ref, qkv_ref, lse_ref, vec_ref, sel_ref, mgrad_ref, tok_ref, gain_ref, wq_ref, wk_ref, wv_ref, *refs = refs
     past_ref = refs.pop(0) if batch else None
     if which:
         seen_ref, part_ref, resgrad_ref, *refs = refs
-        shared_ref, tgrad_ref, *refs = refs
+        tgrad_ref, *refs = refs
     else:
         early_ref = refs.pop(0) if batch else None
-        shared_ref, diag_out_ref, part_out_ref, *refs = refs
+        diag_out_ref, part_out_ref, *refs = refs
+    shared_refs, refs = refs[: 1 + last], refs[1 + last :]
     bands_ref, probs_ref, sgrad_ref, spread_ref, low_ref, qt_ref, kt_ref, vt_ref, diag_ref, stage_ref, rest_ref, *buffers = refs
     *buffers, sems, out_sems = buffers
     half = wq_ref.shape[0] // 2
@@ -609,7 +611,8 @@
     for copy in copies:
         copy.start()
     going = []
-    offset = 0 if which or shared_ref.dtype == F32 else early_ref.shape[0]
+    offset = early_ref.shape[0] if last and not which else 0
+    part_rows = shared_refs[0].shape[0]
     tok_ref, wq_ref, wk_ref, wv_ref, *buffers = buffers
     if past_ref is not None:
         past_ref = buffers.pop(0)
@@ -673,13 +676,23 @@
         copy.wait()
 
     def send(source, first, place):
-        target = shared_ref.at[pl.ds(offset + first, source.shape[0])]
-        going.append(pltpu.make_async_copy(source, target, out_sems.at[place]))
-        going[-1].start()
+        count = source.shape[0]
+        for k in range(1 + last):
+            low, high = max(first, k * part_rows), min(first + count, (k + 1) * part_rows)
+            if low >= high:
+                continue
+            part = source.at[pl.ds(low - first, high - low)]
+            for turn in range(1 + last):
+                there = shared_refs[turn].at[pl.ds(low - k * part_rows, high - low)]
+                copy = pltpu.make_async_copy(part, there, out_sems.at[place, k])
+                going.append((copy, k ^ turn))
+
+                @pl.when(side_ref[0] == (k ^ turn) if last else True)
+                def _():
+                    copy.start()
 
     if offset:
-        going.append(pltpu.make_async_copy(early_ref, shared_ref.at[pl.ds(0, offset)], out_sems.at[0]))
-        going[0].start()
+        send(early_ref, 0, 0)
 
     def past(first, count):
         return 0.0 if past_ref is None else past_ref[first : first + count, :]
@@ -693,7 +706,7 @@
     for matrix, w_ref in enumerate((wq_ref, wk_ref, wv_ref)):
         low = jnp.concatenate([low_ref[matrix, p] for p in range(PAIRS // 2)], axis=1)
         stage_ref[matrix] = (dot(normed_t, low) + past(matrix * width, width)).astype(stage_ref.dtype)
-        send(stage_ref.at[matrix], matrix * width, 1 + matrix)
+        send(stage_ref.at[matrix], offset + matrix * width, 1 + matrix)
         normed_grad = normed_grad + dot_t(low, w_ref[...])
     left = rest_ref.shape[0]
     if which:
@@ -708,23 +721,26 @@
         row = iota((8, half), 0)
         gains = jnp.where(row == 0, gain_part[:, :half], jnp.where(row == 1, gain_part[:, half:], 0.0))
         wide = jnp.concatenate([bias_part, jnp.zeros((16, half - bias_part.shape[1]), F32)], axis=1)
-        last = [gains, wide] + ([jnp.zeros((left - 24, half), F32)] if left > 24 else [])
-        rest_ref[...] = (jnp.concatenate(last, axis=0) + past(3 * width, left)).astype(rest_ref.dtype)
+        tail = [gains, wide] + ([jnp.zeros((left - 24, half), F32)] if left > 24 else [])
+        rest_ref[...] = (jnp.concatenate(tail, axis=0) + past(3 * width, left)).astype(rest_ref.dtype)
         send(rest_ref, 3 * width, 4)
         upstream = normed_grad * gain
         middle = jnp.mean(upstream * scaled, axis=-1, keepdims=True)
-        tgrad_ref[...] = (resgrad_ref[...] + inverse * (upstream - scaled * middle)).astype(BF16)
+        tgrad_ref[0, 0] = (resgrad_ref[...] + inverse * (upstream - scaled * middle)).astype(BF16)
     else:
-        if offset and offset + 3 * width < shared_ref.shape[0]:
+        if offset and offset + 3 * width < 2 * part_rows:
             rest_ref[...] = jnp.zeros_like(rest_ref)
-            send(rest_ref, 3 * width, 4)
+            send(rest_ref, offset + 3 * width, 4)
         diag_out_ref[...] = diag_ref[...]
         part_out_ref[...] = normed_grad
-    for copy in going:
-        copy.wait()
-
-
-def attention_backward(batch, which, last, after, counts, qkv, lse, vector, selector, mixed_grad, tokens, gain, wq, wk, wv, past, more, rows):
+    for copy, turn in going:
+
+        @pl.when(side_ref[0] == turn if last else True)
+        def _():
+            copy.wait()
+
+
+def attention_backward(batch, which, last, after, grads, side, counts, qkv, lse, vector, selector, mixed_grad, tokens, gain, wq, wk, wv, past, more, rows):
     length, width = tokens.shape[2:]
     half = width // 2
     size = vector.shape[-1]
@@ -732,23 +748,28 @@
     buffers = [((length, width), BF16)] + [((width, half), BF16)] * 3 + [(array.shape, array.dtype) for array in late]
     sent = 0 if which or not last else more[0].shape[0]
     rest = max(rows - sent - 3 * width, 16)
-    shared = jax.ShapeDtypeStruct((rows, half), BF16 if last else F32)
+    shared = jax.ShapeDtypeStruct((rows // 2 if last else rows, half), BF16 if last else F32)
     if which:
-        outs = [shared, jax.ShapeDtypeStruct((length, width), BF16)]
+        outs = [jax.ShapeDtypeStruct(tokens.shape, BF16)]
+        out_specs = [batch_block(tokens, batch)]
     else:
-        outs = [shared, jax.ShapeDtypeStruct((16, size), F32), jax.ShapeDtypeStruct((length, width), F32)]
+        outs = [jax.ShapeDtypeStruct((16, size), F32), jax.ShapeDtypeStruct((length, width), F32)]
+        out_specs = [WHOLE] * 2
+    outs += [shared] * (2 if last else 1)
+    out_specs += [ANYWHERE] * (2 if last else 1)
     return pl.pallas_call(
-        functools.partial(attn_back_kernel, batch, which, len(after)),
+        functools.partial(attn_back_kernel, batch, which, last, len(after) + len(grads)),
         grid=(1,),
-        in_specs=[ANYWHERE] * len(after)
-        + [SCALARS, pl.BlockSpec((3, PAIRS // 2, length, PAIR), lambda _: (0, which, 0, 0))]
+        in_specs=[ANYWHERE] * (len(after) + len(grads))
+        + [SCALARS, SCALARS, pl.BlockSpec((3, PAIRS // 2, length, PAIR), lambda _: (0, which, 0, 0))]
         + [WHOLE] * 3
         + [pl.BlockSpec((PAIRS // 2, length, PAIR), lambda _: (which, 0, 0))]
         + [ANYWHERE, WHOLE]
         + [ANYWHERE] * (3 + len(past))
         + [WHOLE if which and k == 0 else ANYWHERE for k in range(len(more))],
-        out_specs=[ANYWHERE] + [WHOLE] * (len(outs) - 1),
+        out_specs=out_specs,
         out_shape=outs,
+        input_output_aliases={len(after): 0} if grads else {},
         scratch_shapes=[
             pltpu.VMEM((2, ROWS, size), F32),
             pltpu.VMEM((2, length, length), BF16),
@@ -763,51 +784,72 @@
             pltpu.VMEM((rest, half), shared.dtype),
             *(pltpu.VMEM(shape, kind) for shape, kind in buffers),
             pltpu.SemaphoreType.DMA((len(buffers),)),
-            pltpu.SemaphoreType.DMA((5,)),
+            pltpu.SemaphoreType.DMA((5, 2)),
         ],
         compiler_params=params(60),
         cost_estimate=cost(),
-    )(*after, counts, qkv, lse, vector, selector, mixed_grad, tokens, gain, wq, wk, wv, *past, *more)
-
-
-def unpack_kernel(early, side_ref, first_ref, first_other_ref, second_ref, second_other_ref, *refs):
-    q_ref, k_ref, v_ref, output_ref, router_ref, gain_f_ref, gain_a_ref, bias_ref = refs
+    )(*after, *grads, side, counts, qkv, lse, vector, selector, mixed_grad, tokens, gain, wq, wk, wv, *past, *more)
+
+
+def unpack_kernel(early, side_ref, *refs):
+    arrived, refs = refs[:4], refs[4:]
+    q_ref, k_ref, v_ref, output_ref, router_ref, gain_f_ref, gain_a_ref, bias_ref, *refs = refs
+    buffers, (stage_ref, in_sems, out_sems) = refs[:4], refs[4:]
+    copies = [
+        pltpu.make_async_copy(ref, buffer, in_sems.at[k]) for k, (ref, buffer) in enumerate(zip(arrived, buffers))
+    ]
+    for copy in copies:
+        copy.start()
     swapped = side_ref[0] == 1
 
-    def whole(mine_ref, other_ref):
-        mine, other = mine_ref[...], other_ref[...]
+    def whole(k):
+        copies[k].wait()
+        copies[k + 1].wait()
+        mine, other = buffers[k][...], buffers[k + 1][...]
         parts = [jnp.where(swapped, other, mine), jnp.where(swapped, mine, other)]
         return jnp.concatenate(parts, axis=0).astype(F32)
 
-    rows = whole(first_ref, first_other_ref)
-    width = 2 * rows.shape[1]
+    leaving = [
+        pltpu.make_async_copy(stage_ref.at[k], ref, out_sems.at[k])
+        for k, ref in enumerate((q_ref, k_ref, v_ref, output_ref))
+    ]
+    rows = whole(0)
     half = rows.shape[1]
+    width = 2 * half
     last = early - 16
-    output_ref[...] = jnp.concatenate([rows[:width], rows[early : early + width]], axis=1)
+    stage_ref[3, :, :half] = rows[:width]
+    stage_ref[3, :, half:] = rows[early : early + width]
+    leaving[3].start()
     router_ref[...] = jnp.concatenate([rows[width:last], rows[early + width : early + last]], axis=1)
     gain_f_ref[...] = jnp.concatenate([rows[last], rows[early + last]])
-    for k, ref in enumerate((q_ref, k_ref, v_ref)):
-        ref[:, :half] = rows[2 * early + k * width : 2 * early + (k + 1) * width]
-    rows = whole(second_ref, second_other_ref)
+    for k in range(3):
+        stage_ref[k, :, :half] = rows[2 * early + k * width : 2 * early + (k + 1) * width]
+    rows = whole(2)
+    for k in range(3):
+        stage_ref[k, :, half:] = rows[k * width : (k + 1) * width]
+        leaving[k].start()
     gain_a_ref[...] = jnp.concatenate([rows[3 * width], rows[3 * width + 1]])
     bias_ref[...] = rows[3 * width + 8 : 3 * width + 8 + HEADS, :BUCKETS]
-    for k, ref in enumerate((q_ref, k_ref, v_ref)):
-        ref[:, half:] = rows[k * width : (k + 1) * width]
+    for copy in leaving:
+        copy.wait()
 
 
 def unpack(early, experts, side, first, first_other, second, second_other):
     width = 2 * first.shape[1]
     matrix = jax.ShapeDtypeStruct((width, width), F32)
     line = jax.ShapeDtypeStruct((width,), F32)
+    arrays = (first, first_other, second, second_other)
     return pl.pallas_call(
         functools.partial(unpack_kernel, early),
-        in_specs=[SCALARS] + [WHOLE] * 4,
-        out_specs=[WHOLE] * 8,
+        in_specs=[SCALARS] + [ANYWHERE] * 4,
+        out_specs=[ANYWHERE] * 4 + [WHOLE] * 4,
         out_shape=[matrix] * 4
         + [jax.ShapeDtypeStruct((experts, width), F32), line, line, jax.ShapeDtypeStruct((HEADS, BUCKETS), F32)],
+        scratch_shapes=[pltpu.VMEM(array.shape, array.dtype) for array in arrays]
+        + [pltpu.VMEM((4, width, width), F32), pltpu.SemaphoreType.DMA((4,)), pltpu.SemaphoreType.DMA((4,))],
         compiler_params=params(60),
         cost_estimate=cost(),
-    )(side, first, first_other, second, second_other)
+    )(side, *arrays)
 
 
 def upward(planes, first, last):
@@ -946,11 +988,7 @@
     return values, swap(values, "expert", 1)
 
 
-def share_half(values):
-    side = lax.axis_index("expert") % 2
-    parts = values.reshape(2, values.shape[0] // 2, values.shape[1])
-    mine = lax.dynamic_index_in_dim(parts, side, 0, keepdims=False)
-    other = lax.dynamic_index_in_dim(parts, 1 - side, 0, keepdims=False)
+def add_half(mine, other):
     return mine + swap(other, "expert", 1)
 
 
@@ -1026,7 +1064,8 @@
     first_rows = first_rows + -first_rows % unit
     second_rows = 3 * width + 24
     second_rows = second_rows + -second_rows % unit
-    kept, layer_rows, token_grads = [], [], []
+    kept, layers, token_grads = [], (), ()
+    side = (lax.axis_index("expert") % 2)[None]
     early_part, first_part, second_part = (), (), ()
 
     def back_tokens(b, after, low, high):
@@ -1034,6 +1073,7 @@
             b,
             b + 1 == batches,
             after,
+            layers,
             counts,
             low,
             high,
@@ -1058,6 +1098,8 @@
             which,
             last,
             after,
+            token_grads if which else (),
+            side,
             counts,
             qkv,
             lse,
@@ -1136,8 +1178,8 @@
                 continue
             low, high = (arriving(chain) for chain in before)
             layer, res_grad, mixed_grad, early_part = back_tokens(b - 1, (), low, high)
-            first_part, *more = back_half(b - 1, 0, (), mixed_grad, (early_part,) if b > 1 else ())
-            second_part, token_grad = back_half(b - 1, 1, (), mixed_grad, (*more, res_grad))
+            *more, first_part = back_half(b - 1, 0, (), mixed_grad, (early_part,) if b > 1 else ())
+            token_grad, second_part = back_half(b - 1, 1, (), mixed_grad, (*more, res_grad))
         else:
             low = arriving(before[0], before[1].up, before[1].down)
             high = arriving(before[1])
@@ -1151,33 +1193,29 @@
             layer, res_grad, mixed_grad, early_part = back_tokens(b - 1, (low_chain.mixed,), low, high)
             high_chain.mix(mixed_grad)
             high_chain.send()
-            first_part, *more = back_half(
+            *more, first_part = back_half(
                 b - 1, 0, (high_chain.mixed,), mixed_grad, (early_part,) if b > 1 else ()
             )
             low = returning(low_chain, first_part)
-            second_part, token_grad = back_half(b - 1, 1, (low,), mixed_grad, (*more, res_grad))
+            token_grad, second_part = back_half(b - 1, 1, (low,), mixed_grad, (*more, res_grad))
             low = to_groups(low)
             high = returning(high_chain, second_part, low)
             totals = grads_half(1, (high,), totals)
             high = to_groups(high)
-        layer_rows.append(layer)
-        token_grads.append(token_grad)
+        layers, token_grads = (layer,), (token_grad,)
         early_part, first_part, second_part = (early_part,), (first_part,), (second_part,)
     layer, res_grad, mixed_grad, early_part = back_tokens(batches - 1, (totals[0],), low, high)
-    first_part, *more = back_half(batches - 1, 0, (), mixed_grad, (early_part,))
-    side = (lax.axis_index("expert") % 2)[None]
-    first_half = share_half(first_part)
-    second_part, token_grad = back_half(batches - 1, 1, (first_half,), mixed_grad, (*more, res_grad))
+    diagonal, part, *first_part = back_half(batches - 1, 0, (), mixed_grad, (early_part,))
+    first_half = add_half(*first_part)
+    token_grad, *second_part = back_half(batches - 1, 1, (first_half,), mixed_grad, (diagonal, part, res_grad))
     mine, other = sum_everywhere(first_half)
-    mine_second, other_second = sum_everywhere(share_half(second_part))
-    layer_rows.append(layer)
-    token_grads.append(token_grad)
+    mine_second, other_second = sum_everywhere(add_half(*second_part))
     query_grad, key_grad, value_grad, output_grad, router_grad, gain_f_grad, gain_a_grad, bias_grad = unpack(
         early_rows, experts, side, mine, other, mine_second, other_second
     )
     return (
-        jnp.stack(layer_rows)[:, None],
-        jnp.stack(token_grads)[:, None],
+        layer,
+        token_grad,
         gain_a_grad,
         query_grad,
         key_grad,

time: 649 us -> 642 us (0.989)
    unnamed x114 -> x106, local copies, waits for them, and re-layouts: 17.7 us -> 16 us
  transfers between devices with their start and end apart: 76 -> 76, of which waited for: 33 -> 36; matrix products, arithmetic and copies ran while one was open for 2% -> 1% of each run, Pallas kernels for 36% -> 36%
where the time goes in v6:
time: 642 us; the launch traced here: 638 us
  Pallas kernels  266 us (41%)
  starting transfers between devices  174 us (27%)
  waiting for transfers between devices  168 us (26%)
  local copies, waits for them, and re-layouts  20.1 us (3%)
  other arithmetic  7.15 us (1%)
    ppermute x20, waiting for transfers between devices, send(): self.down = lax.ppermute(self.down, 'hidden', downward(planes, first, last))  68.3 us
    ppermute x20, starting transfers between devices, send(): self.up = lax.ppermute(self.up, 'hidden', upward(planes, first, last))  64.5 us
    pallas_call x4, Pallas kernels, attention_backward(): pl.pallas_call(functools.partial(attn_back_kernel, batch, which, last, le...  58 us
    pallas_call x4, Pallas kernels, experts_half(): pl.pallas_call(functools.partial(expert_kernel, planes, gated, first, len...  55.9 us
    ppermute x20, waiting for transfers between devices, send(): self.up = lax.ppermute(self.up, 'hidden', upward(planes, first, last))  44 us
    ppermute x20, starting transfers between devices, send(): self.down = lax.ppermute(self.down, 'hidden', downward(planes, first, last))  40.6 us
    ppermute x28, waiting for transfers between devices, swap(): lax.ppermute(values, axis, [(k, k ^ distance) for k in range(lax.axis_siz...  39 us
    ppermute x28, starting transfers between devices, swap(): lax.ppermute(values, axis, [(k, k ^ distance) for k in range(lax.axis_siz...  34.6 us
  transfers between devices with their start and end apart: 76, of which 36 were waited for; matrix products, arithmetic and copies ran while one was open for 1% of the time, Pallas kernels for 36%

profile of v6, /device:TPU:0, one launch (start us, length us, event | category | flops | bytes accessed | tf_op | source)
XLA Modules:
  0.0 638.0 jit_solution(421483161408621799)
XLA Ops:
  6.1 5.2 all-to-all-start
  13.1 15.3 %shard_map.239 = (bf16[3,6,512,128]{3,2,1,0:T(8,128)(2,1)}, bf16[6,512,128]{2,1,0:T(8,128)(2,1)}, f32[512,128]{1,0:T(8,128)}) custom-call(bf16[8,80,768]{2,1,0:T(8,128)(2,1)} %get-tuple-element.114.refs_0_, s32[2]{0:T(128)} %bitcast.64, bf16[2,1,512,768]{3,2,1,0:T(8,128)(2,1)} %refs_9_.5, f32[1,768]{1,0:T(1,128)} %broadcast_in_dim.20.refs_3_.refs_5_.refs_9_.refs_8_.refs_10_, ...), custom_call_target="tpu_custom_call" | custom-call | flops 1 | bytes 1 | tf_op jit(solution)/shard_map/pallas_call | solution.py:273
  29.0 5.6 shard_map.240
  34.7 4.2 all-to-all-start.1
  46.9 8.8 %all-to-all-done.1.refs_1_ = bf16[8,96,768]{2,1,0:T(8,128)(2,1)S(1)} async-done(((bf16[8,96,768]{2,1,0:T(8,128)(2,1)}), bf16[8,96,768]{2,1,0:T(8,128)(2,1)S(1)}, u32[]{:S(2)}, u32[]{:S(2)}) %all-to-all-start.1) | async-done | bytes 1179680 | tf_op jit(solution)/shard_map/all_to_all | solution.py:1039
  74.0 15.3 %shard_map.243 = (bf16[3,6,512,128]{3,2,1,0:T(8,128)(2,1)}, bf16[6,512,128]{2,1,0:T(8,128)(2,1)}, f32[512,128]{1,0:T(8,128)}) custom-call(bf16[656,768]{1,0:T(8,128)(2,1)} %shard_map.242.refs_0_.refs_3_.refs_17_, bf16[640,768]{1,0:T(8,128)(2,1)} %copy-done.39, bf16[640,768]{1,0:T(8,128)(2,1)} %collective-permute-done.3.refs_2_.refs_11_, s32[2]{0:T(128)} %bitcast.65, ...), custom_call_target="tpu_custom_call" | custom-call | flops 1 | bytes 1 | tf_op jit(solution)/shard_map/pallas_call | solution.py:273
  89.3 4.7 collective-permute-done.1.refs_1_
  97.7 17.4 %collective-permute-done.8.refs_1_.refs_12_ = bf16[640,768]{1,0:T(8,128)(2,1)} collective-permute-done((bf16[640,768]{1,0:T(8,128)(2,1)}, bf16[640,768]{1,0:T(8,128)(2,1)}, u32[]{:S(2)}, u32[]{:S(2)}) %collective-permute-start.8) | collective-permute-done | bytes 983072 | tf_op jit(solution)/shard_map/ppermute | solution.py:924
  116.4 6.6 %shard_map.245 = (f32[512,768]{1,0:T(8,128)}, f32[512,64]{1,0:T(8,128)}, bf16[8,80,768]{2,1,0:T(8,128)(2,1)}, bf16[8,80,768]{2,1,0:T(8,128)(2,1)}) custom-call(bf16[640,768]{1,0:T(8,128)(2,1)} %collective-permute-done.6.refs_0_.refs_15_, bf16[640,768]{1,0:T(8,128)(2,1)} %collective-permute-done.8.refs_1_.refs_12_, bf16[2,1,512,768]{3,2,1,0:T(8,128)(2,1)} %refs_9_.5, ...), custom_call_target="tpu_custom_call" | custom-call | flops 1 | bytes 1 | tf_op jit(solution)/shard_map/pallas_call | solution.py:343
  122.9 4.2 all-to-all-start.3
  127.2 9.4 %collective-permute-done.5.refs_1_.refs_5_.refs_19_ = bf16[656,768]{1,0:T(8,128)(2,1)S(1)} collective-permute-done((bf16[656,768]{1,0:T(8,128)(2,1)}, bf16[656,768]{1,0:T(8,128)(2,1)S(1)}, u32[]{:S(2)}, u32[]{:S(2)}) %collective-permute-start.5) | collective-permute-done | bytes 1007648 | tf_op jit(solution)/shard_map/ppermute | solution.py:924
  142.0 4.2 all-to-all-start.2
  146.3 11.3 %collective-permute-done.9.refs_3_.refs_13_ = bf16[640,768]{1,0:T(8,128)(2,1)S(1)} collective-permute-done((bf16[640,768]{1,0:T(8,128)(2,1)}, bf16[640,768]{1,0:T(8,128)(2,1)S(1)}, u32[]{:S(2)}, u32[]{:S(2)}) %collective-permute-start.9) | collective-permute-done | bytes 983072 | tf_op jit(solution)/shard_map/ppermute | solution.py:924
  167.8 4.6 collective-permute-start.10
  172.4 6.9 %collective-permute-done.12.refs_6_.refs_20_ = bf16[656,768]{1,0:T(8,128)(2,1)} collective-permute-done((bf16[656,768]{1,0:T(8,128)(2,1)S(1)}, bf16[656,768]{1,0:T(8,128)(2,1)}, u32[]{:S(2)}, u32[]{:S(2)}) %collective-permute-start.12) | collective-permute-done | bytes 1007648 | tf_op jit(solution)/shard_map/ppermute | solution.py:924
  180.6 14.0 %shard_map.251 = (bf16[2,320,768]{2,1,0:T(8,128)(2,1)}, bf16[2,320,768]{2,1,0:T(8,128)(2,1)}, bf16[2,320,768]{2,1,0:T(8,128)(2,1)}, bf16[2,320,768]{2,1,0:T(8,12...) custom-call(bf16[2,320,768]{2,1,0:T(8,128)(2,1)} %shard_map.247.refs, ...), custom_call_target="tpu_custom_call" | custom-call | flops 1 | bytes 1 | tf_op jit(solution)/shard_map/pallas_call | solution.py:440
  194.6 5.7 collective-permute-done.19.down_ref.refs_4_.refs_11_
  208.0 13.9 %collective-permute-start.21 = (bf16[2,320,768]{2,1,0:T(8,128)(2,1)}, bf16[2,320,768]{2,1,0:T(8,128)(2,1)S(1)}, u32[]{:S(2)}, u32[]{:S(2)}) collective-permute-start(bf16[2,320,768]{2,1,0:T(8,128)(2,1)} %get-tuple-element.133), channel_id=1, source_target_pairs={{3,2},{2,1},{1,0},{7,6},{6,5},{5,4},{11,10},{10,9},{9,8},{15,14},{... | collective-permute-start | bytes 2949128 | tf_op jit(solution)/shard_map/ppermute | solution.py:924
  221.9 13.9 %shard_map.248 = (bf16[2,320,768]{2,1,0:T(8,128)(2,1)}, bf16[2,320,768]{2,1,0:T(8,128)(2,1)}, bf16[2,320,768]{2,1,0:T(8,128)(2,1)}, bf16[2,320,768]{2,1,0:T(8,12...) custom-call(bf16[2,320,768]{2,1,0:T(8,128)(2,1)} %shard_map.247.refs, ...), custom_call_target="tpu_custom_call" | custom-call | flops 1 | bytes 1 | tf_op jit(solution)/shard_map/pallas_call | solution.py:440
  239.3 4.6 collective-permute-start.14
  246.6 4.6 collective-permute-start.22
  252.5 13.6 %collective-permute-done.14.up_ref.refs_10_.refs_17_ = bf16[2,320,768]{2,1,0:T(8,128)(2,1)S(1)} collective-permute-done((bf16[2,320,768]{2,1,0:T(8,128)(2,1)S(1)}, bf16[2,320,768]{2,1,0:T(8,128)(2,1)S(1)}, u32[]{:S(2)}, u32[]{:S(2)}) %collective-permute-start.14) | collective-permute-done | bytes 983072 | tf_op jit(solution)/shard_map/ppermute | solution.py:923
  266.1 4.5 collective-permute-done.15.down_ref.refs_7_.refs_14_
  275.7 11.5 %collective-permute-done.22.up_ref.refs_9_.refs_16_ = bf16[2,320,768]{2,1,0:T(8,128)(2,1)S(1)} collective-permute-done((bf16[2,320,768]{2,1,0:T(8,128)(2,1)S(1)}, bf16[2,320,768]{2,1,0:T(8,128)(2,1)S(1)}, u32[]{:S(2)}, u32[]{:S(2)}) %collective-permute-start.22) | collective-permute-done | bytes 983072 | tf_op jit(solution)/shard_map/ppermute | solution.py:923
  287.2 4.5 collective-permute-done.23.down_ref.refs_6_.refs_13_
  297.9 14.0 %shard_map.255 = (bf16[2,320,768]{2,1,0:T(8,128)(2,1)}, bf16[2,320,768]{2,1,0:T(8,128)(2,1)}, bf16[2,320,768]{2,1,0:T(8,128)(2,1)}, bf16[2,320,768]{2,1,0:T(8,12...) custom-call(bf16[2,320,768]{2,1,0:T(8,128)(2,1)} %get-tuple-element., ...), custom_call_target="tpu_custom_call" | custom-call | flops 1 | bytes 1 | tf_op jit(solution)/shard_map/pallas_call | solution.py:440
  311.9 5.5 collective-permute-start.28
  323.8 5.6 collective-permute-done.24.refs_2_.refs_3_
  331.9 14.0 %shard_map.257 = (bf16[2,320,768]{2,1,0:T(8,128)(2,1)}, bf16[2,320,768]{2,1,0:T(8,128)(2,1)}, bf16[2,320,768]{2,1,0:T(8,128)(2,1)}, bf16[2,320,768]{2,1,0:T(8,12...) custom-call(bf16[2,320,768]{2,1,0:T(8,128)(2,1)} %get-tuple-element., ...), custom_call_target="tpu_custom_call" | custom-call | flops 1 | bytes 1 | tf_op jit(solution)/shard_map/pallas_call | solution.py:440
  356.0 5.3 collective-permute-start.32
  361.3 10.2 %collective-permute-done.34.refs_1_.refs_0_ = bf16[2,320,768]{2,1,0:T(8,128)(2,1)S(1)} collective-permute-done((bf16[2,320,768]{2,1,0:T(8,128)(2,1)}, bf16[2,320,768]{2,1,0:T(8,128)(2,1)S(1)}, u32[]{:S(2)}, u32[]{:S(2)}) %collective-permute-start.34) | collective-permute-done | bytes 983072 | tf_op jit(solution)/shard_map/ppermute | solution.py:923
  377.0 4.2 all-to-all-start.4
  381.3 14.5 %shard_map.259 = (f32[8,768,768]{2,1,0:T(8,128)}, f32[8,768,768]{2,1,0:T(8,128)}) custom-call(bf16[2,320,768]{2,1,0:T(8,128)(2,1)} %get-tuple-element.148.refs_0_, bf16[4,320,768]{2,1,0:T(8,128)(2,1)} %get-tuple-element.149.refs_1_, bf16[4,320,768]{2,1,0:T(8,128)(2,1)} %get-tuple-element.150.refs_2_, bf16[4,320,768]{2,1,0:T(8,128)(2,1)} %get-tuple-element.151.refs_3_, ...), custom_call_target="tpu_custom_call" | custom-call | flops 1 | bytes 1 | tf_op jit(solution)/shard_map/pallas_call | solution.py:469
  399.4 4.9 collective-permute-start.30
  409.8 4.5 all-to-all-start.5
  418.2 4.7 collective-permute-start.36
  424.1 4.9 all-to-all-done.5.refs_2_
  429.0 9.2 %shard_map.264 = (bf16[2,1,512,768]{3,2,1,0:T(8,128)(2,1)}, f32[512,768]{1,0:T(8,128)}, bf16[6,512,128]{2,1,0:T(8,128)(2,1)}, f32[1696,384]{1,0:T(8,128)}) custom-call(bf16[2,320,768]{2,1,0:T(8,128)(2,1)} %get-tuple-element.162.refs_0_, s32[2]{0:T(128)} %bitcast.66, bf16[8,80,768]{2,1,0:T(8,128)(2,1)} %all-to-all-done.5.refs_2_, ...), custom_call_target="tpu_custom_call" | custom-call | flops 1 | bytes 1 | tf_op jit(solution)/shard_map/pallas_call | solution.py:560
  442.0 4.2 collective-permute-start.38
  448.0 14.3 %shard_map.266 = (f32[16,1024]{1,0:T(8,128)}, f32[512,768]{1,0:T(8,128)}, f32[2304,384]{1,0:T(8,128)}) custom-call(bf16[2,320,768]{2,1,0:T(8,128)(2,1)} %copy-done.32, s32[1]{0:T(128)} %bitcast.5.refs_1_.refs_0_.refs_2_.side_ref, s32[2]{0:T(128)} %bitcast.67, bf16[3,6,512,128]{3,2,1,0:T(8,128)(2,1)} %get-tuple-element.169.refs_3_, ...), custom_call_target="tpu_custom_call" | custom-call | flops 1 | bytes 1 | tf_op jit(solution)/shard_map/pallas_call | solution.py:760
  469.7 14.7 %shard_map.268 = (bf16[2,1,512,768]{3,2,1,0:T(8,128)(2,1)}, f32[2560,384]{1,0:T(8,128)}) custom-call(bf16[8,80,768]{2,1,0:T(8,128)(2,1)} %shard_map.267.refs_0_, s32[1]{0:T(128)} %bitcast.5.refs_1_.refs_0_.refs_2_.side_ref, s32[2]{0:T(128)} %bitcast.68, bf16[3,6,512,128]{3,2,1,0:T(8,128)(2,1)} %get-tuple-element.169.refs_3_, ...), custom_call_target="tpu_custom_call" | custom-call | flops 1 | bytes 1 | tf_op jit(solution)/shard_map/pallas_call | solution.py:760
  489.2 4.1 all-to-all-start.7
  493.3 14.4 %shard_map.270 = (f32[8,768,768]{2,1,0:T(8,128)}, f32[8,768,768]{2,1,0:T(8,128)}) custom-call(bf16[8,80,768]{2,1,0:T(8,128)(2,1)} %shard_map.269.refs_0_, bf16[4,320,768]{2,1,0:T(8,128)(2,1)} %get-tuple-element.179.refs_1_, bf16[4,320,768]{2,1,0:T(8,128)(2,1)} %get-tuple-element.180.refs_2_, ...), custom_call_target="tpu_custom_call", output_to_operand_aliasing={{0}: (9, {}), {1}: (10, {})} | custom-call | flops 1 | bytes 1 | tf_op jit(solution)/shard_map/pallas_call | solution.py:469
  509.0 8.7 %shard_map.271 = (bf16[2,1,512,768]{3,2,1,0:T(8,128)(2,1)}, f32[512,768]{1,0:T(8,128)}, bf16[6,512,128]{2,1,0:T(8,128)(2,1)}, bf16[1696,384]{1,0:T(8,128)(2,1)}) custom-call(f32[8,768,768]{2,1,0:T(8,128)} %get-tuple-element.113.refs_0_, bf16[2,1,512,768]{3,2,1,0:T(8,128)(2,1)} %get-tuple-element.189.refs_1_, ...), custom_call_target="tpu_custom_call", output_to_operand_aliasing={{0}: (1, {})} | custom-call | flops 1 | bytes 1 | tf_op jit(solution)/shard_map/pallas_call | solution.py:560
  517.7 14.1 %shard_map.272 = (f32[16,1024]{1,0:T(8,128)}, f32[512,768]{1,0:T(8,128)}, bf16[2048,384]{1,0:T(8,128)(2,1)}, bf16[2048,384]{1,0:T(8,128)(2,1)}) custom-call(s32[1]{0:T(128)} %bitcast.5.refs_1_.refs_0_.refs_2_.side_ref, s32[2]{0:T(128)} %bitcast.70, bf16[3,6,512,128]{3,2,1,0:T(8,128)(2,1)} %get-tuple-element.194.refs_2_.refs_4_, ...), custom_call_target="tpu_custom_call" | custom-call | flops 1 | bytes 1 | tf_op jit(solution)/shard_map/pallas_call | solution.py:760
  542.0 14.8 %shard_map.273 = (bf16[2,1,512,768]{3,2,1,0:T(8,128)(2,1)}, bf16[1280,384]{1,0:T(8,128)(2,1)}, bf16[1280,384]{1,0:T(8,128)(2,1)}) custom-call(bf16[2048,384]{1,0:T(8,128)(2,1)} %copy-done.37, bf16[2,1,512,768]{3,2,1,0:T(8,128)(2,1)} %get-tuple-element.200.refs_1_, s32[1]{0:T(128)} %bitcast.5.refs_1_.refs_0_.refs_2_.side_ref, ...), custom_call_target="tpu_custom_call", output_to_operand_aliasing={{0}: (1, {})} | custom-call | flops 1 | bytes 1 | tf_op jit(solution)/shard_map/pallas_call | solution.py:760
  567.8 6.0 collective-permute-done.45
  631.2 6.5 %shard_map.274 = (f32[768,768]{1,0:T(8,128)}, f32[768,768]{1,0:T(8,128)}, f32[768,768]{1,0:T(8,128)}, f32[768,768]{1,0:T(8,128)}, f32[64,768]{1,0:T(8,128)}, /*i...) custom-call(s32[1]{0:T(128)} %bitcast.5.refs_1_.refs_0_.refs_2_.side_ref, bf16[2048,384]{1,0:T(8,128)(2,1)} %copy-done.41, ...), custom_call_target="tpu_custom_call" | custom-call | flops 1 | bytes 1 | tf_op jit(solution)/shard_map/pallas_call | solution.py:842
  (273 shorter events, 218.0 us)
Async XLA Ops:
  6.1 28.5 %all-to-all-start = ((bf16[8,80,768]{2,1,0:T(8,128)(2,1)}), bf16[8,80,768]{2,1,0:T(8,128)(2,1)S(1)}, u32[]{:S(2)}, u32[]{:S(2)}) async-start(bf16[8,80,768]{2,1,0:T(8,128)(2,1)} %get-tuple-element.114.refs_0_), calls=%async_computation | async-start | bytes 1966080 | tf_op jit(solution)/shard_map/all_to_all | solution.py:1039
  34.7 21.0 %all-to-all-start.1 = ((bf16[8,96,768]{2,1,0:T(8,128)(2,1)}), bf16[8,96,768]{2,1,0:T(8,128)(2,1)S(1)}, u32[]{:S(2)}, u32[]{:S(2)}) async-start(bf16[8,96,768]{2,1,0:T(8,128)(2,1)} %get-tuple-element.117.refs_0_), calls=%async_computation.1 | async-start | bytes 2359296 | tf_op jit(solution)/shard_map/all_to_all | solution.py:1039
  42.1 25.8 %collective-permute-start.2 = (bf16[640,768]{1,0:T(8,128)(2,1)}, bf16[640,768]{1,0:T(8,128)(2,1)S(1)}, u32[]{:S(2)}, u32[]{:S(2)}) collective-permute-start(bf16[640,768]{1,0:T(8,128)(2,1)} %shard_map.241.refs_0_.refs_10_), channel_id=1, source_target_pairs={{0,1},{1,2},{2,3},{4,5},{5,6},{6,7},{8,9},{9,10},{10,11},{12,13},{... | collective-permute-start | bytes 2949128 | tf_op jit(solution)/shard_map/ppermute | solution.py:923
  45.6 26.8 %collective-permute-start.3 = (bf16[640,768]{1,0:T(8,128)(2,1)}, bf16[640,768]{1,0:T(8,128)(2,1)}, u32[]{:S(2)}, u32[]{:S(2)}) collective-permute-start(bf16[640,768]{1,0:T(8,128)(2,1)} %shard_map.241.refs_0_.refs_10_), channel_id=1, source_target_pairs={{3,2},{2,1},{1,0},{7,6},{6,5},{5,4},{11,10},{10,9},{9,8},{15,14},{... | collective-permute-start | bytes 2949128 | tf_op jit(solution)/shard_map/ppermute | solution.py:924
  60.5 28.8 %collective-permute-start = (bf16[656,768]{1,0:T(8,128)(2,1)}, bf16[656,768]{1,0:T(8,128)(2,1)S(1)}, u32[]{:S(2)}, u32[]{:S(2)}) collective-permute-start(bf16[656,768]{1,0:T(8,128)(2,1)} %shard_map.242.refs_0_.refs_3_.refs_17_), channel_id=1, source_target_pairs={{0,1},{1,2},{2,3},{4,5},{5,6},{6,7},{8,9},{9,10},{10,11},{12,13},{... | collective-permute-start | bytes 3022856 | tf_op jit(solution)/shard_map/ppermute | solution.py:923
  64.0 30.0 %collective-permute-start.1 = (bf16[656,768]{1,0:T(8,128)(2,1)}, bf16[656,768]{1,0:T(8,128)(2,1)}, u32[]{:S(2)}, u32[]{:S(2)}) collective-permute-start(bf16[656,768]{1,0:T(8,128)(2,1)} %shard_map.242.refs_0_.refs_3_.refs_17_), channel_id=1, source_target_pairs={{3,2},{2,1},{1,0},{7,6},{6,5},{5,4},{11,10},{10,9},{9,8},{15,14},{... | collective-permute-start | bytes 3022856 | tf_op jit(solution)/shard_map/ppermute | solution.py:924
  67.9 29.0 %collective-permute-start.6 = (bf16[640,768]{1,0:T(8,128)(2,1)S(1)}, bf16[640,768]{1,0:T(8,128)(2,1)}, u32[]{:S(2)}, u32[]{:S(2)}) collective-permute-start(bf16[640,768]{1,0:T(8,128)(2,1)S(1)} %collective-permute-done.2.refs_1_.refs_14_), channel_id=1, source_target_pairs={{1,2},{2,3},{5,6},{6,7},{9,10},{10,11},{13,14},{14,15},{17,18},{18... | collective-permute-start | bytes 2949128 | tf_op jit(solution)/shard_map/ppermute | solution.py:923
  72.4 42.7 %collective-permute-start.8 = (bf16[640,768]{1,0:T(8,128)(2,1)}, bf16[640,768]{1,0:T(8,128)(2,1)}, u32[]{:S(2)}, u32[]{:S(2)}) collective-permute-start(bf16[640,768]{1,0:T(8,128)(2,1)} %collective-permute-done.3.refs_2_.refs_11_), channel_id=1, source_target_pairs={{2,1},{1,0},{6,5},{5,4},{10,9},{9,8},{14,13},{13,12},{18,17},{17,1... | collective-permute-start | bytes 2949128 | tf_op jit(solution)/shard_map/ppermute | solution.py:924
  94.0 42.5 %collective-permute-start.5 = (bf16[656,768]{1,0:T(8,128)(2,1)}, bf16[656,768]{1,0:T(8,128)(2,1)S(1)}, u32[]{:S(2)}, u32[]{:S(2)}) collective-permute-start(bf16[656,768]{1,0:T(8,128)(2,1)} %get-tuple-element.120.refs_4_.refs_18_), channel_id=1, source_target_pairs={{2,1},{1,0},{6,5},{5,4},{10,9},{9,8},{14,13},{13,12},{18,17},{17,1... | collective-permute-start | bytes 3022856 | tf_op jit(solution)/shard_map/ppermute | solution.py:924
  95.3 42.6 %collective-permute-start.4 = (bf16[656,768]{1,0:T(8,128)(2,1)}, bf16[656,768]{1,0:T(8,128)(2,1)}, u32[]{:S(2)}, u32[]{:S(2)}) collective-permute-start(bf16[656,768]{1,0:T(8,128)(2,1)} %get-tuple-element.119.refs_7_.refs_21_), channel_id=1, source_target_pairs={{1,2},{2,3},{5,6},{6,7},{9,10},{10,11},{13,14},{14,15},{17,18},{18... | collective-permute-start | bytes 3022856 | tf_op jit(solution)/shard_map/ppermute | solution.py:923
  96.9 49.3 %collective-permute-start.7 = (bf16[640,768]{1,0:T(8,128)(2,1)}, bf16[640,768]{1,0:T(8,128)(2,1)S(1)}, u32[]{:S(2)}, u32[]{:S(2)}) collective-permute-start(bf16[640,768]{1,0:T(8,128)(2,1)} %collective-permute-done.6.refs_0_.refs_15_), channel_id=1, source_target_pairs={{2,3},{6,7},{10,11},{14,15},{18,19},{22,23},{26,27},{30,31}} | collective-permute-start | bytes 2949128 | tf_op jit(solution)/shard_map/ppermute | solution.py:923
  115.1 42.6 %collective-permute-start.9 = (bf16[640,768]{1,0:T(8,128)(2,1)}, bf16[640,768]{1,0:T(8,128)(2,1)S(1)}, u32[]{:S(2)}, u32[]{:S(2)}) collective-permute-start(bf16[640,768]{1,0:T(8,128)(2,1)} %collective-permute-done.8.refs_1_.refs_12_), channel_id=1, source_target_pairs={{1,0},{5,4},{9,8},{13,12},{17,16},{21,20},{25,24},{29,28}} | collective-permute-start | bytes 2949128 | tf_op jit(solution)/shard_map/ppermute | solution.py:924
  136.6 42.8 %collective-permute-start.12 = (bf16[656,768]{1,0:T(8,128)(2,1)S(1)}, bf16[656,768]{1,0:T(8,128)(2,1)}, u32[]{:S(2)}, u32[]{:S(2)}) collective-permute-start(bf16[656,768]{1,0:T(8,128)(2,1)S(1)} %collective-permute-done.5.refs_1_.refs_5_.refs_19_), channel_id=1, source_target_pairs={{1,0},{5,4},{9,8},{13,12},{17,16},{21,20},{25,24},{29,28}} | collective-permute-start | bytes 3022856 | tf_op jit(solution)/shard_map/ppermute | solution.py:924
  137.9 42.8 %collective-permute-start.13 = (bf16[656,768]{1,0:T(8,128)(2,1)}, bf16[656,768]{1,0:T(8,128)(2,1)}, u32[]{:S(2)}, u32[]{:S(2)}) collective-permute-start(bf16[656,768]{1,0:T(8,128)(2,1)} %collective-permute-done.4.refs_0_.refs_8_.refs_22_), channel_id=1, source_target_pairs={{2,3},{6,7},{10,11},{14,15},{18,19},{22,23},{26,27},{30,31}} | collective-permute-start | bytes 3022856 | tf_op jit(solution)/shard_map/ppermute | solution.py:923
  142.0 22.7 %all-to-all-start.2 = ((bf16[8,80,768]{2,1,0:T(8,128)(2,1)}), bf16[8,80,768]{2,1,0:T(8,128)(2,1)}, u32[]{:S(2)}, u32[]{:S(2)}) async-start(bf16[8,80,768]{2,1,0:T(8,128)(2,1)} %get-tuple-element.121), calls=%async_computation.2 | async-start | bytes 1966080 | tf_op jit(solution)/shard_map/all_to_all | solution.py:1039
  161.8 32.8 %collective-permute-start.18 = (bf16[2,320,768]{2,1,0:T(8,128)(2,1)}, bf16[2,320,768]{2,1,0:T(8,128)(2,1)S(1)}, u32[]{:S(2)}, u32[]{:S(2)}) collective-permute-start(bf16[2,320,768]{2,1,0:T(8,128)(2,1)} %shard_map.247.refs_0_.refs_3_.refs_10_), channel_id=1, source_target_pairs={{0,1},{1,2},{2,3},{4,5},{5,6},{6,7},{8,9},{9,10},{10,11},{12,13},{... | collective-permute-start | bytes 2949128 | tf_op jit(solution)/shard_map/ppermute | solution.py:923
  163.4 37.0 %collective-permute-start.19 = (bf16[2,320,768]{2,1,0:T(8,128)(2,1)}, bf16[2,320,768]{2,1,0:T(8,128)(2,1)}, u32[]{:S(2)}, u32[]{:S(2)}) collective-permute-start(bf16[2,320,768]{2,1,0:T(8,128)(2,1)} %shard_map.247.refs_0_.refs_3_.refs_10_), channel_id=1, source_target_pairs={{3,2},{2,1},{1,0},{7,6},{6,5},{5,4},{11,10},{10,9},{9,8},{15,14},{... | collective-permute-start | bytes 2949128 | tf_op jit(solution)/shard_map/ppermute | solution.py:924
  167.8 68.0 %collective-permute-start.10 = (bf16[2,320,768]{2,1,0:T(8,128)(2,1)}, bf16[2,320,768]{2,1,0:T(8,128)(2,1)S(1)}, u32[]{:S(2)}, u32[]{:S(2)}) collective-permute-start(bf16[2,320,768]{2,1,0:T(8,128)(2,1)} %shard_map.246.refs_1_.refs_5_.refs_12_), channel_id=1, source_target_pairs={{0,1},{1,2},{2,3},{4,5},{5,6},{6,7},{8,9},{9,10},{10,11},{12,13},{... | collective-permute-start | bytes 2949128 | tf_op jit(solution)/shard_map/ppermute | solution.py:923
  179.3 56.5 %collective-permute-start.11 = (bf16[2,320,768]{2,1,0:T(8,128)(2,1)}, bf16[2,320,768]{2,1,0:T(8,128)(2,1)S(1)}, u32[]{:S(2)}, u32[]{:S(2)}) collective-permute-start(bf16[2,320,768]{2,1,0:T(8,128)(2,1)} %shard_map.246.refs_1_.refs_5_.refs_12_), channel_id=1, source_target_pairs={{3,2},{2,1},{1,0},{7,6},{6,5},{5,4},{11,10},{10,9},{9,8},{15,14},{... | collective-permute-start | bytes 2949128 | tf_op jit(solution)/shard_map/ppermute | solution.py:924
  206.5 38.8 %collective-permute-start.20 = (bf16[2,320,768]{2,1,0:T(8,128)(2,1)}, bf16[2,320,768]{2,1,0:T(8,128)(2,1)S(1)}, u32[]{:S(2)}, u32[]{:S(2)}) collective-permute-start(bf16[2,320,768]{2,1,0:T(8,128)(2,1)} %get-tuple-element.132), channel_id=1, source_target_pairs={{0,1},{1,2},{2,3},{4,5},{5,6},{6,7},{8,9},{9,10},{10,11},{12,13},{... | collective-permute-start | bytes 2949128 | tf_op jit(solution)/shard_map/ppermute | solution.py:923
  208.0 37.3 %collective-permute-start.21 = (bf16[2,320,768]{2,1,0:T(8,128)(2,1)}, bf16[2,320,768]{2,1,0:T(8,128)(2,1)S(1)}, u32[]{:S(2)}, u32[]{:S(2)}) collective-permute-start(bf16[2,320,768]{2,1,0:T(8,128)(2,1)} %get-tuple-element.133), channel_id=1, source_target_pairs={{3,2},{2,1},{1,0},{7,6},{6,5},{5,4},{11,10},{10,9},{9,8},{15,14},{... | collective-permute-start | bytes 2949128 | tf_op jit(solution)/shard_map/ppermute | solution.py:924
  239.3 26.7 %collective-permute-start.14 = (bf16[2,320,768]{2,1,0:T(8,128)(2,1)S(1)}, bf16[2,320,768]{2,1,0:T(8,128)(2,1)S(1)}, u32[]{:S(2)}, u32[]{:S(2)}) collective-permute-start(bf16[2,320,768]{2,1,0:T(8,128)(2,1)S(1)} %get-tuple-element.125), channel_id=1, source_target_pairs={{0,1},{1,2},{2,3},{4,5},{5,6},{6,7},{8,9},{9,10},{10,11},{12,13},{... | collective-permute-start | bytes 2949128 | tf_op jit(solution)/shard_map/ppermute | solution.py:923
  244.0 26.6 %collective-permute-start.15 = (bf16[2,320,768]{2,1,0:T(8,128)(2,1)S(1)}, bf16[2,320,768]{2,1,0:T(8,128)(2,1)S(1)}, u32[]{:S(2)}, u32[]{:S(2)}) collective-permute-start(bf16[2,320,768]{2,1,0:T(8,128)(2,1)S(1)} %get-tuple-element.126), channel_id=1, source_target_pairs={{3,2},{2,1},{1,0},{7,6},{6,5},{5,4},{11,10},{10,9},{9,8},{15,14},{... | collective-permute-start | bytes 2949128 | tf_op jit(solution)/shard_map/ppermute | solution.py:924
  246.6 40.6 %collective-permute-start.22 = (bf16[2,320,768]{2,1,0:T(8,128)(2,1)S(1)}, bf16[2,320,768]{2,1,0:T(8,128)(2,1)S(1)}, u32[]{:S(2)}, u32[]{:S(2)}) collective-permute-start(bf16[2,320,768]{2,1,0:T(8,128)(2,1)S(1)} %get-tuple-element.135), channel_id=1, source_target_pairs={{0,1},{1,2},{2,3},{4,5},{5,6},{6,7},{8,9},{9,10},{10,11},{12,13},{... | collective-permute-start | bytes 2949128 | tf_op jit(solution)/shard_map/ppermute | solution.py:923
  251.2 40.4 %collective-permute-start.23 = (bf16[2,320,768]{2,1,0:T(8,128)(2,1)S(1)}, bf16[2,320,768]{2,1,0:T(8,128)(2,1)S(1)}, u32[]{:S(2)}, u32[]{:S(2)}) collective-permute-start(bf16[2,320,768]{2,1,0:T(8,128)(2,1)S(1)} %get-tuple-element.136), channel_id=1, source_target_pairs={{3,2},{2,1},{1,0},{7,6},{6,5},{5,4},{11,10},{10,9},{9,8},{15,14},{... | collective-permute-start | bytes 2949128 | tf_op jit(solution)/shard_map/ppermute | solution.py:924
  272.5 45.0 %collective-permute-start.16 = (bf16[2,320,768]{2,1,0:T(8,128)(2,1)}, bf16[2,320,768]{2,1,0:T(8,128)(2,1)S(1)}, u32[]{:S(2)}, u32[]{:S(2)}) collective-permute-start(bf16[2,320,768]{2,1,0:T(8,128)(2,1)} %get-tuple-element.128), channel_id=1, source_target_pairs={{0,1},{1,2},{2,3},{4,5},{5,6},{6,7},{8,9},{9,10},{10,11},{12,13},{... | collective-permute-start | bytes 2949128 | tf_op jit(solution)/shard_map/ppermute | solution.py:923
  274.4 44.7 %collective-permute-start.17 = (bf16[2,320,768]{2,1,0:T(8,128)(2,1)}, bf16[2,320,768]{2,1,0:T(8,128)(2,1)S(1)}, u32[]{:S(2)}, u32[]{:S(2)}) collective-permute-start(bf16[2,320,768]{2,1,0:T(8,128)(2,1)} %get-tuple-element.129), channel_id=1, source_target_pairs={{3,2},{2,1},{1,0},{7,6},{6,5},{5,4},{11,10},{10,9},{9,8},{15,14},{... | collective-permute-start | bytes 2949128 | tf_op jit(solution)/shard_map/ppermute | solution.py:924
  293.7 35.7 %collective-permute-start.24 = (bf16[2,320,768]{2,1,0:T(8,128)(2,1)}, bf16[2,320,768]{2,1,0:T(8,128)(2,1)}, u32[]{:S(2)}, u32[]{:S(2)}) collective-permute-start(bf16[2,320,768]{2,1,0:T(8,128)(2,1)} %get-tuple-element.137.refs_0_), channel_id=1, source_target_pairs={{0,1},{1,2},{2,3},{4,5},{5,6},{6,7},{8,9},{9,10},{10,11},{12,13},{... | collective-permute-start | bytes 2949128 | tf_op jit(solution)/shard_map/ppermute | solution.py:923
  296.5 35.4 %collective-permute-start.25 = (bf16[2,320,768]{2,1,0:T(8,128)(2,1)}, bf16[2,320,768]{2,1,0:T(8,128)(2,1)}, u32[]{:S(2)}, u32[]{:S(2)}) collective-permute-start(bf16[2,320,768]{2,1,0:T(8,128)(2,1)} %get-tuple-element.138.refs_1_), channel_id=1, source_target_pairs={{3,2},{2,1},{1,0},{7,6},{6,5},{5,4},{11,10},{10,9},{9,8},{15,14},{... | collective-permute-start | bytes 2949128 | tf_op jit(solution)/shard_map/ppermute | solution.py:924
  311.9 38.5 %collective-permute-start.28 = (bf16[2,320,768]{2,1,0:T(8,128)(2,1)}, bf16[2,320,768]{2,1,0:T(8,128)(2,1)}, u32[]{:S(2)}, u32[]{:S(2)}) collective-permute-start(bf16[2,320,768]{2,1,0:T(8,128)(2,1)} %get-tuple-element.145.downsum_ref), channel_id=1, source_target_pairs={{0,1},{4,5},{8,9},{12,13},{16,17},{20,21},{24,25},{28,29}} | collective-permute-start | bytes 2949128 | tf_op jit(solution)/shard_map/ppermute | solution.py:923
  317.5 34.6 %collective-permute-start.29 = (bf16[2,320,768]{2,1,0:T(8,128)(2,1)}, bf16[2,320,768]{2,1,0:T(8,128)(2,1)}, u32[]{:S(2)}, u32[]{:S(2)}) collective-permute-start(bf16[2,320,768]{2,1,0:T(8,128)(2,1)} %get-tuple-element.146.upsum_ref), channel_id=1, source_target_pairs={{3,2},{7,6},{11,10},{15,14},{19,18},{23,22},{27,26},{31,30}} | collective-permute-start | bytes 2949128 | tf_op jit(solution)/shard_map/ppermute | solution.py:924
  322.5 49.0 %collective-permute-start.34 = (bf16[2,320,768]{2,1,0:T(8,128)(2,1)}, bf16[2,320,768]{2,1,0:T(8,128)(2,1)S(1)}, u32[]{:S(2)}, u32[]{:S(2)}) collective-permute-start(bf16[2,320,768]{2,1,0:T(8,128)(2,1)} %get-tuple-element.140.refs_0_), channel_id=1, source_target_pairs={{0,1},{1,2},{2,3},{4,5},{5,6},{6,7},{8,9},{9,10},{10,11},{12,13},{... | collective-permute-start | bytes 2949128 | tf_op jit(solution)/shard_map/ppermute | solution.py:923
  329.4 43.8 %collective-permute-start.35 = (bf16[2,320,768]{2,1,0:T(8,128)(2,1)}, bf16[2,320,768]{2,1,0:T(8,128)(2,1)}, u32[]{:S(2)}, u32[]{:S(2)}) collective-permute-start(bf16[2,320,768]{2,1,0:T(8,128)(2,1)} %get-tuple-element.141.refs_1_), channel_id=1, source_target_pairs={{3,2},{2,1},{1,0},{7,6},{6,5},{5,4},{11,10},{10,9},{9,8},{15,14},{... | collective-permute-start | bytes 2949128 | tf_op jit(solution)/shard_map/ppermute | solution.py:924
  345.9 49.8 %collective-permute-start.26 = (bf16[2,320,768]{2,1,0:T(8,128)(2,1)}, bf16[2,320,768]{2,1,0:T(8,128)(2,1)S(1)}, u32[]{:S(2)}, u32[]{:S(2)}) collective-permute-start(bf16[2,320,768]{2,1,0:T(8,128)(2,1)} %get-tuple-element.142.downsum_ref), channel_id=1, source_target_pairs={{0,1},{4,5},{8,9},{12,13},{16,17},{20,21},{24,25},{28,29}} | collective-permute-start | bytes 2949128 | tf_op jit(solution)/shard_map/ppermute | solution.py:923
  350.5 45.3 %collective-permute-start.27 = (bf16[2,320,768]{2,1,0:T(8,128)(2,1)}, bf16[2,320,768]{2,1,0:T(8,128)(2,1)}, u32[]{:S(2)}, u32[]{:S(2)}) collective-permute-start(bf16[2,320,768]{2,1,0:T(8,128)(2,1)} %get-tuple-element.143.upsum_ref), channel_id=1, source_target_pairs={{3,2},{7,6},{11,10},{15,14},{19,18},{23,22},{27,26},{31,30}} | collective-permute-start | bytes 2949128 | tf_op jit(solution)/shard_map/ppermute | solution.py:924
  356.0 58.3 %collective-permute-start.32 = (bf16[2,320,768]{2,1,0:T(8,128)(2,1)}, bf16[2,320,768]{2,1,0:T(8,128)(2,1)}, u32[]{:S(2)}, u32[]{:S(2)}) collective-permute-start(bf16[2,320,768]{2,1,0:T(8,128)(2,1)} %get-tuple-element.148.refs_0_), channel_id=1, source_target_pairs={{0,1},{1,2},{4,5},{5,6},{8,9},{9,10},{12,13},{13,14},{16,17},{17,1... | collective-permute-start | bytes 2949128 | tf_op jit(solution)/shard_map/ppermute | solution.py:923
  371.5 42.8 %collective-permute-start.33 = (bf16[2,320,768]{2,1,0:T(8,128)(2,1)}, bf16[2,320,768]{2,1,0:T(8,128)(2,1)}, u32[]{:S(2)}, u32[]{:S(2)}) collective-permute-start(bf16[2,320,768]{2,1,0:T(8,128)(2,1)} %get-tuple-element.160), channel_id=1, source_target_pairs={{3,2},{2,1},{7,6},{6,5},{11,10},{10,9},{15,14},{14,13},{19,18},{18... | collective-permute-start | bytes 2949128 | tf_op jit(solution)/shard_map/ppermute | solution.py:924
  377.0 32.7 %all-to-all-start.4 = ((bf16[8,80,768]{2,1,0:T(8,128)(2,1)}), bf16[8,80,768]{2,1,0:T(8,128)(2,1)S(1)}, u32[]{:S(2)}, u32[]{:S(2)}) async-start(bf16[8,80,768]{2,1,0:T(8,128)(2,1)} %shard_map.261), calls=%async_computation.4 | async-start | bytes 1966080 | tf_op jit(solution)/shard_map/all_to_all | solution.py:1039
  399.4 38.9 %collective-permute-start.30 = (bf16[2,320,768]{2,1,0:T(8,128)(2,1)}, bf16[2,320,768]{2,1,0:T(8,128)(2,1)}, u32[]{:S(2)}, u32[]{:S(2)}) collective-permute-start(bf16[2,320,768]{2,1,0:T(8,128)(2,1)} %get-tuple-element.158), channel_id=1, source_target_pairs={{0,1},{1,2},{4,5},{5,6},{8,9},{9,10},{12,13},{13,14},{16,17},{17,1... | collective-permute-start | bytes 2949128 | tf_op jit(solution)/shard_map/ppermute | solution.py:923
  404.3 34.0 %collective-permute-start.31 = (bf16[2,320,768]{2,1,0:T(8,128)(2,1)}, bf16[2,320,768]{2,1,0:T(8,128)(2,1)}, u32[]{:S(2)}, u32[]{:S(2)}) collective-permute-start(bf16[2,320,768]{2,1,0:T(8,128)(2,1)} %get-tuple-element.159), channel_id=1, source_target_pairs={{3,2},{2,1},{7,6},{6,5},{11,10},{10,9},{15,14},{14,13},{19,18},{18... | collective-permute-start | bytes 2949128 | tf_op jit(solution)/shard_map/ppermute | solution.py:924
  418.2 44.1 %collective-permute-start.36 = (bf16[2,320,768]{2,1,0:T(8,128)(2,1)}, bf16[2,320,768]{2,1,0:T(8,128)(2,1)}, u32[]{:S(2)}, u32[]{:S(2)}) collective-permute-start(bf16[2,320,768]{2,1,0:T(8,128)(2,1)} %get-tuple-element.162.refs_0_), channel_id=1, source_target_pairs={{0,1},{1,2},{2,3},{4,5},{5,6},{6,7},{8,9},{9,10},{10,11},{12,13},{... | collective-permute-start | bytes 2949128 | tf_op jit(solution)/shard_map/ppermute | solution.py:923
  422.9 39.4 %collective-permute-start.37 = (bf16[2,320,768]{2,1,0:T(8,128)(2,1)}, bf16[2,320,768]{2,1,0:T(8,128)(2,1)}, u32[]{:S(2)}, u32[]{:S(2)}) collective-permute-start(bf16[2,320,768]{2,1,0:T(8,128)(2,1)} %get-tuple-element.172), channel_id=1, source_target_pairs={{3,2},{2,1},{1,0},{7,6},{6,5},{5,4},{11,10},{10,9},{9,8},{15,14},{... | collective-permute-start | bytes 2949128 | tf_op jit(solution)/shard_map/ppermute | solution.py:924
  442.0 42.4 %collective-permute-start.38 = (bf16[2,320,768]{2,1,0:T(8,128)(2,1)S(1)}, bf16[2,320,768]{2,1,0:T(8,128)(2,1)}, u32[]{:S(2)}, u32[]{:S(2)}) collective-permute-start(bf16[2,320,768]{2,1,0:T(8,128)(2,1)S(1)} %get-tuple-element.168.refs_0_), channel_id=1, source_target_pairs={{0,1},{1,2},{2,3},{4,5},{5,6},{6,7},{8,9},{9,10},{10,11},{12,13},{... | collective-permute-start | bytes 2949128 | tf_op jit(solution)/shard_map/ppermute | solution.py:923
  446.3 38.2 %collective-permute-start.39 = (bf16[2,320,768]{2,1,0:T(8,128)(2,1)S(1)}, bf16[2,320,768]{2,1,0:T(8,128)(2,1)}, u32[]{:S(2)}, u32[]{:S(2)}) collective-permute-start(bf16[2,320,768]{2,1,0:T(8,128)(2,1)S(1)} %get-tuple-element.178), channel_id=1, source_target_pairs={{3,2},{2,1},{1,0},{7,6},{6,5},{5,4},{11,10},{10,9},{9,8},{15,14},{... | collective-permute-start | bytes 2949128 | tf_op jit(solution)/shard_map/ppermute | solution.py:924
  540.2 19.6 %collective-permute-start.42 = (bf16[512,384]{1,0:T(8,128)(2,1)}, bf16[512,384]{1,0:T(8,128)(2,1)}, u32[]{:S(2)}, u32[]{:S(2)}) collective-permute-start(bf16[512,384]{1,0:T(8,128)(2,1)} %get-tuple-element.222), channel_id=1, source_target_pairs={{0,16},{4,20},{8,24},{12,28},{16,0},{20,4},{24,8},{28,12},{1,17},{... | collective-permute-start | bytes 1179656 | tf_op jit(solution)/shard_map/ppermute | solution.py:956
  556.8 21.5 %collective-permute-start.54 = (bf16[1280,384]{1,0:T(8,128)(2,1)}, bf16[1280,384]{1,0:T(8,128)(2,1)S(1)}, u32[]{:S(2)}, u32[]{:S(2)}) collective-permute-start(bf16[1280,384]{1,0:T(8,128)(2,1)} %get-tuple-element.206), channel_id=1, source_target_pairs={{0,4},{4,0},{8,12},{12,8},{16,20},{20,16},{24,28},{28,24},{1,5},{5... | collective-permute-start | bytes 2949128 | tf_op jit(solution)/shard_map/ppermute | solution.py:956
  586.5 21.2 %collective-permute-start.51 = (bf16[512,384]{1,0:T(8,128)(2,1)S(1)}, bf16[512,384]{1,0:T(8,128)(2,1)S(1)}, u32[]{:S(2)}, u32[]{:S(2)}) collective-permute-start(bf16[512,384]{1,0:T(8,128)(2,1)S(1)} %pad_maximum_fusion.2), channel_id=1, source_target_pairs={{0,16},{4,20},{8,24},{12,28},{16,0},{20,4},{24,8},{28,12},{1,17},{... | collective-permute-start | bytes 1179656 | tf_op jit(solution)/shard_map/ppermute | solution.py:956
  588.4 19.3 %collective-permute-start.52 = (bf16[512,384]{1,0:T(8,128)(2,1)S(1)}, bf16[512,384]{1,0:T(8,128)(2,1)S(1)}, u32[]{:S(2)}, u32[]{:S(2)}) collective-permute-start(bf16[512,384]{1,0:T(8,128)(2,1)S(1)} %pad_maximum_fusion.2), channel_id=1, source_target_pairs={{0,24},{4,28},{8,16},{12,20},{16,8},{20,12},{24,0},{28,4},{1,25},{... | collective-permute-start | bytes 1179656 | tf_op jit(solution)/shard_map/ppermute | solution.py:956
  (81 other events, 693.5 us)

commit v7 on v6

--- a/solution.py
+++ b/solution.py
@@ -87,50 +87,55 @@
     return jnp.where(held, group * message + inside - first, -1)
 
 
-def prep_kernel(per, capacity, len_ref, row_ref, col_ref, cot_ref, srow_ref, scol_ref, slots_ref):
-    batches, _, length = row_ref.shape
-    groups, message, width = slots_ref.shape
-    experts = groups * per // capacity
+def prep_kernel(batch, experts, capacity, waits, *refs):
+    refs = refs[waits:]
+    len_ref, row_ref, col_ref, *refs = refs
+    length = row_ref.shape[-1]
     before = one_hot(iota((length, length), 0) < iota((length, length), 1))
     after = one_hot(iota((length, length), 1) < iota((length, length), 0))
-    for b in range(batches):
-        count = len_ref[b]
-        row = row_ref[b]
-        col = col_ref[b]
-        valid_row = iota((1, length), 1) < count
-        valid_col = iota((length, 1), 0) < count
-        chosen_row = iota((experts, length), 0) == row
-        chosen_col = iota((length, experts), 1) == col
-        earlier_row = dot(one_hot(chosen_row & valid_row), before)
-        rank_row = jnp.sum(jnp.where(chosen_row, earlier_row, 0.0), axis=0, keepdims=True).astype(jnp.int32)
-        earlier_col = dot(after, one_hot(chosen_col & valid_col))
-        rank_col = jnp.sum(jnp.where(chosen_col, earlier_col, 0.0), axis=1, keepdims=True).astype(jnp.int32)
-        slot_row = jnp.where(valid_row & (rank_row < capacity), row * capacity + rank_row, -1)
-        srow_ref[b] = slot_row
-        scol_ref[b] = jnp.where(valid_col & (rank_col < capacity), col * capacity + rank_col, -1)
-        if b == 0:
-            dispatch = one_hot(iota((groups * message, length), 0) == spread_slots(slot_row, per, message))
-            slots_ref[...] = dot(dispatch, cot_ref[0, 0]).astype(BF16).reshape(groups, message, width)
-
-
-def prep(lengths, routes, cot, groups, per, capacity):
+    count = len_ref[batch]
+    row = row_ref[0]
+    col = col_ref[0]
+    valid_row = iota((1, length), 1) < count
+    valid_col = iota((length, 1), 0) < count
+    chosen_row = iota((experts, length), 0) == row
+    chosen_col = iota((length, experts), 1) == col
+    earlier_row = dot(one_hot(chosen_row & valid_row), before)
+    rank_row = jnp.sum(jnp.where(chosen_row, earlier_row, 0.0), axis=0, keepdims=True).astype(jnp.int32)
+    earlier_col = dot(after, one_hot(chosen_col & valid_col))
+    rank_col = jnp.sum(jnp.where(chosen_col, earlier_col, 0.0), axis=1, keepdims=True).astype(jnp.int32)
+    slot_row = jnp.where(valid_row & (rank_row < capacity), row * capacity + rank_row, -1)
+    if batch:
+        srow_ref, scol_ref = refs
+    else:
+        cot_ref, srow_ref, scol_ref, slots_ref = refs
+        groups, message, width = slots_ref.shape
+        place = spread_slots(slot_row, experts * capacity // groups, message)
+        dispatch = one_hot(iota((groups * message, length), 0) == place)
+        slots_ref[...] = dot(dispatch, cot_ref[0, 0]).astype(BF16).reshape(groups, message, width)
+    srow_ref[0] = slot_row
+    scol_ref[0] = jnp.where(valid_col & (rank_col < capacity), col * capacity + rank_col, -1)
+
+
+def prep(batch, after, lengths, routes, cot, groups, experts, capacity):
     batches, length = routes.shape
     width = cot.shape[-1]
-    vmem = WHOLE
-    message = padded(per)
+    rows = routes.reshape(batches, 1, length)
+    columns = routes.reshape(batches, length, 1)
+    first = batch == 0
+    message = padded(experts // groups * capacity)
     return pl.pallas_call(
-        functools.partial(prep_kernel, per, capacity),
+        functools.partial(prep_kernel, batch, experts, capacity, len(after)),
         grid=(1,),
-        in_specs=[SCALARS, vmem, vmem, batch_block(cot, 0)],
-        out_specs=[vmem] * 3,
-        out_shape=[
-            jax.ShapeDtypeStruct((batches, 1, length), jnp.int32),
-            jax.ShapeDtypeStruct((batches, length, 1), jnp.int32),
-            jax.ShapeDtypeStruct((groups, message, width), BF16),
-        ],
+        in_specs=[ANYWHERE] * len(after)
+        + [SCALARS, batch_block(rows, batch), batch_block(columns, batch)]
+        + ([batch_block(cot, 0)] if first else []),
+        out_specs=[WHOLE] * (3 if first else 2),
+        out_shape=[jax.ShapeDtypeStruct((1, 1, length), jnp.int32), jax.ShapeDtypeStruct((1, length, 1), jnp.int32)]
+        + ([jax.ShapeDtypeStruct((groups, message, width), BF16)] if first else []),
         compiler_params=params(60),
         cost_estimate=cost(),
-    )(lengths, routes.reshape(batches, 1, length), routes.reshape(batches, length, 1), cot)
+    )(*after, lengths, rows, columns, *((cot,) if first else ()))
 
 
 def slot_places(kinds, local, groups, capacity, message):
@@ -265,7 +270,7 @@
         mixed_ref[pair] = mixed_t_ref[...].T.astype(BF16)
         return carry
 
-    lax.fori_loop(0, PAIRS, one_pair, 0)
+    lax.fori_loop(0, PAIRS, one_pair, 0, unroll=3)
 
 
 def attention_forward(batch, after, counts, tokens, gain, wq, wk, wv, vector):
@@ -344,9 +349,9 @@
         functools.partial(route_kernel, per, gated, len(after)),
         grid=(1,),
         in_specs=[ANYWHERE] * len(after)
-        + [batch_block(tokens, batch), batch_block(cot, batch)]
-        + [WHOLE] * 4
-        + [batch_block(srow, batch), batch_block(rcol, batch)],
+        + [batch_block(tokens, batch), batch_block(cot, batch) if gated else ANYWHERE]
+        + [WHOLE] * 5
+        + [batch_block(rcol, batch)],
         out_specs=[WHOLE] * (4 if gated else 3),
         out_shape=[
             jax.ShapeDtypeStruct((length, width), F32),
@@ -561,7 +566,7 @@
         functools.partial(combine_kernel, per, batch, len(after) + len(layers)),
         grid=(1,),
         in_specs=[ANYWHERE] * (len(after) + len(layers))
-        + [SCALARS, WHOLE, WHOLE, batch_block(scol, batch), batch_block(rcol, batch), ANYWHERE, WHOLE, ANYWHERE]
+        + [SCALARS, WHOLE, WHOLE, WHOLE, batch_block(rcol, batch), ANYWHERE, WHOLE, ANYWHERE]
         + [WHOLE] * 2
         + [ANYWHERE] * (2 + len(past)),
         out_specs=[batch_block(cot, batch)] + [WHOLE] * 3,
@@ -1053,10 +1058,14 @@
 
     def routing(b, *after):
         return route(
-            b, after, tokens, cotangent, forward[b][1], w_output, gain_f, router_rows, srow, rcol, groups, per, b > 0
+            b, after, tokens, cotangent, forward[b][1], w_output, gain_f, router_rows, slots[b][0], rcol, groups, per, b > 0
         )
 
-    srow, scol, cot_slots = prep(counts, routes.reshape(batches, length), cotangent, groups, per, capacity)
+    def place(b, *after):
+        return prep(b, after, counts, routes.reshape(batches, length), cotangent, groups, experts, capacity)
+
+    *placed, cot_slots = place(0)
+    slots = [placed]
     rcol = routes.reshape(batches, length, 1)
     early_rows = width + experts + 16
     unit = 16 * groups * planes
@@ -1077,7 +1086,7 @@
             counts,
             low,
             high,
-            scol,
+            slots[b][1],
             rcol,
             *routed[b][:2],
             cotangent,
@@ -1127,6 +1136,7 @@
     inputs = regroup_gated(to_groups(routed[0][2]), local * rows, capacity, (grads,))
     input_chain = Chain(planes, inputs)
     input_chain.send()
+    slots.append(place(1, inputs))
     forward.append(attend(1, inputs, grad_chain.up, grad_chain.down))
     grad_chain.send()
     routed.append(routing(1, grad_chain.up, grad_chain.down))
@@ -1144,6 +1154,7 @@
         ready = ()
         if not last:
             if b:
+                slots.append(place(b + 1))
                 forward.append(attend(b + 1))
                 routed.append(routing(b + 1))
             messages = [leaving(m, *held) for m in routed[b + 1][2:]]

time: 642 us -> 634 us (0.988); the launches traced: 638 us -> 623 us
  starting transfers between devices: 174 us -> 152 us
  waiting for transfers between devices: 168 us -> 177 us
    ppermute x20, waiting for transfers between devices: 68.3 us -> 92.3 us  [send(): self.down = lax.ppermute(self.down, 'hidden', downward(planes, first, last))]
    ppermute x20, waiting for transfers between devices: 44 us -> 27.1 us  [send(): self.up = lax.ppermute(self.up, 'hidden', upward(planes, first, last))]
    ppermute x20, starting transfers between devices: 40.6 us -> 27.8 us  [send(): self.down = lax.ppermute(self.down, 'hidden', downward(planes, first, last))]
    ppermute x20, starting transfers between devices: 64.5 us -> 54.9 us  [send(): self.up = lax.ppermute(self.up, 'hidden', upward(planes, first, last))]
  transfers between devices with their start and end apart: 76 -> 76, of which waited for: 36 -> 37; matrix products, arithmetic and copies ran while one was open for 1% -> 1% of each run, Pallas kernels for 36% -> 37%
where the time goes in v7:
time: 634 us; the launch traced here: 623 us
  Pallas kernels  264 us (42%)
  waiting for transfers between devices  177 us (28%)
  starting transfers between devices  152 us (24%)
  local copies, waits for them, and re-layouts  19.9 us (3%)
  other arithmetic  7.15 us (1%)
    ppermute x20, waiting for transfers between devices, send(): self.down = lax.ppermute(self.down, 'hidden', downward(planes, first, last))  92.3 us
    pallas_call x4, Pallas kernels, attention_backward(): pl.pallas_call(functools.partial(attn_back_kernel, batch, which, last, le...  58 us
    pallas_call x4, Pallas kernels, experts_half(): pl.pallas_call(functools.partial(expert_kernel, planes, gated, first, len...  55.9 us
    ppermute x20, starting transfers between devices, send(): self.up = lax.ppermute(self.up, 'hidden', upward(planes, first, last))  54.9 us
    ppermute x28, waiting for transfers between devices, swap(): lax.ppermute(values, axis, [(k, k ^ distance) for k in range(lax.axis_siz...  38.9 us
    ppermute x28, starting transfers between devices, swap(): lax.ppermute(values, axis, [(k, k ^ distance) for k in range(lax.axis_siz...  34.7 us
    all_to_all x8, starting transfers between devices, to_groups(): lax.all_to_all(values, 'expert', split_axis=0, concat_axis=0, tiled=True)  34.3 us
    pallas_call x2, Pallas kernels, expert_grads(): pl.pallas_call(functools.partial(expert_grad_kernel, batches, len(after))...  28.9 us
  transfers between devices with their start and end apart: 76, of which 37 were waited for; matrix products, arithmetic and copies ran while one was open for 1% of the time, Pallas kernels for 37%

profile of v7, /device:TPU:0, one launch (start us, length us, event | category | flops | bytes accessed | tf_op | source)
XLA Modules:
  0.0 623.3 jit_solution(11820541546688898620)
XLA Ops:
  5.6 5.2 all-to-all-start
  12.6 13.6 %shard_map.239 = (bf16[3,6,512,128]{3,2,1,0:T(8,128)(2,1)}, bf16[6,512,128]{2,1,0:T(8,128)(2,1)}, f32[512,128]{1,0:T(8,128)}) custom-call(bf16[8,80,768]{2,1,0:T(8,128)(2,1)} %get-tuple-element.116.refs_0_, s32[2]{0:T(128)} %bitcast.64, bf16[2,1,512,768]{3,2,1,0:T(8,128)(2,1)} %refs_9_.5, f32[1,768]{1,0:T(1,128)} %broadcast_in_dim.20.refs_3_.refs_5_.refs_9_.refs_8_.refs_10_, ...), custom_call_target="tpu_custom_call" | custom-call | flops 1 | bytes 1 | tf_op jit(solution)/shard_map/pallas_call | solution.py:278
  26.8 5.4 shard_map.240
  32.2 4.2 all-to-all-start.1
  44.4 8.8 %all-to-all-done.1.refs_1_ = bf16[8,96,768]{2,1,0:T(8,128)(2,1)S(1)} async-done(((bf16[8,96,768]{2,1,0:T(8,128)(2,1)}), bf16[8,96,768]{2,1,0:T(8,128)(2,1)S(1)}, u32[]{:S(2)}, u32[]{:S(2)}) %all-to-all-start.1) | async-done | bytes 1179680 | tf_op jit(solution)/shard_map/all_to_all | solution.py:1044
  71.2 13.6 %shard_map.243 = (bf16[3,6,512,128]{3,2,1,0:T(8,128)(2,1)}, bf16[6,512,128]{2,1,0:T(8,128)(2,1)}, f32[512,128]{1,0:T(8,128)}) custom-call(bf16[656,768]{1,0:T(8,128)(2,1)} %shard_map.242.refs_0_.refs_3_.refs_17_, bf16[640,768]{1,0:T(8,128)(2,1)} %copy-done.39, bf16[640,768]{1,0:T(8,128)(2,1)} %collective-permute-done.3.refs_2_.refs_11_, s32[2]{0:T(128)} %bitcast.65, ...), custom_call_target="tpu_custom_call" | custom-call | flops 1 | bytes 1 | tf_op jit(solution)/shard_map/pallas_call | solution.py:278
  86.6 4.9 collective-permute-done.1.refs_1_
  95.2 17.4 %collective-permute-done.8.refs_1_.refs_12_ = bf16[640,768]{1,0:T(8,128)(2,1)} collective-permute-done((bf16[640,768]{1,0:T(8,128)(2,1)}, bf16[640,768]{1,0:T(8,128)(2,1)}, u32[]{:S(2)}, u32[]{:S(2)}) %collective-permute-start.8) | collective-permute-done | bytes 983072 | tf_op jit(solution)/shard_map/ppermute | solution.py:929
  116.0 6.6 %shard_map.246 = (f32[512,768]{1,0:T(8,128)}, f32[512,64]{1,0:T(8,128)}, bf16[8,80,768]{2,1,0:T(8,128)(2,1)}, bf16[8,80,768]{2,1,0:T(8,128)(2,1)}) custom-call(bf16[640,768]{1,0:T(8,128)(2,1)} %collective-permute-done.6.refs_0_.refs_15_, bf16[640,768]{1,0:T(8,128)(2,1)} %collective-permute-done.8.refs_1_.refs_12_, bf16[2,1,512,768]{3,2,1,0:T(8,128)(2,1)} %refs_9_.5, ...), custom_call_target="tpu_custom_call" | custom-call | flops 1 | bytes 1 | tf_op jit(solution)/shard_map/pallas_call | solution.py:348
  122.6 4.2 all-to-all-start.3
  126.9 7.2 %collective-permute-done.5.refs_1_.refs_5_.refs_19_ = bf16[656,768]{1,0:T(8,128)(2,1)S(1)} collective-permute-done((bf16[656,768]{1,0:T(8,128)(2,1)}, bf16[656,768]{1,0:T(8,128)(2,1)S(1)}, u32[]{:S(2)}, u32[]{:S(2)}) %collective-permute-start.5) | collective-permute-done | bytes 1007648 | tf_op jit(solution)/shard_map/ppermute | solution.py:929
  137.0 4.7 all-to-all-done.3.refs_4_
  141.7 4.2 all-to-all-start.2
  145.9 9.2 %collective-permute-done.9.refs_3_.refs_13_ = bf16[640,768]{1,0:T(8,128)(2,1)S(1)} collective-permute-done((bf16[640,768]{1,0:T(8,128)(2,1)}, bf16[640,768]{1,0:T(8,128)(2,1)S(1)}, u32[]{:S(2)}, u32[]{:S(2)}) %collective-permute-start.9) | collective-permute-done | bytes 983072 | tf_op jit(solution)/shard_map/ppermute | solution.py:929
  165.4 4.8 collective-permute-start.10
  170.2 6.6 %collective-permute-done.12.refs_6_.refs_20_ = bf16[656,768]{1,0:T(8,128)(2,1)} collective-permute-done((bf16[656,768]{1,0:T(8,128)(2,1)S(1)}, bf16[656,768]{1,0:T(8,128)(2,1)}, u32[]{:S(2)}, u32[]{:S(2)}) %collective-permute-start.12) | collective-permute-done | bytes 1007648 | tf_op jit(solution)/shard_map/ppermute | solution.py:929
  178.1 14.0 %shard_map.252 = (bf16[2,320,768]{2,1,0:T(8,128)(2,1)}, bf16[2,320,768]{2,1,0:T(8,128)(2,1)}, bf16[2,320,768]{2,1,0:T(8,128)(2,1)}, bf16[2,320,768]{2,1,0:T(8,12...) custom-call(bf16[2,320,768]{2,1,0:T(8,128)(2,1)} %shard_map.248.refs, ...), custom_call_target="tpu_custom_call" | custom-call | flops 1 | bytes 1 | tf_op jit(solution)/shard_map/pallas_call | solution.py:445
  192.1 5.8 collective-permute-done.19.down_ref.refs_4_.refs_11_
  206.8 13.9 %shard_map.249 = (bf16[2,320,768]{2,1,0:T(8,128)(2,1)}, bf16[2,320,768]{2,1,0:T(8,128)(2,1)}, bf16[2,320,768]{2,1,0:T(8,128)(2,1)}, bf16[2,320,768]{2,1,0:T(8,12...) custom-call(bf16[2,320,768]{2,1,0:T(8,128)(2,1)} %shard_map.248.refs, ...), custom_call_target="tpu_custom_call" | custom-call | flops 1 | bytes 1 | tf_op jit(solution)/shard_map/pallas_call | solution.py:445
  224.2 4.6 collective-permute-start.14
  230.1 9.8 %collective-permute-done.21.down_ref.refs_5_.refs_12_ = bf16[2,320,768]{2,1,0:T(8,128)(2,1)S(1)} collective-permute-done((bf16[2,320,768]{2,1,0:T(8,128)(2,1)}, bf16[2,320,768]{2,1,0:T(8,128)(2,1)S(1)}, u32[]{:S(2)}, u32[]{:S(2)}) %collective-permute-start.21) | collective-permute-done | bytes 983072 | tf_op jit(solution)/shard_map/ppermute | solution.py:929
  243.8 7.2 %collective-permute-done.14.up_ref.refs_10_.refs_17_ = bf16[2,320,768]{2,1,0:T(8,128)(2,1)S(1)} collective-permute-done((bf16[2,320,768]{2,1,0:T(8,128)(2,1)S(1)}, bf16[2,320,768]{2,1,0:T(8,128)(2,1)S(1)}, u32[]{:S(2)}, u32[]{:S(2)}) %collective-permute-start.14) | collective-permute-done | bytes 983072 | tf_op jit(solution)/shard_map/ppermute | solution.py:928
  251.0 10.0 %collective-permute-done.15.down_ref.refs_7_.refs_14_ = bf16[2,320,768]{2,1,0:T(8,128)(2,1)S(1)} collective-permute-done((bf16[2,320,768]{2,1,0:T(8,128)(2,1)S(1)}, bf16[2,320,768]{2,1,0:T(8,128)(2,1)S(1)}, u32[]{:S(2)}, u32[]{:S(2)}) %collective-permute-start.15) | collective-permute-done | bytes 983072 | tf_op jit(solution)/shard_map/ppermute | solution.py:929
  265.7 6.3 %collective-permute-done.22.up_ref.refs_9_.refs_16_ = bf16[2,320,768]{2,1,0:T(8,128)(2,1)S(1)} collective-permute-done((bf16[2,320,768]{2,1,0:T(8,128)(2,1)S(1)}, bf16[2,320,768]{2,1,0:T(8,128)(2,1)S(1)}, u32[]{:S(2)}, u32[]{:S(2)}) %collective-permute-start.22) | collective-permute-done | bytes 983072 | tf_op jit(solution)/shard_map/ppermute | solution.py:928
  272.0 10.0 %collective-permute-done.23.down_ref.refs_6_.refs_13_ = bf16[2,320,768]{2,1,0:T(8,128)(2,1)S(1)} collective-permute-done((bf16[2,320,768]{2,1,0:T(8,128)(2,1)S(1)}, bf16[2,320,768]{2,1,0:T(8,128)(2,1)S(1)}, u32[]{:S(2)}, u32[]{:S(2)}) %collective-permute-start.23) | collective-permute-done | bytes 983072 | tf_op jit(solution)/shard_map/ppermute | solution.py:929
  287.9 14.0 %shard_map.256 = (bf16[2,320,768]{2,1,0:T(8,128)(2,1)}, bf16[2,320,768]{2,1,0:T(8,128)(2,1)}, bf16[2,320,768]{2,1,0:T(8,128)(2,1)}, bf16[2,320,768]{2,1,0:T(8,12...) custom-call(bf16[2,320,768]{2,1,0:T(8,128)(2,1)} %get-tuple-element., ...), custom_call_target="tpu_custom_call" | custom-call | flops 1 | bytes 1 | tf_op jit(solution)/shard_map/pallas_call | solution.py:445
  302.0 5.5 collective-permute-start.28
  315.7 8.6 %collective-permute-done.25.refs_3_.refs_4_ = bf16[2,320,768]{2,1,0:T(8,128)(2,1)} collective-permute-done((bf16[2,320,768]{2,1,0:T(8,128)(2,1)}, bf16[2,320,768]{2,1,0:T(8,128)(2,1)}, u32[]{:S(2)}, u32[]{:S(2)}) %collective-permute-start.25) | collective-permute-done | bytes 983072 | tf_op jit(solution)/shard_map/ppermute | solution.py:929
  324.3 14.0 %shard_map.258 = (bf16[2,320,768]{2,1,0:T(8,128)(2,1)}, bf16[2,320,768]{2,1,0:T(8,128)(2,1)}, bf16[2,320,768]{2,1,0:T(8,128)(2,1)}, bf16[2,320,768]{2,1,0:T(8,12...) custom-call(bf16[2,320,768]{2,1,0:T(8,128)(2,1)} %get-tuple-element., ...), custom_call_target="tpu_custom_call" | custom-call | flops 1 | bytes 1 | tf_op jit(solution)/shard_map/pallas_call | solution.py:445
  341.4 3.9 shard_map.259
  347.5 8.9 %collective-permute-done.34.refs_1_.refs_0_ = bf16[2,320,768]{2,1,0:T(8,128)(2,1)S(1)} collective-permute-done((bf16[2,320,768]{2,1,0:T(8,128)(2,1)}, bf16[2,320,768]{2,1,0:T(8,128)(2,1)S(1)}, u32[]{:S(2)}, u32[]{:S(2)}) %collective-permute-start.34) | collective-permute-done | bytes 983072 | tf_op jit(solution)/shard_map/ppermute | solution.py:928
  362.3 4.2 all-to-all-start.4
  366.5 14.5 %shard_map.260 = (f32[8,768,768]{2,1,0:T(8,128)}, f32[8,768,768]{2,1,0:T(8,128)}) custom-call(bf16[2,320,768]{2,1,0:T(8,128)(2,1)} %get-tuple-element.151.refs_0_, bf16[4,320,768]{2,1,0:T(8,128)(2,1)} %get-tuple-element.152.refs_1_, bf16[4,320,768]{2,1,0:T(8,128)(2,1)} %get-tuple-element.153.refs_2_, bf16[4,320,768]{2,1,0:T(8,128)(2,1)} %get-tuple-element.154.refs_3_, ...), custom_call_target="tpu_custom_call" | custom-call | flops 1 | bytes 1 | tf_op jit(solution)/shard_map/pallas_call | solution.py:474
  384.7 4.9 collective-permute-start.30
  395.0 4.5 all-to-all-start.5
  403.4 4.3 collective-permute-start.36
  409.0 5.3 all-to-all-done.5.refs_2_
  414.3 9.2 %shard_map.265 = (bf16[2,1,512,768]{3,2,1,0:T(8,128)(2,1)}, f32[512,768]{1,0:T(8,128)}, bf16[6,512,128]{2,1,0:T(8,128)(2,1)}, f32[1696,384]{1,0:T(8,128)}) custom-call(bf16[2,320,768]{2,1,0:T(8,128)(2,1)} %get-tuple-element.165.refs_0_, s32[2]{0:T(128)} %bitcast.67, bf16[8,80,768]{2,1,0:T(8,128)(2,1)} %all-to-all-done.5.refs_2_, ...), custom_call_target="tpu_custom_call" | custom-call | flops 1 | bytes 1 | tf_op jit(solution)/shard_map/pallas_call | solution.py:565
  427.3 4.2 collective-permute-start.38
  433.0 14.3 %shard_map.267 = (f32[16,1024]{1,0:T(8,128)}, f32[512,768]{1,0:T(8,128)}, f32[2304,384]{1,0:T(8,128)}) custom-call(bf16[2,320,768]{2,1,0:T(8,128)(2,1)} %copy-done.32, s32[1]{0:T(128)} %bitcast.5.refs_1_.refs_0_.refs_2_.side_ref, s32[2]{0:T(128)} %bitcast.68, bf16[3,6,512,128]{3,2,1,0:T(8,128)(2,1)} %get-tuple-element.172.refs_3_, ...), custom_call_target="tpu_custom_call" | custom-call | flops 1 | bytes 1 | tf_op jit(solution)/shard_map/pallas_call | solution.py:765
  454.8 14.7 %shard_map.269 = (bf16[2,1,512,768]{3,2,1,0:T(8,128)(2,1)}, f32[2560,384]{1,0:T(8,128)}) custom-call(bf16[8,80,768]{2,1,0:T(8,128)(2,1)} %shard_map.268.refs_0_, s32[1]{0:T(128)} %bitcast.5.refs_1_.refs_0_.refs_2_.side_ref, s32[2]{0:T(128)} %bitcast.69, bf16[3,6,512,128]{3,2,1,0:T(8,128)(2,1)} %get-tuple-element.172.refs_3_, ...), custom_call_target="tpu_custom_call" | custom-call | flops 1 | bytes 1 | tf_op jit(solution)/shard_map/pallas_call | solution.py:765
  474.3 4.1 all-to-all-start.7
  478.4 14.4 %shard_map.271 = (f32[8,768,768]{2,1,0:T(8,128)}, f32[8,768,768]{2,1,0:T(8,128)}) custom-call(bf16[8,80,768]{2,1,0:T(8,128)(2,1)} %shard_map.270.refs_0_, bf16[4,320,768]{2,1,0:T(8,128)(2,1)} %get-tuple-element.182.refs_1_, bf16[4,320,768]{2,1,0:T(8,128)(2,1)} %get-tuple-element.183.refs_2_, ...), custom_call_target="tpu_custom_call", output_to_operand_aliasing={{0}: (9, {}), {1}: (10, {})} | custom-call | flops 1 | bytes 1 | tf_op jit(solution)/shard_map/pallas_call | solution.py:474
  494.0 8.7 %shard_map.272 = (bf16[2,1,512,768]{3,2,1,0:T(8,128)(2,1)}, f32[512,768]{1,0:T(8,128)}, bf16[6,512,128]{2,1,0:T(8,128)(2,1)}, bf16[1696,384]{1,0:T(8,128)(2,1)}) custom-call(f32[8,768,768]{2,1,0:T(8,128)} %get-tuple-element.115.refs_0_, bf16[2,1,512,768]{3,2,1,0:T(8,128)(2,1)} %get-tuple-element.192.refs_1_, ...), custom_call_target="tpu_custom_call", output_to_operand_aliasing={{0}: (1, {})} | custom-call | flops 1 | bytes 1 | tf_op jit(solution)/shard_map/pallas_call | solution.py:565
  502.8 14.1 %shard_map.273 = (f32[16,1024]{1,0:T(8,128)}, f32[512,768]{1,0:T(8,128)}, bf16[2048,384]{1,0:T(8,128)(2,1)}, bf16[2048,384]{1,0:T(8,128)(2,1)}) custom-call(s32[1]{0:T(128)} %bitcast.5.refs_1_.refs_0_.refs_2_.side_ref, s32[2]{0:T(128)} %bitcast.71, bf16[3,6,512,128]{3,2,1,0:T(8,128)(2,1)} %get-tuple-element.198.refs_2_.refs_4_, ...), custom_call_target="tpu_custom_call" | custom-call | flops 1 | bytes 1 | tf_op jit(solution)/shard_map/pallas_call | solution.py:765
  527.1 14.9 %shard_map.274 = (bf16[2,1,512,768]{3,2,1,0:T(8,128)(2,1)}, bf16[1280,384]{1,0:T(8,128)(2,1)}, bf16[1280,384]{1,0:T(8,128)(2,1)}) custom-call(bf16[2048,384]{1,0:T(8,128)(2,1)} %copy-done.37, bf16[2,1,512,768]{3,2,1,0:T(8,128)(2,1)} %get-tuple-element.204.refs_1_, s32[1]{0:T(128)} %bitcast.5.refs_1_.refs_0_.refs_2_.side_ref, ...), custom_call_target="tpu_custom_call", output_to_operand_aliasing={{0}: (1, {})} | custom-call | flops 1 | bytes 1 | tf_op jit(solution)/shard_map/pallas_call | solution.py:765
  552.9 6.0 collective-permute-done.45
  616.4 6.5 %shard_map.275 = (f32[768,768]{1,0:T(8,128)}, f32[768,768]{1,0:T(8,128)}, f32[768,768]{1,0:T(8,128)}, f32[768,768]{1,0:T(8,128)}, f32[64,768]{1,0:T(8,128)}, /*i...) custom-call(s32[1]{0:T(128)} %bitcast.5.refs_1_.refs_0_.refs_2_.side_ref, bf16[2048,384]{1,0:T(8,128)(2,1)} %copy-done.41, ...), custom_call_target="tpu_custom_call" | custom-call | flops 1 | bytes 1 | tf_op jit(solution)/shard_map/pallas_call | solution.py:847
  (274 shorter events, 215.1 us)
Async XLA Ops:
  5.6 26.6 %all-to-all-start = ((bf16[8,80,768]{2,1,0:T(8,128)(2,1)}), bf16[8,80,768]{2,1,0:T(8,128)(2,1)S(1)}, u32[]{:S(2)}, u32[]{:S(2)}) async-start(bf16[8,80,768]{2,1,0:T(8,128)(2,1)} %get-tuple-element.116.refs_0_), calls=%async_computation | async-start | bytes 1966080 | tf_op jit(solution)/shard_map/all_to_all | solution.py:1044
  32.2 21.0 %all-to-all-start.1 = ((bf16[8,96,768]{2,1,0:T(8,128)(2,1)}), bf16[8,96,768]{2,1,0:T(8,128)(2,1)S(1)}, u32[]{:S(2)}, u32[]{:S(2)}) async-start(bf16[8,96,768]{2,1,0:T(8,128)(2,1)} %get-tuple-element.119.refs_0_), calls=%async_computation.1 | async-start | bytes 2359296 | tf_op jit(solution)/shard_map/all_to_all | solution.py:1044
  39.6 25.8 %collective-permute-start.2 = (bf16[640,768]{1,0:T(8,128)(2,1)}, bf16[640,768]{1,0:T(8,128)(2,1)S(1)}, u32[]{:S(2)}, u32[]{:S(2)}) collective-permute-start(bf16[640,768]{1,0:T(8,128)(2,1)} %shard_map.241.refs_0_.refs_10_), channel_id=1, source_target_pairs={{0,1},{1,2},{2,3},{4,5},{5,6},{6,7},{8,9},{9,10},{10,11},{12,13},{... | collective-permute-start | bytes 2949128 | tf_op jit(solution)/shard_map/ppermute | solution.py:928
  43.1 26.8 %collective-permute-start.3 = (bf16[640,768]{1,0:T(8,128)(2,1)}, bf16[640,768]{1,0:T(8,128)(2,1)}, u32[]{:S(2)}, u32[]{:S(2)}) collective-permute-start(bf16[640,768]{1,0:T(8,128)(2,1)} %shard_map.241.refs_0_.refs_10_), channel_id=1, source_target_pairs={{3,2},{2,1},{1,0},{7,6},{6,5},{5,4},{11,10},{10,9},{9,8},{15,14},{... | collective-permute-start | bytes 2949128 | tf_op jit(solution)/shard_map/ppermute | solution.py:929
  58.0 28.6 %collective-permute-start = (bf16[656,768]{1,0:T(8,128)(2,1)}, bf16[656,768]{1,0:T(8,128)(2,1)S(1)}, u32[]{:S(2)}, u32[]{:S(2)}) collective-permute-start(bf16[656,768]{1,0:T(8,128)(2,1)} %shard_map.242.refs_0_.refs_3_.refs_17_), channel_id=1, source_target_pairs={{0,1},{1,2},{2,3},{4,5},{5,6},{6,7},{8,9},{9,10},{10,11},{12,13},{... | collective-permute-start | bytes 3022856 | tf_op jit(solution)/shard_map/ppermute | solution.py:928
  61.7 29.8 %collective-permute-start.1 = (bf16[656,768]{1,0:T(8,128)(2,1)}, bf16[656,768]{1,0:T(8,128)(2,1)}, u32[]{:S(2)}, u32[]{:S(2)}) collective-permute-start(bf16[656,768]{1,0:T(8,128)(2,1)} %shard_map.242.refs_0_.refs_3_.refs_17_), channel_id=1, source_target_pairs={{3,2},{2,1},{1,0},{7,6},{6,5},{5,4},{11,10},{10,9},{9,8},{15,14},{... | collective-permute-start | bytes 3022856 | tf_op jit(solution)/shard_map/ppermute | solution.py:929
  65.4 29.0 %collective-permute-start.6 = (bf16[640,768]{1,0:T(8,128)(2,1)S(1)}, bf16[640,768]{1,0:T(8,128)(2,1)}, u32[]{:S(2)}, u32[]{:S(2)}) collective-permute-start(bf16[640,768]{1,0:T(8,128)(2,1)S(1)} %collective-permute-done.2.refs_1_.refs_14_), channel_id=1, source_target_pairs={{1,2},{2,3},{5,6},{6,7},{9,10},{10,11},{13,14},{14,15},{17,18},{18... | collective-permute-start | bytes 2949128 | tf_op jit(solution)/shard_map/ppermute | solution.py:928
  69.9 42.7 %collective-permute-start.8 = (bf16[640,768]{1,0:T(8,128)(2,1)}, bf16[640,768]{1,0:T(8,128)(2,1)}, u32[]{:S(2)}, u32[]{:S(2)}) collective-permute-start(bf16[640,768]{1,0:T(8,128)(2,1)} %collective-permute-done.3.refs_2_.refs_11_), channel_id=1, source_target_pairs={{2,1},{1,0},{6,5},{5,4},{10,9},{9,8},{14,13},{13,12},{18,17},{17,1... | collective-permute-start | bytes 2949128 | tf_op jit(solution)/shard_map/ppermute | solution.py:929
  91.5 42.5 %collective-permute-start.5 = (bf16[656,768]{1,0:T(8,128)(2,1)}, bf16[656,768]{1,0:T(8,128)(2,1)S(1)}, u32[]{:S(2)}, u32[]{:S(2)}) collective-permute-start(bf16[656,768]{1,0:T(8,128)(2,1)} %get-tuple-element.122.refs_4_.refs_18_), channel_id=1, source_target_pairs={{2,1},{1,0},{6,5},{5,4},{10,9},{9,8},{14,13},{13,12},{18,17},{17,1... | collective-permute-start | bytes 3022856 | tf_op jit(solution)/shard_map/ppermute | solution.py:929
  92.8 42.6 %collective-permute-start.4 = (bf16[656,768]{1,0:T(8,128)(2,1)}, bf16[656,768]{1,0:T(8,128)(2,1)}, u32[]{:S(2)}, u32[]{:S(2)}) collective-permute-start(bf16[656,768]{1,0:T(8,128)(2,1)} %get-tuple-element.121.refs_7_.refs_21_), channel_id=1, source_target_pairs={{1,2},{2,3},{5,6},{6,7},{9,10},{10,11},{13,14},{14,15},{17,18},{18... | collective-permute-start | bytes 3022856 | tf_op jit(solution)/shard_map/ppermute | solution.py:928
  94.4 51.5 %collective-permute-start.7 = (bf16[640,768]{1,0:T(8,128)(2,1)}, bf16[640,768]{1,0:T(8,128)(2,1)S(1)}, u32[]{:S(2)}, u32[]{:S(2)}) collective-permute-start(bf16[640,768]{1,0:T(8,128)(2,1)} %collective-permute-done.6.refs_0_.refs_15_), channel_id=1, source_target_pairs={{2,3},{6,7},{10,11},{14,15},{18,19},{22,23},{26,27},{30,31}} | collective-permute-start | bytes 2949128 | tf_op jit(solution)/shard_map/ppermute | solution.py:928
  112.6 42.6 %collective-permute-start.9 = (bf16[640,768]{1,0:T(8,128)(2,1)}, bf16[640,768]{1,0:T(8,128)(2,1)S(1)}, u32[]{:S(2)}, u32[]{:S(2)}) collective-permute-start(bf16[640,768]{1,0:T(8,128)(2,1)} %collective-permute-done.8.refs_1_.refs_12_), channel_id=1, source_target_pairs={{1,0},{5,4},{9,8},{13,12},{17,16},{21,20},{25,24},{29,28}} | collective-permute-start | bytes 2949128 | tf_op jit(solution)/shard_map/ppermute | solution.py:929
  134.1 42.8 %collective-permute-start.12 = (bf16[656,768]{1,0:T(8,128)(2,1)S(1)}, bf16[656,768]{1,0:T(8,128)(2,1)}, u32[]{:S(2)}, u32[]{:S(2)}) collective-permute-start(bf16[656,768]{1,0:T(8,128)(2,1)S(1)} %collective-permute-done.5.refs_1_.refs_5_.refs_19_), channel_id=1, source_target_pairs={{1,0},{5,4},{9,8},{13,12},{17,16},{21,20},{25,24},{29,28}} | collective-permute-start | bytes 3022856 | tf_op jit(solution)/shard_map/ppermute | solution.py:929
  135.4 42.8 %collective-permute-start.13 = (bf16[656,768]{1,0:T(8,128)(2,1)}, bf16[656,768]{1,0:T(8,128)(2,1)}, u32[]{:S(2)}, u32[]{:S(2)}) collective-permute-start(bf16[656,768]{1,0:T(8,128)(2,1)} %collective-permute-done.4.refs_0_.refs_8_.refs_22_), channel_id=1, source_target_pairs={{2,3},{6,7},{10,11},{14,15},{18,19},{22,23},{26,27},{30,31}} | collective-permute-start | bytes 3022856 | tf_op jit(solution)/shard_map/ppermute | solution.py:928
  141.7 20.6 %all-to-all-start.2 = ((bf16[8,80,768]{2,1,0:T(8,128)(2,1)}), bf16[8,80,768]{2,1,0:T(8,128)(2,1)}, u32[]{:S(2)}, u32[]{:S(2)}) async-start(bf16[8,80,768]{2,1,0:T(8,128)(2,1)} %get-tuple-element.124), calls=%async_computation.2 | async-start | bytes 1966080 | tf_op jit(solution)/shard_map/all_to_all | solution.py:1044
  159.3 32.8 %collective-permute-start.18 = (bf16[2,320,768]{2,1,0:T(8,128)(2,1)}, bf16[2,320,768]{2,1,0:T(8,128)(2,1)S(1)}, u32[]{:S(2)}, u32[]{:S(2)}) collective-permute-start(bf16[2,320,768]{2,1,0:T(8,128)(2,1)} %shard_map.248.refs_0_.refs_3_.refs_10_), channel_id=1, source_target_pairs={{0,1},{1,2},{2,3},{4,5},{5,6},{6,7},{8,9},{9,10},{10,11},{12,13},{... | collective-permute-start | bytes 2949128 | tf_op jit(solution)/shard_map/ppermute | solution.py:928
  160.9 37.0 %collective-permute-start.19 = (bf16[2,320,768]{2,1,0:T(8,128)(2,1)}, bf16[2,320,768]{2,1,0:T(8,128)(2,1)}, u32[]{:S(2)}, u32[]{:S(2)}) collective-permute-start(bf16[2,320,768]{2,1,0:T(8,128)(2,1)} %shard_map.248.refs_0_.refs_3_.refs_10_), channel_id=1, source_target_pairs={{3,2},{2,1},{1,0},{7,6},{6,5},{5,4},{11,10},{10,9},{9,8},{15,14},{... | collective-permute-start | bytes 2949128 | tf_op jit(solution)/shard_map/ppermute | solution.py:929
  165.4 55.3 %collective-permute-start.10 = (bf16[2,320,768]{2,1,0:T(8,128)(2,1)}, bf16[2,320,768]{2,1,0:T(8,128)(2,1)S(1)}, u32[]{:S(2)}, u32[]{:S(2)}) collective-permute-start(bf16[2,320,768]{2,1,0:T(8,128)(2,1)} %shard_map.247.refs_1_.refs_5_.refs_12_), channel_id=1, source_target_pairs={{0,1},{1,2},{2,3},{4,5},{5,6},{6,7},{8,9},{9,10},{10,11},{12,13},{... | collective-permute-start | bytes 2949128 | tf_op jit(solution)/shard_map/ppermute | solution.py:928
  176.8 43.9 %collective-permute-start.11 = (bf16[2,320,768]{2,1,0:T(8,128)(2,1)}, bf16[2,320,768]{2,1,0:T(8,128)(2,1)S(1)}, u32[]{:S(2)}, u32[]{:S(2)}) collective-permute-start(bf16[2,320,768]{2,1,0:T(8,128)(2,1)} %shard_map.247.refs_1_.refs_5_.refs_12_), channel_id=1, source_target_pairs={{3,2},{2,1},{1,0},{7,6},{6,5},{5,4},{11,10},{10,9},{9,8},{15,14},{... | collective-permute-start | bytes 2949128 | tf_op jit(solution)/shard_map/ppermute | solution.py:929
  204.0 26.2 %collective-permute-start.20 = (bf16[2,320,768]{2,1,0:T(8,128)(2,1)}, bf16[2,320,768]{2,1,0:T(8,128)(2,1)S(1)}, u32[]{:S(2)}, u32[]{:S(2)}) collective-permute-start(bf16[2,320,768]{2,1,0:T(8,128)(2,1)} %get-tuple-element.135), channel_id=1, source_target_pairs={{0,1},{1,2},{2,3},{4,5},{5,6},{6,7},{8,9},{9,10},{10,11},{12,13},{... | collective-permute-start | bytes 2949128 | tf_op jit(solution)/shard_map/ppermute | solution.py:928
  205.5 34.4 %collective-permute-start.21 = (bf16[2,320,768]{2,1,0:T(8,128)(2,1)}, bf16[2,320,768]{2,1,0:T(8,128)(2,1)S(1)}, u32[]{:S(2)}, u32[]{:S(2)}) collective-permute-start(bf16[2,320,768]{2,1,0:T(8,128)(2,1)} %get-tuple-element.136), channel_id=1, source_target_pairs={{3,2},{2,1},{1,0},{7,6},{6,5},{5,4},{11,10},{10,9},{9,8},{15,14},{... | collective-permute-start | bytes 2949128 | tf_op jit(solution)/shard_map/ppermute | solution.py:929
  224.2 26.7 %collective-permute-start.14 = (bf16[2,320,768]{2,1,0:T(8,128)(2,1)S(1)}, bf16[2,320,768]{2,1,0:T(8,128)(2,1)S(1)}, u32[]{:S(2)}, u32[]{:S(2)}) collective-permute-start(bf16[2,320,768]{2,1,0:T(8,128)(2,1)S(1)} %get-tuple-element.128), channel_id=1, source_target_pairs={{0,1},{1,2},{2,3},{4,5},{5,6},{6,7},{8,9},{9,10},{10,11},{12,13},{... | collective-permute-start | bytes 2949128 | tf_op jit(solution)/shard_map/ppermute | solution.py:928
  228.8 32.1 %collective-permute-start.15 = (bf16[2,320,768]{2,1,0:T(8,128)(2,1)S(1)}, bf16[2,320,768]{2,1,0:T(8,128)(2,1)S(1)}, u32[]{:S(2)}, u32[]{:S(2)}) collective-permute-start(bf16[2,320,768]{2,1,0:T(8,128)(2,1)S(1)} %get-tuple-element.129), channel_id=1, source_target_pairs={{3,2},{2,1},{1,0},{7,6},{6,5},{5,4},{11,10},{10,9},{9,8},{15,14},{... | collective-permute-start | bytes 2949128 | tf_op jit(solution)/shard_map/ppermute | solution.py:929
  240.9 31.2 %collective-permute-start.22 = (bf16[2,320,768]{2,1,0:T(8,128)(2,1)S(1)}, bf16[2,320,768]{2,1,0:T(8,128)(2,1)S(1)}, u32[]{:S(2)}, u32[]{:S(2)}) collective-permute-start(bf16[2,320,768]{2,1,0:T(8,128)(2,1)S(1)} %get-tuple-element.138), channel_id=1, source_target_pairs={{0,1},{1,2},{2,3},{4,5},{5,6},{6,7},{8,9},{9,10},{10,11},{12,13},{... | collective-permute-start | bytes 2949128 | tf_op jit(solution)/shard_map/ppermute | solution.py:928
  242.5 39.6 %collective-permute-start.23 = (bf16[2,320,768]{2,1,0:T(8,128)(2,1)S(1)}, bf16[2,320,768]{2,1,0:T(8,128)(2,1)S(1)}, u32[]{:S(2)}, u32[]{:S(2)}) collective-permute-start(bf16[2,320,768]{2,1,0:T(8,128)(2,1)S(1)} %get-tuple-element.139), channel_id=1, source_target_pairs={{3,2},{2,1},{1,0},{7,6},{6,5},{5,4},{11,10},{10,9},{9,8},{15,14},{... | collective-permute-start | bytes 2949128 | tf_op jit(solution)/shard_map/ppermute | solution.py:929
  262.9 44.6 %collective-permute-start.16 = (bf16[2,320,768]{2,1,0:T(8,128)(2,1)}, bf16[2,320,768]{2,1,0:T(8,128)(2,1)S(1)}, u32[]{:S(2)}, u32[]{:S(2)}) collective-permute-start(bf16[2,320,768]{2,1,0:T(8,128)(2,1)} %get-tuple-element.131), channel_id=1, source_target_pairs={{0,1},{1,2},{2,3},{4,5},{5,6},{6,7},{8,9},{9,10},{10,11},{12,13},{... | collective-permute-start | bytes 2949128 | tf_op jit(solution)/shard_map/ppermute | solution.py:928
  264.4 44.7 %collective-permute-start.17 = (bf16[2,320,768]{2,1,0:T(8,128)(2,1)}, bf16[2,320,768]{2,1,0:T(8,128)(2,1)S(1)}, u32[]{:S(2)}, u32[]{:S(2)}) collective-permute-start(bf16[2,320,768]{2,1,0:T(8,128)(2,1)} %get-tuple-element.132), channel_id=1, source_target_pairs={{3,2},{2,1},{1,0},{7,6},{6,5},{5,4},{11,10},{10,9},{9,8},{15,14},{... | collective-permute-start | bytes 2949128 | tf_op jit(solution)/shard_map/ppermute | solution.py:929
  284.1 30.2 %collective-permute-start.24 = (bf16[2,320,768]{2,1,0:T(8,128)(2,1)}, bf16[2,320,768]{2,1,0:T(8,128)(2,1)}, u32[]{:S(2)}, u32[]{:S(2)}) collective-permute-start(bf16[2,320,768]{2,1,0:T(8,128)(2,1)} %get-tuple-element.140.refs_0_), channel_id=1, source_target_pairs={{0,1},{1,2},{2,3},{4,5},{5,6},{6,7},{8,9},{9,10},{10,11},{12,13},{... | collective-permute-start | bytes 2949128 | tf_op jit(solution)/shard_map/ppermute | solution.py:928
  286.5 37.8 %collective-permute-start.25 = (bf16[2,320,768]{2,1,0:T(8,128)(2,1)}, bf16[2,320,768]{2,1,0:T(8,128)(2,1)}, u32[]{:S(2)}, u32[]{:S(2)}) collective-permute-start(bf16[2,320,768]{2,1,0:T(8,128)(2,1)} %get-tuple-element.141.refs_1_), channel_id=1, source_target_pairs={{3,2},{2,1},{1,0},{7,6},{6,5},{5,4},{11,10},{10,9},{9,8},{15,14},{... | collective-permute-start | bytes 2949128 | tf_op jit(solution)/shard_map/ppermute | solution.py:929
  302.0 37.9 %collective-permute-start.28 = (bf16[2,320,768]{2,1,0:T(8,128)(2,1)}, bf16[2,320,768]{2,1,0:T(8,128)(2,1)}, u32[]{:S(2)}, u32[]{:S(2)}) collective-permute-start(bf16[2,320,768]{2,1,0:T(8,128)(2,1)} %get-tuple-element.148.downsum_ref), channel_id=1, source_target_pairs={{0,1},{4,5},{8,9},{12,13},{16,17},{20,21},{24,25},{28,29}} | collective-permute-start | bytes 2949128 | tf_op jit(solution)/shard_map/ppermute | solution.py:928
  307.5 33.9 %collective-permute-start.29 = (bf16[2,320,768]{2,1,0:T(8,128)(2,1)}, bf16[2,320,768]{2,1,0:T(8,128)(2,1)}, u32[]{:S(2)}, u32[]{:S(2)}) collective-permute-start(bf16[2,320,768]{2,1,0:T(8,128)(2,1)} %get-tuple-element.149.upsum_ref), channel_id=1, source_target_pairs={{3,2},{7,6},{11,10},{15,14},{19,18},{23,22},{27,26},{31,30}} | collective-permute-start | bytes 2949128 | tf_op jit(solution)/shard_map/ppermute | solution.py:929
  312.5 43.9 %collective-permute-start.34 = (bf16[2,320,768]{2,1,0:T(8,128)(2,1)}, bf16[2,320,768]{2,1,0:T(8,128)(2,1)S(1)}, u32[]{:S(2)}, u32[]{:S(2)}) collective-permute-start(bf16[2,320,768]{2,1,0:T(8,128)(2,1)} %get-tuple-element.143.refs_0_), channel_id=1, source_target_pairs={{0,1},{1,2},{2,3},{4,5},{5,6},{6,7},{8,9},{9,10},{10,11},{12,13},{... | collective-permute-start | bytes 2949128 | tf_op jit(solution)/shard_map/ppermute | solution.py:928
  314.3 44.2 %collective-permute-start.35 = (bf16[2,320,768]{2,1,0:T(8,128)(2,1)}, bf16[2,320,768]{2,1,0:T(8,128)(2,1)}, u32[]{:S(2)}, u32[]{:S(2)}) collective-permute-start(bf16[2,320,768]{2,1,0:T(8,128)(2,1)} %get-tuple-element.144.refs_1_), channel_id=1, source_target_pairs={{3,2},{2,1},{1,0},{7,6},{6,5},{5,4},{11,10},{10,9},{9,8},{15,14},{... | collective-permute-start | bytes 2949128 | tf_op jit(solution)/shard_map/ppermute | solution.py:929
  338.3 42.7 %collective-permute-start.26 = (bf16[2,320,768]{2,1,0:T(8,128)(2,1)}, bf16[2,320,768]{2,1,0:T(8,128)(2,1)S(1)}, u32[]{:S(2)}, u32[]{:S(2)}) collective-permute-start(bf16[2,320,768]{2,1,0:T(8,128)(2,1)} %get-tuple-element.145.downsum_ref), channel_id=1, source_target_pairs={{0,1},{4,5},{8,9},{12,13},{16,17},{20,21},{24,25},{28,29}} | collective-permute-start | bytes 2949128 | tf_op jit(solution)/shard_map/ppermute | solution.py:928
  339.8 41.2 %collective-permute-start.27 = (bf16[2,320,768]{2,1,0:T(8,128)(2,1)}, bf16[2,320,768]{2,1,0:T(8,128)(2,1)}, u32[]{:S(2)}, u32[]{:S(2)}) collective-permute-start(bf16[2,320,768]{2,1,0:T(8,128)(2,1)} %get-tuple-element.146.upsum_ref), channel_id=1, source_target_pairs={{3,2},{7,6},{11,10},{15,14},{19,18},{23,22},{27,26},{31,30}} | collective-permute-start | bytes 2949128 | tf_op jit(solution)/shard_map/ppermute | solution.py:929
  345.3 54.2 %collective-permute-start.32 = (bf16[2,320,768]{2,1,0:T(8,128)(2,1)}, bf16[2,320,768]{2,1,0:T(8,128)(2,1)}, u32[]{:S(2)}, u32[]{:S(2)}) collective-permute-start(bf16[2,320,768]{2,1,0:T(8,128)(2,1)} %get-tuple-element.151.refs_0_), channel_id=1, source_target_pairs={{0,1},{1,2},{4,5},{5,6},{8,9},{9,10},{12,13},{13,14},{16,17},{17,1... | collective-permute-start | bytes 2949128 | tf_op jit(solution)/shard_map/ppermute | solution.py:928
  356.4 43.1 %collective-permute-start.33 = (bf16[2,320,768]{2,1,0:T(8,128)(2,1)}, bf16[2,320,768]{2,1,0:T(8,128)(2,1)}, u32[]{:S(2)}, u32[]{:S(2)}) collective-permute-start(bf16[2,320,768]{2,1,0:T(8,128)(2,1)} %get-tuple-element.163), channel_id=1, source_target_pairs={{3,2},{2,1},{7,6},{6,5},{11,10},{10,9},{15,14},{14,13},{19,18},{18... | collective-permute-start | bytes 2949128 | tf_op jit(solution)/shard_map/ppermute | solution.py:929
  362.3 32.7 %all-to-all-start.4 = ((bf16[8,80,768]{2,1,0:T(8,128)(2,1)}), bf16[8,80,768]{2,1,0:T(8,128)(2,1)S(1)}, u32[]{:S(2)}, u32[]{:S(2)}) async-start(bf16[8,80,768]{2,1,0:T(8,128)(2,1)} %shard_map.262), calls=%async_computation.4 | async-start | bytes 1966080 | tf_op jit(solution)/shard_map/all_to_all | solution.py:1044
  384.7 38.9 %collective-permute-start.30 = (bf16[2,320,768]{2,1,0:T(8,128)(2,1)}, bf16[2,320,768]{2,1,0:T(8,128)(2,1)}, u32[]{:S(2)}, u32[]{:S(2)}) collective-permute-start(bf16[2,320,768]{2,1,0:T(8,128)(2,1)} %get-tuple-element.161), channel_id=1, source_target_pairs={{0,1},{1,2},{4,5},{5,6},{8,9},{9,10},{12,13},{13,14},{16,17},{17,1... | collective-permute-start | bytes 2949128 | tf_op jit(solution)/shard_map/ppermute | solution.py:928
  389.6 34.0 %collective-permute-start.31 = (bf16[2,320,768]{2,1,0:T(8,128)(2,1)}, bf16[2,320,768]{2,1,0:T(8,128)(2,1)}, u32[]{:S(2)}, u32[]{:S(2)}) collective-permute-start(bf16[2,320,768]{2,1,0:T(8,128)(2,1)} %get-tuple-element.162), channel_id=1, source_target_pairs={{3,2},{2,1},{7,6},{6,5},{11,10},{10,9},{15,14},{14,13},{19,18},{18... | collective-permute-start | bytes 2949128 | tf_op jit(solution)/shard_map/ppermute | solution.py:929
  403.4 43.9 %collective-permute-start.36 = (bf16[2,320,768]{2,1,0:T(8,128)(2,1)}, bf16[2,320,768]{2,1,0:T(8,128)(2,1)}, u32[]{:S(2)}, u32[]{:S(2)}) collective-permute-start(bf16[2,320,768]{2,1,0:T(8,128)(2,1)} %get-tuple-element.165.refs_0_), channel_id=1, source_target_pairs={{0,1},{1,2},{2,3},{4,5},{5,6},{6,7},{8,9},{9,10},{10,11},{12,13},{... | collective-permute-start | bytes 2949128 | tf_op jit(solution)/shard_map/ppermute | solution.py:928
  407.7 39.6 %collective-permute-start.37 = (bf16[2,320,768]{2,1,0:T(8,128)(2,1)}, bf16[2,320,768]{2,1,0:T(8,128)(2,1)}, u32[]{:S(2)}, u32[]{:S(2)}) collective-permute-start(bf16[2,320,768]{2,1,0:T(8,128)(2,1)} %get-tuple-element.175), channel_id=1, source_target_pairs={{3,2},{2,1},{1,0},{7,6},{6,5},{5,4},{11,10},{10,9},{9,8},{15,14},{... | collective-permute-start | bytes 2949128 | tf_op jit(solution)/shard_map/ppermute | solution.py:929
  427.3 42.2 %collective-permute-start.38 = (bf16[2,320,768]{2,1,0:T(8,128)(2,1)S(1)}, bf16[2,320,768]{2,1,0:T(8,128)(2,1)}, u32[]{:S(2)}, u32[]{:S(2)}) collective-permute-start(bf16[2,320,768]{2,1,0:T(8,128)(2,1)S(1)} %get-tuple-element.171.refs_0_), channel_id=1, source_target_pairs={{0,1},{1,2},{2,3},{4,5},{5,6},{6,7},{8,9},{9,10},{10,11},{12,13},{... | collective-permute-start | bytes 2949128 | tf_op jit(solution)/shard_map/ppermute | solution.py:928
  431.5 38.0 %collective-permute-start.39 = (bf16[2,320,768]{2,1,0:T(8,128)(2,1)S(1)}, bf16[2,320,768]{2,1,0:T(8,128)(2,1)}, u32[]{:S(2)}, u32[]{:S(2)}) collective-permute-start(bf16[2,320,768]{2,1,0:T(8,128)(2,1)S(1)} %get-tuple-element.181), channel_id=1, source_target_pairs={{3,2},{2,1},{1,0},{7,6},{6,5},{5,4},{11,10},{10,9},{9,8},{15,14},{... | collective-permute-start | bytes 2949128 | tf_op jit(solution)/shard_map/ppermute | solution.py:929
  525.3 19.6 %collective-permute-start.42 = (bf16[512,384]{1,0:T(8,128)(2,1)}, bf16[512,384]{1,0:T(8,128)(2,1)}, u32[]{:S(2)}, u32[]{:S(2)}) collective-permute-start(bf16[512,384]{1,0:T(8,128)(2,1)} %get-tuple-element.226), channel_id=1, source_target_pairs={{0,16},{4,20},{8,24},{12,28},{16,0},{20,4},{24,8},{28,12},{1,17},{... | collective-permute-start | bytes 1179656 | tf_op jit(solution)/shard_map/ppermute | solution.py:961
  542.0 21.5 %collective-permute-start.54 = (bf16[1280,384]{1,0:T(8,128)(2,1)}, bf16[1280,384]{1,0:T(8,128)(2,1)S(1)}, u32[]{:S(2)}, u32[]{:S(2)}) collective-permute-start(bf16[1280,384]{1,0:T(8,128)(2,1)} %get-tuple-element.210), channel_id=1, source_target_pairs={{0,4},{4,0},{8,12},{12,8},{16,20},{20,16},{24,28},{28,24},{1,5},{5... | collective-permute-start | bytes 2949128 | tf_op jit(solution)/shard_map/ppermute | solution.py:961
  571.5 21.2 %collective-permute-start.51 = (bf16[512,384]{1,0:T(8,128)(2,1)S(1)}, bf16[512,384]{1,0:T(8,128)(2,1)S(1)}, u32[]{:S(2)}, u32[]{:S(2)}) collective-permute-start(bf16[512,384]{1,0:T(8,128)(2,1)S(1)} %pad_maximum_fusion.2), channel_id=1, source_target_pairs={{0,16},{4,20},{8,24},{12,28},{16,0},{20,4},{24,8},{28,12},{1,17},{... | collective-permute-start | bytes 1179656 | tf_op jit(solution)/shard_map/ppermute | solution.py:961
  573.4 19.3 %collective-permute-start.52 = (bf16[512,384]{1,0:T(8,128)(2,1)S(1)}, bf16[512,384]{1,0:T(8,128)(2,1)S(1)}, u32[]{:S(2)}, u32[]{:S(2)}) collective-permute-start(bf16[512,384]{1,0:T(8,128)(2,1)S(1)} %pad_maximum_fusion.2), channel_id=1, source_target_pairs={{0,24},{4,28},{8,16},{12,20},{16,8},{20,12},{24,0},{28,4},{1,25},{... | collective-permute-start | bytes 1179656 | tf_op jit(solution)/shard_map/ppermute | solution.py:961
  (81 other events, 718.0 us)

commit v8 on v7

--- a/solution.py
+++ b/solution.py
@@ -14,7 +14,7 @@
 MAXDIST = 128
 PAIR = 2 * HEAD_DIM
 PAIRS = HEADS // 2
-ROWS = 128
+ROWS = 256
 
 epsilon = 1e-06
 negative = -1e30
@@ -981,16 +981,6 @@
             piece = jnp.where(me ^ k == j, found[k], piece)
         joined.append(piece)
     return jnp.concatenate(joined)
-
-
-def sum_everywhere(values):
-    size = lax.axis_size("expert")
-    planes = lax.axis_size("hidden")
-    values = share_sums(values, "expert", 2, size // 2)
-    values = share_sums(values, "hidden", 1, planes)
-    values = join_sums(values, "hidden", 1, planes)
-    values = join_sums(values, "expert", 2, size // 2)
-    return values, swap(values, "expert", 1)
 
 
 def add_half(mine, other):
@@ -1219,8 +1209,21 @@
     diagonal, part, *first_part = back_half(batches - 1, 0, (), mixed_grad, (early_part,))
     first_half = add_half(*first_part)
     token_grad, *second_part = back_half(batches - 1, 1, (first_half,), mixed_grad, (diagonal, part, res_grad))
-    mine, other = sum_everywhere(first_half)
-    mine_second, other_second = sum_everywhere(add_half(*second_part))
+    far = groups // 2
+    first = share_sums(first_half, "expert", 2, far)
+    second_mine, second_other = second_part
+    (second_other,) = gate((second_other,), (first,))
+    first = share_sums(first, "hidden", 1, planes)
+    second = add_half(second_mine, second_other)
+    (first,) = gate((first,), (second,))
+    second = share_sums(second, "expert", 2, far)
+    first = join_sums(first, "hidden", 1, planes)
+    first = join_sums(first, "expert", 2, far)
+    second = share_sums(second, "hidden", 1, planes)
+    second = join_sums(second, "hidden", 1, planes)
+    second = join_sums(second, "expert", 2, far)
+    mine, other = first, swap(first, "expert", 1)
+    mine_second, other_second = second, swap(second, "expert", 1)
     query_grad, key_grad, value_grad, output_grad, router_grad, gain_f_grad, gain_a_grad, bias_grad = unpack(
         early_rows, experts, side, mine, other, mine_second, other_second
     )

time: 634 us -> 634 us (level)
  transfers between devices with their start and end apart: 76 -> 76, of which waited for: 37 -> 34; matrix products, arithmetic and copies ran while one was open for 1% -> 1% of each run, Pallas kernels for 37% -> 36%
where the time goes in v8:
time: 634 us; the launch traced here: 623 us
  Pallas kernels  263 us (41%)
  waiting for transfers between devices  178 us (28%)
  starting transfers between devices  150 us (24%)
  local copies, waits for them, and re-layouts  18.5 us (3%)
  other arithmetic  9.84 us (2%)
    ppermute x20, waiting for transfers between devices, send(): self.down = lax.ppermute(self.down, 'hidden', downward(planes, first, last))  92.3 us
    pallas_call x4, Pallas kernels, attention_backward(): pl.pallas_call(functools.partial(attn_back_kernel, batch, which, last, le...  56.8 us
    pallas_call x4, Pallas kernels, experts_half(): pl.pallas_call(functools.partial(expert_kernel, planes, gated, first, len...  55.9 us
    ppermute x20, starting transfers between devices, send(): self.up = lax.ppermute(self.up, 'hidden', upward(planes, first, last))  55 us
    ppermute x28, waiting for transfers between devices, swap(): lax.ppermute(values, axis, [(k, k ^ distance) for k in range(lax.axis_siz...  39.6 us
    all_to_all x8, starting transfers between devices, to_groups(): lax.all_to_all(values, 'expert', split_axis=0, concat_axis=0, tiled=True)  34.3 us
    ppermute x28, starting transfers between devices, swap(): lax.ppermute(values, axis, [(k, k ^ distance) for k in range(lax.axis_siz...  33.2 us
    pallas_call x2, Pallas kernels, expert_grads(): pl.pallas_call(functools.partial(expert_grad_kernel, batches, len(after))...  28.9 us
  transfers between devices with their start and end apart: 76, of which 34 were waited for; matrix products, arithmetic and copies ran while one was open for 1% of the time, Pallas kernels for 36%

profile of v8, /device:TPU:0, one launch (start us, length us, event | category | flops | bytes accessed | tf_op | source)
XLA Modules:
  0.0 622.7 jit_solution(17786081823868137847)
XLA Ops:
  5.6 5.2 all-to-all-start
  12.6 13.6 %shard_map.239 = (bf16[3,6,512,128]{3,2,1,0:T(8,128)(2,1)}, bf16[6,512,128]{2,1,0:T(8,128)(2,1)}, f32[512,128]{1,0:T(8,128)}) custom-call(bf16[8,80,768]{2,1,0:T(8,128)(2,1)} %get-tuple-element.116.refs_0_, s32[2]{0:T(128)} %bitcast.64, bf16[2,1,512,768]{3,2,1,0:T(8,128)(2,1)} %refs_9_.5, f32[1,768]{1,0:T(1,128)} %broadcast_in_dim.20.refs_3_.refs_5_.refs_9_.refs_8_.refs_10_, ...), custom_call_target="tpu_custom_call" | custom-call | flops 1 | bytes 1 | tf_op jit(solution)/shard_map/pallas_call | solution.py:278
  26.8 5.4 shard_map.240
  32.1 4.2 all-to-all-start.1
  44.4 8.8 %all-to-all-done.1.refs_1_ = bf16[8,96,768]{2,1,0:T(8,128)(2,1)S(1)} async-done(((bf16[8,96,768]{2,1,0:T(8,128)(2,1)}), bf16[8,96,768]{2,1,0:T(8,128)(2,1)S(1)}, u32[]{:S(2)}, u32[]{:S(2)}) %all-to-all-start.1) | async-done | bytes 1179680 | tf_op jit(solution)/shard_map/all_to_all | solution.py:1034
  71.2 13.6 %shard_map.243 = (bf16[3,6,512,128]{3,2,1,0:T(8,128)(2,1)}, bf16[6,512,128]{2,1,0:T(8,128)(2,1)}, f32[512,128]{1,0:T(8,128)}) custom-call(bf16[656,768]{1,0:T(8,128)(2,1)} %shard_map.242.refs_0_.refs_3_.refs_17_, bf16[640,768]{1,0:T(8,128)(2,1)} %copy-done.39, bf16[640,768]{1,0:T(8,128)(2,1)} %collective-permute-done.3.refs_2_.refs_11_, s32[2]{0:T(128)} %bitcast.65, ...), custom_call_target="tpu_custom_call" | custom-call | flops 1 | bytes 1 | tf_op jit(solution)/shard_map/pallas_call | solution.py:278
  86.6 4.9 collective-permute-done.1.refs_1_
  95.1 17.4 %collective-permute-done.8.refs_1_.refs_12_ = bf16[640,768]{1,0:T(8,128)(2,1)} collective-permute-done((bf16[640,768]{1,0:T(8,128)(2,1)}, bf16[640,768]{1,0:T(8,128)(2,1)}, u32[]{:S(2)}, u32[]{:S(2)}) %collective-permute-start.8) | collective-permute-done | bytes 983072 | tf_op jit(solution)/shard_map/ppermute | solution.py:929
  116.0 6.6 %shard_map.246 = (f32[512,768]{1,0:T(8,128)}, f32[512,64]{1,0:T(8,128)}, bf16[8,80,768]{2,1,0:T(8,128)(2,1)}, bf16[8,80,768]{2,1,0:T(8,128)(2,1)}) custom-call(bf16[640,768]{1,0:T(8,128)(2,1)} %collective-permute-done.6.refs_0_.refs_15_, bf16[640,768]{1,0:T(8,128)(2,1)} %collective-permute-done.8.refs_1_.refs_12_, bf16[2,1,512,768]{3,2,1,0:T(8,128)(2,1)} %refs_9_.5, ...), custom_call_target="tpu_custom_call" | custom-call | flops 1 | bytes 1 | tf_op jit(solution)/shard_map/pallas_call | solution.py:348
  122.6 4.2 all-to-all-start.3
  126.8 7.2 %collective-permute-done.5.refs_1_.refs_5_.refs_19_ = bf16[656,768]{1,0:T(8,128)(2,1)S(1)} collective-permute-done((bf16[656,768]{1,0:T(8,128)(2,1)}, bf16[656,768]{1,0:T(8,128)(2,1)S(1)}, u32[]{:S(2)}, u32[]{:S(2)}) %collective-permute-start.5) | collective-permute-done | bytes 1007648 | tf_op jit(solution)/shard_map/ppermute | solution.py:929
  136.9 4.7 all-to-all-done.3.refs_4_
  141.7 4.2 all-to-all-start.2
  145.9 9.2 %collective-permute-done.9.refs_3_.refs_13_ = bf16[640,768]{1,0:T(8,128)(2,1)S(1)} collective-permute-done((bf16[640,768]{1,0:T(8,128)(2,1)}, bf16[640,768]{1,0:T(8,128)(2,1)S(1)}, u32[]{:S(2)}, u32[]{:S(2)}) %collective-permute-start.9) | collective-permute-done | bytes 983072 | tf_op jit(solution)/shard_map/ppermute | solution.py:929
  165.3 4.8 collective-permute-start.10
  170.2 6.6 %collective-permute-done.12.refs_6_.refs_20_ = bf16[656,768]{1,0:T(8,128)(2,1)} collective-permute-done((bf16[656,768]{1,0:T(8,128)(2,1)S(1)}, bf16[656,768]{1,0:T(8,128)(2,1)}, u32[]{:S(2)}, u32[]{:S(2)}) %collective-permute-start.12) | collective-permute-done | bytes 1007648 | tf_op jit(solution)/shard_map/ppermute | solution.py:929
  178.1 14.0 %shard_map.252 = (bf16[2,320,768]{2,1,0:T(8,128)(2,1)}, bf16[2,320,768]{2,1,0:T(8,128)(2,1)}, bf16[2,320,768]{2,1,0:T(8,128)(2,1)}, bf16[2,320,768]{2,1,0:T(8,12...) custom-call(bf16[2,320,768]{2,1,0:T(8,128)(2,1)} %shard_map.248.refs, ...), custom_call_target="tpu_custom_call" | custom-call | flops 1 | bytes 1 | tf_op jit(solution)/shard_map/pallas_call | solution.py:445
  192.1 5.8 collective-permute-done.19.down_ref.refs_4_.refs_11_
  206.7 13.9 %shard_map.249 = (bf16[2,320,768]{2,1,0:T(8,128)(2,1)}, bf16[2,320,768]{2,1,0:T(8,128)(2,1)}, bf16[2,320,768]{2,1,0:T(8,128)(2,1)}, bf16[2,320,768]{2,1,0:T(8,12...) custom-call(bf16[2,320,768]{2,1,0:T(8,128)(2,1)} %shard_map.248.refs, ...), custom_call_target="tpu_custom_call" | custom-call | flops 1 | bytes 1 | tf_op jit(solution)/shard_map/pallas_call | solution.py:445
  224.2 4.6 collective-permute-start.14
  230.1 9.8 %collective-permute-done.21.down_ref.refs_5_.refs_12_ = bf16[2,320,768]{2,1,0:T(8,128)(2,1)S(1)} collective-permute-done((bf16[2,320,768]{2,1,0:T(8,128)(2,1)}, bf16[2,320,768]{2,1,0:T(8,128)(2,1)S(1)}, u32[]{:S(2)}, u32[]{:S(2)}) %collective-permute-start.21) | collective-permute-done | bytes 983072 | tf_op jit(solution)/shard_map/ppermute | solution.py:929
  243.7 7.2 %collective-permute-done.14.up_ref.refs_10_.refs_17_ = bf16[2,320,768]{2,1,0:T(8,128)(2,1)S(1)} collective-permute-done((bf16[2,320,768]{2,1,0:T(8,128)(2,1)S(1)}, bf16[2,320,768]{2,1,0:T(8,128)(2,1)S(1)}, u32[]{:S(2)}, u32[]{:S(2)}) %collective-permute-start.14) | collective-permute-done | bytes 983072 | tf_op jit(solution)/shard_map/ppermute | solution.py:928
  250.9 10.0 %collective-permute-done.15.down_ref.refs_7_.refs_14_ = bf16[2,320,768]{2,1,0:T(8,128)(2,1)S(1)} collective-permute-done((bf16[2,320,768]{2,1,0:T(8,128)(2,1)S(1)}, bf16[2,320,768]{2,1,0:T(8,128)(2,1)S(1)}, u32[]{:S(2)}, u32[]{:S(2)}) %collective-permute-start.15) | collective-permute-done | bytes 983072 | tf_op jit(solution)/shard_map/ppermute | solution.py:929
  265.7 6.3 %collective-permute-done.22.up_ref.refs_9_.refs_16_ = bf16[2,320,768]{2,1,0:T(8,128)(2,1)S(1)} collective-permute-done((bf16[2,320,768]{2,1,0:T(8,128)(2,1)S(1)}, bf16[2,320,768]{2,1,0:T(8,128)(2,1)S(1)}, u32[]{:S(2)}, u32[]{:S(2)}) %collective-permute-start.22) | collective-permute-done | bytes 983072 | tf_op jit(solution)/shard_map/ppermute | solution.py:928
  272.0 10.0 %collective-permute-done.23.down_ref.refs_6_.refs_13_ = bf16[2,320,768]{2,1,0:T(8,128)(2,1)S(1)} collective-permute-done((bf16[2,320,768]{2,1,0:T(8,128)(2,1)S(1)}, bf16[2,320,768]{2,1,0:T(8,128)(2,1)S(1)}, u32[]{:S(2)}, u32[]{:S(2)}) %collective-permute-start.23) | collective-permute-done | bytes 983072 | tf_op jit(solution)/shard_map/ppermute | solution.py:929
  287.9 14.0 %shard_map.256 = (bf16[2,320,768]{2,1,0:T(8,128)(2,1)}, bf16[2,320,768]{2,1,0:T(8,128)(2,1)}, bf16[2,320,768]{2,1,0:T(8,128)(2,1)}, bf16[2,320,768]{2,1,0:T(8,12...) custom-call(bf16[2,320,768]{2,1,0:T(8,128)(2,1)} %get-tuple-element., ...), custom_call_target="tpu_custom_call" | custom-call | flops 1 | bytes 1 | tf_op jit(solution)/shard_map/pallas_call | solution.py:445
  301.9 5.5 collective-permute-start.28
  315.7 8.6 %collective-permute-done.25.refs_3_.refs_4_ = bf16[2,320,768]{2,1,0:T(8,128)(2,1)} collective-permute-done((bf16[2,320,768]{2,1,0:T(8,128)(2,1)}, bf16[2,320,768]{2,1,0:T(8,128)(2,1)}, u32[]{:S(2)}, u32[]{:S(2)}) %collective-permute-start.25) | collective-permute-done | bytes 983072 | tf_op jit(solution)/shard_map/ppermute | solution.py:929
  324.3 14.0 %shard_map.258 = (bf16[2,320,768]{2,1,0:T(8,128)(2,1)}, bf16[2,320,768]{2,1,0:T(8,128)(2,1)}, bf16[2,320,768]{2,1,0:T(8,128)(2,1)}, bf16[2,320,768]{2,1,0:T(8,12...) custom-call(bf16[2,320,768]{2,1,0:T(8,128)(2,1)} %get-tuple-element., ...), custom_call_target="tpu_custom_call" | custom-call | flops 1 | bytes 1 | tf_op jit(solution)/shard_map/pallas_call | solution.py:445
  347.5 8.9 %collective-permute-done.34.refs_1_.refs_0_ = bf16[2,320,768]{2,1,0:T(8,128)(2,1)S(1)} collective-permute-done((bf16[2,320,768]{2,1,0:T(8,128)(2,1)}, bf16[2,320,768]{2,1,0:T(8,128)(2,1)S(1)}, u32[]{:S(2)}, u32[]{:S(2)}) %collective-permute-start.34) | collective-permute-done | bytes 983072 | tf_op jit(solution)/shard_map/ppermute | solution.py:928
  362.2 4.2 all-to-all-start.4
  366.5 14.5 %shard_map.260 = (f32[8,768,768]{2,1,0:T(8,128)}, f32[8,768,768]{2,1,0:T(8,128)}) custom-call(bf16[2,320,768]{2,1,0:T(8,128)(2,1)} %get-tuple-element.151.refs_0_, bf16[4,320,768]{2,1,0:T(8,128)(2,1)} %get-tuple-element.152.refs_1_, bf16[4,320,768]{2,1,0:T(8,128)(2,1)} %get-tuple-element.153.refs_2_, bf16[4,320,768]{2,1,0:T(8,128)(2,1)} %get-tuple-element.154.refs_3_, ...), custom_call_target="tpu_custom_call" | custom-call | flops 1 | bytes 1 | tf_op jit(solution)/shard_map/pallas_call | solution.py:474
  384.6 4.9 collective-permute-start.30
  395.0 4.5 all-to-all-start.5
  403.4 4.3 collective-permute-start.36
  409.0 5.3 all-to-all-done.5.refs_2_
  414.3 9.2 %shard_map.265 = (bf16[2,1,512,768]{3,2,1,0:T(8,128)(2,1)}, f32[512,768]{1,0:T(8,128)}, bf16[6,512,128]{2,1,0:T(8,128)(2,1)}, f32[1696,384]{1,0:T(8,128)}) custom-call(bf16[2,320,768]{2,1,0:T(8,128)(2,1)} %get-tuple-element.165.refs_0_, s32[2]{0:T(128)} %bitcast.67, bf16[8,80,768]{2,1,0:T(8,128)(2,1)} %all-to-all-done.5.refs_2_, ...), custom_call_target="tpu_custom_call" | custom-call | flops 1 | bytes 1 | tf_op jit(solution)/shard_map/pallas_call | solution.py:565
  427.2 4.2 collective-permute-start.38
  433.0 14.0 %shard_map.267 = (f32[16,1024]{1,0:T(8,128)}, f32[512,768]{1,0:T(8,128)}, f32[2304,384]{1,0:T(8,128)}) custom-call(bf16[2,320,768]{2,1,0:T(8,128)(2,1)} %copy-done.32, s32[1]{0:T(128)} %bitcast.5.refs_1_.refs_0_.refs_2_.side_ref, s32[2]{0:T(128)} %bitcast.68, bf16[3,6,512,128]{3,2,1,0:T(8,128)(2,1)} %get-tuple-element.172.refs_3_, ...), custom_call_target="tpu_custom_call" | custom-call | flops 1 | bytes 1 | tf_op jit(solution)/shard_map/pallas_call | solution.py:765
  454.4 14.4 %shard_map.269 = (bf16[2,1,512,768]{3,2,1,0:T(8,128)(2,1)}, f32[2560,384]{1,0:T(8,128)}) custom-call(bf16[8,80,768]{2,1,0:T(8,128)(2,1)} %shard_map.268.refs_0_, s32[1]{0:T(128)} %bitcast.5.refs_1_.refs_0_.refs_2_.side_ref, s32[2]{0:T(128)} %bitcast.69, bf16[3,6,512,128]{3,2,1,0:T(8,128)(2,1)} %get-tuple-element.172.refs_3_, ...), custom_call_target="tpu_custom_call" | custom-call | flops 1 | bytes 1 | tf_op jit(solution)/shard_map/pallas_call | solution.py:765
  473.9 4.1 all-to-all-start.7
  478.0 14.4 %shard_map.271 = (f32[8,768,768]{2,1,0:T(8,128)}, f32[8,768,768]{2,1,0:T(8,128)}) custom-call(bf16[8,80,768]{2,1,0:T(8,128)(2,1)} %shard_map.270.refs_0_, bf16[4,320,768]{2,1,0:T(8,128)(2,1)} %get-tuple-element.182.refs_1_, bf16[4,320,768]{2,1,0:T(8,128)(2,1)} %get-tuple-element.183.refs_2_, ...), custom_call_target="tpu_custom_call", output_to_operand_aliasing={{0}: (9, {}), {1}: (10, {})} | custom-call | flops 1 | bytes 1 | tf_op jit(solution)/shard_map/pallas_call | solution.py:474
  493.6 8.7 %shard_map.272 = (bf16[2,1,512,768]{3,2,1,0:T(8,128)(2,1)}, f32[512,768]{1,0:T(8,128)}, bf16[6,512,128]{2,1,0:T(8,128)(2,1)}, bf16[1696,384]{1,0:T(8,128)(2,1)}) custom-call(f32[8,768,768]{2,1,0:T(8,128)} %get-tuple-element.115.refs_0_, bf16[2,1,512,768]{3,2,1,0:T(8,128)(2,1)} %get-tuple-element.192.refs_1_, ...), custom_call_target="tpu_custom_call", output_to_operand_aliasing={{0}: (1, {})} | custom-call | flops 1 | bytes 1 | tf_op jit(solution)/shard_map/pallas_call | solution.py:565
  502.3 13.8 %shard_map.273 = (f32[16,1024]{1,0:T(8,128)}, f32[512,768]{1,0:T(8,128)}, bf16[2048,384]{1,0:T(8,128)(2,1)}, bf16[2048,384]{1,0:T(8,128)(2,1)}) custom-call(s32[1]{0:T(128)} %bitcast.5.refs_1_.refs_0_.refs_2_.side_ref, s32[2]{0:T(128)} %bitcast.71, bf16[3,6,512,128]{3,2,1,0:T(8,128)(2,1)} %get-tuple-element.198.refs_2_.refs_4_, ...), custom_call_target="tpu_custom_call" | custom-call | flops 1 | bytes 1 | tf_op jit(solution)/shard_map/pallas_call | solution.py:765
  525.4 14.6 %shard_map.274 = (bf16[2,1,512,768]{3,2,1,0:T(8,128)(2,1)}, bf16[1280,384]{1,0:T(8,128)(2,1)}, bf16[1280,384]{1,0:T(8,128)(2,1)}) custom-call(bf16[2048,384]{1,0:T(8,128)(2,1)} %copy-done.37, bf16[2,1,512,768]{3,2,1,0:T(8,128)(2,1)} %get-tuple-element.204.refs_1_, s32[1]{0:T(128)} %bitcast.5.refs_1_.refs_0_.refs_2_.side_ref, ...), custom_call_target="tpu_custom_call", output_to_operand_aliasing={{0}: (1, {})} | custom-call | flops 1 | bytes 1 | tf_op jit(solution)/shard_map/pallas_call | solution.py:765
  589.8 5.4 collective-permute-done.51
  596.7 8.0 %collective-permute-done.52 = bf16[512,384]{1,0:T(8,128)(2,1)S(1)} collective-permute-done((bf16[512,384]{1,0:T(8,128)(2,1)S(1)}, bf16[512,384]{1,0:T(8,128)(2,1)S(1)}, u32[]{:S(2)}, u32[]{:S(2)}) %collective-permute-start.52) | collective-permute-done | bytes 393248 | tf_op jit(solution)/shard_map/ppermute | solution.py:961
  615.8 6.5 %shard_map.277 = (f32[768,768]{1,0:T(8,128)}, f32[768,768]{1,0:T(8,128)}, f32[768,768]{1,0:T(8,128)}, f32[768,768]{1,0:T(8,128)}, f32[64,768]{1,0:T(8,128)}, /*i...) custom-call(s32[1]{0:T(128)} %bitcast.5.refs_1_.refs_0_.refs_2_.side_ref, bf16[2048,384]{1,0:T(8,128)(2,1)} %copy-done.42, ...), custom_call_target="tpu_custom_call" | custom-call | flops 1 | bytes 1 | tf_op jit(solution)/shard_map/pallas_call | solution.py:847
  (276 shorter events, 212.5 us)
Async XLA Ops:
  5.6 26.5 %all-to-all-start = ((bf16[8,80,768]{2,1,0:T(8,128)(2,1)}), bf16[8,80,768]{2,1,0:T(8,128)(2,1)S(1)}, u32[]{:S(2)}, u32[]{:S(2)}) async-start(bf16[8,80,768]{2,1,0:T(8,128)(2,1)} %get-tuple-element.116.refs_0_), calls=%async_computation | async-start | bytes 1966080 | tf_op jit(solution)/shard_map/all_to_all | solution.py:1034
  32.1 21.0 %all-to-all-start.1 = ((bf16[8,96,768]{2,1,0:T(8,128)(2,1)}), bf16[8,96,768]{2,1,0:T(8,128)(2,1)S(1)}, u32[]{:S(2)}, u32[]{:S(2)}) async-start(bf16[8,96,768]{2,1,0:T(8,128)(2,1)} %get-tuple-element.119.refs_0_), calls=%async_computation.1 | async-start | bytes 2359296 | tf_op jit(solution)/shard_map/all_to_all | solution.py:1034
  39.5 25.8 %collective-permute-start.2 = (bf16[640,768]{1,0:T(8,128)(2,1)}, bf16[640,768]{1,0:T(8,128)(2,1)S(1)}, u32[]{:S(2)}, u32[]{:S(2)}) collective-permute-start(bf16[640,768]{1,0:T(8,128)(2,1)} %shard_map.241.refs_0_.refs_10_), channel_id=1, source_target_pairs={{0,1},{1,2},{2,3},{4,5},{5,6},{6,7},{8,9},{9,10},{10,11},{12,13},{... | collective-permute-start | bytes 2949128 | tf_op jit(solution)/shard_map/ppermute | solution.py:928
  43.1 26.8 %collective-permute-start.3 = (bf16[640,768]{1,0:T(8,128)(2,1)}, bf16[640,768]{1,0:T(8,128)(2,1)}, u32[]{:S(2)}, u32[]{:S(2)}) collective-permute-start(bf16[640,768]{1,0:T(8,128)(2,1)} %shard_map.241.refs_0_.refs_10_), channel_id=1, source_target_pairs={{3,2},{2,1},{1,0},{7,6},{6,5},{5,4},{11,10},{10,9},{9,8},{15,14},{... | collective-permute-start | bytes 2949128 | tf_op jit(solution)/shard_map/ppermute | solution.py:929
  58.0 28.6 %collective-permute-start = (bf16[656,768]{1,0:T(8,128)(2,1)}, bf16[656,768]{1,0:T(8,128)(2,1)S(1)}, u32[]{:S(2)}, u32[]{:S(2)}) collective-permute-start(bf16[656,768]{1,0:T(8,128)(2,1)} %shard_map.242.refs_0_.refs_3_.refs_17_), channel_id=1, source_target_pairs={{0,1},{1,2},{2,3},{4,5},{5,6},{6,7},{8,9},{9,10},{10,11},{12,13},{... | collective-permute-start | bytes 3022856 | tf_op jit(solution)/shard_map/ppermute | solution.py:928
  61.7 29.8 %collective-permute-start.1 = (bf16[656,768]{1,0:T(8,128)(2,1)}, bf16[656,768]{1,0:T(8,128)(2,1)}, u32[]{:S(2)}, u32[]{:S(2)}) collective-permute-start(bf16[656,768]{1,0:T(8,128)(2,1)} %shard_map.242.refs_0_.refs_3_.refs_17_), channel_id=1, source_target_pairs={{3,2},{2,1},{1,0},{7,6},{6,5},{5,4},{11,10},{10,9},{9,8},{15,14},{... | collective-permute-start | bytes 3022856 | tf_op jit(solution)/shard_map/ppermute | solution.py:929
  65.4 29.0 %collective-permute-start.6 = (bf16[640,768]{1,0:T(8,128)(2,1)S(1)}, bf16[640,768]{1,0:T(8,128)(2,1)}, u32[]{:S(2)}, u32[]{:S(2)}) collective-permute-start(bf16[640,768]{1,0:T(8,128)(2,1)S(1)} %collective-permute-done.2.refs_1_.refs_14_), channel_id=1, source_target_pairs={{1,2},{2,3},{5,6},{6,7},{9,10},{10,11},{13,14},{14,15},{17,18},{18... | collective-permute-start | bytes 2949128 | tf_op jit(solution)/shard_map/ppermute | solution.py:928
  69.9 42.7 %collective-permute-start.8 = (bf16[640,768]{1,0:T(8,128)(2,1)}, bf16[640,768]{1,0:T(8,128)(2,1)}, u32[]{:S(2)}, u32[]{:S(2)}) collective-permute-start(bf16[640,768]{1,0:T(8,128)(2,1)} %collective-permute-done.3.refs_2_.refs_11_), channel_id=1, source_target_pairs={{2,1},{1,0},{6,5},{5,4},{10,9},{9,8},{14,13},{13,12},{18,17},{17,1... | collective-permute-start | bytes 2949128 | tf_op jit(solution)/shard_map/ppermute | solution.py:929
  91.5 42.5 %collective-permute-start.5 = (bf16[656,768]{1,0:T(8,128)(2,1)}, bf16[656,768]{1,0:T(8,128)(2,1)S(1)}, u32[]{:S(2)}, u32[]{:S(2)}) collective-permute-start(bf16[656,768]{1,0:T(8,128)(2,1)} %get-tuple-element.122.refs_4_.refs_18_), channel_id=1, source_target_pairs={{2,1},{1,0},{6,5},{5,4},{10,9},{9,8},{14,13},{13,12},{18,17},{17,1... | collective-permute-start | bytes 3022856 | tf_op jit(solution)/shard_map/ppermute | solution.py:929
  92.8 42.6 %collective-permute-start.4 = (bf16[656,768]{1,0:T(8,128)(2,1)}, bf16[656,768]{1,0:T(8,128)(2,1)}, u32[]{:S(2)}, u32[]{:S(2)}) collective-permute-start(bf16[656,768]{1,0:T(8,128)(2,1)} %get-tuple-element.121.refs_7_.refs_21_), channel_id=1, source_target_pairs={{1,2},{2,3},{5,6},{6,7},{9,10},{10,11},{13,14},{14,15},{17,18},{18... | collective-permute-start | bytes 3022856 | tf_op jit(solution)/shard_map/ppermute | solution.py:928
  94.4 51.5 %collective-permute-start.7 = (bf16[640,768]{1,0:T(8,128)(2,1)}, bf16[640,768]{1,0:T(8,128)(2,1)S(1)}, u32[]{:S(2)}, u32[]{:S(2)}) collective-permute-start(bf16[640,768]{1,0:T(8,128)(2,1)} %collective-permute-done.6.refs_0_.refs_15_), channel_id=1, source_target_pairs={{2,3},{6,7},{10,11},{14,15},{18,19},{22,23},{26,27},{30,31}} | collective-permute-start | bytes 2949128 | tf_op jit(solution)/shard_map/ppermute | solution.py:928
  112.5 42.6 %collective-permute-start.9 = (bf16[640,768]{1,0:T(8,128)(2,1)}, bf16[640,768]{1,0:T(8,128)(2,1)S(1)}, u32[]{:S(2)}, u32[]{:S(2)}) collective-permute-start(bf16[640,768]{1,0:T(8,128)(2,1)} %collective-permute-done.8.refs_1_.refs_12_), channel_id=1, source_target_pairs={{1,0},{5,4},{9,8},{13,12},{17,16},{21,20},{25,24},{29,28}} | collective-permute-start | bytes 2949128 | tf_op jit(solution)/shard_map/ppermute | solution.py:929
  134.0 42.8 %collective-permute-start.12 = (bf16[656,768]{1,0:T(8,128)(2,1)S(1)}, bf16[656,768]{1,0:T(8,128)(2,1)}, u32[]{:S(2)}, u32[]{:S(2)}) collective-permute-start(bf16[656,768]{1,0:T(8,128)(2,1)S(1)} %collective-permute-done.5.refs_1_.refs_5_.refs_19_), channel_id=1, source_target_pairs={{1,0},{5,4},{9,8},{13,12},{17,16},{21,20},{25,24},{29,28}} | collective-permute-start | bytes 3022856 | tf_op jit(solution)/shard_map/ppermute | solution.py:929
  135.3 42.8 %collective-permute-start.13 = (bf16[656,768]{1,0:T(8,128)(2,1)}, bf16[656,768]{1,0:T(8,128)(2,1)}, u32[]{:S(2)}, u32[]{:S(2)}) collective-permute-start(bf16[656,768]{1,0:T(8,128)(2,1)} %collective-permute-done.4.refs_0_.refs_8_.refs_22_), channel_id=1, source_target_pairs={{2,3},{6,7},{10,11},{14,15},{18,19},{22,23},{26,27},{30,31}} | collective-permute-start | bytes 3022856 | tf_op jit(solution)/shard_map/ppermute | solution.py:928
  141.7 20.6 %all-to-all-start.2 = ((bf16[8,80,768]{2,1,0:T(8,128)(2,1)}), bf16[8,80,768]{2,1,0:T(8,128)(2,1)}, u32[]{:S(2)}, u32[]{:S(2)}) async-start(bf16[8,80,768]{2,1,0:T(8,128)(2,1)} %get-tuple-element.124), calls=%async_computation.2 | async-start | bytes 1966080 | tf_op jit(solution)/shard_map/all_to_all | solution.py:1034
  159.3 32.8 %collective-permute-start.18 = (bf16[2,320,768]{2,1,0:T(8,128)(2,1)}, bf16[2,320,768]{2,1,0:T(8,128)(2,1)S(1)}, u32[]{:S(2)}, u32[]{:S(2)}) collective-permute-start(bf16[2,320,768]{2,1,0:T(8,128)(2,1)} %shard_map.248.refs_0_.refs_3_.refs_10_), channel_id=1, source_target_pairs={{0,1},{1,2},{2,3},{4,5},{5,6},{6,7},{8,9},{9,10},{10,11},{12,13},{... | collective-permute-start | bytes 2949128 | tf_op jit(solution)/shard_map/ppermute | solution.py:928
  160.9 37.0 %collective-permute-start.19 = (bf16[2,320,768]{2,1,0:T(8,128)(2,1)}, bf16[2,320,768]{2,1,0:T(8,128)(2,1)}, u32[]{:S(2)}, u32[]{:S(2)}) collective-permute-start(bf16[2,320,768]{2,1,0:T(8,128)(2,1)} %shard_map.248.refs_0_.refs_3_.refs_10_), channel_id=1, source_target_pairs={{3,2},{2,1},{1,0},{7,6},{6,5},{5,4},{11,10},{10,9},{9,8},{15,14},{... | collective-permute-start | bytes 2949128 | tf_op jit(solution)/shard_map/ppermute | solution.py:929
  165.3 55.3 %collective-permute-start.10 = (bf16[2,320,768]{2,1,0:T(8,128)(2,1)}, bf16[2,320,768]{2,1,0:T(8,128)(2,1)S(1)}, u32[]{:S(2)}, u32[]{:S(2)}) collective-permute-start(bf16[2,320,768]{2,1,0:T(8,128)(2,1)} %shard_map.247.refs_1_.refs_5_.refs_12_), channel_id=1, source_target_pairs={{0,1},{1,2},{2,3},{4,5},{5,6},{6,7},{8,9},{9,10},{10,11},{12,13},{... | collective-permute-start | bytes 2949128 | tf_op jit(solution)/shard_map/ppermute | solution.py:928
  176.8 43.9 %collective-permute-start.11 = (bf16[2,320,768]{2,1,0:T(8,128)(2,1)}, bf16[2,320,768]{2,1,0:T(8,128)(2,1)S(1)}, u32[]{:S(2)}, u32[]{:S(2)}) collective-permute-start(bf16[2,320,768]{2,1,0:T(8,128)(2,1)} %shard_map.247.refs_1_.refs_5_.refs_12_), channel_id=1, source_target_pairs={{3,2},{2,1},{1,0},{7,6},{6,5},{5,4},{11,10},{10,9},{9,8},{15,14},{... | collective-permute-start | bytes 2949128 | tf_op jit(solution)/shard_map/ppermute | solution.py:929
  203.9 26.2 %collective-permute-start.20 = (bf16[2,320,768]{2,1,0:T(8,128)(2,1)}, bf16[2,320,768]{2,1,0:T(8,128)(2,1)S(1)}, u32[]{:S(2)}, u32[]{:S(2)}) collective-permute-start(bf16[2,320,768]{2,1,0:T(8,128)(2,1)} %get-tuple-element.135), channel_id=1, source_target_pairs={{0,1},{1,2},{2,3},{4,5},{5,6},{6,7},{8,9},{9,10},{10,11},{12,13},{... | collective-permute-start | bytes 2949128 | tf_op jit(solution)/shard_map/ppermute | solution.py:928
  205.4 34.4 %collective-permute-start.21 = (bf16[2,320,768]{2,1,0:T(8,128)(2,1)}, bf16[2,320,768]{2,1,0:T(8,128)(2,1)S(1)}, u32[]{:S(2)}, u32[]{:S(2)}) collective-permute-start(bf16[2,320,768]{2,1,0:T(8,128)(2,1)} %get-tuple-element.136), channel_id=1, source_target_pairs={{3,2},{2,1},{1,0},{7,6},{6,5},{5,4},{11,10},{10,9},{9,8},{15,14},{... | collective-permute-start | bytes 2949128 | tf_op jit(solution)/shard_map/ppermute | solution.py:929
  224.2 26.7 %collective-permute-start.14 = (bf16[2,320,768]{2,1,0:T(8,128)(2,1)S(1)}, bf16[2,320,768]{2,1,0:T(8,128)(2,1)S(1)}, u32[]{:S(2)}, u32[]{:S(2)}) collective-permute-start(bf16[2,320,768]{2,1,0:T(8,128)(2,1)S(1)} %get-tuple-element.128), channel_id=1, source_target_pairs={{0,1},{1,2},{2,3},{4,5},{5,6},{6,7},{8,9},{9,10},{10,11},{12,13},{... | collective-permute-start | bytes 2949128 | tf_op jit(solution)/shard_map/ppermute | solution.py:928
  228.8 32.1 %collective-permute-start.15 = (bf16[2,320,768]{2,1,0:T(8,128)(2,1)S(1)}, bf16[2,320,768]{2,1,0:T(8,128)(2,1)S(1)}, u32[]{:S(2)}, u32[]{:S(2)}) collective-permute-start(bf16[2,320,768]{2,1,0:T(8,128)(2,1)S(1)} %get-tuple-element.129), channel_id=1, source_target_pairs={{3,2},{2,1},{1,0},{7,6},{6,5},{5,4},{11,10},{10,9},{9,8},{15,14},{... | collective-permute-start | bytes 2949128 | tf_op jit(solution)/shard_map/ppermute | solution.py:929
  240.8 31.2 %collective-permute-start.22 = (bf16[2,320,768]{2,1,0:T(8,128)(2,1)S(1)}, bf16[2,320,768]{2,1,0:T(8,128)(2,1)S(1)}, u32[]{:S(2)}, u32[]{:S(2)}) collective-permute-start(bf16[2,320,768]{2,1,0:T(8,128)(2,1)S(1)} %get-tuple-element.138), channel_id=1, source_target_pairs={{0,1},{1,2},{2,3},{4,5},{5,6},{6,7},{8,9},{9,10},{10,11},{12,13},{... | collective-permute-start | bytes 2949128 | tf_op jit(solution)/shard_map/ppermute | solution.py:928
  242.4 39.6 %collective-permute-start.23 = (bf16[2,320,768]{2,1,0:T(8,128)(2,1)S(1)}, bf16[2,320,768]{2,1,0:T(8,128)(2,1)S(1)}, u32[]{:S(2)}, u32[]{:S(2)}) collective-permute-start(bf16[2,320,768]{2,1,0:T(8,128)(2,1)S(1)} %get-tuple-element.139), channel_id=1, source_target_pairs={{3,2},{2,1},{1,0},{7,6},{6,5},{5,4},{11,10},{10,9},{9,8},{15,14},{... | collective-permute-start | bytes 2949128 | tf_op jit(solution)/shard_map/ppermute | solution.py:929
  262.9 44.6 %collective-permute-start.16 = (bf16[2,320,768]{2,1,0:T(8,128)(2,1)}, bf16[2,320,768]{2,1,0:T(8,128)(2,1)S(1)}, u32[]{:S(2)}, u32[]{:S(2)}) collective-permute-start(bf16[2,320,768]{2,1,0:T(8,128)(2,1)} %get-tuple-element.131), channel_id=1, source_target_pairs={{0,1},{1,2},{2,3},{4,5},{5,6},{6,7},{8,9},{9,10},{10,11},{12,13},{... | collective-permute-start | bytes 2949128 | tf_op jit(solution)/shard_map/ppermute | solution.py:928
  264.4 44.7 %collective-permute-start.17 = (bf16[2,320,768]{2,1,0:T(8,128)(2,1)}, bf16[2,320,768]{2,1,0:T(8,128)(2,1)S(1)}, u32[]{:S(2)}, u32[]{:S(2)}) collective-permute-start(bf16[2,320,768]{2,1,0:T(8,128)(2,1)} %get-tuple-element.132), channel_id=1, source_target_pairs={{3,2},{2,1},{1,0},{7,6},{6,5},{5,4},{11,10},{10,9},{9,8},{15,14},{... | collective-permute-start | bytes 2949128 | tf_op jit(solution)/shard_map/ppermute | solution.py:929
  284.0 30.2 %collective-permute-start.24 = (bf16[2,320,768]{2,1,0:T(8,128)(2,1)}, bf16[2,320,768]{2,1,0:T(8,128)(2,1)}, u32[]{:S(2)}, u32[]{:S(2)}) collective-permute-start(bf16[2,320,768]{2,1,0:T(8,128)(2,1)} %get-tuple-element.140.refs_0_), channel_id=1, source_target_pairs={{0,1},{1,2},{2,3},{4,5},{5,6},{6,7},{8,9},{9,10},{10,11},{12,13},{... | collective-permute-start | bytes 2949128 | tf_op jit(solution)/shard_map/ppermute | solution.py:928
  286.5 37.8 %collective-permute-start.25 = (bf16[2,320,768]{2,1,0:T(8,128)(2,1)}, bf16[2,320,768]{2,1,0:T(8,128)(2,1)}, u32[]{:S(2)}, u32[]{:S(2)}) collective-permute-start(bf16[2,320,768]{2,1,0:T(8,128)(2,1)} %get-tuple-element.141.refs_1_), channel_id=1, source_target_pairs={{3,2},{2,1},{1,0},{7,6},{6,5},{5,4},{11,10},{10,9},{9,8},{15,14},{... | collective-permute-start | bytes 2949128 | tf_op jit(solution)/shard_map/ppermute | solution.py:929
  301.9 37.9 %collective-permute-start.28 = (bf16[2,320,768]{2,1,0:T(8,128)(2,1)}, bf16[2,320,768]{2,1,0:T(8,128)(2,1)}, u32[]{:S(2)}, u32[]{:S(2)}) collective-permute-start(bf16[2,320,768]{2,1,0:T(8,128)(2,1)} %get-tuple-element.148.downsum_ref), channel_id=1, source_target_pairs={{0,1},{4,5},{8,9},{12,13},{16,17},{20,21},{24,25},{28,29}} | collective-permute-start | bytes 2949128 | tf_op jit(solution)/shard_map/ppermute | solution.py:928
  307.5 33.9 %collective-permute-start.29 = (bf16[2,320,768]{2,1,0:T(8,128)(2,1)}, bf16[2,320,768]{2,1,0:T(8,128)(2,1)}, u32[]{:S(2)}, u32[]{:S(2)}) collective-permute-start(bf16[2,320,768]{2,1,0:T(8,128)(2,1)} %get-tuple-element.149.upsum_ref), channel_id=1, source_target_pairs={{3,2},{7,6},{11,10},{15,14},{19,18},{23,22},{27,26},{31,30}} | collective-permute-start | bytes 2949128 | tf_op jit(solution)/shard_map/ppermute | solution.py:929
  312.5 43.9 %collective-permute-start.34 = (bf16[2,320,768]{2,1,0:T(8,128)(2,1)}, bf16[2,320,768]{2,1,0:T(8,128)(2,1)S(1)}, u32[]{:S(2)}, u32[]{:S(2)}) collective-permute-start(bf16[2,320,768]{2,1,0:T(8,128)(2,1)} %get-tuple-element.143.refs_0_), channel_id=1, source_target_pairs={{0,1},{1,2},{2,3},{4,5},{5,6},{6,7},{8,9},{9,10},{10,11},{12,13},{... | collective-permute-start | bytes 2949128 | tf_op jit(solution)/shard_map/ppermute | solution.py:928
  314.2 44.2 %collective-permute-start.35 = (bf16[2,320,768]{2,1,0:T(8,128)(2,1)}, bf16[2,320,768]{2,1,0:T(8,128)(2,1)}, u32[]{:S(2)}, u32[]{:S(2)}) collective-permute-start(bf16[2,320,768]{2,1,0:T(8,128)(2,1)} %get-tuple-element.144.refs_1_), channel_id=1, source_target_pairs={{3,2},{2,1},{1,0},{7,6},{6,5},{5,4},{11,10},{10,9},{9,8},{15,14},{... | collective-permute-start | bytes 2949128 | tf_op jit(solution)/shard_map/ppermute | solution.py:929
  338.3 42.7 %collective-permute-start.26 = (bf16[2,320,768]{2,1,0:T(8,128)(2,1)}, bf16[2,320,768]{2,1,0:T(8,128)(2,1)S(1)}, u32[]{:S(2)}, u32[]{:S(2)}) collective-permute-start(bf16[2,320,768]{2,1,0:T(8,128)(2,1)} %get-tuple-element.145.downsum_ref), channel_id=1, source_target_pairs={{0,1},{4,5},{8,9},{12,13},{16,17},{20,21},{24,25},{28,29}} | collective-permute-start | bytes 2949128 | tf_op jit(solution)/shard_map/ppermute | solution.py:928
  339.8 41.2 %collective-permute-start.27 = (bf16[2,320,768]{2,1,0:T(8,128)(2,1)}, bf16[2,320,768]{2,1,0:T(8,128)(2,1)}, u32[]{:S(2)}, u32[]{:S(2)}) collective-permute-start(bf16[2,320,768]{2,1,0:T(8,128)(2,1)} %get-tuple-element.146.upsum_ref), channel_id=1, source_target_pairs={{3,2},{7,6},{11,10},{15,14},{19,18},{23,22},{27,26},{31,30}} | collective-permute-start | bytes 2949128 | tf_op jit(solution)/shard_map/ppermute | solution.py:929
  345.3 54.2 %collective-permute-start.32 = (bf16[2,320,768]{2,1,0:T(8,128)(2,1)}, bf16[2,320,768]{2,1,0:T(8,128)(2,1)}, u32[]{:S(2)}, u32[]{:S(2)}) collective-permute-start(bf16[2,320,768]{2,1,0:T(8,128)(2,1)} %get-tuple-element.151.refs_0_), channel_id=1, source_target_pairs={{0,1},{1,2},{4,5},{5,6},{8,9},{9,10},{12,13},{13,14},{16,17},{17,1... | collective-permute-start | bytes 2949128 | tf_op jit(solution)/shard_map/ppermute | solution.py:928
  356.4 43.1 %collective-permute-start.33 = (bf16[2,320,768]{2,1,0:T(8,128)(2,1)}, bf16[2,320,768]{2,1,0:T(8,128)(2,1)}, u32[]{:S(2)}, u32[]{:S(2)}) collective-permute-start(bf16[2,320,768]{2,1,0:T(8,128)(2,1)} %get-tuple-element.163), channel_id=1, source_target_pairs={{3,2},{2,1},{7,6},{6,5},{11,10},{10,9},{15,14},{14,13},{19,18},{18... | collective-permute-start | bytes 2949128 | tf_op jit(solution)/shard_map/ppermute | solution.py:929
  362.2 32.7 %all-to-all-start.4 = ((bf16[8,80,768]{2,1,0:T(8,128)(2,1)}), bf16[8,80,768]{2,1,0:T(8,128)(2,1)S(1)}, u32[]{:S(2)}, u32[]{:S(2)}) async-start(bf16[8,80,768]{2,1,0:T(8,128)(2,1)} %shard_map.262), calls=%async_computation.4 | async-start | bytes 1966080 | tf_op jit(solution)/shard_map/all_to_all | solution.py:1034
  384.6 38.9 %collective-permute-start.30 = (bf16[2,320,768]{2,1,0:T(8,128)(2,1)}, bf16[2,320,768]{2,1,0:T(8,128)(2,1)}, u32[]{:S(2)}, u32[]{:S(2)}) collective-permute-start(bf16[2,320,768]{2,1,0:T(8,128)(2,1)} %get-tuple-element.161), channel_id=1, source_target_pairs={{0,1},{1,2},{4,5},{5,6},{8,9},{9,10},{12,13},{13,14},{16,17},{17,1... | collective-permute-start | bytes 2949128 | tf_op jit(solution)/shard_map/ppermute | solution.py:928
  389.6 33.9 %collective-permute-start.31 = (bf16[2,320,768]{2,1,0:T(8,128)(2,1)}, bf16[2,320,768]{2,1,0:T(8,128)(2,1)}, u32[]{:S(2)}, u32[]{:S(2)}) collective-permute-start(bf16[2,320,768]{2,1,0:T(8,128)(2,1)} %get-tuple-element.162), channel_id=1, source_target_pairs={{3,2},{2,1},{7,6},{6,5},{11,10},{10,9},{15,14},{14,13},{19,18},{18... | collective-permute-start | bytes 2949128 | tf_op jit(solution)/shard_map/ppermute | solution.py:929
  403.4 43.6 %collective-permute-start.36 = (bf16[2,320,768]{2,1,0:T(8,128)(2,1)}, bf16[2,320,768]{2,1,0:T(8,128)(2,1)}, u32[]{:S(2)}, u32[]{:S(2)}) collective-permute-start(bf16[2,320,768]{2,1,0:T(8,128)(2,1)} %get-tuple-element.165.refs_0_), channel_id=1, source_target_pairs={{0,1},{1,2},{2,3},{4,5},{5,6},{6,7},{8,9},{9,10},{10,11},{12,13},{... | collective-permute-start | bytes 2949128 | tf_op jit(solution)/shard_map/ppermute | solution.py:928
  407.7 39.3 %collective-permute-start.37 = (bf16[2,320,768]{2,1,0:T(8,128)(2,1)}, bf16[2,320,768]{2,1,0:T(8,128)(2,1)}, u32[]{:S(2)}, u32[]{:S(2)}) collective-permute-start(bf16[2,320,768]{2,1,0:T(8,128)(2,1)} %get-tuple-element.175), channel_id=1, source_target_pairs={{3,2},{2,1},{1,0},{7,6},{6,5},{5,4},{11,10},{10,9},{9,8},{15,14},{... | collective-permute-start | bytes 2949128 | tf_op jit(solution)/shard_map/ppermute | solution.py:929
  427.2 41.8 %collective-permute-start.38 = (bf16[2,320,768]{2,1,0:T(8,128)(2,1)S(1)}, bf16[2,320,768]{2,1,0:T(8,128)(2,1)}, u32[]{:S(2)}, u32[]{:S(2)}) collective-permute-start(bf16[2,320,768]{2,1,0:T(8,128)(2,1)S(1)} %get-tuple-element.171.refs_0_), channel_id=1, source_target_pairs={{0,1},{1,2},{2,3},{4,5},{5,6},{6,7},{8,9},{9,10},{10,11},{12,13},{... | collective-permute-start | bytes 2949128 | tf_op jit(solution)/shard_map/ppermute | solution.py:928
  431.5 37.6 %collective-permute-start.39 = (bf16[2,320,768]{2,1,0:T(8,128)(2,1)S(1)}, bf16[2,320,768]{2,1,0:T(8,128)(2,1)}, u32[]{:S(2)}, u32[]{:S(2)}) collective-permute-start(bf16[2,320,768]{2,1,0:T(8,128)(2,1)S(1)} %get-tuple-element.181), channel_id=1, source_target_pairs={{3,2},{2,1},{1,0},{7,6},{6,5},{5,4},{11,10},{10,9},{9,8},{15,14},{... | collective-permute-start | bytes 2949128 | tf_op jit(solution)/shard_map/ppermute | solution.py:929
  584.5 20.2 %collective-permute-start.52 = (bf16[512,384]{1,0:T(8,128)(2,1)S(1)}, bf16[512,384]{1,0:T(8,128)(2,1)S(1)}, u32[]{:S(2)}, u32[]{:S(2)}) collective-permute-start(bf16[512,384]{1,0:T(8,128)(2,1)S(1)} %pad_maximum_fusion.2), channel_id=1, source_target_pairs={{0,16},{4,20},{8,24},{12,28},{16,0},{20,4},{24,8},{28,12},{1,17},{... | collective-permute-start | bytes 1179656 | tf_op jit(solution)/shard_map/ppermute | solution.py:961
  585.2 19.5 %collective-permute-start.53 = (bf16[512,384]{1,0:T(8,128)(2,1)S(1)}, bf16[512,384]{1,0:T(8,128)(2,1)S(1)}, u32[]{:S(2)}, u32[]{:S(2)}) collective-permute-start(bf16[512,384]{1,0:T(8,128)(2,1)S(1)} %pad_maximum_fusion.2), channel_id=1, source_target_pairs={{0,24},{4,28},{8,16},{12,20},{16,8},{20,12},{24,0},{28,4},{1,25},{... | collective-permute-start | bytes 1179656 | tf_op jit(solution)/shard_map/ppermute | solution.py:961
  587.7 20.3 %collective-permute-start.64 = (bf16[320,384]{1,0:T(8,128)(2,1)S(1)}, bf16[320,384]{1,0:T(8,128)(2,1)S(1)}, u32[]{:S(2)}, u32[]{:S(2)}) collective-permute-start(bf16[320,384]{1,0:T(8,128)(2,1)S(1)} %pad_maximum_fusion.3), channel_id=1, source_target_pairs={{0,8},{4,12},{8,0},{12,4},{16,24},{20,28},{24,16},{28,20},{1,9},{5... | collective-permute-start | bytes 737288 | tf_op jit(solution)/shard_map/ppermute | solution.py:961
  589.1 20.0 %collective-permute-start.65 = (bf16[320,384]{1,0:T(8,128)(2,1)S(1)}, bf16[320,384]{1,0:T(8,128)(2,1)S(1)}, u32[]{:S(2)}, u32[]{:S(2)}) collective-permute-start(bf16[320,384]{1,0:T(8,128)(2,1)S(1)} %pad_maximum_fusion.3), channel_id=1, source_target_pairs={{0,16},{4,20},{8,24},{12,28},{16,0},{20,4},{24,8},{28,12},{1,17},{... | collective-permute-start | bytes 737288 | tf_op jit(solution)/shard_map/ppermute | solution.py:961
  (81 other events, 737.3 us)
